TPU v7x, 32 devices: a whole 2x2x4 slice. The times are simulated.
32 devices in a mesh: rep: 8 (over y, x, core), fsdp: 4 (over z).
Axes of the slice: x: 2, y: 2, z: 4, core: 2. Of those that a mesh axis runs over, the one named last changes fastest.
Arguments:
- inputs: bfloat16 [4096, 2048], P(('rep', 'fsdp')), may hold values from -6 to 6
- doc_lengths: int32 [8, 8], P('rep'), may hold values from 1 to 385, as said below
- attn_gain: bfloat16 [2048], P('fsdp'), may hold values from 0.25 to 1.75
- query_weight: bfloat16 [2048, 2048], P('fsdp'), may hold values from -0.125 to 0.125
- key_projection: bfloat16 [2048, 512], P('fsdp'), may hold values from -0.125 to 0.125
- value_projection: bfloat16 [2048, 512], P('fsdp'), may hold values from -0.125 to 0.125
- query_gain: bfloat16 [64], P('fsdp'), may hold values from 0.099609375 to 1.8984375
- key_norm_gain: bfloat16 [64], P('fsdp'), may hold values from 0.099609375 to 1.8984375
- out_weight: bfloat16 [2048, 2048], P('fsdp'), may hold values from -0.5 to 0.5
- ffn_gain: bfloat16 [2048], P('fsdp'), may hold values from 0.25 to 1.75
- gate_weight: bfloat16 [2048, 8192], P('fsdp'), may hold values from -0.125 to 0.125
- up_weight: bfloat16 [2048, 8192], P('fsdp'), may hold values from -0.125 to 0.125
- down_weight: bfloat16 [8192, 2048], P('fsdp'), may hold values from -0.0625 to 0.0625
- cotangent: bfloat16 [4096, 2048], P(('rep', 'fsdp')), may hold values from -6 to 6
Outputs:
- output: bfloat16 [4096, 2048], P(('rep', 'fsdp'))
- input_grad: bfloat16 [4096, 2048], P(('rep', 'fsdp'))
- attn_gain_grad: float32 [2048], P('fsdp')
- query_weight_grad: float32 [2048, 2048], P('fsdp')
- key_weight_grad: float32 [2048, 512], P('fsdp')
- value_weight_grad: float32 [2048, 512], P('fsdp')
- query_gain_grad: float32 [64], P('fsdp')
- key_gain_grad: float32 [64], P('fsdp')
- out_weight_grad: float32 [2048, 2048], P('fsdp')
- ffn_gain_grad: float32 [2048], P('fsdp')
- gate_weight_grad: float32 [2048, 8192], P('fsdp')
- up_weight_grad: float32 [2048, 8192], P('fsdp')
- down_weight_grad: float32 [8192, 2048], P('fsdp')
Inputs may be any that keep to these rules, and one draw needn't show every extreme that they name: `doc_lengths`: each row lists the lengths of 8 documents packed in order into the 512 tokens of one sequence and sums to 512; in each row one document, at a place drawn from the seed, has exactly 385 tokens, starts before position 128 and ends at or after position 384.
All inputs are finite; a program needn't handle non-finite values.
Results may differ from a plain program's by a relative error of at most 0.019.
Values may be sent and summed in bfloat16 or wider, within the bound.
No kernel may reach another device: no remote copies, remote signals or barrier semaphores. Data moves between devices by JAX's collectives and lax.ppermute only.
A program may use at most 448 MiB of HBM per device.

v0:
```python
import jax
import jax.numpy as jnp
from jax import lax
from jax.sharding import PartitionSpec as P

HEAD_SIZE = 64


EPSILON = 1e-05
THETA_BASE = 1000000.0
NEG_FILL = -1e30
CONTRACT_LAST = (((1,), (1,)), ((), ()))
CONTRACT_FIRST = (((0,), (0,)), ((), ()))


def rotary_tables(positions, head_dim):
    half_dim = head_dim // 2
    inverse = THETA_BASE ** (-(jnp.arange(half_dim, dtype=jnp.float32) * 2.0) / head_dim)
    angles = positions.astype(jnp.float32)[:, None] * inverse[None, :]
    return (jnp.cos(angles)[:, None, :], jnp.sin(angles)[:, None, :])


def apply_rotary(values, cosine_table, sine_values):
    half_dim = values.shape[-1] // 2
    first_part = values[..., :half_dim]
    second_part = values[..., half_dim:]
    return jnp.concatenate(
        [
            first_part * cosine_table - second_part * sine_values,
            second_part * cosine_table + first_part * sine_values,
        ],
        axis=-1,
    )


def unit_rows(values):
    inverse = lax.rsqrt(jnp.mean(values * values, axis=-1, keepdims=True) + EPSILON)
    return (values * inverse, inverse)


def unit_back(grad_unit, unit_vals, inverse):
    return inverse * (
        grad_unit - unit_vals * jnp.mean(grad_unit * unit_vals, axis=-1, keepdims=True)
    )


def dot_last(left_side, right_side):
    return lax.dot_general(left_side, right_side, CONTRACT_LAST, preferred_element_type=jnp.float32)


def dot_first(left_side, right_side):
    return lax.dot_general(
        left_side, right_side, CONTRACT_FIRST, preferred_element_type=jnp.float32
    )


def head_scores(query_block, key_block, allowed, score_scale):
    scores = (
        jnp.einsum("tgd,sd->tgs", query_block, key_block, preferred_element_type=jnp.float32)
        * score_scale
    )
    return jnp.where(allowed[:, None, :], scores, NEG_FILL)


def attend_heads(grouped_heads, keys_all, values_all, allowed, score_scale):
    outputs = []
    maxima = []
    totals = []
    for head_idx in range(grouped_heads.shape[1]):
        scores = head_scores(
            grouped_heads[:, head_idx], keys_all[:, head_idx], allowed, score_scale
        )
        row_max = jnp.max(scores, axis=-1, keepdims=True)
        expo_terms = jnp.exp(scores - row_max)
        row_sum = jnp.sum(expo_terms, axis=-1, keepdims=True)
        probs_low = (expo_terms / row_sum).astype(jnp.bfloat16)
        outputs.append(
            jnp.einsum(
                "tgs,sd->tgd",
                probs_low,
                values_all[:, head_idx],
                preferred_element_type=jnp.float32,
            )
        )
        maxima.append(row_max)
        totals.append(row_sum)
    return (jnp.stack(outputs, axis=1), jnp.stack(maxima, axis=1), jnp.stack(totals, axis=1))


def attend_back(
    grouped_heads, keys_all, values_all, allowed, score_scale, grad_grouped, maxima, totals
):
    query_terms = []
    key_terms = []
    value_terms = []
    for head_idx in range(grouped_heads.shape[1]):
        query_block = grouped_heads[:, head_idx]
        key_block = keys_all[:, head_idx]
        grad_block = grad_grouped[:, head_idx]
        scores = head_scores(query_block, key_block, allowed, score_scale)
        probs = jnp.exp(scores - maxima[:, head_idx]) / totals[:, head_idx]
        grad_probs = jnp.einsum(
            "tgd,sd->tgs", grad_block, values_all[:, head_idx], preferred_element_type=jnp.float32
        )
        row_delta = jnp.sum(probs * grad_probs, axis=-1, keepdims=True)
        grad_scores = (probs * (grad_probs - row_delta)).astype(jnp.bfloat16)
        query_terms.append(
            jnp.einsum("tgs,sd->tgd", grad_scores, key_block, preferred_element_type=jnp.float32)
            * score_scale
        )
        key_terms.append(
            jnp.einsum("tgs,tgd->sd", grad_scores, query_block, preferred_element_type=jnp.float32)
            * score_scale
        )
        value_terms.append(
            jnp.einsum(
                "tgs,tgd->sd",
                probs.astype(jnp.bfloat16),
                grad_block,
                preferred_element_type=jnp.float32,
            )
        )
    return (
        jnp.stack(query_terms, axis=1),
        jnp.stack(key_terms, axis=1),
        jnp.stack(value_terms, axis=1),
    )


def shards(
    inputs,
    doc_lengths,
    attn_gain,
    query_weight,
    key_projection,
    value_projection,
    query_gain,
    key_norm_gain,
    out_weight,
    ffn_gain,
    gate_weight,
    up_weight,
    down_weight,
    cotangent,
):
    tok_rows, model_width = inputs.shape
    fsdp_count = lax.axis_size("fsdp")
    seq_len = tok_rows * fsdp_count
    head_dim = HEAD_SIZE
    query_heads = query_weight.shape[1] // head_dim
    kv_heads = key_projection.shape[1] // head_dim
    groups = query_heads // kv_heads
    score_scale = head_dim ** (-0.5)
    shard_index = lax.axis_index("fsdp")
    row_start = shard_index * tok_rows
    all_positions = jnp.arange(seq_len, dtype=jnp.int32)
    doc_ends = jnp.cumsum(doc_lengths[0])
    seg_all = jnp.sum((all_positions[:, None] >= doc_ends[None, :]).astype(jnp.int32), axis=1)
    query_pos = row_start + jnp.arange(tok_rows, dtype=jnp.int32)
    query_seg = lax.dynamic_slice_in_dim(seg_all, row_start, tok_rows)
    allowed = (query_seg[:, None] == seg_all[None, :]) & (
        all_positions[None, :] <= query_pos[:, None]
    )
    cosine_table, sine_values = rotary_tables(query_pos, head_dim)
    gain_one, gain_two, gain_query, gain_key, query_full, key_full, value_full, out_full = (
        lax.all_gather(attn_gain, "fsdp", axis=0, tiled=True),
        lax.all_gather(ffn_gain, "fsdp", axis=0, tiled=True),
        lax.all_gather(query_gain, "fsdp", axis=0, tiled=True),
        lax.all_gather(key_norm_gain, "fsdp", axis=0, tiled=True),
        lax.all_gather(query_weight, "fsdp", axis=0, tiled=True),
        lax.all_gather(key_projection, "fsdp", axis=0, tiled=True),
        lax.all_gather(value_projection, "fsdp", axis=0, tiled=True),
        lax.all_gather(out_weight, "fsdp", axis=0, tiled=True),
    )
    gain_one = gain_one.astype(jnp.float32)
    gain_two = gain_two.astype(jnp.float32)
    gain_query = gain_query.astype(jnp.float32)
    gain_key = gain_key.astype(jnp.float32)
    inputs_wide = inputs.astype(jnp.float32)
    unit_one, inverse_one = unit_rows(inputs_wide)
    normed_one = (unit_one * gain_one).astype(jnp.bfloat16)
    query_pre = jnp.dot(normed_one, query_full, preferred_element_type=jnp.float32).reshape(
        tok_rows, query_heads, head_dim
    )
    key_before_norm = jnp.dot(normed_one, key_full, preferred_element_type=jnp.float32).reshape(
        tok_rows, kv_heads, head_dim
    )
    value_matrix = jnp.dot(normed_one, value_full, preferred_element_type=jnp.float32).astype(
        jnp.bfloat16
    )
    query_unit, query_inverse = unit_rows(query_pre)
    key_unit, key_inverse = unit_rows(key_before_norm)
    query_rows = apply_rotary(query_unit * gain_query, cosine_table, sine_values).astype(
        jnp.bfloat16
    )
    rotated_keys = apply_rotary(key_unit * gain_key, cosine_table, sine_values).astype(jnp.bfloat16)
    keys_all, values_all = (
        lax.all_gather(
            rotated_keys.reshape(tok_rows, kv_heads * head_dim), "fsdp", axis=0, tiled=True
        ),
        lax.all_gather(value_matrix, "fsdp", axis=0, tiled=True),
    )
    keys_all = keys_all.reshape(seq_len, kv_heads, head_dim)
    values_all = values_all.reshape(seq_len, kv_heads, head_dim)
    grouped_heads = query_rows.reshape(tok_rows, kv_heads, groups, head_dim)
    attended, maxima, totals = attend_heads(
        grouped_heads, keys_all, values_all, allowed, score_scale
    )
    attended_low = attended.astype(jnp.bfloat16).reshape(tok_rows, query_heads * head_dim)
    hidden_one = inputs_wide + jnp.dot(attended_low, out_full, preferred_element_type=jnp.float32)
    unit_two, inverse_two = unit_rows(hidden_one)
    normed_two = (unit_two * gain_two).astype(jnp.bfloat16)
    columns = normed_two
    gate_pre = jnp.dot(
        columns,
        lax.all_gather(gate_weight, "fsdp", axis=0, tiled=True),
        preferred_element_type=jnp.float32,
    )
    upward = jnp.dot(
        columns,
        lax.all_gather(up_weight, "fsdp", axis=0, tiled=True),
        preferred_element_type=jnp.float32,
    )
    sigmoid_gate = jax.nn.sigmoid(gate_pre)
    silu_gate = gate_pre * sigmoid_gate
    hidden = (silu_gate * upward).astype(jnp.bfloat16)
    columns = hidden
    mlp_out = jnp.dot(
        columns,
        lax.all_gather(down_weight, "fsdp", axis=0, tiled=True),
        preferred_element_type=jnp.float32,
    )
    output = (hidden_one + mlp_out).astype(jnp.bfloat16)
    grad_hidden = dot_last(cotangent, lax.all_gather(down_weight, "fsdp", axis=0, tiled=True))
    grad_gate = (
        grad_hidden * upward * sigmoid_gate * (1.0 + gate_pre * (1.0 - sigmoid_gate))
    ).astype(jnp.bfloat16)
    grad_up = (grad_hidden * silu_gate).astype(jnp.bfloat16)
    gate_full, up_full, query_back, key_back, value_back, out_back = (
        lax.all_gather(gate_weight, "fsdp", axis=0, tiled=True),
        lax.all_gather(up_weight, "fsdp", axis=0, tiled=True),
        lax.all_gather(query_weight, "fsdp", axis=0, tiled=True),
        lax.all_gather(key_projection, "fsdp", axis=0, tiled=True),
        lax.all_gather(value_projection, "fsdp", axis=0, tiled=True),
        lax.all_gather(out_weight, "fsdp", axis=0, tiled=True),
    )
    grad_normed_two = dot_last(grad_gate, gate_full) + dot_last(grad_up, up_full)
    gain_two_sum = jnp.sum(grad_normed_two * unit_two, axis=0)
    grad_hidden_one = cotangent.astype(jnp.float32) + unit_back(
        grad_normed_two * gain_two, unit_two, inverse_two
    )
    grad_attn = grad_hidden_one.astype(jnp.bfloat16)
    grad_attended = (
        dot_last(grad_attn, out_back)
        .astype(jnp.bfloat16)
        .reshape(tok_rows, kv_heads, groups, head_dim)
    )
    grad_grouped, key_terms, value_terms = attend_back(
        grouped_heads, keys_all, values_all, allowed, score_scale, grad_attended, maxima, totals
    )
    grad_keys, grad_values = (
        lax.psum_scatter(
            key_terms.reshape(seq_len, kv_heads * head_dim).astype(jnp.bfloat16),
            "fsdp",
            scatter_dimension=0,
            tiled=True,
        ).astype(jnp.float32),
        lax.psum_scatter(
            value_terms.reshape(seq_len, kv_heads * head_dim).astype(jnp.bfloat16),
            "fsdp",
            scatter_dimension=0,
            tiled=True,
        ).astype(jnp.float32),
    )
    grad_query_unit = apply_rotary(
        grad_grouped.reshape(tok_rows, query_heads, head_dim), cosine_table, -sine_values
    )
    grad_key_unit = apply_rotary(
        grad_keys.reshape(tok_rows, kv_heads, head_dim), cosine_table, -sine_values
    )
    query_gain_sum = jnp.sum(grad_query_unit * query_unit, axis=(0, 1))
    key_gain_sum = jnp.sum(grad_key_unit * key_unit, axis=(0, 1))
    grad_query_pre = (
        unit_back(grad_query_unit * gain_query, query_unit, query_inverse)
        .astype(jnp.bfloat16)
        .reshape(tok_rows, query_heads * head_dim)
    )
    grad_key_pre = (
        unit_back(grad_key_unit * gain_key, key_unit, key_inverse)
        .astype(jnp.bfloat16)
        .reshape(tok_rows, kv_heads * head_dim)
    )
    grad_value_rows = grad_values.astype(jnp.bfloat16)
    grad_normed_one = (
        dot_last(grad_query_pre, query_back)
        + dot_last(grad_key_pre, key_back)
        + dot_last(grad_value_rows, value_back)
    )
    gain_one_sum = jnp.sum(grad_normed_one * unit_one, axis=0)
    input_grad = (
        grad_hidden_one + unit_back(grad_normed_one * gain_one, unit_one, inverse_one)
    ).astype(jnp.bfloat16)
    grad_proj = jnp.concatenate([grad_query_pre, grad_key_pre, grad_value_rows], axis=1)
    query_cols = query_heads * head_dim
    kv_cols = kv_heads * head_dim
    swap_two, swap_one, swap_attended, swap_hidden = (
        lax.all_to_all(normed_two, "fsdp", split_axis=1, concat_axis=0, tiled=True),
        lax.all_to_all(normed_one, "fsdp", split_axis=1, concat_axis=0, tiled=True),
        lax.all_to_all(attended_low, "fsdp", split_axis=1, concat_axis=0, tiled=True),
        lax.all_to_all(hidden, "fsdp", split_axis=1, concat_axis=0, tiled=True),
    )
    piece_gate = lax.all_gather(grad_gate, "fsdp", axis=0, tiled=True)
    piece_up = lax.all_gather(grad_up, "fsdp", axis=0, tiled=True)
    piece_cot = lax.all_gather(cotangent, "fsdp", axis=0, tiled=True)
    piece_proj = lax.all_gather(grad_proj, "fsdp", axis=0, tiled=True)
    piece_attn = lax.all_gather(grad_attn, "fsdp", axis=0, tiled=True)
    gate_weight_grad, up_weight_grad, down_weight_grad, proj_grad, out_weight_grad = (
        lax.psum(dot_first(swap_two, piece_gate).astype(jnp.bfloat16), "rep").astype(jnp.float32),
        lax.psum(dot_first(swap_two, piece_up).astype(jnp.bfloat16), "rep").astype(jnp.float32),
        lax.psum(dot_first(swap_hidden, piece_cot).astype(jnp.bfloat16), "rep").astype(jnp.float32),
        lax.psum(dot_first(swap_one, piece_proj).astype(jnp.bfloat16), "rep").astype(jnp.float32),
        lax.psum(dot_first(swap_attended, piece_attn).astype(jnp.bfloat16), "rep").astype(
            jnp.float32
        ),
    )
    query_weight_grad = proj_grad[:, :query_cols]
    key_weight_grad = proj_grad[:, query_cols : query_cols + kv_cols]
    value_weight_grad = proj_grad[:, query_cols + kv_cols :]
    sum_one, sum_two, sum_query, sum_key = lax.psum(
        (gain_one_sum, gain_two_sum, query_gain_sum, key_gain_sum), ("rep", "fsdp")
    )
    gain_rows = model_width // fsdp_count
    head_rows = head_dim // fsdp_count
    attn_gain_grad = lax.dynamic_slice_in_dim(sum_one, shard_index * gain_rows, gain_rows)
    ffn_gain_grad = lax.dynamic_slice_in_dim(sum_two, shard_index * gain_rows, gain_rows)
    query_gain_grad = lax.dynamic_slice_in_dim(sum_query, shard_index * head_rows, head_rows)
    key_gain_grad = lax.dynamic_slice_in_dim(sum_key, shard_index * head_rows, head_rows)
    return (
        output,
        input_grad,
        attn_gain_grad,
        query_weight_grad,
        key_weight_grad,
        value_weight_grad,
        query_gain_grad,
        key_gain_grad,
        out_weight_grad,
        ffn_gain_grad,
        gate_weight_grad,
        up_weight_grad,
        down_weight_grad,
    )


def solution(mesh):
    in_specs = (
        P(("rep", "fsdp"), None),
        P("rep", None),
        P("fsdp"),
        P("fsdp", None),
        P("fsdp", None),
        P("fsdp", None),
        P("fsdp"),
        P("fsdp"),
        P("fsdp", None),
        P("fsdp"),
        P("fsdp", None),
        P("fsdp", None),
        P("fsdp", None),
        P(("rep", "fsdp"), None),
    )
    out_specs = (
        P(("rep", "fsdp"), None),
        P(("rep", "fsdp"), None),
        P("fsdp"),
        P("fsdp", None),
        P("fsdp", None),
        P("fsdp", None),
        P("fsdp"),
        P("fsdp"),
        P("fsdp", None),
        P("fsdp"),
        P("fsdp", None),
        P("fsdp", None),
        P("fsdp", None),
    )
    return jax.shard_map(shards, mesh=mesh, in_specs=in_specs, out_specs=out_specs, check_vma=False)
```

profile of v0, /device:TPU:0, one launch (start us, length us, event | category | flops | bytes accessed | tf_op | source)
XLA Modules:
  0.0 3176.3 jit_solution(9576412927014782421)
XLA Ops:
  12.0 13.7 all-gather
  27.5 11.0 all-reduce.4
  38.7 12.0 all-gather.1
  52.2 6.4 all-gather.17.cloned.1.call-done
  60.8 44.2 %all-gather.19.cloned.1.call-done = bf16[2048,512]{1,0:T(8,128)(2,1)} async-done(((bf16[512,512]{1,0:T(8,128)(2,1)}), bf16[2048,512]{1,0:T(8,128)(2,1)}) %all-gather.19.cloned.1.call-update) | async-done | bytes 2097168 | tf_op jit(solution)/shard_map/all_gather | solution.py:172
  107.1 17.6 all_gather.68
  125.9 29.1 all_gather.66
  155.0 109.7 %all-gather.15.cloned.1.call-done = bf16[2048,2048]{1,0:T(8,128)(2,1)} async-done(((bf16[512,2048]{1,0:T(8,128)(2,1)}), bf16[2048,2048]{1,0:T(8,128)(2,1)}) %all-gather.15.cloned.1.call-update) | async-done | bytes 8388624 | tf_op jit(solution)/shard_map/all_gather | solution.py:170
  264.7 4.6 fusion.335
  270.3 2.3 fusion.313
  284.6 2.3 fusion.322
  289.0 2.3 fusion.325
  293.4 2.3 fusion.328
  297.8 2.3 fusion.331
  302.2 2.3 fusion.334
  306.6 108.6 %all-gather.21.cloned.1.call-done = bf16[2048,2048]{1,0:T(8,128)(2,1)} async-done(((bf16[512,2048]{1,0:T(8,128)(2,1)}), bf16[2048,2048]{1,0:T(8,128)(2,1)}) %all-gather.21.cloned.1.call-update) | async-done | bytes 8388624 | tf_op jit(solution)/shard_map/all_gather | solution.py:173
  415.2 5.2 multiply_reduce_fusion.12
  421.3 554.9 %all-gather.23.cloned.1.call-done = bf16[2048,8192]{1,0:T(8,128)(2,1)} async-done(((bf16[512,8192]{1,0:T(8,128)(2,1)}), bf16[2048,8192]{1,0:T(8,128)(2,1)}) %all-gather.23.cloned.1.call-update) | async-done | bytes 33554448 | tf_op jit(solution)/shard_map/all_gather | solution.py:216
  976.3 21.6 fusion.337
  997.8 539.5 %all-gather.25.cloned.1.call-done = bf16[2048,8192]{1,0:T(8,128)(2,1)} async-done(((bf16[512,8192]{1,0:T(8,128)(2,1)}), bf16[2048,8192]{1,0:T(8,128)(2,1)}) %all-gather.25.cloned.1.call-update) | async-done | bytes 33554448 | tf_op jit(solution)/shard_map/all_gather | solution.py:221
  1537.3 21.5 fusion.338
  1558.8 539.7 %all-gather.27.cloned.1.call-done = bf16[8192,2048]{1,0:T(8,128)(2,1)} async-done(((bf16[2048,2048]{1,0:T(8,128)(2,1)}), bf16[8192,2048]{1,0:T(8,128)(2,1)}) %all-gather.27.cloned.1.call-update) | async-done | bytes 33554448 | tf_op jit(solution)/shard_map/all_gather | solution.py:230
  2098.5 21.3 multiply_convert_fusion
  2119.8 17.3 fusion.339
  2137.1 17.2 multiply_reduce_fusion
  2156.4 7.3 convolution_convert_fusion.5
  2165.7 2.6 fusion.117
  2168.3 2.6 fusion.115
  2171.0 2.6 fusion.113
  2188.4 2.6 fusion.111
  2191.0 2.6 fusion.109
  2193.7 2.6 fusion.107
  2196.3 2.6 fusion.105
  2199.0 2.7 fusion.103
  2208.7 2.5 copy.95
  2230.4 2.5 copy.94
  2233.0 2.5 copy.92
  2235.5 2.4 multiply_reduce_fusion.1
  2244.9 4.3 all-to-all-start
  2251.2 27.5 all-to-all-done
  2278.7 4.1 all-to-all-start.1
  2284.3 13.8 all-to-all-done.1
  2298.1 4.5 all-to-all-start.3
  2304.5 75.9 %all-to-all-done.3 = bf16[128,4,2048]{2,0,1:T(8,128)(2,1)} async-done(((bf16[128,4,2048]{2,0,1:T(8,128)(2,1)}), bf16[128,4,2048]{2,0,1:T(8,128)(2,1)}, u32[]{:S(2)}, u32[]{:S(2)}) %all-to-all-start.3) | async-done | bytes 2097184 | tf_op jit(solution)/shard_map/all_to_all | solution.py:310
  2380.3 4.1 all-to-all-start.2
  2385.0 10.2 convolution_convert_fusion.2
  2395.2 4.4 convolution_convert_fusion.4
  2399.5 48.4 %all-gather.29.cloned.1.call-done = bf16[512,3072]{1,0:T(8,128)(2,1)} async-done(((bf16[128,3072]{1,0:T(8,128)(2,1)}), bf16[512,3072]{1,0:T(8,128)(2,1)}) %all-gather.29.cloned.1.call-update) | async-done | bytes 3145744 | tf_op jit(solution)/shard_map/all_gather | solution.py:315
  2447.9 5.5 convolution_convert_fusion.3
  2453.4 144.8 %all-gather.35.cloned.1.call-done = bf16[512,8192]{1,0:T(8,128)(2,1)} async-done(((bf16[128,8192]{1,0:T(8,128)(2,1)}), bf16[512,8192]{1,0:T(8,128)(2,1)}) %all-gather.35.cloned.1.call-update) | async-done | bytes 8388624 | tf_op jit(solution)/shard_map/all_gather | solution.py:313
  2598.3 11.8 convolution_convert_fusion
  2610.1 137.5 %all-gather.33.cloned.1.call-done = bf16[512,8192]{1,0:T(8,128)(2,1)} async-done(((bf16[128,8192]{1,0:T(8,128)(2,1)}), bf16[512,8192]{1,0:T(8,128)(2,1)}) %all-gather.33.cloned.1.call-update) | async-done | bytes 8388624 | tf_op jit(solution)/shard_map/all_gather | solution.py:312
  2747.6 11.7 convolution_convert_fusion.1
  2759.4 7.4 fusion.340
  2766.9 14.3 fusion.9
  2781.3 2.9 convolution_add_fusion.1
  2786.2 40.1 %all-reduce.2 = (f32[2048]{0:T(1024)S(1)}, f32[64]{0:T(128)S(1)}, f32[64]{0:T(128)S(1)}, f32[2048]{0:T(1024)S(1)}) all-reduce(f32[2048]{0:T(1024)S(1)} %get-tuple-element.15, f32[64]{0:T(128)S(1)} %reduce_sum.303, f32[64]{0:T(128)S(1)} %reduce_sum.306, f32[2048]{0:T(1024)S(1)} %get-tuple-element.13), channel_id=1, replica_groups=mesh['rep'=8,'fsdp'=4] {'rep','fsdp'}, use_global_device_ids=true, to_apply=%region_37.38 | all-reduce | flops 4224 | bytes 33792 | tf_op jit(solution)/shard_map/psum | solution.py:329
  2828.7 2.6 fusion.123
  2831.3 294.5 %all-reduce.7.cloned.1.call-done = (bf16[512,3072]{1,0:T(8,128)(2,1)}, bf16[512,2048]{1,0:T(8,128)(2,1)}, bf16[512,8192]{1,0:T(8,128)(2,1)}, bf16[512,8192]{1,0:T(8,128)(2,1)}, bf16[2048,2048]{1,0:T(8,128)(2,1)}) async-done(((bf16[512,3072]{1,0:T(8,128)(2,1)}, bf16[512,2048]{1,0:T(8,128)(2,1)}, bf16[512,8192]{1,0:T(8,128)(2,1)}, bf16[512,8192]{1,0:T(8,128)(2,1)}, bf16[2048,2048]{1,0:T(8,128)(2,1)}), ...) | async-done | bytes 30408720 | tf_op jit(solution)/shard_map/psum | solution.py:321
  3125.8 4.3 slice.242
  3131.7 11.7 convert_element_type.228
  3143.4 11.7 convert_element_type.230
  3155.2 11.8 convert_element_type.232
  3167.0 2.5 convert_element_type.226
  (297 shorter events, 100.5 us)
Async XLA Ops:
  7.2 51.5 %all-gather.17.cloned.1.call-start = ((), (), s32[]{:S(2)}) async-start(), calls=%async_computation.7 | async-start | bytes 2621440 | tf_op jit(solution)/shard_map/all_gather | solution.py:171
  7.9 97.1 %all-gather.19.cloned.1.call-start = ((), (), s32[]{:S(2)}) async-start(), calls=%async_computation.8 | async-start | bytes 2621440 | tf_op jit(solution)/shard_map/all_gather | solution.py:172
  8.7 256.0 %all-gather.15.cloned.1.call-start = ((), (), s32[]{:S(2)}) async-start(), calls=%async_computation.6 | async-start | bytes 10485760 | tf_op jit(solution)/shard_map/all_gather | solution.py:170
  9.4 405.8 %all-gather.21.cloned.1.call-start = ((), (), s32[]{:S(2)}) async-start(), calls=%async_computation.9 | async-start | bytes 10485760 | tf_op jit(solution)/shard_map/all_gather | solution.py:173
  10.0 966.3 %all-gather.23.cloned.1.call-start = ((), (), s32[]{:S(2)}) async-start(), calls=%async_computation.10 | async-start | bytes 41943040 | tf_op jit(solution)/shard_map/all_gather | solution.py:216
  10.6 1526.7 %all-gather.25.cloned.1.call-start = ((), (), s32[]{:S(2)}) async-start(), calls=%async_computation.11 | async-start | bytes 41943040 | tf_op jit(solution)/shard_map/all_gather | solution.py:221
  11.1 14.6 copy-start.69
  11.2 15.8 copy-start.66
  11.2 16.1 copy-start.67
  11.2 27.4 copy-start.68
  11.2 27.5 copy-start.62
  11.2 39.7 %copy-start = (bf16[128,2048]{1,0:T(8,128)(2,1)S(1)}, bf16[128,2048]{1,0:T(8,128)(2,1)}, u32[]{:S(2)}) copy-start(bf16[128,2048]{1,0:T(8,128)(2,1)} %param.14) | copy-start | bytes 1572868
  11.2 2087.3 %all-gather.27.cloned.1.call-start = ((), (), s32[]{:S(2)}) async-start(), calls=%async_computation.12 | async-start | bytes 41943040 | tf_op jit(solution)/shard_map/all_gather | solution.py:230
  12.0 2226.0 %reduce-scatter.7.cloned.1.call-start = ((), (), s32[]{:S(2)}) async-start(), calls=%async_computation.19 | async-start | bytes 655360
  25.7 99.0 %copy-start.38 = (f32[4,1,512]{2,1,0:T(1,128)}, f32[4,1,512]{2,1,0:T(1,128)S(1)}, u32[]{:S(2)}) copy-start(f32[4,1,512]{2,1,0:T(1,128)S(1)} %convert_element_type.233) | copy-start | bytes 24580
  38.5 12.3 copy-start.65
  38.5 12.4 copy-start.63
  38.5 231.3 %copy-start.59 = (f32[64]{0:T(128)}, f32[64]{0:T(128)S(1)}, u32[]{:S(2)}) copy-start(f32[64]{0:T(128)S(1)} %convert_element_type.185) | copy-start | bytes 772
  38.5 87.3 %copy-start.57 = (f32[64]{0:T(128)}, f32[64]{0:T(128)S(1)}, u32[]{:S(2)}) copy-start(f32[64]{0:T(128)S(1)} %convert_element_type.187) | copy-start | bytes 772
  51.1 74.6 %copy-start.40 = (f32[128]{0:T(128)}, f32[128]{0:T(128)S(1)}, u32[]{:S(2)}) copy-start(f32[128]{0:T(128)S(1)} %add_rsqrt_fusion.3) | copy-start | bytes 1540
  60.7 94.3 %copy-start.23 = (f32[128,512]{1,0:T(8,128)}, f32[128,512]{1,0:T(8,128)S(1)}, u32[]{:S(2)}) copy-start(f32[128,512]{1,0:T(8,128)S(1)} %fusion.336) | copy-start | bytes 786436
  269.3 3.2 copy-start.6
  272.6 2.7 copy-start.25
  282.5 6.5 copy-start.50
  295.7 6.5 copy-start.42
  300.1 6.5 copy-start.44
  304.5 115.9 %copy-start.47 = (f32[128,4]{0,1:T(4,128)}, f32[128,4]{0,1:T(4,128)S(1)}, u32[]{:S(2)}) copy-start(f32[128,4]{0,1:T(4,128)S(1)} %get-tuple-element.66) | copy-start | bytes 6148
  306.6 108.6 %copy-start.22 = (bf16[128,8,4,64]{0,3,2,1:T(8,128)(2,1)}, bf16[128,8,4,64]{0,3,2,1:T(8,128)(2,1)S(1)}, u32[]{:S(2)}) copy-start(bf16[128,8,4,64]{0,3,2,1:T(8,128)(2,1)S(1)} %fusion.54) | copy-start | bytes 1572868
  2137.1 18.1 copy-start.20
  2173.6 3.1 copy-start.32
  2173.6 3.1 copy-start.36
  2173.6 3.1 copy-start.37
  2173.7 3.2 copy-start.53
  2188.1 52.7 %reduce-scatter.5.cloned.1.call-start = ((), (), s32[]{:S(2)}) async-start(), calls=%async_computation.13 | async-start | bytes 655360 | tf_op jit(solution)/shard_map/reduce_scatter | solution.py:268
  2191.0 5.3 copy-start.46
  2193.7 5.3 copy-start.49
  2199.0 6.1 copy-start.64
  2199.0 12.2 copy-start.11
  2203.7 181.2 %all-gather.37.cloned.1.call-start = ((), (), s32[]{:S(2)}) async-start(), calls=%async_computation.18 | async-start | bytes 2621440 | tf_op jit(solution)/shard_map/all_gather | solution.py:314
  2204.3 190.8 %all-gather.31.cloned.1.call-start = ((), (), s32[]{:S(2)}) async-start(), calls=%async_computation.15 | async-start | bytes 2621440 | tf_op jit(solution)/shard_map/all_gather | solution.py:316
  2211.2 17.0 copy-start.60
  2213.0 10.1 copy-start.18
  2219.0 228.8 %all-gather.29.cloned.1.call-start = ((), (), s32[]{:S(2)}) async-start(), calls=%async_computation.14 | async-start | bytes 3932160 | tf_op jit(solution)/shard_map/all_gather | solution.py:315
  2229.4 6.1 copy-start.7
  2233.0 6.3 copy-start.58
  2237.9 5.5 copy-start.9
  2242.7 355.6 %all-gather.35.cloned.1.call-start = ((), (), s32[]{:S(2)}) async-start(), calls=%async_computation.17 | async-start | bytes 10485760 | tf_op jit(solution)/shard_map/all_gather | solution.py:313
  2243.4 504.1 %all-gather.33.cloned.1.call-start = ((), (), s32[]{:S(2)}) async-start(), calls=%async_computation.16 | async-start | bytes 10485760 | tf_op jit(solution)/shard_map/all_gather | solution.py:312
  2244.9 38.0 %copy-start.3 = (bf16[128,8192]{1,0:T(8,128)(2,1)S(1)}, bf16[128,8192]{1,0:T(8,128)(2,1)}, u32[]{:S(2)}) copy-start(bf16[128,8192]{1,0:T(8,128)(2,1)} %get-tuple-element.30) | copy-start | bytes 6291460
  2244.9 33.9 %all-to-all-start = ((bf16[128,4,512]{2,0,1:T(8,128)(2,1)}), bf16[128,4,512]{2,0,1:T(8,128)(2,1)}, u32[]{:S(2)}, u32[]{:S(2)}) async-start(bf16[128,4,512]{2,0,1:T(8,128)(2,1)} %bitcast.839), calls=%async_computation.1 | async-start | bytes 1048576 | tf_op jit(solution)/shard_map/all_to_all | solution.py:308
  2278.7 19.4 all-to-all-start.1
  2298.1 82.2 %all-to-all-start.3 = ((bf16[128,4,2048]{2,0,1:T(8,128)(2,1)}), bf16[128,4,2048]{2,0,1:T(8,128)(2,1)}, u32[]{:S(2)}, u32[]{:S(2)}) async-start(bf16[128,4,2048]{2,0,1:T(8,128)(2,1)} %bitcast.832), calls=%async_computation.4 | async-start | bytes 4194304 | tf_op jit(solution)/shard_map/all_to_all | solution.py:310
  2380.3 73.1 %all-to-all-start.2 = ((bf16[128,4,512]{2,0,1:T(8,128)(2,1)}), bf16[128,4,512]{2,0,1:T(8,128)(2,1)}, u32[]{:S(2)}, u32[]{:S(2)}) async-start(bf16[128,4,512]{2,0,1:T(8,128)(2,1)} %bitcast.838), calls=%async_computation.3 | async-start | bytes 1048576 | tf_op jit(solution)/shard_map/all_to_all | solution.py:307
  2384.5 741.3 %all-reduce.7.cloned.1.call-start = ((), (), s32[]{:S(2)}) async-start(), calls=%async_computation.20 | async-start | bytes 60817408 | tf_op jit(solution)/shard_map/psum | solution.py:321
  2781.2 3.1 copy-start.1
  2781.2 3.1 copy-start.35
  2781.2 3.1 copy-start.39
  2781.2 3.1 copy-start.41
  2781.3 3.0 copy-start.8
  2781.3 47.4 %copy-start.5 = (f32[128,2048]{1,0:T(8,128)S(1)}, f32[128,2048]{1,0:T(8,128)}, u32[]{:S(2)}) copy-start(f32[128,2048]{1,0:T(8,128)} %copy-done.4) | copy-start | bytes 3145732
  2781.3 47.4 %copy-start.21 = (bf16[128,2048]{1,0:T(8,128)(2,1)S(1)}, bf16[128,2048]{1,0:T(8,128)(2,1)}, u32[]{:S(2)}) copy-start(bf16[128,2048]{1,0:T(8,128)(2,1)} %param.27) | copy-start | bytes 1572868
  2781.3 47.4 %copy-start.56 = (f32[128]{0:T(128)S(1)}, f32[128]{0:T(128)}, u32[]{:S(2)}) copy-start(f32[128]{0:T(128)} %copy-done.55) | copy-start | bytes 1540
  3125.8 4.3 copy-start.2
  3155.2 11.8 copy-start.24
  (25 other events, 29.0 us)
Sparse Core Ops, SparseCore 0:
  9.6 49.0 all-gather.16
  60.2 44.7 all-gather.18
  106.6 158.0 all-gather.14
  266.1 148.9 all-gather.20
  416.6 559.6 all-gather.22
  977.7 559.5 all-gather.24
  1538.9 559.5 all-gather.26
  2188.2 19.8 reduce-scatter.6
  2210.4 19.9 reduce-scatter.4
  2231.8 58.0 all-gather.36
  2291.5 81.3 all-gather.30
  2374.9 72.8 all-gather.28
  2450.0 148.1 all-gather.34
  2599.7 147.8 all-gather.32
  2759.5 366.2 all-reduce.6
where the time goes:
time: 3180 us
  waiting for transfers between devices  2650 us (83%)
  matrix products  268 us (8%)
  blocking collectives  123 us (4%)
  other arithmetic  55.5 us (2%)
  local copies, waits for them, and re-layouts  43.3 us (1%)
    all_gather x1, waiting for transfers between devices, shards(): lax.all_gather(gate_weight, 'fsdp', axis=0, tiled=True)  555 us
    all_gather x1, waiting for transfers between devices, shards(): lax.all_gather(down_weight, 'fsdp', axis=0, tiled=True)  540 us
    all_gather x1, waiting for transfers between devices, shards(): lax.all_gather(up_weight, 'fsdp', axis=0, tiled=True)  539 us
    psum x1, waiting for transfers between devices, shards(): lax.psum(dot_first(swap_one, piece_proj).astype(jnp.bfloat16), 'rep')  294 us
    all_gather x1, waiting for transfers between devices, shards(): piece_up = lax.all_gather(grad_up, 'fsdp', axis=0, tiled=True)  145 us
    all_gather x1, waiting for transfers between devices, shards(): piece_gate = lax.all_gather(grad_gate, 'fsdp', axis=0, tiled=True)  137 us
    all_gather x1, waiting for transfers between devices, shards(): lax.all_gather(query_weight, 'fsdp', axis=0, tiled=True)  110 us
    all_gather x1, waiting for transfers between devices, shards(): lax.all_gather(out_weight, 'fsdp', axis=0, tiled=True)  109 us
  transfers between devices with their start and end apart: 19, of which 14 were waited for; matrix products, arithmetic and copies ran while one was open for 7% of the time, Pallas kernels for 0%

commit v1 on v0

v1 whole, which is shorter than its diff:
```python
import jax
import jax.numpy as jnp
from jax import lax
from jax.sharding import Mesh, PartitionSpec as P

HEAD_SIZE = 64
EPSILON = 1e-05
THETA_BASE = 1000000.0
NEG_FILL = -1e30
BF = jnp.bfloat16
F32 = jnp.float32
PLANE = ("chip", "core")


def rotary_tables(positions, head_dim):
    half_dim = head_dim // 2
    inverse = THETA_BASE ** (-(jnp.arange(half_dim, dtype=F32) * 2.0) / head_dim)
    angles = positions.astype(F32)[:, None] * inverse[None, :]
    return (jnp.cos(angles)[:, None, :], jnp.sin(angles)[:, None, :])


def apply_rotary(values, cosine_table, sine_values):
    half_dim = values.shape[-1] // 2
    first_part = values[..., :half_dim]
    second_part = values[..., half_dim:]
    return jnp.concatenate(
        [
            first_part * cosine_table - second_part * sine_values,
            second_part * cosine_table + first_part * sine_values,
        ],
        axis=-1,
    )


def unit_rows(values):
    inverse = lax.rsqrt(jnp.mean(values * values, axis=-1, keepdims=True) + EPSILON)
    return (values * inverse, inverse)


def unit_back(grad_unit, unit_vals, inverse):
    return inverse * (
        grad_unit - unit_vals * jnp.mean(grad_unit * unit_vals, axis=-1, keepdims=True)
    )


def mm(a, b):
    return jnp.dot(a, b, preferred_element_type=F32)


def mm_last(a, b):
    return lax.dot_general(a, b, (((1,), (1,)), ((), ())), preferred_element_type=F32)


def mm_first(a, b):
    return lax.dot_general(a, b, (((0,), (0,)), ((), ())), preferred_element_type=F32)


def swap_cores(a):
    return lax.ppermute(a, "core", [(0, 1), (1, 0)])


def line_gather(own):
    count = lax.axis_size("fsdp")
    ahead = [(i, i + 1) for i in range(count - 1)]
    back = [(i + 1, i) for i in range(count - 1)]
    right, left, rights, lefts = own, own, [], []
    for _ in range(count - 1):
        right = lax.ppermute(right, "fsdp", ahead)
        left = lax.ppermute(left, "fsdp", back)
        rights.append(right)
        lefts.append(left)
    mine = lax.axis_index("fsdp")
    return [own] + [
        jnp.where(mine >= d, rights[d - 1], lefts[count - d - 1]) for d in range(1, count)
    ]


def line_scatter(parts):
    count = lax.axis_size("fsdp")
    right = left = None
    for t in range(count - 1):
        low = parts[t + 1].astype(F32)
        high = parts[count - 1 - t].astype(F32)
        if t:
            low, high = low + right.astype(F32), high + left.astype(F32)
        right = lax.ppermute(low.astype(BF), "fsdp", [(i, i + 1) for i in range(t + 1)])
        left = lax.ppermute(
            high.astype(BF), "fsdp", [(count - 1 - i, count - 2 - i) for i in range(t + 1)]
        )
    return parts[0].astype(F32) + right.astype(F32) + left.astype(F32)


def transpose_line(pieces):
    return lax.all_to_all(pieces, "fsdp", split_axis=0, concat_axis=0, tiled=True)


def gather_small(own):
    count = lax.axis_size("fsdp")
    mine = lax.axis_index("fsdp")
    ring = [own] + [
        lax.ppermute(own, "fsdp", [((i + d) % count, i) for i in range(count)])
        for d in range(1, count)
    ]
    twice = jnp.stack(ring + ring)
    return lax.dynamic_slice_in_dim(twice, count - mine, count)


def sum_small(rows):
    count = lax.axis_size("fsdp")
    chips = lax.axis_size("chip")
    mine = lax.axis_index("fsdp")
    total = lax.dynamic_index_in_dim(rows, mine, keepdims=False)
    for d in range(1, count):
        term = lax.dynamic_index_in_dim(rows, (mine + d) % count, keepdims=False)
        total = total + lax.ppermute(
            term, "fsdp", [(i, (i + d) % count) for i in range(count)]
        )
    total = total + swap_cores(total)
    bit = 1
    while bit < chips:
        total = total + lax.ppermute(total, "chip", [(i, i ^ bit) for i in range(chips)])
        bit *= 2
    return total


def shards(
    inputs,
    doc_lengths,
    attn_gain,
    query_weight,
    key_projection,
    value_projection,
    query_gain,
    key_norm_gain,
    out_weight,
    ffn_gain,
    gate_weight,
    up_weight,
    down_weight,
    cotangent,
):
    tok, width = inputs.shape
    count = lax.axis_size("fsdp")
    chips = lax.axis_size("chip")
    rep = chips * 2
    mine = lax.axis_index("fsdp")
    chip = lax.axis_index("chip")
    core = lax.axis_index("core")
    seq = tok * count
    hd = HEAD_SIZE
    rows = query_weight.shape[0]
    q_cols = query_weight.shape[1] // count
    kv_cols = key_projection.shape[1] // count
    ff = gate_weight.shape[1]
    ff_own = ff // count // 2
    q_heads, kv_heads = q_cols // hd, kv_cols // hd
    groups = q_heads // kv_heads
    scale = hd ** (-0.5)

    share = rows // rep
    at = (chip * 2 + core) * share
    piece = jnp.concatenate(
        [
            lax.dynamic_slice_in_dim(w, at, share).reshape(share, count, -1)
            for w in (query_weight, key_projection, value_projection)
        ],
        axis=2,
    )
    piece = transpose_line(piece.transpose(1, 0, 2))
    proj = lax.all_gather(piece, PLANE, axis=0)
    proj = proj.transpose(1, 0, 2, 3).reshape(width, q_cols + 2 * kv_cols)

    x_all = jnp.concatenate(line_gather(inputs), axis=0)

    gains = gather_small(jnp.concatenate([attn_gain, ffn_gain, query_gain, key_norm_gain]))
    gains = gains.astype(F32)
    gain_one = gains[:, :rows].reshape(-1)
    gain_two = gains[:, rows : 2 * rows].reshape(-1)
    small = hd // count
    gain_query = gains[:, 2 * rows : 2 * rows + small].reshape(-1)
    gain_key = gains[:, 2 * rows + small :].reshape(-1)

    part = rows // chips
    slabs = [
        lax.dynamic_slice_in_dim(w, chip * part, part).reshape(part, count, 2, ff_own)
        for w in (gate_weight, up_weight)
    ]
    slab = jnp.concatenate(
        [lax.dynamic_index_in_dim(s, core, axis=2, keepdims=False) for s in slabs], axis=2
    )
    slab = transpose_line(slab.transpose(1, 0, 2))
    pair = lax.all_gather(slab, "chip", axis=0)
    pair = pair.transpose(1, 0, 2, 3).reshape(width, 2 * ff_own)

    order = (mine - jnp.arange(count, dtype=jnp.int32)) % count
    positions = (order[:, None] * tok + jnp.arange(tok, dtype=jnp.int32)[None, :]).reshape(-1)
    lengths = doc_lengths[0]
    docs = lengths.shape[0]
    upto = jnp.arange(docs)[None, :] <= jnp.arange(docs)[:, None]
    ends = jnp.sum(jnp.where(upto, lengths[None, :], 0), axis=1)
    segment = jnp.sum((positions[:, None] >= ends[None, :]).astype(jnp.int32), axis=1)
    allowed = (segment[:, None] == segment[None, :]) & (positions[None, :] <= positions[:, None])
    cosine, sine = rotary_tables(positions, hd)

    unit_one, inverse_one = unit_rows(x_all.astype(F32))
    normed_one = (unit_one * gain_one).astype(BF)
    qkv = mm(normed_one, proj)
    q_unit, q_inv = unit_rows(qkv[:, :q_cols].reshape(seq, q_heads, hd))
    k_unit, k_inv = unit_rows(qkv[:, q_cols : q_cols + kv_cols].reshape(seq, kv_heads, hd))
    values = qkv[:, q_cols + kv_cols :].astype(BF).reshape(seq, kv_heads, hd)
    queries = apply_rotary(q_unit * gain_query, cosine, sine).astype(BF)
    keys = apply_rotary(k_unit * gain_key, cosine, sine).astype(BF)
    grouped = queries.reshape(seq, kv_heads, groups, hd)
    scores = jnp.einsum("tngd,snd->ngts", grouped, keys, preferred_element_type=F32) * scale
    scores = jnp.where(allowed, scores, NEG_FILL)
    expo = jnp.exp(scores - jnp.max(scores, axis=-1, keepdims=True))
    probs = expo / jnp.sum(expo, axis=-1, keepdims=True)
    probs_low = probs.astype(BF)
    attended = jnp.einsum("ngts,snd->tngd", probs_low, values, preferred_element_type=F32)
    attended = attended.astype(BF).reshape(seq, q_cols)
    out_part = mm(attended, out_weight).reshape(count, tok, width)
    inputs_wide = inputs.astype(F32)
    hidden_one = inputs_wide + line_scatter([out_part[d] for d in range(count)])

    unit_two, inverse_two = unit_rows(hidden_one)
    normed_two = jnp.concatenate(
        line_gather((unit_two * gain_two).astype(BF)), axis=0
    )
    normed_two = jnp.concatenate([normed_two, swap_cores(normed_two)], axis=0)
    cot_own = jnp.concatenate(line_gather(cotangent), axis=0)
    cot_all = jnp.concatenate([cot_own, swap_cores(cot_own)], axis=0)
    down_own = lax.dynamic_slice_in_dim(down_weight, core * ff_own, ff_own)
    grad_hidden = mm_last(cot_all, down_own)
    both = mm(normed_two, pair)
    gate_pre, upward = both[:, :ff_own], both[:, ff_own:]
    sigmoid = jax.nn.sigmoid(gate_pre)
    silu = gate_pre * sigmoid
    hidden = (silu * upward).astype(BF)
    grad_both = jnp.concatenate(
        [
            (grad_hidden * upward * sigmoid * (1.0 + gate_pre * (1.0 - sigmoid))).astype(BF),
            (grad_hidden * silu).astype(BF),
        ],
        axis=1,
    )

    def sum_tokens(left, weight, product):
        other = swap_cores(product(left[seq:], weight).astype(BF))
        own = product(left[:seq], weight) + other.astype(F32)
        own = own.reshape(count, tok, width)
        return line_scatter([own[d] for d in range(count)])

    grad_normed_two = sum_tokens(grad_both, pair, mm_last)
    output = (hidden_one + sum_tokens(hidden, down_own, mm)).astype(BF)

    down_sum = lax.psum_scatter(
        mm_first(hidden, cot_all).astype(BF), "chip", scatter_dimension=0, tiled=True
    )
    down_grad = lax.all_gather(down_sum, PLANE, axis=0)
    down_grad = down_grad.reshape(chips, 2, ff_own // chips, width).transpose(1, 0, 2, 3)
    down_grad = down_grad.reshape(2 * ff_own, width).astype(F32)
    pair_part = mm_first(normed_two, grad_both).astype(BF)
    pair_part = pair_part.reshape(count, chips, part, 2 * ff_own).transpose(1, 0, 2, 3)
    pair_part = pair_part.reshape(width, 2 * ff_own)
    pair_sum = lax.psum_scatter(pair_part, "chip", scatter_dimension=0, tiled=True)
    pair_sum = transpose_line(pair_sum.reshape(count, part, 2 * ff_own))
    pair_grad = lax.all_gather(pair_sum, PLANE, axis=0)
    pair_grad = pair_grad.reshape(chips, 2, count, part, 2, ff_own).transpose(4, 0, 3, 2, 1, 5)
    pair_grad = pair_grad.reshape(2, rows, ff).astype(F32)

    gain_two_sum = jnp.sum(grad_normed_two * unit_two, axis=0)
    grad_hidden_one = cotangent.astype(F32) + unit_back(
        grad_normed_two * gain_two, unit_two, inverse_two
    )
    grad_attn = jnp.concatenate(line_gather(grad_hidden_one.astype(BF)), axis=0)
    grad_att = mm_last(grad_attn, out_weight).astype(BF).reshape(seq, kv_heads, groups, hd)
    grad_probs = jnp.einsum("tngd,snd->ngts", grad_att, values, preferred_element_type=F32)
    delta = jnp.sum(probs * grad_probs, axis=-1, keepdims=True)
    grad_scores = (probs * (grad_probs - delta)).astype(BF)
    grad_q = jnp.einsum("ngts,snd->tngd", grad_scores, keys, preferred_element_type=F32) * scale
    grad_k = jnp.einsum("ngts,tngd->snd", grad_scores, grouped, preferred_element_type=F32) * scale
    grad_v = jnp.einsum("ngts,tngd->snd", probs_low, grad_att, preferred_element_type=F32)
    grad_q_unit = apply_rotary(grad_q.reshape(seq, q_heads, hd), cosine, -sine)
    grad_k_unit = apply_rotary(grad_k, cosine, -sine)
    query_gain_sum = jnp.sum(grad_q_unit * q_unit, axis=(0, 1))
    key_gain_sum = jnp.sum(grad_k_unit * k_unit, axis=(0, 1))
    grad_proj = jnp.concatenate(
        [
            unit_back(grad_q_unit * gain_query, q_unit, q_inv).astype(BF).reshape(seq, q_cols),
            unit_back(grad_k_unit * gain_key, k_unit, k_inv).astype(BF).reshape(seq, kv_cols),
            grad_v.astype(BF).reshape(seq, kv_cols),
        ],
        axis=1,
    )
    one_part = mm_last(grad_proj, proj).reshape(count, tok, width)
    grad_normed_one = line_scatter([one_part[d] for d in range(count)])
    unit_own = unit_one[:tok]
    gain_one_sum = jnp.sum(grad_normed_one * unit_own, axis=0)
    input_grad = (
        grad_hidden_one + unit_back(grad_normed_one * gain_one, unit_own, inverse_one[:tok])
    ).astype(BF)

    proj_part = mm_first(normed_one, grad_proj).astype(BF)
    proj_part = proj_part.reshape(count, rep, share, -1).transpose(1, 0, 2, 3)
    proj_part = proj_part.reshape(width, -1)
    proj_sum = lax.psum_scatter(proj_part, PLANE, scatter_dimension=0, tiled=True)
    proj_sum = transpose_line(proj_sum.reshape(count, share, -1))
    proj_grad = lax.all_gather(proj_sum, PLANE, axis=0)

    def rows_of(start, stop):
        columns = proj_grad[..., start:stop].transpose(0, 2, 1, 3)
        return columns.reshape(rows, -1).astype(F32)

    out_sum = lax.psum_scatter(
        mm_first(attended, grad_attn).astype(BF), PLANE, scatter_dimension=0, tiled=True
    )
    out_grad = lax.all_gather(out_sum, PLANE, axis=0, tiled=True).astype(F32)

    sums = sum_small(
        jnp.concatenate(
            [
                v.reshape(count, -1)
                for v in (gain_one_sum, gain_two_sum, query_gain_sum, key_gain_sum)
            ],
            axis=1,
        )
    )
    return (
        output,
        input_grad,
        sums[:rows],
        rows_of(0, q_cols),
        rows_of(q_cols, q_cols + kv_cols),
        rows_of(q_cols + kv_cols, q_cols + 2 * kv_cols),
        sums[2 * rows : 2 * rows + small],
        sums[2 * rows + small :],
        out_grad,
        sums[rows : 2 * rows],
        pair_grad[0],
        pair_grad[1],
        down_grad,
    )


def solution(mesh):
    chips, count = mesh.shape["rep"] // 2, mesh.shape["fsdp"]
    split = Mesh(mesh.devices.reshape(chips, 2, count), ("chip", "core", "fsdp"))
    tokens, reps, fsdp = (*PLANE, "fsdp"), PLANE, "fsdp"
    in_specs = (
        P(tokens, None),
        P(reps, None),
        P(fsdp),
        P(fsdp, None),
        P(fsdp, None),
        P(fsdp, None),
        P(fsdp),
        P(fsdp),
        P(fsdp, None),
        P(fsdp),
        P(fsdp, None),
        P(fsdp, None),
        P(fsdp, None),
        P(tokens, None),
    )
    out_specs = (
        P(tokens, None),
        P(tokens, None),
        P(fsdp),
        P(fsdp, None),
        P(fsdp, None),
        P(fsdp, None),
        P(fsdp),
        P(fsdp),
        P(fsdp, None),
        P(fsdp),
        P(fsdp, None),
        P(fsdp, None),
        P(fsdp, None),
    )
    return jax.shard_map(
        shards, mesh=split, in_specs=in_specs, out_specs=out_specs, check_vma=False
    )
```

time: 3180 us -> 1140 us (0.36)
  waiting for transfers between devices: 2650 us -> 399 us
  local copies, waits for them, and re-layouts: 43.3 us -> 245 us
  matrix products: 268 us -> 110 us
  starting transfers between devices: 18.2 us -> 176 us
  other arithmetic: 55.5 us -> 91.2 us
  blocking collectives: 123 us -> 87.3 us
    all_gather x12 -> x6, waiting for transfers between devices: 2230 us -> 34.3 us  [the longest x1 34.3 us: shards(): pair_grad = lax.all_gather(pair_sum, PLANE, axis=0)]
    psum x1 -> x0, waiting for transfers between devices: 294 us -> none  [shards(): lax.psum(dot_first(swap_one, piece_proj).astype(jnp.bfloat16), 'rep')]
    ppermute x0 -> x61, waiting for transfers between devices: none -> 209 us  [the longest x12 70.6 us: line_gather(): right = lax.ppermute(right, 'fsdp', ahead)]
    ppermute x0 -> x61, starting transfers between devices: none -> 170 us  [the longest x12 80.9 us: line_gather(): right = lax.ppermute(right, 'fsdp', ahead)]
    reduce_scatter x1 -> x4, waiting for transfers between devices: 0.02 us -> 155 us  [the longest x1 90.2 us: shards(): lax.psum_scatter(pair_part, 'chip', scatter_dimension=0, tiled=True)]
    dot_general x59 -> x19, matrix products: 250 us -> 102 us  [the longest x5 30.5 us: mm_last(): lax.dot_general(a, b, (((1,), (1,)), ((), ())), preferred_element_type=F32)]
    all_to_all x4 -> x1, waiting for transfers between devices: 117 us -> 0.01 us  [transpose_line(): lax.all_to_all(pieces, 'fsdp', split_axis=0, concat_axis=0, tiled=True)]
    all_to_all x0 -> x3, blocking collectives: none -> 87.3 us  [transpose_line(): lax.all_to_all(pieces, 'fsdp', split_axis=0, concat_axis=0, tiled=True)]
  transfers between devices with their start and end apart: 19 -> 72, of which waited for: 14 -> 35; matrix products, arithmetic and copies ran while one was open for 7% -> 20% of each run, Pallas kernels for 0% -> 0%
where the time goes in v1:
time: 1140 us; the launch traced here: 1120 us
  waiting for transfers between devices  399 us (35%)
  local copies, waits for them, and re-layouts  245 us (21%)
  starting transfers between devices  176 us (15%)
  matrix products  110 us (10%)
  other arithmetic  91.2 us (8%)
  blocking collectives  87.3 us (8%)
  between operations  16.2 us (1%)
    reduce_scatter x1, waiting for transfers between devices, shards(): lax.psum_scatter(pair_part, 'chip', scatter_dimension=0, tiled=True)  90.2 us
    all_to_all x3, blocking collectives, transpose_line(): lax.all_to_all(pieces, 'fsdp', split_axis=0, concat_axis=0, tiled=True)  87.3 us
    ppermute x12, starting transfers between devices, line_gather(): right = lax.ppermute(right, 'fsdp', ahead)  80.9 us
    ppermute x12, waiting for transfers between devices, line_gather(): right = lax.ppermute(right, 'fsdp', ahead)  70.6 us
    ppermute x12, waiting for transfers between devices, line_scatter(): lax.ppermute(low.astype(BF), 'fsdp', [(i, i + 1) for i in range(t + 1)])  62.7 us
    ppermute x12, starting transfers between devices, line_scatter(): lax.ppermute(low.astype(BF), 'fsdp', [(i, i + 1) for i in range(t + 1)])  51.5 us
    slice x2, local copies, waits for them, and re-layouts, shards(): pair_grad[1]  46.9 us
    reduce_scatter x1, waiting for transfers between devices, shards(): lax.psum_scatter(mm_first(hidden, cot_all).astype(BF), 'chip', scatter_di...  39.5 us
  transfers between devices with their start and end apart: 72, of which 35 were waited for; matrix products, arithmetic and copies ran while one was open for 20% of the time, Pallas kernels for 0%

profile of v1, /device:TPU:0, one launch (start us, length us, event | category | flops | bytes accessed | tf_op | source)
XLA Modules:
  0.0 1125.0 jit_solution(6416244668689470865)
XLA Ops:
  9.8 17.9 %all_to_all.20 = bf16[4,64,768]{2,1,0:T(8,128)(2,1)} all-to-all(bf16[4,64,768]{2,1,0:T(8,128)(2,1)S(1)} %copy.215), channel_id=1, replica_groups=mesh['chip'=4,'core'=2,'fsdp'=4] {'fsdp'}, dimensions={0} | all-to-all | bytes 786432 | tf_op jit(solution)/shard_map/all_to_all | solution.py:94
  61.1 5.2 all-to-all-start.1
  67.6 4.7 collective-permute-start.4
  75.3 34.4 %collective-permute-done.4 = bf16[128,2048]{1,0:T(8,128)(2,1)} collective-permute-done((bf16[128,2048]{1,0:T(8,128)(2,1)S(1)}, bf16[128,2048]{1,0:T(8,128)(2,1)}, u32[]{:S(2)}, u32[]{:S(2)}) %collective-permute-start.4) | collective-permute-done | bytes 524320 | tf_op jit(solution)/shard_map/ppermute | solution.py:68
  109.7 15.9 %collective-permute-start.5 = (bf16[128,2048]{1,0:T(8,128)(2,1)}, bf16[128,2048]{1,0:T(8,128)(2,1)}, u32[]{:S(2)}, u32[]{:S(2)}) collective-permute-start(bf16[128,2048]{1,0:T(8,128)(2,1)} %collective-permute-done.4), channel_id=1, source_target_pairs={{0,1},{1,2},{2,3},{4,5},{5,6},{6,7},{8,9},{9,10},{10,11},{12,13},{... | collective-permute-start | bytes 1572872 | tf_op jit(solution)/shard_map/ppermute | solution.py:68
  134.8 5.0 collective-permute-done.3
  157.2 8.2 fusion.89
  171.1 4.7 collective-permute-start.9
  176.7 6.7 collective-permute-done.9
  188.0 6.6 collective-permute-done.10
  195.6 5.0 collective-permute-start.29
  201.9 5.2 collective-permute-start.11
  208.6 9.4 collective-permute-done.30
  219.3 9.9 collective-permute-start.33
  231.9 8.1 collective-permute-done.31
  241.4 10.4 collective-permute-start.34
  261.9 6.6 collective-permute-done.15
  268.5 5.1 collective-permute-start.19
  287.9 8.4 collective-permute-done.20
  306.5 8.4 copy.225
  314.9 14.6 %fusion.91 = f32[1024,2048]{1,0:T(8,128)} fusion(bf16[1024,2048]{1,0:T(8,128)(2,1)} %constant_dynamic-update-slice_fusion, bf16[2048,2048]{1,0:T(8,128)(2,1)} %bitcast.173), kind=kOutput, calls=%fused_computation.229 | convolution fusion | flops 8589934592 | bytes 20971520 | tf_op jit(solution)/shard_map/dot_general | solution.py:47
  329.5 11.2 multiply_convert_fusion
  340.8 7.5 convolution_convert_fusion.4
  348.5 5.9 fusion.18
  354.7 6.8 convert_add_fusion
  366.1 4.9 convert_add_fusion.1
  373.2 5.1 collective-permute-done.37
  383.6 6.0 collective-permute-done.23
  394.1 6.7 collective-permute-done.38
  401.8 9.4 collective-permute-done.24
  412.4 5.0 collective-permute-start.39
  424.8 4.9 collective-permute-done.39
  429.7 9.1 collective-permute-done.42
  439.8 7.7 collective-permute-done.28
  449.5 6.1 collective-permute-start.43
  456.9 8.4 collective-permute-done.43
  465.2 5.2 collective-permute-start.47
  471.7 6.8 collective-permute-done.47
  478.5 5.4 collective-permute-start.48
  492.8 8.5 collective-permute-done.46
  512.4 7.2 fusion.3
  543.9 9.4 convolution_convert_fusion.1
  553.4 14.1 %convolution_convert_fusion = bf16[2048,2048]{1,0:T(8,128)(2,1)} fusion(bf16[1024,2048]{1,0:T(8,128)(2,1)} %constant_dynamic-update-slice_fusion, bf16[1024,1024]{1,0:T(8,128)(2,1)} %get-tuple-element.41, bf16[1024,1024]{1,0:T(8,128)(2,1)} %get-tuple-element.42), kind=kOutput, calls=%fused_computation.10 | convolution fusion | flops 8602517504 | bytes 16777216 | tf_op jit(solution)/shard_map/dot_general | solution.py:55
  567.4 8.8 copy.246
  577.0 25.5 %reduce-scatter.5.cloned.1.call-done = bf16[256,768]{1,0:T(8,128)(2,1)} async-done(((bf16[2048,768]{1,0:T(8,128)(2,1)}), bf16[256,768]{1,0:T(8,128)(2,1)}) %reduce-scatter.5.cloned.1.call-update) | async-done | bytes 393232 | tf_op jit(solution)/shard_map/reduce_scatter | solution.py:306
  602.5 16.5 %all_to_all.21 = bf16[4,64,768]{2,1,0:T(8,128)(2,1)} all-to-all(bf16[4,64,768]{2,1,0:T(8,128)(2,1)} %bitcast.206), channel_id=1, replica_groups=mesh['chip'=4,'core'=2,'fsdp'=4] {'fsdp'}, dimensions={0} | all-to-all | bytes 786432 | tf_op jit(solution)/shard_map/all_to_all | solution.py:94
  619.1 39.5 %reduce-scatter.11.cloned.1.call-done = bf16[256,2048]{1,0:T(8,128)(2,1)} async-done(((bf16[1024,2048]{1,0:T(8,128)(2,1)}), bf16[256,2048]{1,0:T(8,128)(2,1)}) %reduce-scatter.11.cloned.1.call-update) | async-done | bytes 1048592 | tf_op jit(solution)/shard_map/reduce_scatter | solution.py:256
  658.7 90.2 %reduce-scatter.9.cloned.1.call-done = bf16[512,2048]{1,0:T(8,128)(2,1)} async-done(((bf16[2048,2048]{1,0:T(8,128)(2,1)}), bf16[512,2048]{1,0:T(8,128)(2,1)}) %reduce-scatter.9.cloned.1.call-update) | async-done | bytes 2097168 | tf_op jit(solution)/shard_map/reduce_scatter | solution.py:265
  748.9 52.9 %all_to_all.22 = bf16[4,128,2048]{2,1,0:T(8,128)(2,1)} all-to-all(bf16[4,128,2048]{2,1,0:T(8,128)(2,1)} %bitcast.194), channel_id=1, replica_groups=mesh['chip'=4,'core'=2,'fsdp'=4] {'fsdp'}, dimensions={0} | all-to-all | bytes 4194304 | tf_op jit(solution)/shard_map/all_to_all | solution.py:94
  809.0 8.6 collective-permute-done.49
  817.7 4.8 collective-permute-start.50
  822.5 8.1 collective-permute-done.50
  832.5 5.8 collective-permute-start.51
  845.5 12.9 %collective-permute-done.54 = bf16[128,2048]{1,0:T(8,128)(2,1)} collective-permute-done((bf16[128,2048]{1,0:T(8,128)(2,1)}, bf16[128,2048]{1,0:T(8,128)(2,1)}, u32[]{:S(2)}, u32[]{:S(2)}) %collective-permute-start.54) | collective-permute-done | bytes 524320 | tf_op jit(solution)/shard_map/ppermute | solution.py:87
  899.7 11.7 %convert_bitcast_fusion.1 = f32[2,4,256,2048]{3,2,0,1:T(8,128)} fusion(bf16[4,2,256,2048]{3,2,1,0:T(8,128)(2,1)} %bitcast.171), kind=kLoop, calls=%fused_computation.2 | loop fusion | flops 4194304 | bytes 25165824 | tf_op jit(solution)/shard_map/convert_element_type | solution.py:261
  911.4 15.2 %copy.250 = f32[2,4,256,2048]{3,2,1,0:T(8,128)} copy(f32[2,4,256,2048]{3,2,0,1:T(8,128)} %convert_bitcast_fusion.1) | data formatting | bytes 33554432 | tf_op jit(solution)/shard_map/convert_element_type | solution.py:261
  926.6 34.3 %all-gather.20.cloned.1.call-done = bf16[32,128,2048]{2,1,0:T(8,128)(2,1)} async-done(((bf16[4,128,2048]{2,1,0:T(8,128)(2,1)}), bf16[32,128,2048]{2,1,0:T(8,128)(2,1)}) %all-gather.20.cloned.1.call-update) | async-done | bytes 16777232 | tf_op jit(solution)/shard_map/all_gather | solution.py:267
  960.8 22.4 %copy.247 = bf16[32,128,2048]{1,2,0:T(8,128)(2,1)} copy(bf16[32,128,2048]{2,1,0:T(8,128)(2,1)} %all-gather.20.cloned.1.call-done) | data formatting | bytes 33554432 | tf_op jit(solution)/shard_map/all_gather | solution.py:267
  983.3 18.2 %convert_bitcast_fusion = f32[2,4,128,4,2,1024]{2,5,0,3,4,1:T(8,128)} fusion(bf16[4,2,4,128,2,1024]{3,5,4,2,1,0:T(8,128)(2,1)} %bitcast.164), kind=kLoop, calls=%fused_computation.1 | loop fusion | flops 8388608 | bytes 50331648 | tf_op jit(solution)/shard_map/convert_element_type | solution.py:269
  1001.5 21.8 %fusion.81 = (f32[1,4,128,4,2,1024]{2,5,0,3,4,1:T(8,128)}, f32[1,4,128,4,2,1024]{2,5,0,3,4,1:T(8,128)}) fusion(f32[2,4,128,4,2,1024]{2,5,0,3,4,1:T(8,128)} %convert_bitcast_fusion), kind=kLoop, calls=%fused_computation.219 | loop fusion | bytes 67108864 | tf_op jit(solution)/shard_map/slice | solution.py:340
  1023.3 25.1 %copy.248 = f32[1,4,128,4,2,1024]{5,4,3,2,1,0:T(2,128)} copy(f32[1,4,128,4,2,1024]{2,5,0,3,4,1:T(8,128)} %get-tuple-element.40) | data formatting | bytes 33554432 | tf_op jit(solution)/shard_map/slice | solution.py:339
  1048.4 22.1 %squeeze.48 = f32[512,8192]{1,0:T(8,128)} reshape(f32[1,4,128,4,2,1024]{5,4,3,2,1,0:T(2,128)} %copy.248) | data formatting | bytes 33554432 | tf_op jit(solution)/shard_map/squeeze | solution.py:339
  1070.6 25.1 %copy.249 = f32[1,4,128,4,2,1024]{5,4,3,2,1,0:T(2,128)} copy(f32[1,4,128,4,2,1024]{2,5,0,3,4,1:T(8,128)} %get-tuple-element.39) | data formatting | bytes 33554432 | tf_op jit(solution)/shard_map/slice | solution.py:340
  1095.7 22.3 %squeeze.49 = f32[512,8192]{1,0:T(8,128)} reshape(f32[1,4,128,4,2,1024]{5,4,3,2,1,0:T(2,128)} %copy.249) | data formatting | bytes 33554432 | tf_op jit(solution)/shard_map/squeeze | solution.py:340
  (412 shorter events, 255.2 us)
Async XLA Ops:
  7.2 135.3 %all-gather.14.cloned.1.call-start = ((), (), s32[]{:S(2)}) async-start(), calls=%async_computation.13 | async-start | bytes 3538944 | tf_op jit(solution)/shard_map/all_gather | solution.py:170
  27.9 45.4 %collective-permute-start.6 = (bf16[1056]{0:T(1024)(128)(2,1)S(1)}, bf16[1056]{0:T(1024)(128)(2,1)S(1)}, u32[]{:S(2)}, u32[]{:S(2)}) collective-permute-start(bf16[1056]{0:T(1024)(128)(2,1)S(1)} %concatenate.62), channel_id=1, source_target_pairs={{1,0},{2,1},{3,2},{0,3},{5,4},{6,5},{7,6},{4,7},{9,8},{10,9},{11,1... | collective-permute-start | bytes 6344 | tf_op jit(solution)/shard_map/ppermute | solution.py:101
  29.3 43.9 %collective-permute-start.7 = (bf16[1056]{0:T(1024)(128)(2,1)S(1)}, bf16[1056]{0:T(1024)(128)(2,1)S(1)}, u32[]{:S(2)}, u32[]{:S(2)}) collective-permute-start(bf16[1056]{0:T(1024)(128)(2,1)S(1)} %concatenate.62), channel_id=1, source_target_pairs={{2,0},{3,1},{0,2},{1,3},{6,4},{7,5},{4,6},{5,7},{10,8},{11,9},{8,1... | collective-permute-start | bytes 6344 | tf_op jit(solution)/shard_map/ppermute | solution.py:101
  29.6 43.7 %collective-permute-start.8 = (bf16[1056]{0:T(1024)(128)(2,1)S(1)}, bf16[1056]{0:T(1024)(128)(2,1)S(1)}, u32[]{:S(2)}, u32[]{:S(2)}) collective-permute-start(bf16[1056]{0:T(1024)(128)(2,1)S(1)} %concatenate.62), channel_id=1, source_target_pairs={{3,0},{0,1},{1,2},{2,3},{7,4},{4,5},{5,6},{6,7},{11,8},{8,9},{9,10... | collective-permute-start | bytes 6344 | tf_op jit(solution)/shard_map/ppermute | solution.py:101
  30.1 37.4 %collective-permute-start = (bf16[128,2048]{1,0:T(8,128)(2,1)S(1)}, bf16[128,2048]{1,0:T(8,128)(2,1)S(1)}, u32[]{:S(2)}, u32[]{:S(2)}) collective-permute-start(bf16[128,2048]{1,0:T(8,128)(2,1)S(1)} %copy-done.16), channel_id=1, source_target_pairs={{0,1},{1,2},{2,3},{4,5},{5,6},{6,7},{8,9},{9,10},{10,11},{12,13},{... | collective-permute-start | bytes 1572872 | tf_op jit(solution)/shard_map/ppermute | solution.py:68
  34.8 38.6 %collective-permute-start.1 = (bf16[128,2048]{1,0:T(8,128)(2,1)S(1)}, bf16[128,2048]{1,0:T(8,128)(2,1)}, u32[]{:S(2)}, u32[]{:S(2)}) collective-permute-start(bf16[128,2048]{1,0:T(8,128)(2,1)S(1)} %copy-done.16), channel_id=1, source_target_pairs={{1,0},{2,1},{3,2},{5,4},{6,5},{7,6},{9,8},{10,9},{11,10},{13,12},{... | collective-permute-start | bytes 1572872 | tf_op jit(solution)/shard_map/ppermute | solution.py:69
  61.1 81.2 %all-to-all-start.1 = ((bf16[4,128,2048]{2,1,0:T(8,128)(2,1)}), bf16[4,128,2048]{2,1,0:T(8,128)(2,1)}, u32[]{:S(2)}, u32[]{:S(2)}) async-start(bf16[4,128,2048]{2,1,0:T(8,128)(2,1)} %maximum_bitcast_fusion), calls=%async_computation.1 | async-start | bytes 4194304 | tf_op jit(solution)/shard_map/all_to_all | solution.py:94
  66.3 240.2 %all-gather.16.cloned.1.call-start = ((), (), s32[]{:S(2)}) async-start(), calls=%async_computation.14 | async-start | bytes 10485760 | tf_op jit(solution)/shard_map/all_gather | solution.py:192
  67.6 42.2 %collective-permute-start.4 = (bf16[128,2048]{1,0:T(8,128)(2,1)S(1)}, bf16[128,2048]{1,0:T(8,128)(2,1)}, u32[]{:S(2)}, u32[]{:S(2)}) collective-permute-start(bf16[128,2048]{1,0:T(8,128)(2,1)S(1)} %collective-permute-done), channel_id=1, source_target_pairs={{0,1},{1,2},{2,3},{4,5},{5,6},{6,7},{8,9},{9,10},{10,11},{12,13},{... | collective-permute-start | bytes 1572872 | tf_op jit(solution)/shard_map/ppermute | solution.py:68
  73.4 53.5 %collective-permute-start.2 = (bf16[128,2048]{1,0:T(8,128)(2,1)}, bf16[128,2048]{1,0:T(8,128)(2,1)}, u32[]{:S(2)}, u32[]{:S(2)}) collective-permute-start(bf16[128,2048]{1,0:T(8,128)(2,1)} %collective-permute-done.1), channel_id=1, source_target_pairs={{1,0},{2,1},{3,2},{5,4},{6,5},{7,6},{9,8},{10,9},{11,10},{13,12},{... | collective-permute-start | bytes 1572872 | tf_op jit(solution)/shard_map/ppermute | solution.py:69
  109.7 24.0 %collective-permute-start.5 = (bf16[128,2048]{1,0:T(8,128)(2,1)}, bf16[128,2048]{1,0:T(8,128)(2,1)}, u32[]{:S(2)}, u32[]{:S(2)}) collective-permute-start(bf16[128,2048]{1,0:T(8,128)(2,1)} %collective-permute-done.4), channel_id=1, source_target_pairs={{0,1},{1,2},{2,3},{4,5},{5,6},{6,7},{8,9},{9,10},{10,11},{12,13},{... | collective-permute-start | bytes 1572872 | tf_op jit(solution)/shard_map/ppermute | solution.py:68
  126.9 12.9 %collective-permute-start.3 = (bf16[128,2048]{1,0:T(8,128)(2,1)}, bf16[128,2048]{1,0:T(8,128)(2,1)S(1)}, u32[]{:S(2)}, u32[]{:S(2)}) collective-permute-start(bf16[128,2048]{1,0:T(8,128)(2,1)} %collective-permute-done.2), channel_id=1, source_target_pairs={{1,0},{2,1},{3,2},{5,4},{6,5},{7,6},{9,8},{10,9},{11,10},{13,12},{... | collective-permute-start | bytes 1572872 | tf_op jit(solution)/shard_map/ppermute | solution.py:69
  142.3 434.0 %reduce-scatter.7.cloned.1.call-start = ((), (), s32[]{:S(2)}) async-start(), calls=%async_computation.9 | async-start | bytes 2359296 | tf_op jit(solution)/shard_map/reduce_scatter | solution.py:314
  171.1 12.3 %collective-permute-start.9 = (bf16[128,2048]{1,0:T(8,128)(2,1)S(1)}, bf16[128,2048]{1,0:T(8,128)(2,1)S(1)}, u32[]{:S(2)}, u32[]{:S(2)}) collective-permute-start(bf16[128,2048]{1,0:T(8,128)(2,1)S(1)} %get-tuple-element.58), channel_id=1, source_target_pairs={{0,1},{4,5},{8,9},{12,13},{16,17},{20,21},{24,25},{28,29}} | collective-permute-start | bytes 1572872 | tf_op jit(solution)/shard_map/ppermute | solution.py:86
  175.9 12.1 %collective-permute-start.12 = (bf16[128,2048]{1,0:T(8,128)(2,1)S(1)}, bf16[128,2048]{1,0:T(8,128)(2,1)S(1)}, u32[]{:S(2)}, u32[]{:S(2)}) collective-permute-start(bf16[128,2048]{1,0:T(8,128)(2,1)S(1)} %get-tuple-element.59), channel_id=1, source_target_pairs={{3,2},{7,6},{11,10},{15,14},{19,18},{23,22},{27,26},{31,30}} | collective-permute-start | bytes 1572872 | tf_op jit(solution)/shard_map/ppermute | solution.py:87
  183.5 11.1 collective-permute-start.10
  194.9 12.2 %collective-permute-start.13 = (bf16[128,2048]{1,0:T(8,128)(2,1)S(1)}, bf16[128,2048]{1,0:T(8,128)(2,1)S(1)}, u32[]{:S(2)}, u32[]{:S(2)}) collective-permute-start(bf16[128,2048]{1,0:T(8,128)(2,1)S(1)} %get-tuple-element.57), channel_id=1, source_target_pairs={{3,2},{2,1},{7,6},{6,5},{11,10},{10,9},{15,14},{14,13},{19,18},{18... | collective-permute-start | bytes 1572872 | tf_op jit(solution)/shard_map/ppermute | solution.py:87
  195.6 23.7 %collective-permute-start.29 = (bf16[128,2048]{1,0:T(8,128)(2,1)S(1)}, bf16[128,2048]{1,0:T(8,128)(2,1)S(1)}, u32[]{:S(2)}, u32[]{:S(2)}) collective-permute-start(bf16[128,2048]{1,0:T(8,128)(2,1)S(1)} %copy-done.21), channel_id=1, source_target_pairs={{0,1},{1,2},{2,3},{4,5},{5,6},{6,7},{8,9},{9,10},{10,11},{12,13},{... | collective-permute-start | bytes 1572872 | tf_op jit(solution)/shard_map/ppermute | solution.py:68
  200.6 17.4 %collective-permute-start.30 = (bf16[128,2048]{1,0:T(8,128)(2,1)S(1)}, bf16[128,2048]{1,0:T(8,128)(2,1)S(1)}, u32[]{:S(2)}, u32[]{:S(2)}) collective-permute-start(bf16[128,2048]{1,0:T(8,128)(2,1)S(1)} %copy-done.21), channel_id=1, source_target_pairs={{1,0},{2,1},{3,2},{5,4},{6,5},{7,6},{9,8},{10,9},{11,10},{13,12},{... | collective-permute-start | bytes 1572872 | tf_op jit(solution)/shard_map/ppermute | solution.py:69
  201.9 27.3 %collective-permute-start.11 = (bf16[128,2048]{1,0:T(8,128)(2,1)S(1)}, bf16[128,2048]{1,0:T(8,128)(2,1)S(1)}, u32[]{:S(2)}, u32[]{:S(2)}) collective-permute-start(bf16[128,2048]{1,0:T(8,128)(2,1)S(1)} %get-tuple-element.56), channel_id=1, source_target_pairs={{0,1},{1,2},{2,3},{4,5},{5,6},{6,7},{8,9},{9,10},{10,11},{12,13},{... | collective-permute-start | bytes 1572872 | tf_op jit(solution)/shard_map/ppermute | solution.py:86
  207.2 22.0 %collective-permute-start.14 = (bf16[128,2048]{1,0:T(8,128)(2,1)S(1)}, bf16[128,2048]{1,0:T(8,128)(2,1)S(1)}, u32[]{:S(2)}, u32[]{:S(2)}) collective-permute-start(bf16[128,2048]{1,0:T(8,128)(2,1)S(1)} %add_convert_fusion.13), channel_id=1, source_target_pairs={{3,2},{2,1},{1,0},{7,6},{6,5},{5,4},{11,10},{10,9},{9,8},{15,14},{... | collective-permute-start | bytes 1572872 | tf_op jit(solution)/shard_map/ppermute | solution.py:87
  218.0 22.1 %collective-permute-start.31 = (bf16[128,2048]{1,0:T(8,128)(2,1)S(1)}, bf16[128,2048]{1,0:T(8,128)(2,1)S(1)}, u32[]{:S(2)}, u32[]{:S(2)}) collective-permute-start(bf16[128,2048]{1,0:T(8,128)(2,1)S(1)} %collective-permute-done.30), channel_id=1, source_target_pairs={{1,0},{2,1},{3,2},{5,4},{6,5},{7,6},{9,8},{10,9},{11,10},{13,12},{... | collective-permute-start | bytes 1572872 | tf_op jit(solution)/shard_map/ppermute | solution.py:69
  219.3 22.1 %collective-permute-start.33 = (bf16[128,2048]{1,0:T(8,128)(2,1)S(1)}, bf16[128,2048]{1,0:T(8,128)(2,1)S(1)}, u32[]{:S(2)}, u32[]{:S(2)}) collective-permute-start(bf16[128,2048]{1,0:T(8,128)(2,1)S(1)} %collective-permute-done.29), channel_id=1, source_target_pairs={{0,1},{1,2},{2,3},{4,5},{5,6},{6,7},{8,9},{9,10},{10,11},{12,13},{... | collective-permute-start | bytes 1572872 | tf_op jit(solution)/shard_map/ppermute | solution.py:68
  230.7 25.0 %collective-permute-start.16 = (bf16[128,2048]{1,0:T(8,128)(2,1)S(1)}, bf16[128,2048]{1,0:T(8,128)(2,1)S(1)}, u32[]{:S(2)}, u32[]{:S(2)}) collective-permute-start(bf16[128,2048]{1,0:T(8,128)(2,1)S(1)} %get-tuple-element.36), channel_id=1, source_target_pairs={{1,0},{2,1},{3,2},{5,4},{6,5},{7,6},{9,8},{10,9},{11,10},{13,12},{... | collective-permute-start | bytes 1572872 | tf_op jit(solution)/shard_map/ppermute | solution.py:69
  240.0 21.6 %collective-permute-start.32 = (bf16[128,2048]{1,0:T(8,128)(2,1)S(1)}, bf16[128,2048]{1,0:T(8,128)(2,1)S(1)}, u32[]{:S(2)}, u32[]{:S(2)}) collective-permute-start(bf16[128,2048]{1,0:T(8,128)(2,1)S(1)} %collective-permute-done.31), channel_id=1, source_target_pairs={{1,0},{2,1},{3,2},{5,4},{6,5},{7,6},{9,8},{10,9},{11,10},{13,12},{... | collective-permute-start | bytes 1572872 | tf_op jit(solution)/shard_map/ppermute | solution.py:69
  241.4 33.5 %collective-permute-start.34 = (bf16[128,2048]{1,0:T(8,128)(2,1)S(1)}, bf16[128,2048]{1,0:T(8,128)(2,1)S(1)}, u32[]{:S(2)}, u32[]{:S(2)}) collective-permute-start(bf16[128,2048]{1,0:T(8,128)(2,1)S(1)} %collective-permute-done.33), channel_id=1, source_target_pairs={{0,1},{1,2},{2,3},{4,5},{5,6},{6,7},{8,9},{9,10},{10,11},{12,13},{... | collective-permute-start | bytes 1572872 | tf_op jit(solution)/shard_map/ppermute | solution.py:68
  251.7 16.8 %collective-permute-start.15 = (bf16[128,2048]{1,0:T(8,128)(2,1)S(1)}, bf16[128,2048]{1,0:T(8,128)(2,1)S(1)}, u32[]{:S(2)}, u32[]{:S(2)}) collective-permute-start(bf16[128,2048]{1,0:T(8,128)(2,1)S(1)} %get-tuple-element.36), channel_id=1, source_target_pairs={{0,1},{1,2},{2,3},{4,5},{5,6},{6,7},{8,9},{9,10},{10,11},{12,13},{... | collective-permute-start | bytes 1572872 | tf_op jit(solution)/shard_map/ppermute | solution.py:68
  255.7 17.9 %collective-permute-start.17 = (bf16[128,2048]{1,0:T(8,128)(2,1)S(1)}, bf16[128,2048]{1,0:T(8,128)(2,1)S(1)}, u32[]{:S(2)}, u32[]{:S(2)}) collective-permute-start(bf16[128,2048]{1,0:T(8,128)(2,1)S(1)} %collective-permute-done.16), channel_id=1, source_target_pairs={{1,0},{2,1},{3,2},{5,4},{6,5},{7,6},{9,8},{10,9},{11,10},{13,12},{... | collective-permute-start | bytes 1572872 | tf_op jit(solution)/shard_map/ppermute | solution.py:69
  268.5 11.7 %collective-permute-start.19 = (bf16[128,2048]{1,0:T(8,128)(2,1)S(1)}, bf16[128,2048]{1,0:T(8,128)(2,1)S(1)}, u32[]{:S(2)}, u32[]{:S(2)}) collective-permute-start(bf16[128,2048]{1,0:T(8,128)(2,1)S(1)} %collective-permute-done.15), channel_id=1, source_target_pairs={{0,1},{1,2},{2,3},{4,5},{5,6},{6,7},{8,9},{9,10},{10,11},{12,13},{... | collective-permute-start | bytes 1572872 | tf_op jit(solution)/shard_map/ppermute | solution.py:68
  273.6 12.3 %collective-permute-start.18 = (bf16[128,2048]{1,0:T(8,128)(2,1)S(1)}, bf16[128,2048]{1,0:T(8,128)(2,1)S(1)}, u32[]{:S(2)}, u32[]{:S(2)}) collective-permute-start(bf16[128,2048]{1,0:T(8,128)(2,1)S(1)} %collective-permute-done.17), channel_id=1, source_target_pairs={{1,0},{2,1},{3,2},{5,4},{6,5},{7,6},{9,8},{10,9},{11,10},{13,12},{... | collective-permute-start | bytes 1572872 | tf_op jit(solution)/shard_map/ppermute | solution.py:69
  278.6 20.2 %collective-permute-start.35 = (bf16[512,2048]{1,0:T(8,128)(2,1)}, bf16[512,2048]{1,0:T(8,128)(2,1)}, u32[]{:S(2)}, u32[]{:S(2)}) collective-permute-start(bf16[512,2048]{1,0:T(8,128)(2,1)} %pad_maximum_fusion.4), channel_id=1, source_target_pairs={{0,4},{4,0},{1,5},{5,1},{2,6},{6,2},{3,7},{7,3},{8,12},{12,8},{9,1... | collective-permute-start | bytes 6291464 | tf_op jit(solution)/shard_map/ppermute | solution.py:59
  280.2 16.1 %collective-permute-start.20 = (bf16[128,2048]{1,0:T(8,128)(2,1)S(1)}, bf16[128,2048]{1,0:T(8,128)(2,1)S(1)}, u32[]{:S(2)}, u32[]{:S(2)}) collective-permute-start(bf16[128,2048]{1,0:T(8,128)(2,1)S(1)} %collective-permute-done.19), channel_id=1, source_target_pairs={{0,1},{1,2},{2,3},{4,5},{5,6},{6,7},{8,9},{9,10},{10,11},{12,13},{... | collective-permute-start | bytes 1572872 | tf_op jit(solution)/shard_map/ppermute | solution.py:68
  354.3 11.8 %collective-permute-start.22 = (bf16[512,2048]{1,0:T(8,128)(2,1)}, bf16[512,2048]{1,0:T(8,128)(2,1)S(1)}, u32[]{:S(2)}, u32[]{:S(2)}) collective-permute-start(bf16[512,2048]{1,0:T(8,128)(2,1)} %fusion.18), channel_id=1, source_target_pairs={{0,4},{4,0},{1,5},{5,1},{2,6},{6,2},{3,7},{7,3},{8,12},{12,8},{9,1... | collective-permute-start | bytes 6291464 | tf_op jit(solution)/shard_map/ppermute | solution.py:59
  361.7 16.7 %collective-permute-start.37 = (bf16[128,2048]{1,0:T(8,128)(2,1)S(1)}, bf16[128,2048]{1,0:T(8,128)(2,1)S(1)}, u32[]{:S(2)}, u32[]{:S(2)}) collective-permute-start(bf16[128,2048]{1,0:T(8,128)(2,1)S(1)} %get-tuple-element.50), channel_id=1, source_target_pairs={{0,1},{4,5},{8,9},{12,13},{16,17},{20,21},{24,25},{28,29}} | collective-permute-start | bytes 1572872 | tf_op jit(solution)/shard_map/ppermute | solution.py:86
  371.1 18.4 %collective-permute-start.23 = (bf16[128,2048]{1,0:T(8,128)(2,1)S(1)}, bf16[128,2048]{1,0:T(8,128)(2,1)S(1)}, u32[]{:S(2)}, u32[]{:S(2)}) collective-permute-start(bf16[128,2048]{1,0:T(8,128)(2,1)S(1)} %get-tuple-element.54), channel_id=1, source_target_pairs={{0,1},{4,5},{8,9},{12,13},{16,17},{20,21},{24,25},{28,29}} | collective-permute-start | bytes 1572872 | tf_op jit(solution)/shard_map/ppermute | solution.py:86
  372.5 21.6 %collective-permute-start.40 = (bf16[128,2048]{1,0:T(8,128)(2,1)S(1)}, bf16[128,2048]{1,0:T(8,128)(2,1)S(1)}, u32[]{:S(2)}, u32[]{:S(2)}) collective-permute-start(bf16[128,2048]{1,0:T(8,128)(2,1)S(1)} %get-tuple-element.51), channel_id=1, source_target_pairs={{3,2},{7,6},{11,10},{15,14},{19,18},{23,22},{27,26},{31,30}} | collective-permute-start | bytes 1572872 | tf_op jit(solution)/shard_map/ppermute | solution.py:87
  378.4 22.4 %collective-permute-start.38 = (bf16[128,2048]{1,0:T(8,128)(2,1)S(1)}, bf16[128,2048]{1,0:T(8,128)(2,1)S(1)}, u32[]{:S(2)}, u32[]{:S(2)}) collective-permute-start(bf16[128,2048]{1,0:T(8,128)(2,1)S(1)} %add_convert_fusion.8), channel_id=1, source_target_pairs={{0,1},{1,2},{4,5},{5,6},{8,9},{9,10},{12,13},{13,14},{16,17},{17,1... | collective-permute-start | bytes 1572872 | tf_op jit(solution)/shard_map/ppermute | solution.py:86
  382.9 19.0 %collective-permute-start.26 = (bf16[128,2048]{1,0:T(8,128)(2,1)S(1)}, bf16[128,2048]{1,0:T(8,128)(2,1)S(1)}, u32[]{:S(2)}, u32[]{:S(2)}) collective-permute-start(bf16[128,2048]{1,0:T(8,128)(2,1)S(1)} %get-tuple-element.55), channel_id=1, source_target_pairs={{3,2},{7,6},{11,10},{15,14},{19,18},{23,22},{27,26},{31,30}} | collective-permute-start | bytes 1572872 | tf_op jit(solution)/shard_map/ppermute | solution.py:87
  389.7 21.6 %collective-permute-start.24 = (bf16[128,2048]{1,0:T(8,128)(2,1)S(1)}, bf16[128,2048]{1,0:T(8,128)(2,1)S(1)}, u32[]{:S(2)}, u32[]{:S(2)}) collective-permute-start(bf16[128,2048]{1,0:T(8,128)(2,1)S(1)} %add_convert_fusion.12), channel_id=1, source_target_pairs={{0,1},{1,2},{4,5},{5,6},{8,9},{9,10},{12,13},{13,14},{16,17},{17,1... | collective-permute-start | bytes 1572872 | tf_op jit(solution)/shard_map/ppermute | solution.py:86
  401.1 20.8 %collective-permute-start.41 = (bf16[128,2048]{1,0:T(8,128)(2,1)S(1)}, bf16[128,2048]{1,0:T(8,128)(2,1)S(1)}, u32[]{:S(2)}, u32[]{:S(2)}) collective-permute-start(bf16[128,2048]{1,0:T(8,128)(2,1)S(1)} %get-tuple-element.49), channel_id=1, source_target_pairs={{3,2},{2,1},{7,6},{6,5},{11,10},{10,9},{15,14},{14,13},{19,18},{18... | collective-permute-start | bytes 1572872 | tf_op jit(solution)/shard_map/ppermute | solution.py:87
  411.5 11.8 %collective-permute-start.27 = (bf16[128,2048]{1,0:T(8,128)(2,1)S(1)}, bf16[128,2048]{1,0:T(8,128)(2,1)S(1)}, u32[]{:S(2)}, u32[]{:S(2)}) collective-permute-start(bf16[128,2048]{1,0:T(8,128)(2,1)S(1)} %get-tuple-element.53), channel_id=1, source_target_pairs={{3,2},{2,1},{7,6},{6,5},{11,10},{10,9},{15,14},{14,13},{19,18},{18... | collective-permute-start | bytes 1572872 | tf_op jit(solution)/shard_map/ppermute | solution.py:87
  412.4 17.4 %collective-permute-start.39 = (bf16[128,2048]{1,0:T(8,128)(2,1)S(1)}, bf16[128,2048]{1,0:T(8,128)(2,1)S(1)}, u32[]{:S(2)}, u32[]{:S(2)}) collective-permute-start(bf16[128,2048]{1,0:T(8,128)(2,1)S(1)} %get-tuple-element.48), channel_id=1, source_target_pairs={{0,1},{1,2},{2,3},{4,5},{5,6},{6,7},{8,9},{9,10},{10,11},{12,13},{... | collective-permute-start | bytes 1572872 | tf_op jit(solution)/shard_map/ppermute | solution.py:86
  417.4 22.4 %collective-permute-start.25 = (bf16[128,2048]{1,0:T(8,128)(2,1)S(1)}, bf16[128,2048]{1,0:T(8,128)(2,1)S(1)}, u32[]{:S(2)}, u32[]{:S(2)}) collective-permute-start(bf16[128,2048]{1,0:T(8,128)(2,1)S(1)} %get-tuple-element.52), channel_id=1, source_target_pairs={{0,1},{1,2},{2,3},{4,5},{5,6},{6,7},{8,9},{9,10},{10,11},{12,13},{... | collective-permute-start | bytes 1572872 | tf_op jit(solution)/shard_map/ppermute | solution.py:86
  422.1 16.8 %collective-permute-start.42 = (bf16[128,2048]{1,0:T(8,128)(2,1)S(1)}, bf16[128,2048]{1,0:T(8,128)(2,1)S(1)}, u32[]{:S(2)}, u32[]{:S(2)}) collective-permute-start(bf16[128,2048]{1,0:T(8,128)(2,1)S(1)} %add_convert_fusion.5), channel_id=1, source_target_pairs={{3,2},{2,1},{1,0},{7,6},{6,5},{5,4},{11,10},{10,9},{9,8},{15,14},{... | collective-permute-start | bytes 1572872 | tf_op jit(solution)/shard_map/ppermute | solution.py:87
  423.5 24.0 %collective-permute-start.28 = (bf16[128,2048]{1,0:T(8,128)(2,1)S(1)}, bf16[128,2048]{1,0:T(8,128)(2,1)S(1)}, u32[]{:S(2)}, u32[]{:S(2)}) collective-permute-start(bf16[128,2048]{1,0:T(8,128)(2,1)S(1)} %add_convert_fusion.9), channel_id=1, source_target_pairs={{3,2},{2,1},{1,0},{7,6},{6,5},{5,4},{11,10},{10,9},{9,8},{15,14},{... | collective-permute-start | bytes 1572872 | tf_op jit(solution)/shard_map/ppermute | solution.py:87
  449.5 15.8 %collective-permute-start.43 = (bf16[128,2048]{1,0:T(8,128)(2,1)S(1)}, bf16[128,2048]{1,0:T(8,128)(2,1)S(1)}, u32[]{:S(2)}, u32[]{:S(2)}) collective-permute-start(bf16[128,2048]{1,0:T(8,128)(2,1)S(1)} %get-tuple-element.21), channel_id=1, source_target_pairs={{0,1},{1,2},{2,3},{4,5},{5,6},{6,7},{8,9},{9,10},{10,11},{12,13},{... | collective-permute-start | bytes 1572872 | tf_op jit(solution)/shard_map/ppermute | solution.py:68
  455.6 14.9 %collective-permute-start.44 = (bf16[128,2048]{1,0:T(8,128)(2,1)S(1)}, bf16[128,2048]{1,0:T(8,128)(2,1)}, u32[]{:S(2)}, u32[]{:S(2)}) collective-permute-start(bf16[128,2048]{1,0:T(8,128)(2,1)S(1)} %get-tuple-element.21), channel_id=1, source_target_pairs={{1,0},{2,1},{3,2},{5,4},{6,5},{7,6},{9,8},{10,9},{11,10},{13,12},{... | collective-permute-start | bytes 1572872 | tf_op jit(solution)/shard_map/ppermute | solution.py:69
  465.2 13.3 %collective-permute-start.47 = (bf16[128,2048]{1,0:T(8,128)(2,1)S(1)}, bf16[128,2048]{1,0:T(8,128)(2,1)}, u32[]{:S(2)}, u32[]{:S(2)}) collective-permute-start(bf16[128,2048]{1,0:T(8,128)(2,1)S(1)} %collective-permute-done.43), channel_id=1, source_target_pairs={{0,1},{1,2},{2,3},{4,5},{5,6},{6,7},{8,9},{9,10},{10,11},{12,13},{... | collective-permute-start | bytes 1572872 | tf_op jit(solution)/shard_map/ppermute | solution.py:68
  470.4 18.4 %collective-permute-start.45 = (bf16[128,2048]{1,0:T(8,128)(2,1)}, bf16[128,2048]{1,0:T(8,128)(2,1)}, u32[]{:S(2)}, u32[]{:S(2)}) collective-permute-start(bf16[128,2048]{1,0:T(8,128)(2,1)} %collective-permute-done.44), channel_id=1, source_target_pairs={{1,0},{2,1},{3,2},{5,4},{6,5},{7,6},{9,8},{10,9},{11,10},{13,12},{... | collective-permute-start | bytes 1572872 | tf_op jit(solution)/shard_map/ppermute | solution.py:69
  478.5 13.0 %collective-permute-start.48 = (bf16[128,2048]{1,0:T(8,128)(2,1)}, bf16[128,2048]{1,0:T(8,128)(2,1)}, u32[]{:S(2)}, u32[]{:S(2)}) collective-permute-start(bf16[128,2048]{1,0:T(8,128)(2,1)} %collective-permute-done.47), channel_id=1, source_target_pairs={{0,1},{1,2},{2,3},{4,5},{5,6},{6,7},{8,9},{9,10},{10,11},{12,13},{... | collective-permute-start | bytes 1572872 | tf_op jit(solution)/shard_map/ppermute | solution.py:68
  488.9 12.4 %collective-permute-start.46 = (bf16[128,2048]{1,0:T(8,128)(2,1)}, bf16[128,2048]{1,0:T(8,128)(2,1)S(1)}, u32[]{:S(2)}, u32[]{:S(2)}) collective-permute-start(bf16[128,2048]{1,0:T(8,128)(2,1)} %collective-permute-done.45), channel_id=1, source_target_pairs={{1,0},{2,1},{3,2},{5,4},{6,5},{7,6},{9,8},{10,9},{11,10},{13,12},{... | collective-permute-start | bytes 1572872 | tf_op jit(solution)/shard_map/ppermute | solution.py:69
  512.4 90.1 %reduce-scatter.5.cloned.1.call-start = ((), (), s32[]{:S(2)}) async-start(), calls=%async_computation.8 | async-start | bytes 3538944 | tf_op jit(solution)/shard_map/reduce_scatter | solution.py:306
  543.6 115.0 %reduce-scatter.11.cloned.1.call-start = ((), (), s32[]{:S(2)}) async-start(), calls=%async_computation.12 | async-start | bytes 5242880 | tf_op jit(solution)/shard_map/reduce_scatter | solution.py:256
  553.3 195.5 %reduce-scatter.9.cloned.1.call-start = ((), (), s32[]{:S(2)}) async-start(), calls=%async_computation.11 | async-start | bytes 10485760 | tf_op jit(solution)/shard_map/reduce_scatter | solution.py:265
  576.2 305.2 %all-gather.12.cloned.1.call-start = ((), (), s32[]{:S(2)}) async-start(), calls=%async_computation.10 | async-start | bytes 2359296 | tf_op jit(solution)/shard_map/all_gather | solution.py:317
  577.0 309.0 %all-gather.18.cloned.1.call-start = ((), (), s32[]{:S(2)}) async-start(), calls=%async_computation.15 | async-start | bytes 3538944 | tf_op jit(solution)/shard_map/all_gather | solution.py:308
  619.1 280.7 %all-gather.22.cloned.1.call-start = ((), (), s32[]{:S(2)}) async-start(), calls=%async_computation.17 | async-start | bytes 9437184 | tf_op jit(solution)/shard_map/all_gather | solution.py:259
  658.6 302.2 %all-gather.20.cloned.1.call-start = ((), (), s32[]{:S(2)}) async-start(), calls=%async_computation.16 | async-start | bytes 18874368 | tf_op jit(solution)/shard_map/all_gather | solution.py:267
  805.7 11.9 %collective-permute-start.49 = (bf16[128,2048]{1,0:T(8,128)(2,1)S(1)}, bf16[128,2048]{1,0:T(8,128)(2,1)S(1)}, u32[]{:S(2)}, u32[]{:S(2)}) collective-permute-start(bf16[128,2048]{1,0:T(8,128)(2,1)S(1)} %get-tuple-element.46), channel_id=1, source_target_pairs={{0,1},{4,5},{8,9},{12,13},{16,17},{20,21},{24,25},{28,29}} | collective-permute-start | bytes 1572872 | tf_op jit(solution)/shard_map/ppermute | solution.py:86
  808.1 14.4 %collective-permute-start.52 = (bf16[128,2048]{1,0:T(8,128)(2,1)S(1)}, bf16[128,2048]{1,0:T(8,128)(2,1)S(1)}, u32[]{:S(2)}, u32[]{:S(2)}) collective-permute-start(bf16[128,2048]{1,0:T(8,128)(2,1)S(1)} %get-tuple-element.47), channel_id=1, source_target_pairs={{3,2},{7,6},{11,10},{15,14},{19,18},{23,22},{27,26},{31,30}} | collective-permute-start | bytes 1572872 | tf_op jit(solution)/shard_map/ppermute | solution.py:87
  817.7 12.9 %collective-permute-start.50 = (bf16[128,2048]{1,0:T(8,128)(2,1)S(1)}, bf16[128,2048]{1,0:T(8,128)(2,1)S(1)}, u32[]{:S(2)}, u32[]{:S(2)}) collective-permute-start(bf16[128,2048]{1,0:T(8,128)(2,1)S(1)} %add_convert_fusion.4), channel_id=1, source_target_pairs={{0,1},{1,2},{4,5},{5,6},{8,9},{9,10},{12,13},{13,14},{16,17},{17,1... | collective-permute-start | bytes 1572872 | tf_op jit(solution)/shard_map/ppermute | solution.py:86
  831.7 6.6 collective-permute-start.53
  832.5 13.0 %collective-permute-start.51 = (bf16[128,2048]{1,0:T(8,128)(2,1)}, bf16[128,2048]{1,0:T(8,128)(2,1)}, u32[]{:S(2)}, u32[]{:S(2)}) collective-permute-start(bf16[128,2048]{1,0:T(8,128)(2,1)} %get-tuple-element.44), channel_id=1, source_target_pairs={{0,1},{1,2},{2,3},{4,5},{5,6},{6,7},{8,9},{9,10},{10,11},{12,13},{... | collective-permute-start | bytes 1572872 | tf_op jit(solution)/shard_map/ppermute | solution.py:86
  840.4 18.0 %collective-permute-start.54 = (bf16[128,2048]{1,0:T(8,128)(2,1)}, bf16[128,2048]{1,0:T(8,128)(2,1)}, u32[]{:S(2)}, u32[]{:S(2)}) collective-permute-start(bf16[128,2048]{1,0:T(8,128)(2,1)} %add_convert_fusion.1), channel_id=1, source_target_pairs={{3,2},{2,1},{1,0},{7,6},{6,5},{5,4},{11,10},{10,9},{9,8},{15,14},{... | collective-permute-start | bytes 1572872 | tf_op jit(solution)/shard_map/ppermute | solution.py:87
  (79 other events, 1584.5 us)
Sparse Core Ops, SparseCore 0:
  27.9 31.4 all-gather.13
  142.4 88.0 all-gather.15
  512.5 40.0 reduce-scatter.6
  556.2 46.2 reduce-scatter.4
  605.9 52.6 reduce-scatter.10
  662.4 86.4 reduce-scatter.8
  750.7 27.8 all-gather.11
  780.5 32.3 all-gather.17
  814.8 54.3 all-gather.21
  870.9 89.8 all-gather.19

commit v2 on v1

--- a/solution.py
+++ b/solution.py
@@ -1,6 +1,7 @@
 import jax
 import jax.numpy as jnp
 from jax import lax
+from jax.experimental import pallas as pl
 from jax.sharding import Mesh, PartitionSpec as P
 
 HEAD_SIZE = 64
@@ -75,13 +76,15 @@
     ]
 
 
-def line_scatter(parts):
+def line_scatter(parts, ahead_of=()):
     count = lax.axis_size("fsdp")
     right = left = None
     for t in range(count - 1):
         low = parts[t + 1].astype(F32)
         high = parts[count - 1 - t].astype(F32)
         if t:
+            if t <= len(ahead_of):
+                right, left, _ = lax.optimization_barrier((right, left, ahead_of[t - 1]))
             low, high = low + right.astype(F32), high + left.astype(F32)
         right = lax.ppermute(low.astype(BF), "fsdp", [(i, i + 1) for i in range(t + 1)])
         left = lax.ppermute(
@@ -90,19 +93,34 @@
     return parts[0].astype(F32) + right.astype(F32) + left.astype(F32)
 
 
-def transpose_line(pieces):
-    return lax.all_to_all(pieces, "fsdp", split_axis=0, concat_axis=0, tiled=True)
-
-
-def gather_small(own):
+def absolute(ring):
+    count = len(ring)
+    twice = jnp.stack(ring + ring)
+    return lax.dynamic_slice_in_dim(twice, count - lax.axis_index("fsdp"), count)
+
+
+def exchange_line(piece_for):
     count = lax.axis_size("fsdp")
     mine = lax.axis_index("fsdp")
-    ring = [own] + [
-        lax.ppermute(own, "fsdp", [((i + d) % count, i) for i in range(count)])
-        for d in range(1, count)
-    ]
-    twice = jnp.stack(ring + ring)
-    return lax.dynamic_slice_in_dim(twice, count - mine, count)
+    return absolute(
+        [piece_for(mine)]
+        + [
+            lax.ppermute(
+                piece_for((mine - e) % count),
+                "fsdp",
+                [(i, (i - e) % count) for i in range(count)],
+            )
+            for e in range(1, count)
+        ]
+    )
+
+
+def after(value, *others):
+    return lax.optimization_barrier((value, *others))[0]
+
+
+def gather_small(own):
+    return exchange_line(lambda j: own)
 
 
 def sum_small(rows):
@@ -121,6 +139,38 @@
         total = total + lax.ppermute(total, "chip", [(i, i ^ bit) for i in range(chips)])
         bit *= 2
     return total
+
+
+def cast_pair(own, gate, up):
+    half = gate.shape[1]
+    gate[...] = own[0, :, :half].astype(F32)
+    up[...] = own[0, :, half:].astype(F32)
+
+
+def place_pair(own, chips, count, part, half):
+    block = pl.BlockSpec((part, half), lambda c, j, k: (c, j * 2 + k))
+    shape = jax.ShapeDtypeStruct((chips * part, count * 2 * half), F32)
+    return pl.pallas_call(
+        cast_pair,
+        grid=(chips, count, 2),
+        in_specs=[pl.BlockSpec((1, part, 2 * half), lambda c, j, k: (c * 2 + k, j, 0))],
+        out_specs=[block, block],
+        out_shape=[shape, shape],
+    )(own)
+
+
+def cast_down(own, out):
+    out[...] = own[0].astype(F32)
+
+
+def place_down(own, chips, part, width):
+    return pl.pallas_call(
+        cast_down,
+        grid=(2, chips),
+        in_specs=[pl.BlockSpec((1, part, width), lambda k, c: (c * 2 + k, 0, 0))],
+        out_specs=pl.BlockSpec((part, width), lambda k, c: (k * chips + c, 0)),
+        out_shape=jax.ShapeDtypeStruct((2 * chips * part, width), F32),
+    )(own)
 
 
 def shards(
@@ -159,18 +209,23 @@
 
     share = rows // rep
     at = (chip * 2 + core) * share
-    piece = jnp.concatenate(
-        [
-            lax.dynamic_slice_in_dim(w, at, share).reshape(share, count, -1)
-            for w in (query_weight, key_projection, value_projection)
-        ],
-        axis=2,
-    )
-    piece = transpose_line(piece.transpose(1, 0, 2))
-    proj = lax.all_gather(piece, PLANE, axis=0)
+
+    def proj_piece(j):
+        return jnp.concatenate(
+            [
+                lax.dynamic_slice(w, (at, j * wide), (share, wide))
+                for w, wide in (
+                    (query_weight, q_cols),
+                    (key_projection, kv_cols),
+                    (value_projection, kv_cols),
+                )
+            ],
+            axis=1,
+        )
+
+    x_all = jnp.concatenate(line_gather(inputs), axis=0)
+    proj = lax.all_gather(exchange_line(proj_piece), PLANE, axis=0)
     proj = proj.transpose(1, 0, 2, 3).reshape(width, q_cols + 2 * kv_cols)
-
-    x_all = jnp.concatenate(line_gather(inputs), axis=0)
 
     gains = gather_small(jnp.concatenate([attn_gain, ffn_gain, query_gain, key_norm_gain]))
     gains = gains.astype(F32)
@@ -181,16 +236,25 @@
     gain_key = gains[:, 2 * rows + small :].reshape(-1)
 
     part = rows // chips
-    slabs = [
-        lax.dynamic_slice_in_dim(w, chip * part, part).reshape(part, count, 2, ff_own)
-        for w in (gate_weight, up_weight)
-    ]
-    slab = jnp.concatenate(
-        [lax.dynamic_index_in_dim(s, core, axis=2, keepdims=False) for s in slabs], axis=2
-    )
-    slab = transpose_line(slab.transpose(1, 0, 2))
-    pair = lax.all_gather(slab, "chip", axis=0)
-    pair = pair.transpose(1, 0, 2, 3).reshape(width, 2 * ff_own)
+    gate_up = after((gate_weight, up_weight), x_all)
+
+    def pair_piece(j):
+        return jnp.concatenate(
+            [
+                lax.dynamic_slice(w, (chip * part, (j * 2 + core) * ff_own), (part, ff_own))
+                for w in gate_up
+            ],
+            axis=1,
+        )
+
+    pair = lax.all_gather(exchange_line(pair_piece), "chip", axis=0)
+    pair = pair.reshape(width, 2 * ff_own)
+
+    def to_chip_order(a):
+        return a.reshape(tok, count, chips, part).transpose(0, 2, 1, 3).reshape(tok, width)
+
+    def from_chip_order(a):
+        return a.reshape(tok, chips, count, part).transpose(0, 2, 1, 3).reshape(tok, width)
 
     order = (mine - jnp.arange(count, dtype=jnp.int32)) % count
     positions = (order[:, None] * tok + jnp.arange(tok, dtype=jnp.int32)[None, :]).reshape(-1)
@@ -224,10 +288,10 @@
 
     unit_two, inverse_two = unit_rows(hidden_one)
     normed_two = jnp.concatenate(
-        line_gather((unit_two * gain_two).astype(BF)), axis=0
+        line_gather(to_chip_order((unit_two * gain_two).astype(BF))), axis=0
     )
     normed_two = jnp.concatenate([normed_two, swap_cores(normed_two)], axis=0)
-    cot_own = jnp.concatenate(line_gather(cotangent), axis=0)
+    cot_own = jnp.concatenate(line_gather(after(cotangent, normed_two)), axis=0)
     cot_all = jnp.concatenate([cot_own, swap_cores(cot_own)], axis=0)
     down_own = lax.dynamic_slice_in_dim(down_weight, core * ff_own, ff_own)
     grad_hidden = mm_last(cot_all, down_own)
@@ -244,35 +308,32 @@
         axis=1,
     )
 
-    def sum_tokens(left, weight, product):
+    def sum_tokens(left, weight, product, ahead_of=()):
         other = swap_cores(product(left[seq:], weight).astype(BF))
         own = product(left[:seq], weight) + other.astype(F32)
         own = own.reshape(count, tok, width)
-        return line_scatter([own[d] for d in range(count)])
-
-    grad_normed_two = sum_tokens(grad_both, pair, mm_last)
-    output = (hidden_one + sum_tokens(hidden, down_own, mm)).astype(BF)
-
-    down_sum = lax.psum_scatter(
-        mm_first(hidden, cot_all).astype(BF), "chip", scatter_dimension=0, tiled=True
-    )
-    down_grad = lax.all_gather(down_sum, PLANE, axis=0)
-    down_grad = down_grad.reshape(chips, 2, ff_own // chips, width).transpose(1, 0, 2, 3)
-    down_grad = down_grad.reshape(2 * ff_own, width).astype(F32)
+        return line_scatter([own[d] for d in range(count)], ahead_of)
+
+    down_part = mm_first(hidden, cot_all).astype(BF)
     pair_part = mm_first(normed_two, grad_both).astype(BF)
-    pair_part = pair_part.reshape(count, chips, part, 2 * ff_own).transpose(1, 0, 2, 3)
-    pair_part = pair_part.reshape(width, 2 * ff_own)
+    grad_normed_two = from_chip_order(
+        sum_tokens(grad_both, pair, mm_last, (down_part, pair_part))
+    )
+
+    down_sum = lax.psum_scatter(down_part, "chip", scatter_dimension=0, tiled=True)
     pair_sum = lax.psum_scatter(pair_part, "chip", scatter_dimension=0, tiled=True)
-    pair_sum = transpose_line(pair_sum.reshape(count, part, 2 * ff_own))
-    pair_grad = lax.all_gather(pair_sum, PLANE, axis=0)
-    pair_grad = pair_grad.reshape(chips, 2, count, part, 2, ff_own).transpose(4, 0, 3, 2, 1, 5)
-    pair_grad = pair_grad.reshape(2, rows, ff).astype(F32)
+    pair_sum = pair_sum.reshape(count, part, 2 * ff_own)
+    pair_sum = exchange_line(
+        lambda j: lax.dynamic_index_in_dim(pair_sum, j, keepdims=False)
+    )
+    ffn_sum = pair_sum.reshape(count * part, 2 * ff_own)
 
     gain_two_sum = jnp.sum(grad_normed_two * unit_two, axis=0)
     grad_hidden_one = cotangent.astype(F32) + unit_back(
         grad_normed_two * gain_two, unit_two, inverse_two
     )
     grad_attn = jnp.concatenate(line_gather(grad_hidden_one.astype(BF)), axis=0)
+    output = (hidden_one + sum_tokens(after(hidden, grad_attn), down_own, mm)).astype(BF)
     grad_att = mm_last(grad_attn, out_weight).astype(BF).reshape(seq, kv_heads, groups, hd)
     grad_probs = jnp.einsum("tngd,snd->ngts", grad_att, values, preferred_element_type=F32)
     delta = jnp.sum(probs * grad_probs, axis=-1, keepdims=True)
@@ -301,20 +362,28 @@
     ).astype(BF)
 
     proj_part = mm_first(normed_one, grad_proj).astype(BF)
-    proj_part = proj_part.reshape(count, rep, share, -1).transpose(1, 0, 2, 3)
-    proj_part = proj_part.reshape(width, -1)
-    proj_sum = lax.psum_scatter(proj_part, PLANE, scatter_dimension=0, tiled=True)
-    proj_sum = transpose_line(proj_sum.reshape(count, share, -1))
-    proj_grad = lax.all_gather(proj_sum, PLANE, axis=0)
-
-    def rows_of(start, stop):
-        columns = proj_grad[..., start:stop].transpose(0, 2, 1, 3)
-        return columns.reshape(rows, -1).astype(F32)
-
-    out_sum = lax.psum_scatter(
-        mm_first(attended, grad_attn).astype(BF), PLANE, scatter_dimension=0, tiled=True
-    )
-    out_grad = lax.all_gather(out_sum, PLANE, axis=0, tiled=True).astype(F32)
+    out_term = mm_first(attended, grad_attn).astype(BF)
+    att_part = jnp.concatenate(
+        [proj_part[j * rows : (j + 1) * rows] for j in range(count)] + [out_term], axis=1
+    )
+    att_sum = lax.psum_scatter(att_part, PLANE, scatter_dimension=0, tiled=True)
+    cols = q_cols + 2 * kv_cols
+    got = exchange_line(lambda j: lax.dynamic_slice(att_sum, (0, j * cols), (share, cols)))
+    cuts = ((0, q_cols), (q_cols, q_cols + kv_cols), (q_cols + kv_cols, cols))
+    att_sum = jnp.concatenate(
+        [got[j, :, a:b] for a, b in cuts for j in range(count)] + [att_sum[:, count * cols :]],
+        axis=1,
+    )
+
+    down_all = lax.all_gather(down_sum, PLANE, axis=0)
+    ffn_all = lax.all_gather(ffn_sum, PLANE, axis=0)
+    gate_grad, up_grad = place_pair(ffn_all, chips, count, part, ff_own)
+    down_grad = place_down(down_all, chips, ff_own // chips, width)
+    att_all = lax.all_gather(att_sum, PLANE, axis=0, tiled=True)
+    edges = [0, q_cols * count, (q_cols + kv_cols) * count, cols * count, att_all.shape[1]]
+    query_grad, key_grad, value_grad, out_grad = (
+        att_all[:, a:b].astype(F32) for a, b in zip(edges[:-1], edges[1:])
+    )
 
     sums = sum_small(
         jnp.concatenate(
@@ -329,15 +398,15 @@
         output,
         input_grad,
         sums[:rows],
-        rows_of(0, q_cols),
-        rows_of(q_cols, q_cols + kv_cols),
-        rows_of(q_cols + kv_cols, q_cols + 2 * kv_cols),
+        query_grad,
+        key_grad,
+        value_grad,
         sums[2 * rows : 2 * rows + small],
         sums[2 * rows + small :],
         out_grad,
         sums[rows : 2 * rows],
-        pair_grad[0],
-        pair_grad[1],
+        gate_grad,
+        up_grad,
         down_grad,
     )
 

time: 1140 us -> 986 us (0.86)
  local copies, waits for them, and re-layouts: 245 us -> 109 us
  blocking collectives: 87.3 us -> 0 us
  waiting for transfers between devices: 399 us -> 454 us
  Pallas kernels: 0 us -> 35.6 us
  other arithmetic: 91.2 us -> 74.8 us
    ppermute x3 -> x15, waiting for transfers between devices: 0.01 us -> 98.2 us  [exchange_line(): lax.ppermute(piece_for((mine - e) % count), 'fsdp', [(i, (i - e) % count)...]
    all_to_all x3 -> x0, blocking collectives: 87.3 us -> none  [transpose_line(): lax.all_to_all(pieces, 'fsdp', split_axis=0, concat_axis=0, tiled=True)]
    slice x5 -> x7, local copies, waits for them, and re-layouts: 72.4 us -> 13.3 us  [the longest x5 10.9 us: shards(): proj_part[j * rows:(j + 1) * rows]]
    ppermute x12, waiting for transfers between devices: 70.6 us -> 24.4 us  [line_gather(): right = lax.ppermute(right, 'fsdp', ahead)]
    squeeze x2 -> x1, local copies, waits for them, and re-layouts: 44.4 us -> 1.67 us  [shards(): lax.dynamic_index_in_dim(pair_sum, j, keepdims=False)]
    pallas_call x0 -> x2, Pallas kernels: none -> 35.6 us  [the longest x1 25.2 us: place_pair(): pl.pallas_call(cast_pair, grid=(chips, count, 2), in_specs=[pl.BlockSpec(...]
    convert_element_type x5 -> x3, other arithmetic: 38 us -> 10.6 us  [the longest x2 9.69 us: shards(): att_all[:, a:b].astype(F32)]
    all_gather x6 -> x5, waiting for transfers between devices: 34.3 us -> 7.09 us  [the longest x1 7.08 us: shards(): ffn_all = lax.all_gather(ffn_sum, PLANE, axis=0)]
  transfers between devices with their start and end apart: 72 -> 81, of which waited for: 35 -> 46; matrix products, arithmetic and copies ran while one was open for 20% -> 15% of each run, Pallas kernels for 0% -> 1%
where the time goes in v2:
time: 986 us; the launch traced here: 971 us
  waiting for transfers between devices  454 us (46%)
  starting transfers between devices  178 us (18%)
  local copies, waits for them, and re-layouts  109 us (11%)
  matrix products  102 us (10%)
  other arithmetic  74.8 us (8%)
  Pallas kernels  35.6 us (4%)
  between operations  17.7 us (2%)
    ppermute x15, waiting for transfers between devices, exchange_line(): lax.ppermute(piece_for((mine - e) % count), 'fsdp', [(i, (i - e) % count)...  98.2 us
    reduce_scatter x1, waiting for transfers between devices, shards(): lax.psum_scatter(pair_part, 'chip', scatter_dimension=0, tiled=True)  89.8 us
    ppermute x12, waiting for transfers between devices, line_gather(): left = lax.ppermute(left, 'fsdp', back)  58.9 us
    ppermute x12, starting transfers between devices, line_gather(): right = lax.ppermute(right, 'fsdp', ahead)  57.4 us
    reduce_scatter x1, waiting for transfers between devices, shards(): att_sum = lax.psum_scatter(att_part, PLANE, scatter_dimension=0, tiled=True)  54.9 us
    ppermute x12, starting transfers between devices, line_scatter(): lax.ppermute(low.astype(BF), 'fsdp', [(i, i + 1) for i in range(t + 1)])  53.4 us
    ppermute x12, waiting for transfers between devices, line_scatter(): lax.ppermute(low.astype(BF), 'fsdp', [(i, i + 1) for i in range(t + 1)])  43.5 us
    reduce_scatter x1, waiting for transfers between devices, shards(): lax.psum_scatter(down_part, 'chip', scatter_dimension=0, tiled=True)  33.2 us
  transfers between devices with their start and end apart: 81, of which 46 were waited for; matrix products, arithmetic and copies ran while one was open for 15% of the time, Pallas kernels for 1%

profile of v2, /device:TPU:0, one launch (start us, length us, event | category | flops | bytes accessed | tf_op | source)
XLA Modules:
  0.0 970.9 jit_solution(6405734319216811206)
XLA Ops:
  8.1 5.1 collective-permute-start
  17.3 5.5 collective-permute-start.6
  38.1 4.7 collective-permute-done.11
  54.7 5.3 collective-permute-start.5
  67.3 5.2 collective-permute-done.3
  83.2 8.5 collective-permute-done.25
  92.5 27.7 %collective-permute-done.26 = bf16[128,2048]{1,0:T(8,128)(2,1)S(1)} collective-permute-done((bf16[128,2048]{1,0:T(8,128)(2,1)S(1)}, bf16[128,2048]{1,0:T(8,128)(2,1)S(1)}, u32[]{:S(2)}, u32[]{:S(2)}) %collective-permute-start.26) | collective-permute-done | bytes 524320 | tf_op jit(solution)/shard_map/ppermute | solution.py:108
  136.6 7.6 fusion.99
  144.2 4.3 fusion.33
  156.0 7.7 collective-permute-done.12
  163.8 5.4 collective-permute-start.13
  173.3 4.8 collective-permute-done.13
  181.6 5.1 collective-permute-start.14
  188.1 7.1 collective-permute-done.14
  195.3 11.8 %collective-permute-done.17 = bf16[128,2048]{1,0:T(8,128)(2,1)S(1)} collective-permute-done((bf16[128,2048]{1,0:T(8,128)(2,1)S(1)}, bf16[128,2048]{1,0:T(8,128)(2,1)S(1)}, u32[]{:S(2)}, u32[]{:S(2)}) %collective-permute-start.17) | collective-permute-done | bytes 524320 | tf_op jit(solution)/shard_map/ppermute | solution.py:90
  217.5 4.6 collective-permute-start.18
  222.1 6.3 collective-permute-done.19
  229.7 4.6 collective-permute-start.22
  234.3 6.3 collective-permute-done.20
  243.0 4.7 collective-permute-start.23
  260.5 5.0 collective-permute-start.28
  265.5 10.3 %collective-permute-done.29 = bf16[128,2048]{1,0:T(8,128)(2,1)S(1)} collective-permute-done((bf16[128,2048]{1,0:T(8,128)(2,1)S(1)}, bf16[128,2048]{1,0:T(8,128)(2,1)S(1)}, u32[]{:S(2)}, u32[]{:S(2)}) %collective-permute-start.29) | collective-permute-done | bytes 524320 | tf_op jit(solution)/shard_map/ppermute | solution.py:70
  277.1 4.6 collective-permute-start.32
  281.7 9.7 %collective-permute-done.30 = bf16[128,2048]{1,0:T(8,128)(2,1)S(1)} collective-permute-done((bf16[128,2048]{1,0:T(8,128)(2,1)S(1)}, bf16[128,2048]{1,0:T(8,128)(2,1)S(1)}, u32[]{:S(2)}, u32[]{:S(2)}) %collective-permute-start.30) | collective-permute-done | bytes 524320 | tf_op jit(solution)/shard_map/ppermute | solution.py:70
  292.8 4.6 collective-permute-start.33
  297.4 8.8 collective-permute-done.31
  311.2 14.6 %fusion.101 = f32[1024,2048]{1,0:T(8,128)} fusion(bf16[1024,2048]{1,0:T(8,128)(2,1)} %copy-done.56, bf16[2048,2048]{1,0:T(8,128)(2,1)} %bitcast.263), kind=kOutput, calls=%fused_computation.305 | convolution fusion | flops 8589934592 | bytes 20971520 | tf_op jit(solution)/shard_map/dot_general | solution.py:48
  327.5 9.7 multiply_convert_fusion
  337.2 10.3 %convolution_convert_fusion.4 = bf16[512,2048]{1,0:T(8,128)(2,1)S(1)} fusion(bf16[2048,2048]{1,0:T(8,128)(2,1)} %bitcast.264, bf16[1024,1024]{1,0:T(8,128)(2,1)S(1)} %get-tuple-element.58, bf16[1024,1024]{1,0:T(8,128)(2,1)S(1)} %get-tuple-element.57), kind=kOutput, calls=%fused_computation.41 | convolution fusion | flops 4300210176 | bytes 14680064 | tf_op jit(solution)/shard_map/dot_general | solution.py:52
  351.9 7.3 convert_add_fusion.1
  362.3 5.2 collective-permute-start.36
  369.4 6.2 convolution_convert_fusion.1
  381.5 5.2 collective-permute-start.38
  388.1 14.0 %convolution_convert_fusion = bf16[2048,2048]{1,0:T(8,128)(2,1)} fusion(bf16[1024,2048]{1,0:T(8,128)(2,1)} %copy-done.56, bf16[1024,1024]{1,0:T(8,128)(2,1)} %copy-done.73, bf16[1024,1024]{1,0:T(8,128)(2,1)} %copy-done.74), kind=kOutput, calls=%fused_computation.8 | convolution fusion | flops 8602517504 | bytes 16777216 | tf_op jit(solution)/shard_map/dot_general | solution.py:56
  405.6 4.6 collective-permute-start.40
  410.2 9.3 collective-permute-done.41
  434.9 4.4 collective-permute-start.42
  440.7 8.3 collective-permute-done.42
  449.7 5.2 collective-permute-start.46
  456.2 6.7 collective-permute-done.46
  462.9 5.3 collective-permute-start.47
  479.8 8.2 collective-permute-done.45
  543.9 54.9 %reduce-scatter.4.cloned.1.call-done = bf16[64,5120]{1,0:T(8,128)(2,1)} async-done(((bf16[512,5120]{1,0:T(8,128)(2,1)}), bf16[64,5120]{1,0:T(8,128)(2,1)}) %reduce-scatter.4.cloned.1.call-update) | async-done | bytes 655376 | tf_op jit(solution)/shard_map/reduce_scatter | solution.py:369
  606.5 5.6 collective-permute-done.68
  622.2 33.2 %reduce-scatter.8.cloned.1.call-done = bf16[256,2048]{1,0:T(8,128)(2,1)} async-done(((bf16[1024,2048]{1,0:T(8,128)(2,1)}), bf16[256,2048]{1,0:T(8,128)(2,1)}) %reduce-scatter.8.cloned.1.call-update) | async-done | bytes 1048592 | tf_op jit(solution)/shard_map/reduce_scatter | solution.py:323
  655.5 89.8 %reduce-scatter.6.cloned.1.call-done = bf16[512,2048]{1,0:T(8,128)(2,1)} async-done(((bf16[2048,2048]{1,0:T(8,128)(2,1)}), bf16[512,2048]{1,0:T(8,128)(2,1)}) %reduce-scatter.6.cloned.1.call-update) | async-done | bytes 2097168 | tf_op jit(solution)/shard_map/reduce_scatter | solution.py:324
  751.7 11.1 %collective-permute-done.70 = bf16[128,2048]{1,0:T(8,128)(2,1)S(1)} collective-permute-done((bf16[128,2048]{1,0:T(8,128)(2,1)S(1)}, bf16[128,2048]{1,0:T(8,128)(2,1)S(1)}, u32[]{:S(2)}, u32[]{:S(2)}) %collective-permute-start.70) | collective-permute-done | bytes 524320 | tf_op jit(solution)/shard_map/ppermute | solution.py:108
  762.8 32.5 %collective-permute-done.71 = bf16[128,2048]{1,0:T(8,128)(2,1)S(1)} collective-permute-done((bf16[128,2048]{1,0:T(8,128)(2,1)S(1)}, bf16[128,2048]{1,0:T(8,128)(2,1)S(1)}, u32[]{:S(2)}, u32[]{:S(2)}) %collective-permute-start.71) | collective-permute-done | bytes 524320 | tf_op jit(solution)/shard_map/ppermute | solution.py:108
  798.1 5.5 fusion.18
  809.5 4.5 convert_add_fusion
  822.5 5.2 collective-permute-start.56
  828.6 4.4 collective-permute-done.49
  834.5 4.4 collective-permute-start.50
  838.9 5.3 collective-permute-done.56
  847.8 7.1 collective-permute-done.50
  856.7 5.8 collective-permute-start.57
  868.5 6.5 collective-permute-start.51
  877.6 4.6 collective-permute-done.60
  884.8 8.7 collective-permute-start.62
  893.7 4.6 collective-permute-done.62
  913.6 6.9 slice_convert_fusion
  920.5 10.3 %shard_map.238 = f32[2048,2048]{1,0:T(8,128)} custom-call(bf16[8,256,2048]{2,1,0:T(8,128)(2,1)} %bitcast.228), custom_call_target="tpu_custom_call" | custom-call | tf_op jit(solution)/shard_map/pallas_call | solution.py:167
  930.9 7.1 all-gather.11.cloned.1.call-done.own
  937.9 25.2 %shard_map.237 = (f32[512,8192]{1,0:T(8,128)}, f32[512,8192]{1,0:T(8,128)}) custom-call(bf16[8,512,2048]{2,1,0:T(8,128)(2,1)} %all-gather.11.cloned.1.call-done.own), custom_call_target="tpu_custom_call" | custom-call | tf_op jit(solution)/shard_map/pallas_call | solution.py:153
  (481 shorter events, 300.1 us)
Async XLA Ops:
  8.0 114.8 %all-gather.13.cloned.1.call-start = ((), (), s32[]{:S(2)}) async-start(), calls=%async_computation.8 | async-start | bytes 3538944 | tf_op jit(solution)/shard_map/all_gather | solution.py:227
  8.1 35.7 %collective-permute-start = (bf16[128,2048]{1,0:T(8,128)(2,1)}, bf16[128,2048]{1,0:T(8,128)(2,1)S(1)}, u32[]{:S(2)}, u32[]{:S(2)}) collective-permute-start(bf16[128,2048]{1,0:T(8,128)(2,1)} %param.14), channel_id=1, source_target_pairs={{0,1},{1,2},{2,3},{4,5},{5,6},{6,7},{8,9},{9,10},{10,11},{12,13},{... | collective-permute-start | bytes 1572872 | tf_op jit(solution)/shard_map/ppermute | solution.py:69
  13.2 35.8 %collective-permute-start.1 = (bf16[128,2048]{1,0:T(8,128)(2,1)}, bf16[128,2048]{1,0:T(8,128)(2,1)}, u32[]{:S(2)}, u32[]{:S(2)}) collective-permute-start(bf16[128,2048]{1,0:T(8,128)(2,1)} %param.14), channel_id=1, source_target_pairs={{1,0},{2,1},{3,2},{5,4},{6,5},{7,6},{9,8},{10,9},{11,10},{13,12},{... | collective-permute-start | bytes 1572872 | tf_op jit(solution)/shard_map/ppermute | solution.py:70
  17.3 31.6 %collective-permute-start.6 = (bf16[1056]{0:T(1024)(128)(2,1)S(1)}, bf16[1056]{0:T(1024)(128)(2,1)S(1)}, u32[]{:S(2)}, u32[]{:S(2)}) collective-permute-start(bf16[1056]{0:T(1024)(128)(2,1)S(1)} %concatenate.86), channel_id=1, source_target_pairs={{0,3},{1,0},{2,1},{3,2},{4,7},{5,4},{6,5},{7,6},{8,11},{9,8},{10,9... | collective-permute-start | bytes 6344 | tf_op jit(solution)/shard_map/ppermute | solution.py:108
  22.7 26.1 %collective-permute-start.7 = (bf16[1056]{0:T(1024)(128)(2,1)S(1)}, bf16[1056]{0:T(1024)(128)(2,1)S(1)}, u32[]{:S(2)}, u32[]{:S(2)}) collective-permute-start(bf16[1056]{0:T(1024)(128)(2,1)S(1)} %concatenate.86), channel_id=1, source_target_pairs={{0,2},{1,3},{2,0},{3,1},{4,6},{5,7},{6,4},{7,5},{8,10},{9,11},{10,... | collective-permute-start | bytes 6344 | tf_op jit(solution)/shard_map/ppermute | solution.py:108
  43.7 267.4 %all-gather.15.cloned.1.call-start = ((), (), s32[]{:S(2)}) async-start(), calls=%async_computation.9 | async-start | bytes 10485760 | tf_op jit(solution)/shard_map/all_gather | solution.py:250
  49.0 12.3 %collective-permute-start.2 = (bf16[128,2048]{1,0:T(8,128)(2,1)}, bf16[128,2048]{1,0:T(8,128)(2,1)}, u32[]{:S(2)}, u32[]{:S(2)}) collective-permute-start(bf16[128,2048]{1,0:T(8,128)(2,1)} %collective-permute-done.1), channel_id=1, source_target_pairs={{1,0},{2,1},{3,2},{5,4},{6,5},{7,6},{9,8},{10,9},{11,10},{13,12},{... | collective-permute-start | bytes 1572872 | tf_op jit(solution)/shard_map/ppermute | solution.py:70
  54.7 11.5 %collective-permute-start.5 = (bf16[128,2048]{1,0:T(8,128)(2,1)}, bf16[128,2048]{1,0:T(8,128)(2,1)}, u32[]{:S(2)}, u32[]{:S(2)}) collective-permute-start(bf16[128,2048]{1,0:T(8,128)(2,1)} %collective-permute-done.4), channel_id=1, source_target_pairs={{0,1},{1,2},{2,3},{4,5},{5,6},{6,7},{8,9},{9,10},{10,11},{12,13},{... | collective-permute-start | bytes 1572872 | tf_op jit(solution)/shard_map/ppermute | solution.py:69
  61.3 11.3 %collective-permute-start.3 = (bf16[128,2048]{1,0:T(8,128)(2,1)}, bf16[128,2048]{1,0:T(8,128)(2,1)S(1)}, u32[]{:S(2)}, u32[]{:S(2)}) collective-permute-start(bf16[128,2048]{1,0:T(8,128)(2,1)} %collective-permute-done.2), channel_id=1, source_target_pairs={{1,0},{2,1},{3,2},{5,4},{6,5},{7,6},{9,8},{10,9},{11,10},{13,12},{... | collective-permute-start | bytes 1572872 | tf_op jit(solution)/shard_map/ppermute | solution.py:70
  76.9 14.7 %collective-permute-start.25 = (bf16[128,2048]{1,0:T(8,128)(2,1)S(1)}, bf16[128,2048]{1,0:T(8,128)(2,1)S(1)}, u32[]{:S(2)}, u32[]{:S(2)}) collective-permute-start(bf16[128,2048]{1,0:T(8,128)(2,1)S(1)} %pad_maximum_fusion.9), channel_id=1, source_target_pairs={{0,3},{1,0},{2,1},{3,2},{4,7},{5,4},{6,5},{7,6},{8,11},{9,8},{10,9... | collective-permute-start | bytes 1572872 | tf_op jit(solution)/shard_map/ppermute | solution.py:108
  79.3 40.9 %collective-permute-start.26 = (bf16[128,2048]{1,0:T(8,128)(2,1)S(1)}, bf16[128,2048]{1,0:T(8,128)(2,1)S(1)}, u32[]{:S(2)}, u32[]{:S(2)}) collective-permute-start(bf16[128,2048]{1,0:T(8,128)(2,1)S(1)} %pad_maximum_fusion.10), channel_id=1, source_target_pairs={{0,2},{1,3},{2,0},{3,1},{4,6},{5,7},{6,4},{7,5},{8,10},{9,11},{10,... | collective-permute-start | bytes 1572872 | tf_op jit(solution)/shard_map/ppermute | solution.py:108
  80.3 40.8 %collective-permute-start.27 = (bf16[128,2048]{1,0:T(8,128)(2,1)S(1)}, bf16[128,2048]{1,0:T(8,128)(2,1)S(1)}, u32[]{:S(2)}, u32[]{:S(2)}) collective-permute-start(bf16[128,2048]{1,0:T(8,128)(2,1)S(1)} %pad_maximum_fusion.11), channel_id=1, source_target_pairs={{0,1},{1,2},{2,3},{3,0},{4,5},{5,6},{6,7},{7,4},{8,9},{9,10},{10,1... | collective-permute-start | bytes 1572872 | tf_op jit(solution)/shard_map/ppermute | solution.py:108
  151.5 12.2 %collective-permute-start.12 = (bf16[128,2048]{1,0:T(8,128)(2,1)S(1)}, bf16[128,2048]{1,0:T(8,128)(2,1)S(1)}, u32[]{:S(2)}, u32[]{:S(2)}) collective-permute-start(bf16[128,2048]{1,0:T(8,128)(2,1)S(1)} %get-tuple-element.88), channel_id=1, source_target_pairs={{0,1},{4,5},{8,9},{12,13},{16,17},{20,21},{24,25},{28,29}} | collective-permute-start | bytes 1572872 | tf_op jit(solution)/shard_map/ppermute | solution.py:89
  154.5 18.8 %collective-permute-start.15 = (bf16[128,2048]{1,0:T(8,128)(2,1)}, bf16[128,2048]{1,0:T(8,128)(2,1)}, u32[]{:S(2)}, u32[]{:S(2)}) collective-permute-start(bf16[128,2048]{1,0:T(8,128)(2,1)} %get-tuple-element.89), channel_id=1, source_target_pairs={{3,2},{7,6},{11,10},{15,14},{19,18},{23,22},{27,26},{31,30}} | collective-permute-start | bytes 1572872 | tf_op jit(solution)/shard_map/ppermute | solution.py:90
  163.8 14.3 %collective-permute-start.13 = (bf16[128,2048]{1,0:T(8,128)(2,1)S(1)}, bf16[128,2048]{1,0:T(8,128)(2,1)}, u32[]{:S(2)}, u32[]{:S(2)}) collective-permute-start(bf16[128,2048]{1,0:T(8,128)(2,1)S(1)} %add_convert_fusion.16), channel_id=1, source_target_pairs={{0,1},{1,2},{4,5},{5,6},{8,9},{9,10},{12,13},{13,14},{16,17},{17,1... | collective-permute-start | bytes 1572872 | tf_op jit(solution)/shard_map/ppermute | solution.py:89
  173.2 425.6 %reduce-scatter.4.cloned.1.call-start = ((), (), s32[]{:S(2)}) async-start(), calls=%async_computation.3 | async-start | bytes 5898240 | tf_op jit(solution)/shard_map/reduce_scatter | solution.py:369
  181.6 13.7 %collective-permute-start.14 = (bf16[128,2048]{1,0:T(8,128)(2,1)S(1)}, bf16[128,2048]{1,0:T(8,128)(2,1)S(1)}, u32[]{:S(2)}, u32[]{:S(2)}) collective-permute-start(bf16[128,2048]{1,0:T(8,128)(2,1)S(1)} %get-tuple-element.86), channel_id=1, source_target_pairs={{0,1},{1,2},{2,3},{4,5},{5,6},{6,7},{8,9},{9,10},{10,11},{12,13},{... | collective-permute-start | bytes 1572872 | tf_op jit(solution)/shard_map/ppermute | solution.py:89
  186.8 20.3 %collective-permute-start.17 = (bf16[128,2048]{1,0:T(8,128)(2,1)S(1)}, bf16[128,2048]{1,0:T(8,128)(2,1)S(1)}, u32[]{:S(2)}, u32[]{:S(2)}) collective-permute-start(bf16[128,2048]{1,0:T(8,128)(2,1)S(1)} %add_convert_fusion.13), channel_id=1, source_target_pairs={{3,2},{2,1},{1,0},{7,6},{6,5},{5,4},{11,10},{10,9},{9,8},{15,14},{... | collective-permute-start | bytes 1572872 | tf_op jit(solution)/shard_map/ppermute | solution.py:90
  216.1 12.3 %collective-permute-start.19 = (bf16[128,2048]{1,0:T(8,128)(2,1)}, bf16[128,2048]{1,0:T(8,128)(2,1)S(1)}, u32[]{:S(2)}, u32[]{:S(2)}) collective-permute-start(bf16[128,2048]{1,0:T(8,128)(2,1)} %reshape.350), channel_id=1, source_target_pairs={{1,0},{2,1},{3,2},{5,4},{6,5},{7,6},{9,8},{10,9},{11,10},{13,12},{... | collective-permute-start | bytes 1572872 | tf_op jit(solution)/shard_map/ppermute | solution.py:70
  217.5 12.2 %collective-permute-start.18 = (bf16[128,2048]{1,0:T(8,128)(2,1)}, bf16[128,2048]{1,0:T(8,128)(2,1)S(1)}, u32[]{:S(2)}, u32[]{:S(2)}) collective-permute-start(bf16[128,2048]{1,0:T(8,128)(2,1)} %reshape.350), channel_id=1, source_target_pairs={{0,1},{1,2},{2,3},{4,5},{5,6},{6,7},{8,9},{9,10},{10,11},{12,13},{... | collective-permute-start | bytes 1572872 | tf_op jit(solution)/shard_map/ppermute | solution.py:69
  228.4 12.2 %collective-permute-start.20 = (bf16[128,2048]{1,0:T(8,128)(2,1)S(1)}, bf16[128,2048]{1,0:T(8,128)(2,1)S(1)}, u32[]{:S(2)}, u32[]{:S(2)}) collective-permute-start(bf16[128,2048]{1,0:T(8,128)(2,1)S(1)} %collective-permute-done.19), channel_id=1, source_target_pairs={{1,0},{2,1},{3,2},{5,4},{6,5},{7,6},{9,8},{10,9},{11,10},{13,12},{... | collective-permute-start | bytes 1572872 | tf_op jit(solution)/shard_map/ppermute | solution.py:70
  229.7 13.3 %collective-permute-start.22 = (bf16[128,2048]{1,0:T(8,128)(2,1)S(1)}, bf16[128,2048]{1,0:T(8,128)(2,1)S(1)}, u32[]{:S(2)}, u32[]{:S(2)}) collective-permute-start(bf16[128,2048]{1,0:T(8,128)(2,1)S(1)} %collective-permute-done.18), channel_id=1, source_target_pairs={{0,1},{1,2},{2,3},{4,5},{5,6},{6,7},{8,9},{9,10},{10,11},{12,13},{... | collective-permute-start | bytes 1572872 | tf_op jit(solution)/shard_map/ppermute | solution.py:69
  240.6 11.2 %collective-permute-start.21 = (bf16[128,2048]{1,0:T(8,128)(2,1)S(1)}, bf16[128,2048]{1,0:T(8,128)(2,1)S(1)}, u32[]{:S(2)}, u32[]{:S(2)}) collective-permute-start(bf16[128,2048]{1,0:T(8,128)(2,1)S(1)} %collective-permute-done.20), channel_id=1, source_target_pairs={{1,0},{2,1},{3,2},{5,4},{6,5},{7,6},{9,8},{10,9},{11,10},{13,12},{... | collective-permute-start | bytes 1572872 | tf_op jit(solution)/shard_map/ppermute | solution.py:70
  243.0 11.4 %collective-permute-start.23 = (bf16[128,2048]{1,0:T(8,128)(2,1)S(1)}, bf16[128,2048]{1,0:T(8,128)(2,1)S(1)}, u32[]{:S(2)}, u32[]{:S(2)}) collective-permute-start(bf16[128,2048]{1,0:T(8,128)(2,1)S(1)} %collective-permute-done.22), channel_id=1, source_target_pairs={{0,1},{1,2},{2,3},{4,5},{5,6},{6,7},{8,9},{9,10},{10,11},{12,13},{... | collective-permute-start | bytes 1572872 | tf_op jit(solution)/shard_map/ppermute | solution.py:69
  259.2 16.6 %collective-permute-start.29 = (bf16[128,2048]{1,0:T(8,128)(2,1)S(1)}, bf16[128,2048]{1,0:T(8,128)(2,1)S(1)}, u32[]{:S(2)}, u32[]{:S(2)}) collective-permute-start(bf16[128,2048]{1,0:T(8,128)(2,1)S(1)} %copy-done.12), channel_id=1, source_target_pairs={{1,0},{2,1},{3,2},{5,4},{6,5},{7,6},{9,8},{10,9},{11,10},{13,12},{... | collective-permute-start | bytes 1572872 | tf_op jit(solution)/shard_map/ppermute | solution.py:70
  260.5 16.6 %collective-permute-start.28 = (bf16[128,2048]{1,0:T(8,128)(2,1)S(1)}, bf16[128,2048]{1,0:T(8,128)(2,1)S(1)}, u32[]{:S(2)}, u32[]{:S(2)}) collective-permute-start(bf16[128,2048]{1,0:T(8,128)(2,1)S(1)} %copy-done.12), channel_id=1, source_target_pairs={{0,1},{1,2},{2,3},{4,5},{5,6},{6,7},{8,9},{9,10},{10,11},{12,13},{... | collective-permute-start | bytes 1572872 | tf_op jit(solution)/shard_map/ppermute | solution.py:69
  275.8 15.6 %collective-permute-start.30 = (bf16[128,2048]{1,0:T(8,128)(2,1)S(1)}, bf16[128,2048]{1,0:T(8,128)(2,1)S(1)}, u32[]{:S(2)}, u32[]{:S(2)}) collective-permute-start(bf16[128,2048]{1,0:T(8,128)(2,1)S(1)} %collective-permute-done.29), channel_id=1, source_target_pairs={{1,0},{2,1},{3,2},{5,4},{6,5},{7,6},{9,8},{10,9},{11,10},{13,12},{... | collective-permute-start | bytes 1572872 | tf_op jit(solution)/shard_map/ppermute | solution.py:70
  277.1 15.7 %collective-permute-start.32 = (bf16[128,2048]{1,0:T(8,128)(2,1)S(1)}, bf16[128,2048]{1,0:T(8,128)(2,1)S(1)}, u32[]{:S(2)}, u32[]{:S(2)}) collective-permute-start(bf16[128,2048]{1,0:T(8,128)(2,1)S(1)} %collective-permute-done.28), channel_id=1, source_target_pairs={{0,1},{1,2},{2,3},{4,5},{5,6},{6,7},{8,9},{9,10},{10,11},{12,13},{... | collective-permute-start | bytes 1572872 | tf_op jit(solution)/shard_map/ppermute | solution.py:69
  291.4 14.8 %collective-permute-start.31 = (bf16[128,2048]{1,0:T(8,128)(2,1)S(1)}, bf16[128,2048]{1,0:T(8,128)(2,1)S(1)}, u32[]{:S(2)}, u32[]{:S(2)}) collective-permute-start(bf16[128,2048]{1,0:T(8,128)(2,1)S(1)} %collective-permute-done.30), channel_id=1, source_target_pairs={{1,0},{2,1},{3,2},{5,4},{6,5},{7,6},{9,8},{10,9},{11,10},{13,12},{... | collective-permute-start | bytes 1572872 | tf_op jit(solution)/shard_map/ppermute | solution.py:70
  292.8 14.6 %collective-permute-start.33 = (bf16[128,2048]{1,0:T(8,128)(2,1)S(1)}, bf16[128,2048]{1,0:T(8,128)(2,1)S(1)}, u32[]{:S(2)}, u32[]{:S(2)}) collective-permute-start(bf16[128,2048]{1,0:T(8,128)(2,1)S(1)} %collective-permute-done.32), channel_id=1, source_target_pairs={{0,1},{1,2},{2,3},{4,5},{5,6},{6,7},{8,9},{9,10},{10,11},{12,13},{... | collective-permute-start | bytes 1572872 | tf_op jit(solution)/shard_map/ppermute | solution.py:69
  311.2 14.6 %collective-permute-start.34 = (bf16[512,2048]{1,0:T(8,128)(2,1)}, bf16[512,2048]{1,0:T(8,128)(2,1)}, u32[]{:S(2)}, u32[]{:S(2)}) collective-permute-start(bf16[512,2048]{1,0:T(8,128)(2,1)} %pad_maximum_fusion.4), channel_id=1, source_target_pairs={{0,4},{4,0},{1,5},{5,1},{2,6},{6,2},{3,7},{7,3},{8,12},{12,8},{9,1... | collective-permute-start | bytes 6291464 | tf_op jit(solution)/shard_map/ppermute | solution.py:60
  362.3 16.4 %collective-permute-start.36 = (bf16[128,2048]{1,0:T(8,128)(2,1)}, bf16[128,2048]{1,0:T(8,128)(2,1)}, u32[]{:S(2)}, u32[]{:S(2)}) collective-permute-start(bf16[128,2048]{1,0:T(8,128)(2,1)} %get-tuple-element.81), channel_id=1, source_target_pairs={{0,1},{4,5},{8,9},{12,13},{16,17},{20,21},{24,25},{28,29}} | collective-permute-start | bytes 1572872 | tf_op jit(solution)/shard_map/ppermute | solution.py:89
  367.5 11.2 %collective-permute-start.37 = (bf16[128,2048]{1,0:T(8,128)(2,1)}, bf16[128,2048]{1,0:T(8,128)(2,1)}, u32[]{:S(2)}, u32[]{:S(2)}) collective-permute-start(bf16[128,2048]{1,0:T(8,128)(2,1)} %get-tuple-element.80), channel_id=1, source_target_pairs={{3,2},{7,6},{11,10},{15,14},{19,18},{23,22},{27,26},{31,30}} | collective-permute-start | bytes 1572872 | tf_op jit(solution)/shard_map/ppermute | solution.py:90
  381.5 20.7 %collective-permute-start.38 = (bf16[128,2048]{1,0:T(8,128)(2,1)}, bf16[128,2048]{1,0:T(8,128)(2,1)}, u32[]{:S(2)}, u32[]{:S(2)}) collective-permute-start(bf16[128,2048]{1,0:T(8,128)(2,1)} %get-tuple-element.79), channel_id=1, source_target_pairs={{0,1},{1,2},{4,5},{5,6},{8,9},{9,10},{12,13},{13,14},{16,17},{17,1... | collective-permute-start | bytes 1572872 | tf_op jit(solution)/shard_map/ppermute | solution.py:89
  386.7 15.5 %collective-permute-start.39 = (bf16[128,2048]{1,0:T(8,128)(2,1)}, bf16[128,2048]{1,0:T(8,128)(2,1)}, u32[]{:S(2)}, u32[]{:S(2)}) collective-permute-start(bf16[128,2048]{1,0:T(8,128)(2,1)} %get-tuple-element.78), channel_id=1, source_target_pairs={{3,2},{2,1},{7,6},{6,5},{11,10},{10,9},{15,14},{14,13},{19,18},{18... | collective-permute-start | bytes 1572872 | tf_op jit(solution)/shard_map/ppermute | solution.py:90
  404.3 15.2 %collective-permute-start.41 = (bf16[128,2048]{1,0:T(8,128)(2,1)S(1)}, bf16[128,2048]{1,0:T(8,128)(2,1)S(1)}, u32[]{:S(2)}, u32[]{:S(2)}) collective-permute-start(bf16[128,2048]{1,0:T(8,128)(2,1)S(1)} %get-tuple-element.77), channel_id=1, source_target_pairs={{3,2},{2,1},{1,0},{7,6},{6,5},{5,4},{11,10},{10,9},{9,8},{15,14},{... | collective-permute-start | bytes 1572872 | tf_op jit(solution)/shard_map/ppermute | solution.py:90
  405.6 15.1 %collective-permute-start.40 = (bf16[128,2048]{1,0:T(8,128)(2,1)S(1)}, bf16[128,2048]{1,0:T(8,128)(2,1)S(1)}, u32[]{:S(2)}, u32[]{:S(2)}) collective-permute-start(bf16[128,2048]{1,0:T(8,128)(2,1)S(1)} %get-tuple-element.76), channel_id=1, source_target_pairs={{0,1},{1,2},{2,3},{4,5},{5,6},{6,7},{8,9},{9,10},{10,11},{12,13},{... | collective-permute-start | bytes 1572872 | tf_op jit(solution)/shard_map/ppermute | solution.py:89
  434.9 14.0 %collective-permute-start.42 = (bf16[128,2048]{1,0:T(8,128)(2,1)S(1)}, bf16[128,2048]{1,0:T(8,128)(2,1)S(1)}, u32[]{:S(2)}, u32[]{:S(2)}) collective-permute-start(bf16[128,2048]{1,0:T(8,128)(2,1)S(1)} %fusion.84), channel_id=1, source_target_pairs={{0,1},{1,2},{2,3},{4,5},{5,6},{6,7},{8,9},{9,10},{10,11},{12,13},{... | collective-permute-start | bytes 1572872 | tf_op jit(solution)/shard_map/ppermute | solution.py:69
  439.4 15.6 %collective-permute-start.43 = (bf16[128,2048]{1,0:T(8,128)(2,1)S(1)}, bf16[128,2048]{1,0:T(8,128)(2,1)}, u32[]{:S(2)}, u32[]{:S(2)}) collective-permute-start(bf16[128,2048]{1,0:T(8,128)(2,1)S(1)} %fusion.84), channel_id=1, source_target_pairs={{1,0},{2,1},{3,2},{5,4},{6,5},{7,6},{9,8},{10,9},{11,10},{13,12},{... | collective-permute-start | bytes 1572872 | tf_op jit(solution)/shard_map/ppermute | solution.py:70
  449.7 13.2 %collective-permute-start.46 = (bf16[128,2048]{1,0:T(8,128)(2,1)S(1)}, bf16[128,2048]{1,0:T(8,128)(2,1)}, u32[]{:S(2)}, u32[]{:S(2)}) collective-permute-start(bf16[128,2048]{1,0:T(8,128)(2,1)S(1)} %collective-permute-done.42), channel_id=1, source_target_pairs={{0,1},{1,2},{2,3},{4,5},{5,6},{6,7},{8,9},{9,10},{10,11},{12,13},{... | collective-permute-start | bytes 1572872 | tf_op jit(solution)/shard_map/ppermute | solution.py:69
  454.9 20.8 %collective-permute-start.44 = (bf16[128,2048]{1,0:T(8,128)(2,1)}, bf16[128,2048]{1,0:T(8,128)(2,1)}, u32[]{:S(2)}, u32[]{:S(2)}) collective-permute-start(bf16[128,2048]{1,0:T(8,128)(2,1)} %collective-permute-done.43), channel_id=1, source_target_pairs={{1,0},{2,1},{3,2},{5,4},{6,5},{7,6},{9,8},{10,9},{11,10},{13,12},{... | collective-permute-start | bytes 1572872 | tf_op jit(solution)/shard_map/ppermute | solution.py:70
  462.9 15.5 %collective-permute-start.47 = (bf16[128,2048]{1,0:T(8,128)(2,1)}, bf16[128,2048]{1,0:T(8,128)(2,1)}, u32[]{:S(2)}, u32[]{:S(2)}) collective-permute-start(bf16[128,2048]{1,0:T(8,128)(2,1)} %collective-permute-done.46), channel_id=1, source_target_pairs={{0,1},{1,2},{2,3},{4,5},{5,6},{6,7},{8,9},{9,10},{10,11},{12,13},{... | collective-permute-start | bytes 1572872 | tf_op jit(solution)/shard_map/ppermute | solution.py:69
  475.7 12.3 %collective-permute-start.45 = (bf16[128,2048]{1,0:T(8,128)(2,1)}, bf16[128,2048]{1,0:T(8,128)(2,1)S(1)}, u32[]{:S(2)}, u32[]{:S(2)}) collective-permute-start(bf16[128,2048]{1,0:T(8,128)(2,1)} %collective-permute-done.44), channel_id=1, source_target_pairs={{1,0},{2,1},{3,2},{5,4},{6,5},{7,6},{9,8},{10,9},{11,10},{13,12},{... | collective-permute-start | bytes 1572872 | tf_op jit(solution)/shard_map/ppermute | solution.py:70
  542.6 112.8 %reduce-scatter.8.cloned.1.call-start = ((), (), s32[]{:S(2)}) async-start(), calls=%async_computation.7 | async-start | bytes 5242880 | tf_op jit(solution)/shard_map/reduce_scatter | solution.py:323
  543.3 202.0 %reduce-scatter.6.cloned.1.call-start = ((), (), s32[]{:S(2)}) async-start(), calls=%async_computation.5 | async-start | bytes 10485760 | tf_op jit(solution)/shard_map/reduce_scatter | solution.py:324
  543.9 367.0 %all-gather.9.cloned.1.call-start = ((), (), s32[]{:S(2)}) async-start(), calls=%async_computation.4 | async-start | bytes 5898240 | tf_op jit(solution)/shard_map/all_gather | solution.py:382
  622.1 298.4 %all-gather.17.cloned.1.call-start = ((), (), s32[]{:S(2)}) async-start(), calls=%async_computation.10 | async-start | bytes 9437184 | tf_op jit(solution)/shard_map/all_gather | solution.py:378
  655.4 282.5 %all-gather.11.cloned.1.call-start = ((), (), s32[]{:S(2)}) async-start(), calls=%async_computation.6 | async-start | bytes 18874368 | tf_op jit(solution)/shard_map/all_gather | solution.py:379
  747.0 15.7 %collective-permute-start.70 = (bf16[128,2048]{1,0:T(8,128)(2,1)S(1)}, bf16[128,2048]{1,0:T(8,128)(2,1)S(1)}, u32[]{:S(2)}, u32[]{:S(2)}) collective-permute-start(bf16[128,2048]{1,0:T(8,128)(2,1)S(1)} %get-tuple-element.99), channel_id=1, source_target_pairs={{0,3},{1,0},{2,1},{3,2},{4,7},{5,4},{6,5},{7,6},{8,11},{9,8},{10,9... | collective-permute-start | bytes 1572872 | tf_op jit(solution)/shard_map/ppermute | solution.py:108
  750.4 44.9 %collective-permute-start.71 = (bf16[128,2048]{1,0:T(8,128)(2,1)S(1)}, bf16[128,2048]{1,0:T(8,128)(2,1)S(1)}, u32[]{:S(2)}, u32[]{:S(2)}) collective-permute-start(bf16[128,2048]{1,0:T(8,128)(2,1)S(1)} %get-tuple-element.98), channel_id=1, source_target_pairs={{0,2},{1,3},{2,0},{3,1},{4,6},{5,7},{6,4},{7,5},{8,10},{9,11},{10,... | collective-permute-start | bytes 1572872 | tf_op jit(solution)/shard_map/ppermute | solution.py:108
  750.4 45.0 %collective-permute-start.72 = (bf16[128,2048]{1,0:T(8,128)(2,1)S(1)}, bf16[128,2048]{1,0:T(8,128)(2,1)S(1)}, u32[]{:S(2)}, u32[]{:S(2)}) collective-permute-start(bf16[128,2048]{1,0:T(8,128)(2,1)S(1)} %get-tuple-element.96), channel_id=1, source_target_pairs={{0,1},{1,2},{2,3},{3,0},{4,5},{5,6},{6,7},{7,4},{8,9},{9,10},{10,1... | collective-permute-start | bytes 1572872 | tf_op jit(solution)/shard_map/ppermute | solution.py:108
  806.7 14.9 %collective-permute-start.55 = (bf16[128,2048]{1,0:T(8,128)(2,1)S(1)}, bf16[128,2048]{1,0:T(8,128)(2,1)S(1)}, u32[]{:S(2)}, u32[]{:S(2)}) collective-permute-start(bf16[128,2048]{1,0:T(8,128)(2,1)S(1)} %get-tuple-element.74), channel_id=1, source_target_pairs={{0,1},{4,5},{8,9},{12,13},{16,17},{20,21},{24,25},{28,29}} | collective-permute-start | bytes 1572872 | tf_op jit(solution)/shard_map/ppermute | solution.py:89
  815.3 17.7 %collective-permute-start.49 = (bf16[128,2048]{1,0:T(8,128)(2,1)}, bf16[128,2048]{1,0:T(8,128)(2,1)}, u32[]{:S(2)}, u32[]{:S(2)}) collective-permute-start(bf16[128,2048]{1,0:T(8,128)(2,1)} %get-tuple-element.84), channel_id=1, source_target_pairs={{0,1},{4,5},{8,9},{12,13},{16,17},{20,21},{24,25},{28,29}} | collective-permute-start | bytes 1572872 | tf_op jit(solution)/shard_map/ppermute | solution.py:89
  817.4 21.5 %collective-permute-start.58 = (bf16[128,2048]{1,0:T(8,128)(2,1)}, bf16[128,2048]{1,0:T(8,128)(2,1)}, u32[]{:S(2)}, u32[]{:S(2)}) collective-permute-start(bf16[128,2048]{1,0:T(8,128)(2,1)} %get-tuple-element.75), channel_id=1, source_target_pairs={{3,2},{7,6},{11,10},{15,14},{19,18},{23,22},{27,26},{31,30}} | collective-permute-start | bytes 1572872 | tf_op jit(solution)/shard_map/ppermute | solution.py:90
  822.5 21.7 %collective-permute-start.56 = (bf16[128,2048]{1,0:T(8,128)(2,1)}, bf16[128,2048]{1,0:T(8,128)(2,1)}, u32[]{:S(2)}, u32[]{:S(2)}) collective-permute-start(bf16[128,2048]{1,0:T(8,128)(2,1)} %add_convert_fusion.4), channel_id=1, source_target_pairs={{0,1},{1,2},{4,5},{5,6},{8,9},{9,10},{12,13},{13,14},{16,17},{17,1... | collective-permute-start | bytes 1572872 | tf_op jit(solution)/shard_map/ppermute | solution.py:89
  827.7 20.1 %collective-permute-start.52 = (bf16[128,2048]{1,0:T(8,128)(2,1)}, bf16[128,2048]{1,0:T(8,128)(2,1)S(1)}, u32[]{:S(2)}, u32[]{:S(2)}) collective-permute-start(bf16[128,2048]{1,0:T(8,128)(2,1)} %get-tuple-element.85), channel_id=1, source_target_pairs={{3,2},{7,6},{11,10},{15,14},{19,18},{23,22},{27,26},{31,30}} | collective-permute-start | bytes 1572872 | tf_op jit(solution)/shard_map/ppermute | solution.py:90
  834.5 20.4 %collective-permute-start.50 = (bf16[128,2048]{1,0:T(8,128)(2,1)S(1)}, bf16[128,2048]{1,0:T(8,128)(2,1)S(1)}, u32[]{:S(2)}, u32[]{:S(2)}) collective-permute-start(bf16[128,2048]{1,0:T(8,128)(2,1)S(1)} %add_convert_fusion.8), channel_id=1, source_target_pairs={{0,1},{1,2},{4,5},{5,6},{8,9},{9,10},{12,13},{13,14},{16,17},{17,1... | collective-permute-start | bytes 1572872 | tf_op jit(solution)/shard_map/ppermute | solution.py:89
  847.1 15.4 %collective-permute-start.59 = (bf16[128,2048]{1,0:T(8,128)(2,1)S(1)}, bf16[128,2048]{1,0:T(8,128)(2,1)S(1)}, u32[]{:S(2)}, u32[]{:S(2)}) collective-permute-start(bf16[128,2048]{1,0:T(8,128)(2,1)S(1)} %get-tuple-element.73), channel_id=1, source_target_pairs={{3,2},{2,1},{7,6},{6,5},{11,10},{10,9},{15,14},{14,13},{19,18},{18... | collective-permute-start | bytes 1572872 | tf_op jit(solution)/shard_map/ppermute | solution.py:90
  856.0 19.0 %collective-permute-start.53 = (bf16[128,2048]{1,0:T(8,128)(2,1)S(1)}, bf16[128,2048]{1,0:T(8,128)(2,1)S(1)}, u32[]{:S(2)}, u32[]{:S(2)}) collective-permute-start(bf16[128,2048]{1,0:T(8,128)(2,1)S(1)} %get-tuple-element.83), channel_id=1, source_target_pairs={{3,2},{2,1},{7,6},{6,5},{11,10},{10,9},{15,14},{14,13},{19,18},{18... | collective-permute-start | bytes 1572872 | tf_op jit(solution)/shard_map/ppermute | solution.py:90
  856.7 20.9 %collective-permute-start.57 = (bf16[128,2048]{1,0:T(8,128)(2,1)}, bf16[128,2048]{1,0:T(8,128)(2,1)}, u32[]{:S(2)}, u32[]{:S(2)}) collective-permute-start(bf16[128,2048]{1,0:T(8,128)(2,1)} %get-tuple-element.72), channel_id=1, source_target_pairs={{0,1},{1,2},{2,3},{4,5},{5,6},{6,7},{8,9},{9,10},{10,11},{12,13},{... | collective-permute-start | bytes 1572872 | tf_op jit(solution)/shard_map/ppermute | solution.py:89
  864.7 17.5 %collective-permute-start.60 = (bf16[128,2048]{1,0:T(8,128)(2,1)}, bf16[128,2048]{1,0:T(8,128)(2,1)}, u32[]{:S(2)}, u32[]{:S(2)}) collective-permute-start(bf16[128,2048]{1,0:T(8,128)(2,1)} %add_convert_fusion.1), channel_id=1, source_target_pairs={{3,2},{2,1},{1,0},{7,6},{6,5},{5,4},{11,10},{10,9},{9,8},{15,14},{... | collective-permute-start | bytes 1572872 | tf_op jit(solution)/shard_map/ppermute | solution.py:90
  868.5 36.8 %collective-permute-start.51 = (bf16[128,2048]{1,0:T(8,128)(2,1)}, bf16[128,2048]{1,0:T(8,128)(2,1)S(1)}, u32[]{:S(2)}, u32[]{:S(2)}) collective-permute-start(bf16[128,2048]{1,0:T(8,128)(2,1)} %get-tuple-element.82), channel_id=1, source_target_pairs={{0,1},{1,2},{2,3},{4,5},{5,6},{6,7},{8,9},{9,10},{10,11},{12,13},{... | collective-permute-start | bytes 1572872 | tf_op jit(solution)/shard_map/ppermute | solution.py:89
  875.9 29.4 %collective-permute-start.54 = (bf16[128,2048]{1,0:T(8,128)(2,1)}, bf16[128,2048]{1,0:T(8,128)(2,1)}, u32[]{:S(2)}, u32[]{:S(2)}) collective-permute-start(bf16[128,2048]{1,0:T(8,128)(2,1)} %add_convert_fusion.5), channel_id=1, source_target_pairs={{3,2},{2,1},{1,0},{7,6},{6,5},{5,4},{11,10},{10,9},{9,8},{15,14},{... | collective-permute-start | bytes 1572872 | tf_op jit(solution)/shard_map/ppermute | solution.py:90
  884.8 13.6 %collective-permute-start.62 = (f32[1056]{0:T(1024)S(1)}, f32[1056]{0:T(1024)S(1)}, u32[]{:S(2)}, u32[]{:S(2)}) collective-permute-start(f32[1056]{0:T(1024)S(1)} %get-tuple-element.39), channel_id=1, source_target_pairs={{0,2},{1,3},{2,0},{3,1},{4,6},{5,7},{6,4},{7,5},{8,10},{9,11},{10,... | collective-permute-start | bytes 12680 | tf_op jit(solution)/shard_map/ppermute | solution.py:133
  (95 other events, 1833.6 us)
Sparse Core Ops, SparseCore 0:
  43.9 33.7 all-gather.12
  542.7 56.1 reduce-scatter.3
  602.7 52.6 reduce-scatter.7
  658.9 86.3 reduce-scatter.5
  747.8 41.0 all-gather.8
  790.8 54.3 all-gather.16
  847.9 90.0 all-gather.10
Sparse Core Ops, SparseCore 1:
  173.3 85.6 all-gather.14

commit v3 on v2

--- a/solution.py
+++ b/solution.py
@@ -1,7 +1,10 @@
+import functools
+
 import jax
 import jax.numpy as jnp
 from jax import lax
 from jax.experimental import pallas as pl
+from jax.experimental.pallas import tpu as pltpu
 from jax.sharding import Mesh, PartitionSpec as P
 
 HEAD_SIZE = 64
@@ -60,37 +63,65 @@
     return lax.ppermute(a, "core", [(0, 1), (1, 0)])
 
 
-def line_gather(own):
+def exchanges():
     count = lax.axis_size("fsdp")
-    ahead = [(i, i + 1) for i in range(count - 1)]
-    back = [(i + 1, i) for i in range(count - 1)]
-    right, left, rights, lefts = own, own, [], []
-    for _ in range(count - 1):
-        right = lax.ppermute(right, "fsdp", ahead)
-        left = lax.ppermute(left, "fsdp", back)
-        rights.append(right)
-        lefts.append(left)
+    even = [(i, i ^ 1) for i in range(count)]
+    odd = [(0, 0)] + [(i, ((i - 1) ^ 1) + 1) for i in range(1, count - 1)] + [(count - 1, count - 1)]
+    return even, odd
+
+
+def line_step(first, second):
+    even, odd = exchanges()
+    return lax.ppermute(first, "fsdp", even), lax.ppermute(second, "fsdp", odd)
+
+
+def line_steps(own, ahead_of={}, begun=None, turn=None):
+    steps = []
+    first, second = own, own
+    for t in range(lax.axis_size("fsdp") - 1):
+        if t in ahead_of:
+            first, second = after((first, second), ahead_of[t])
+        if t and turn:
+            first, second = after((first, second), turn((first, second)))
+        if t == 0 and begun:
+            by_even, by_odd = begun
+        else:
+            by_even, by_odd = line_step(first, second)
+        steps.append((by_even, by_odd))
+        first, second = by_odd, by_even
+    return steps
+
+
+def line_pieces(own, steps):
+    count = lax.axis_size("fsdp")
     mine = lax.axis_index("fsdp")
-    return [own] + [
-        jnp.where(mine >= d, rights[d - 1], lefts[count - d - 1]) for d in range(1, count)
-    ]
-
-
-def line_scatter(parts, ahead_of=()):
+    is_even = mine % 2 == 0
+    pieces = [own]
+    for d in range(1, count):
+        below, above = steps[d - 1], steps[count - d - 1]
+        from_below = jnp.where(is_even, below[1], below[0])
+        from_above = jnp.where(is_even, above[0], above[1])
+        pieces.append(jnp.where(mine >= d, from_below, from_above))
+    return pieces
+
+
+def line_scatter(parts, ahead_of=None):
     count = lax.axis_size("fsdp")
-    right = left = None
+    mine = lax.axis_index("fsdp")
+    is_even = mine % 2 == 0
+    is_end = (mine == 0) | (mine == count - 1)
+    by_even = by_odd = None
     for t in range(count - 1):
-        low = parts[t + 1].astype(F32)
-        high = parts[count - 1 - t].astype(F32)
+        up = jnp.where(is_even, t + 1, count - 1 - t)
+        first = lax.dynamic_index_in_dim(parts, up, keepdims=False)
+        second = lax.dynamic_index_in_dim(parts, count - up, keepdims=False)
         if t:
-            if t <= len(ahead_of):
-                right, left, _ = lax.optimization_barrier((right, left, ahead_of[t - 1]))
-            low, high = low + right.astype(F32), high + left.astype(F32)
-        right = lax.ppermute(low.astype(BF), "fsdp", [(i, i + 1) for i in range(t + 1)])
-        left = lax.ppermute(
-            high.astype(BF), "fsdp", [(count - 1 - i, count - 2 - i) for i in range(t + 1)]
-        )
-    return parts[0].astype(F32) + right.astype(F32) + left.astype(F32)
+            if ahead_of:
+                by_even, by_odd = after((by_even, by_odd), ahead_of(t, (by_even, by_odd)))
+            first, second = first + by_odd.astype(F32), second + by_even.astype(F32)
+        second = jnp.where(is_end, 0.0, second)
+        by_even, by_odd = line_step(first.astype(BF), second.astype(BF))
+    return by_even, by_odd
 
 
 def absolute(ring):
@@ -102,17 +133,63 @@
 def exchange_line(piece_for):
     count = lax.axis_size("fsdp")
     mine = lax.axis_index("fsdp")
-    return absolute(
-        [piece_for(mine)]
-        + [
-            lax.ppermute(
-                piece_for((mine - e) % count),
-                "fsdp",
-                [(i, (i - e) % count) for i in range(count)],
-            )
-            for e in range(1, count)
-        ]
-    )
+    return [piece_for(mine)] + [
+        lax.ppermute(
+            piece_for((mine - e) % count),
+            "fsdp",
+            [(i, (i - e) % count) for i in range(count)],
+        )
+        for e in range(1, count)
+    ]
+
+
+def add_low(a, b):
+    return (a.astype(F32) + b.astype(F32)).astype(BF)
+
+
+def halve(blocks, axis, name, bit, pin=()):
+    mybit = (lax.axis_index(name) >> bit) & 1
+    pairs = [(i, i ^ (1 << bit)) for i in range(lax.axis_size(name))]
+    got = lax.ppermute(
+        lax.dynamic_index_in_dim(blocks, 1 - mybit, axis, keepdims=False), name, pairs
+    )
+    got = after(got, pin)
+    return add_low(lax.dynamic_index_in_dim(blocks, mybit, axis, keepdims=False), got)
+
+
+def chip_halves(terms):
+    chips, rows, cols = terms.shape
+    bits = chips.bit_length() - 1
+    return [
+        terms[:, g * rows // 2 : (g + 1) * rows // 2].reshape([2] * bits + [rows // 2, cols])
+        for g in range(2)
+    ]
+
+
+def row_parts(halves):
+    cut = halves[0].shape[-2] // 2
+    return [h[..., :cut, :] for h in halves], [h[..., cut:, :] for h in halves]
+
+
+def join_rows(one, two):
+    return [jnp.concatenate(pair, axis=-2) for pair in zip(one, two)]
+
+
+def chip_stage(halves, step, pin=()):
+    bits = lax.axis_size("chip").bit_length() - 1
+    out = []
+    for g in range(2):
+        done = [(g + k) % bits for k in range(step)]
+        left = [b for b in range(bits - 1, -1, -1) if b not in done]
+        bit = (g + step) % bits
+        out.append(halve(halves[g], left.index(bit), "chip", bit, pin))
+    return out
+
+
+def chip_rest(halves, step, pin=()):
+    for k in range(step, lax.axis_size("chip").bit_length() - 1):
+        halves = chip_stage(halves, k, pin)
+    return halves
 
 
 def after(value, *others):
@@ -120,7 +197,7 @@
 
 
 def gather_small(own):
-    return exchange_line(lambda j: own)
+    return absolute(exchange_line(lambda j: own))
 
 
 def sum_small(rows):
@@ -141,19 +218,114 @@
     return total
 
 
+def lanes(width, chips, count):
+    part = width // chips // count
+    return [
+        (slice((z * chips + c) * part, (z * chips + c + 1) * part),
+         slice((c * count + z) * part, (c * count + z + 1) * part))
+        for z in range(count)
+        for c in range(chips)
+    ]
+
+
+def inverse_root(wide):
+    return lax.rsqrt(jnp.mean(wide * wide, axis=-1, keepdims=True) + EPSILON)
+
+
+def norm_forward(chips, count, own, part, right, left, gain, hidden, normed):
+    wide = own[...].astype(F32) + part[0] + right[...].astype(F32) + left[...].astype(F32)
+    hidden[...] = wide
+    low = (wide * inverse_root(wide) * gain[...]).astype(BF)
+    for here, there in lanes(wide.shape[1], chips, count):
+        normed[:, there] = low[:, here]
+
+
+def norm_backward(chips, count, part, right, left, wide, base, gain, grad, low, total, scratch):
+    summed = part[0] + right[...].astype(F32) + left[...].astype(F32)
+    if chips:
+        for here, there in lanes(summed.shape[1], chips, count):
+            scratch[:, here] = summed[:, there]
+        summed = scratch[...]
+    values = wide[...].astype(F32)
+    inverse = inverse_root(values)
+    unit = values * inverse
+    sums = jnp.sum(summed * unit, axis=0, keepdims=True)
+
+    @pl.when(pl.program_id(0) == 0)
+    def _():
+        total[...] = sums
+
+    @pl.when(pl.program_id(0) > 0)
+    def _():
+        total[...] += sums
+
+    scaled = summed * gain[...]
+    out = base[...].astype(F32) + inverse * (
+        scaled - unit * jnp.mean(scaled * unit, axis=-1, keepdims=True)
+    )
+    grad[...] = out
+    low[...] = out.astype(BF)
+
+
+def row_specs(tok, width):
+    step = min(32, tok)
+    block = pl.BlockSpec((step, width), lambda i: (i, 0))
+    first = pl.BlockSpec((1, step, width), lambda i: (0, i, 0))
+    row = pl.BlockSpec((1, width), lambda i: (0, 0))
+    return tok // step, step, block, first, row
+
+
+def forward_norm(own, parts, right, left, gain, chips, count):
+    tok, width = own.shape
+    grid, _, block, first, row = row_specs(tok, width)
+    return pl.pallas_call(
+        functools.partial(norm_forward, chips, count),
+        grid=(grid,),
+        in_specs=[block, first, block, block, row],
+        out_specs=[block, block],
+        out_shape=[
+            jax.ShapeDtypeStruct((tok, width), F32),
+            jax.ShapeDtypeStruct((tok, width), BF),
+        ],
+    )(own, parts, right, left, gain.reshape(1, width))
+
+
+def backward_norm(parts, right, left, wide, base, gain, chips, count):
+    tok, width = wide.shape
+    grid, step, block, first, row = row_specs(tok, width)
+    return pl.pallas_call(
+        functools.partial(norm_backward, chips, count),
+        grid=(grid,),
+        in_specs=[first, block, block, block, block, row],
+        out_specs=[block, block, row],
+        out_shape=[
+            jax.ShapeDtypeStruct((tok, width), F32),
+            jax.ShapeDtypeStruct((tok, width), BF),
+            jax.ShapeDtypeStruct((1, width), F32),
+        ],
+        scratch_shapes=[pltpu.VMEM((step, width), F32)],
+    )(parts, right, left, wide, base, gain.reshape(1, width))
+
+
 def cast_pair(own, gate, up):
-    half = gate.shape[1]
-    gate[...] = own[0, :, :half].astype(F32)
-    up[...] = own[0, :, half:].astype(F32)
+    _, cores, count, _, cols = own.shape
+    half = cols // 2
+    for j in range(count):
+        for k in range(cores):
+            at = (j * cores + k) * half
+            gate[:, at : at + half] = own[0, k, j, :, :half].astype(F32)
+            up[:, at : at + half] = own[0, k, j, :, half:].astype(F32)
 
 
 def place_pair(own, chips, count, part, half):
-    block = pl.BlockSpec((part, half), lambda c, j, k: (c, j * 2 + k))
+    step = min(32, part)
+    own = own.reshape(chips, 2, count, part, 2 * half)
+    block = pl.BlockSpec((step, count * 2 * half), lambda c, r: (c * (part // step) + r, 0))
     shape = jax.ShapeDtypeStruct((chips * part, count * 2 * half), F32)
     return pl.pallas_call(
         cast_pair,
-        grid=(chips, count, 2),
-        in_specs=[pl.BlockSpec((1, part, 2 * half), lambda c, j, k: (c * 2 + k, j, 0))],
+        grid=(chips, part // step),
+        in_specs=[pl.BlockSpec((1, 2, count, step, 2 * half), lambda c, r: (c, 0, 0, r, 0))],
         out_specs=[block, block],
         out_shape=[shape, shape],
     )(own)
@@ -223,8 +395,10 @@
             axis=1,
         )
 
-    x_all = jnp.concatenate(line_gather(inputs), axis=0)
-    proj = lax.all_gather(exchange_line(proj_piece), PLANE, axis=0)
+    proj_ring = exchange_line(proj_piece)
+    proj_own = absolute(proj_ring)
+    x_all = jnp.concatenate(line_pieces(inputs, line_steps(inputs, {1: proj_own})), axis=0)
+    proj = lax.all_gather(proj_own, PLANE, axis=0)
     proj = proj.transpose(1, 0, 2, 3).reshape(width, q_cols + 2 * kv_cols)
 
     gains = gather_small(jnp.concatenate([attn_gain, ffn_gain, query_gain, key_norm_gain]))
@@ -247,14 +421,7 @@
             axis=1,
         )
 
-    pair = lax.all_gather(exchange_line(pair_piece), "chip", axis=0)
-    pair = pair.reshape(width, 2 * ff_own)
-
-    def to_chip_order(a):
-        return a.reshape(tok, count, chips, part).transpose(0, 2, 1, 3).reshape(tok, width)
-
-    def from_chip_order(a):
-        return a.reshape(tok, chips, count, part).transpose(0, 2, 1, 3).reshape(tok, width)
+    pair_ring = exchange_line(pair_piece)
 
     order = (mine - jnp.arange(count, dtype=jnp.int32)) % count
     positions = (order[:, None] * tok + jnp.arange(tok, dtype=jnp.int32)[None, :]).reshape(-1)
@@ -283,61 +450,96 @@
     attended = jnp.einsum("ngts,snd->tngd", probs_low, values, preferred_element_type=F32)
     attended = attended.astype(BF).reshape(seq, q_cols)
     out_part = mm(attended, out_weight).reshape(count, tok, width)
-    inputs_wide = inputs.astype(F32)
-    hidden_one = inputs_wide + line_scatter([out_part[d] for d in range(count)])
-
-    unit_two, inverse_two = unit_rows(hidden_one)
-    normed_two = jnp.concatenate(
-        line_gather(to_chip_order((unit_two * gain_two).astype(BF))), axis=0
-    )
+    stage = {}
+
+    def slices(t, sides):
+        if t == 1:
+            stage["slices"] = absolute(after(pair_ring, sides))
+            return stage["slices"]
+        return ()
+
+    sides = line_scatter(out_part, slices)
+    pair = lax.all_gather(stage["slices"], "chip", axis=0)
+    pair = pair.reshape(width, 2 * ff_own)
+    hidden_one, normed_own = forward_norm(inputs, out_part, *sides, gain_two, chips, count)
+
+    cot_begun = line_step(*(after(cotangent, sides),) * 2)
+    two_steps = line_steps(after(normed_own, cot_begun))
+    normed_two = jnp.concatenate(line_pieces(normed_own, two_steps), axis=0)
     normed_two = jnp.concatenate([normed_two, swap_cores(normed_two)], axis=0)
-    cot_own = jnp.concatenate(line_gather(after(cotangent, normed_two)), axis=0)
+    down_own = lax.dynamic_slice_in_dim(down_weight, core * ff_own, ff_own)
+    both = mm(normed_two, pair)
+    cot_steps = line_steps(cotangent, {1: two_steps[-1], count - 2: both}, cot_begun)
+    cot_own = jnp.concatenate(line_pieces(cotangent, cot_steps), axis=0)
     cot_all = jnp.concatenate([cot_own, swap_cores(cot_own)], axis=0)
-    down_own = lax.dynamic_slice_in_dim(down_weight, core * ff_own, ff_own)
     grad_hidden = mm_last(cot_all, down_own)
-    both = mm(normed_two, pair)
     gate_pre, upward = both[:, :ff_own], both[:, ff_own:]
     sigmoid = jax.nn.sigmoid(gate_pre)
     silu = gate_pre * sigmoid
     hidden = (silu * upward).astype(BF)
-    grad_both = jnp.concatenate(
-        [
-            (grad_hidden * upward * sigmoid * (1.0 + gate_pre * (1.0 - sigmoid))).astype(BF),
-            (grad_hidden * silu).astype(BF),
-        ],
-        axis=1,
-    )
-
-    def sum_tokens(left, weight, product, ahead_of=()):
-        other = swap_cores(product(left[seq:], weight).astype(BF))
-        own = product(left[:seq], weight) + other.astype(F32)
-        own = own.reshape(count, tok, width)
-        return line_scatter([own[d] for d in range(count)], ahead_of)
+    grad_gate = (grad_hidden * upward * sigmoid * (1.0 + gate_pre * (1.0 - sigmoid))).astype(BF)
+    grad_up = (grad_hidden * silu).astype(BF)
+    grad_both = jnp.concatenate([grad_gate, grad_up], axis=1)
+
+    queue, sums_of = [], {}
+
+    def enqueue(name, terms):
+        one, two = row_parts(chip_halves(terms))
+
+        def begin_one(pin):
+            sums_of[name] = chip_stage(one, 0, pin)
+            return sums_of[name]
+
+        def begin_two(pin):
+            got = chip_stage(two, 0, pin)
+            sums_of[name] = join_rows(sums_of[name], got)
+            return got
+
+        def finish(pin):
+            sums_of[name] = chip_rest(sums_of[name], 1, pin)
+            return sums_of[name]
+
+        return begin_one, begin_two, finish
+
+    def turn(pin):
+        return [piece(pin) for piece in queue.pop(0)] if queue else ()
 
     down_part = mm_first(hidden, cot_all).astype(BF)
-    pair_part = mm_first(normed_two, grad_both).astype(BF)
-    grad_normed_two = from_chip_order(
-        sum_tokens(grad_both, pair, mm_last, (down_part, pair_part))
-    )
-
-    down_sum = lax.psum_scatter(down_part, "chip", scatter_dimension=0, tiled=True)
-    pair_sum = lax.psum_scatter(pair_part, "chip", scatter_dimension=0, tiled=True)
-    pair_sum = pair_sum.reshape(count, part, 2 * ff_own)
-    pair_sum = exchange_line(
-        lambda j: lax.dynamic_index_in_dim(pair_sum, j, keepdims=False)
-    )
-    ffn_sum = pair_sum.reshape(count * part, 2 * ff_own)
-
-    gain_two_sum = jnp.sum(grad_normed_two * unit_two, axis=0)
-    grad_hidden_one = cotangent.astype(F32) + unit_back(
-        grad_normed_two * gain_two, unit_two, inverse_two
-    )
-    grad_attn = jnp.concatenate(line_gather(grad_hidden_one.astype(BF)), axis=0)
-    output = (hidden_one + sum_tokens(after(hidden, grad_attn), down_own, mm)).astype(BF)
-    grad_att = mm_last(grad_attn, out_weight).astype(BF).reshape(seq, kv_heads, groups, hd)
+    gate_part = mm_first(normed_two, after(grad_gate, down_part)).astype(BF)
+    other = mm_last(after(grad_both[seq:], gate_part), pair).astype(BF)
+    up_part = mm_first(normed_two, after(grad_up, other)).astype(BF)
+    down_turns = enqueue("down", down_part.reshape(chips, -1, width))
+    gate_turns = enqueue("gate", gate_part.reshape(chips, -1, ff_own))
+    up_turns = enqueue("up", up_part.reshape(chips, -1, ff_own))
+    queue += [[x] for x in (*down_turns[:2], *gate_turns[:2])]
+    queue += [[down_turns[2], up_turns[0]], [up_turns[1]], [gate_turns[2]], [up_turns[2]]]
+
+    own = after(grad_both[:seq], up_part, turn(other))
+    two_terms = mm_last(own, pair) + swap_cores(other).astype(F32)
+    two_terms = two_terms.reshape(count, tok, width)
+    sides = line_scatter(after(two_terms, turn(two_terms)), lambda t, sides: turn(sides))
+    grad_hidden_one, grad_low, gain_two_sum = backward_norm(
+        two_terms, *sides, hidden_one, cotangent, gain_two, chips, count
+    )
+    attn_steps = line_steps(after(grad_low, turn(sides)), turn=turn)
+    grad_attn = line_pieces(grad_low, attn_steps)
+    grad_attn = after(grad_attn, turn(attn_steps[-1]))
+    down_sum = jnp.concatenate(sums_of["down"], axis=0)
+    pair_sum = jnp.concatenate(
+        [jnp.concatenate(sums_of[name], axis=0) for name in ("gate", "up")], axis=1
+    ).reshape(count, part, 2 * ff_own)
+    ring = exchange_line(lambda j: lax.dynamic_index_in_dim(pair_sum, j, keepdims=False))
+    down_all = lax.all_gather(down_sum, PLANE, axis=0)
+
+    grad_attn = jnp.concatenate(grad_attn, axis=0)
+    grad_att = mm_last(grad_attn, out_weight).astype(BF)
+    grad_att = grad_att.reshape(seq, kv_heads, groups, hd)
     grad_probs = jnp.einsum("tngd,snd->ngts", grad_att, values, preferred_element_type=F32)
     delta = jnp.sum(probs * grad_probs, axis=-1, keepdims=True)
     grad_scores = (probs * (grad_probs - delta)).astype(BF)
+    ffn_sum = absolute(after(ring, grad_scores)).reshape(count * part, 2 * ff_own)
+    ffn_all = lax.all_gather(ffn_sum, PLANE, axis=0)
+    grad_scores = after(grad_scores, ffn_sum)
     grad_q = jnp.einsum("ngts,snd->tngd", grad_scores, keys, preferred_element_type=F32) * scale
     grad_k = jnp.einsum("ngts,tngd->snd", grad_scores, grouped, preferred_element_type=F32) * scale
     grad_v = jnp.einsum("ngts,tngd->snd", probs_low, grad_att, preferred_element_type=F32)
@@ -353,32 +555,54 @@
         ],
         axis=1,
     )
+    grad_proj = after(grad_proj, down_all)
     one_part = mm_last(grad_proj, proj).reshape(count, tok, width)
-    grad_normed_one = line_scatter([one_part[d] for d in range(count)])
-    unit_own = unit_one[:tok]
-    gain_one_sum = jnp.sum(grad_normed_one * unit_own, axis=0)
-    input_grad = (
-        grad_hidden_one + unit_back(grad_normed_one * gain_one, unit_own, inverse_one[:tok])
-    ).astype(BF)
-
-    proj_part = mm_first(normed_one, grad_proj).astype(BF)
+    proj_part = mm_first(normed_one, after(grad_proj, one_part)).astype(BF)
     out_term = mm_first(attended, grad_attn).astype(BF)
     att_part = jnp.concatenate(
         [proj_part[j * rows : (j + 1) * rows] for j in range(count)] + [out_term], axis=1
-    )
-    att_sum = lax.psum_scatter(att_part, PLANE, scatter_dimension=0, tiled=True)
+    ).reshape(chips, 2, share, -1)
+
+    def cores(t, sides):
+        if t == 1:
+            stage["att"] = chip_halves(halve(att_part, 1, "core", 0, sides))
+            return stage["att"]
+        if t == 2:
+            stage["att"] = chip_stage(stage["att"], 0, sides)
+            return stage["att"]
+        return ()
+
+    sides = line_scatter(one_part, cores)
+    att_sum = chip_rest(stage["att"], 1, sides)
+    _, input_grad, gain_one_sum = backward_norm(
+        one_part, *sides, inputs, grad_hidden_one, gain_one, 0, count
+    )
+
+    down_grad = place_down(down_all, chips, ff_own // chips, width)
+    late = after(hidden, att_sum)
+    other = mm(late[seq:], down_own).astype(BF)
+    att_sum = jnp.concatenate(att_sum, axis=0)
     cols = q_cols + 2 * kv_cols
-    got = exchange_line(lambda j: lax.dynamic_slice(att_sum, (0, j * cols), (share, cols)))
+    ring = exchange_line(lambda j: lax.dynamic_slice(att_sum, (0, j * cols), (share, cols)))
+    out_terms = mm(late[:seq], down_own) + swap_cores(other).astype(F32)
+    out_terms = out_terms.reshape(count, tok, width)
+    got = absolute(after(ring, out_terms))
     cuts = ((0, q_cols), (q_cols, q_cols + kv_cols), (q_cols + kv_cols, cols))
     att_sum = jnp.concatenate(
         [got[j, :, a:b] for a, b in cuts for j in range(count)] + [att_sum[:, count * cols :]],
         axis=1,
     )
-
-    down_all = lax.all_gather(down_sum, PLANE, axis=0)
-    ffn_all = lax.all_gather(ffn_sum, PLANE, axis=0)
+    att_sum = after(att_sum, ffn_all)
     gate_grad, up_grad = place_pair(ffn_all, chips, count, part, ff_own)
-    down_grad = place_down(down_all, chips, ff_own // chips, width)
+
+    def casts(t, sides):
+        return (down_grad,) if t == 1 else (gate_grad, up_grad)
+
+    sides = line_scatter(after(out_terms, att_sum), casts)
+    output = (
+        hidden_one + out_terms[0] + sides[0].astype(F32) + sides[1].astype(F32)
+    ).astype(BF)
+
     att_all = lax.all_gather(att_sum, PLANE, axis=0, tiled=True)
     edges = [0, q_cols * count, (q_cols + kv_cols) * count, cols * count, att_all.shape[1]]
     query_grad, key_grad, value_grad, out_grad = (

time: 986 us -> 780 us (0.79)
  waiting for transfers between devices: 454 us -> 235 us
  local copies, waits for them, and re-layouts: 109 us -> 86.9 us
  matrix products: 102 us -> 124 us
    reduce_scatter x3 -> x0, waiting for transfers between devices: 178 us -> none  [the longest x1 89.8 us: shards(): lax.psum_scatter(pair_part, 'chip', scatter_dimension=0, tiled=True)]
    ppermute x15, waiting for transfers between devices: 98.2 us -> 25.7 us  [exchange_line(): lax.ppermute(piece_for((mine - e) % count), 'fsdp', [(i, (i - e) % count)...]
    ppermute x48 -> x71, waiting for transfers between devices: 153 us -> 199 us  [the longest x24 132 us: line_step(): lax.ppermute(first, 'fsdp', even)]
    reshape x6 -> x0, local copies, waits for them, and re-layouts: 14.6 us -> none  [the longest x3 8.01 us: from_chip_order(): a.reshape(tok, chips, count, part).transpose(0, 2, 1, 3).reshape(tok, width)]
    sub x0 -> x1, matrix products: none -> 10.4 us  [shards(): grad_scores = (probs * (grad_probs - delta)).astype(BF)]
    convert_element_type x15 -> x36, other arithmetic: 26.7 us -> 34.8 us  [the longest x23 16.7 us: add_low(): return (a.astype(F32) + b.astype(F32)).astype(BF)]
    ppermute x48 -> x71, starting transfers between devices: 141 us -> 149 us  [the longest x24 71 us: line_step(): lax.ppermute(first, 'fsdp', even)]
    pallas_call x1 -> x4, Pallas kernels: 25.2 us -> 32.4 us  [the longest x1 19.2 us: place_pair(): pl.pallas_call(cast_pair, grid=(chips, part // step), in_specs=[pl.BlockS...]
  transfers between devices with their start and end apart: 81 -> 101, of which waited for: 46 -> 46; matrix products, arithmetic and copies ran while one was open for 15% -> 28% of each run, Pallas kernels for 1% -> 6%
where the time goes in v3:
time: 780 us; the launch traced here: 767 us
  waiting for transfers between devices  235 us (30%)
  starting transfers between devices  184 us (24%)
  matrix products  124 us (16%)
  local copies, waits for them, and re-layouts  86.9 us (11%)
  other arithmetic  78.3 us (10%)
  Pallas kernels  42.8 us (5%)
  between operations  16.3 us (2%)
    ppermute x24, waiting for transfers between devices, line_step(): lax.ppermute(first, 'fsdp', even)  132 us
    ppermute x24, starting transfers between devices, line_step(): lax.ppermute(first, 'fsdp', even)  71 us
    ppermute x23, waiting for transfers between devices, halve(): lax.ppermute(lax.dynamic_index_in_dim(blocks, 1 - mybit, axis, keepdims=F...  66.8 us
    ppermute x24, starting transfers between devices, line_step(): lax.ppermute(second, 'fsdp', odd)  53.5 us
    dot_general x5, matrix products, mm_last(): lax.dot_general(a, b, (((1,), (1,)), ((), ())), preferred_element_type=F32)  36.2 us
    dot_general x5, matrix products, mm(): return jnp.dot(a, b, preferred_element_type=F32)  28.8 us
    unnamed x227, local copies, waits for them, and re-layouts  27.6 us
    ppermute x15, starting transfers between devices, exchange_line(): lax.ppermute(piece_for((mine - e) % count), 'fsdp', [(i, (i - e) % count)...  26.1 us
  transfers between devices with their start and end apart: 101, of which 46 were waited for; matrix products, arithmetic and copies ran while one was open for 28% of the time, Pallas kernels for 6%

profile of v3, /device:TPU:0, one launch (start us, length us, event | category | flops | bytes accessed | tf_op | source)
XLA Modules:
  0.0 766.8 jit_solution(13159413595359639163)
XLA Ops:
  9.4 5.1 collective-permute-start.2
  17.7 5.6 collective-permute-done.3
  25.0 4.1 collective-permute-start.1
  32.5 8.0 %collective-permute-done.1 = bf16[128,2048]{1,0:T(8,128)(2,1)} collective-permute-done((bf16[128,2048]{1,0:T(8,128)(2,1)S(1)}, bf16[128,2048]{1,0:T(8,128)(2,1)}, u32[]{:S(2)}, u32[]{:S(2)}) %collective-permute-start.1) | collective-permute-done | bytes 524320 | tf_op jit(solution)/shard_map/ppermute | solution.py:75
  40.5 5.3 collective-permute-start.5
  47.6 8.6 %collective-permute-start.6 = (bf16[128,2048]{1,0:T(8,128)(2,1)}, bf16[128,2048]{1,0:T(8,128)(2,1)}, u32[]{:S(2)}, u32[]{:S(2)}) collective-permute-start(bf16[128,2048]{1,0:T(8,128)(2,1)} %collective-permute-done.5), channel_id=1, source_target_pairs={{0,1},{1,0},{2,3},{3,2},{4,5},{5,4},{6,7},{7,6},{8,9},{9,8},{10,11... | collective-permute-start | bytes 1572872 | tf_op jit(solution)/shard_map/ppermute | solution.py:75
  56.2 4.6 collective-permute-done.7
  60.8 5.4 collective-permute-start.8
  96.0 7.6 fusion.182
  103.6 4.2 fusion.37
  109.6 10.5 %collective-permute-start.13 = (bf16[128,2048]{1,0:T(8,128)(2,1)S(1)}, bf16[128,2048]{1,0:T(8,128)(2,1)S(1)}, u32[]{:S(2)}, u32[]{:S(2)}) collective-permute-start(bf16[128,2048]{1,0:T(8,128)(2,1)S(1)} %get-tuple-element.254), channel_id=1, source_target_pairs={{0,0},{1,2},{2,1},{3,3},{4,4},{5,6},{6,5},{7,7},{8,8},{9,10},{10,9... | collective-permute-start | bytes 1572872 | tf_op jit(solution)/shard_map/ppermute | solution.py:75
  120.2 7.8 %collective-permute-done.15 = bf16[128,2048]{1,0:T(8,128)(2,1)} collective-permute-done((bf16[128,2048]{1,0:T(8,128)(2,1)}, bf16[128,2048]{1,0:T(8,128)(2,1)}, u32[]{:S(2)}, u32[]{:S(2)}) %collective-permute-start.15) | collective-permute-done | bytes 524320 | tf_op jit(solution)/shard_map/ppermute | solution.py:137
  145.3 5.4 collective-permute-start.18
  150.8 6.8 collective-permute-done.17
  159.5 4.5 collective-permute-start.19
  164.8 10.9 %collective-permute-done.19.right = bf16[128,2048]{1,0:T(8,128)(2,1)S(1)} collective-permute-done((bf16[128,2048]{1,0:T(8,128)(2,1)S(1)}, bf16[128,2048]{1,0:T(8,128)(2,1)S(1)}, u32[]{:S(2)}, u32[]{:S(2)}) %collective-permute-start.19) | collective-permute-done | bytes 524320 | tf_op jit(solution)/shard_map/ppermute | solution.py:75
  181.4 4.1 shard_map.237
  185.5 4.6 collective-permute-done.21
  190.1 4.5 collective-permute-start.24
  196.3 8.4 %collective-permute-done.24 = bf16[128,2048]{1,0:T(8,128)(2,1)S(1)} collective-permute-done((bf16[128,2048]{1,0:T(8,128)(2,1)}, bf16[128,2048]{1,0:T(8,128)(2,1)S(1)}, u32[]{:S(2)}, u32[]{:S(2)}) %collective-permute-start.24) | collective-permute-done | bytes 524320 | tf_op jit(solution)/shard_map/ppermute | solution.py:75
  205.3 3.8 collective-permute-start.27
  209.1 10.4 %collective-permute-start.26 = (bf16[128,2048]{1,0:T(8,128)(2,1)S(1)}, bf16[128,2048]{1,0:T(8,128)(2,1)S(1)}, u32[]{:S(2)}, u32[]{:S(2)}) collective-permute-start(bf16[128,2048]{1,0:T(8,128)(2,1)S(1)} %collective-permute-done.25), channel_id=1, source_target_pairs={{0,1},{1,0},{2,3},{3,2},{4,5},{5,4},{6,7},{7,6},{8,9},{9,8},{10,11... | collective-permute-start | bytes 1572872 | tf_op jit(solution)/shard_map/ppermute | solution.py:75
  222.1 6.7 collective-permute-done.26
  234.2 5.0 collective-permute-start.31
  240.6 14.5 %fusion.183 = f32[1024,2048]{1,0:T(8,128)} fusion(bf16[1024,2048]{1,0:T(8,128)(2,1)} %constant_dynamic-update-slice_fusion.8, bf16[2048,2048]{1,0:T(8,128)(2,1)} %bitcast.554), kind=kOutput, calls=%fused_computation.451 | convolution fusion | flops 8589934592 | bytes 20971520 | tf_op jit(solution)/shard_map/dot_general | solution.py:51
  257.6 11.5 %collective-permute-done.32 = bf16[128,2048]{1,0:T(8,128)(2,1)S(1)} collective-permute-done((bf16[128,2048]{1,0:T(8,128)(2,1)}, bf16[128,2048]{1,0:T(8,128)(2,1)S(1)}, u32[]{:S(2)}, u32[]{:S(2)}) %collective-permute-start.32) | collective-permute-done | bytes 524320 | tf_op jit(solution)/shard_map/ppermute | solution.py:75
  275.8 4.5 collective-permute-done.34
  283.5 12.0 %multiply_convert_fusion = (bf16[1024,1024]{1,0:T(8,128)(2,1)S(1)}, bf16[1024,1024]{1,0:T(8,128)(2,1)S(1)}, bf16[1024,1024]{1,0:T(8,128)(2,1)S(1)}) fusion(f32[1024,2048]{1,0:T(8,128)} %fusion.183, bf16[1024,2048]{1,0:T(8,128)(2,1)} %constant_dynamic-update-slice_fusion.13, bf16[2048,2048]{1,0:T(8,128)(2,1)} %param.26, s32[]{:T(128)S(6)} %select_n.583), kind=kOutput, calls=%fused_computation.20 | convolution fusion | flops 4310695936 | bytes 23068676 | tf_op jit(solution)/shard_map/dot_general | solution.py:55
  295.5 5.3 convolution_convert_fusion.2
  300.9 7.0 convolution_convert_fusion.1
  308.3 9.1 %convolution_convert_fusion.5 = bf16[512,2048]{1,0:T(8,128)(2,1)} fusion(bf16[512,2048]{1,0:T(8,128)(2,1)S(1)} %get-tuple-element.123, bf16[2048,2048]{1,0:T(8,128)(2,1)} %bitcast.555), kind=kOutput, calls=%fused_computation.43 | convolution fusion | flops 4296015872 | bytes 12582912 | tf_op jit(solution)/shard_map/dot_general | solution.py:55
  320.9 8.3 %convolution_convert_fusion = bf16[2048,1024]{1,0:T(8,128)(2,1)} fusion(bf16[1024,2048]{1,0:T(8,128)(2,1)} %constant_dynamic-update-slice_fusion.8, bf16[1024,1024]{1,0:T(8,128)(2,1)S(1)} %get-tuple-element.124), kind=kOutput, calls=%fused_computation.29 | convolution fusion | flops 4297064448 | bytes 10485760 | tf_op jit(solution)/shard_map/dot_general | solution.py:59
  335.1 7.1 convert_add_fusion.2
  345.4 3.7 collective-permute-start.40
  355.4 5.2 collective-permute-done.40
  368.4 7.3 collective-permute-done.44
  376.7 4.5 collective-permute-done.46
  404.7 14.7 %collective-permute-done.53 = bf16[2,128,1024]{2,1,0:T(8,128)(2,1)S(1)} collective-permute-done((bf16[2,128,1024]{2,1,0:T(8,128)(2,1)S(1)}, bf16[2,128,1024]{2,1,0:T(8,128)(2,1)S(1)}, u32[]{:S(2)}, u32[]{:S(2)}) %collective-permute-start.53) | collective-permute-done | bytes 524320 | tf_op jit(solution)/shard_map/ppermute | solution.py:153
  422.5 4.5 shard_map.238
  432.0 3.5 collective-permute-start.55
  439.6 6.8 collective-permute-done.55
  446.4 16.3 %collective-permute-done.56 = bf16[2,128,1024]{2,1,0:T(8,128)(2,1)S(1)} collective-permute-done((bf16[2,128,1024]{2,1,0:T(8,128)(2,1)S(1)}, bf16[2,128,1024]{2,1,0:T(8,128)(2,1)S(1)}, u32[]{:S(2)}, u32[]{:S(2)}) %collective-permute-start.56) | collective-permute-done | bytes 524320 | tf_op jit(solution)/shard_map/ppermute | solution.py:153
  479.0 5.4 collective-permute-start.63
  487.4 14.9 %collective-permute-done.62 = bf16[128,2048]{1,0:T(8,128)(2,1)} collective-permute-done((bf16[128,2048]{1,0:T(8,128)(2,1)}, bf16[128,2048]{1,0:T(8,128)(2,1)}, u32[]{:S(2)}, u32[]{:S(2)}) %collective-permute-start.62) | collective-permute-done | bytes 524320 | tf_op jit(solution)/shard_map/ppermute | solution.py:75
  516.6 10.4 %fusion.3 = bf16[2,4,512,512]{2,3,1,0:T(8,128)(2,1)} fusion(bf16[512,2,64,1]{0,2,3,1:T(8,128)(2,1)S(1)} %bitcast.545, bf16[512,2,4,64]{0,3,2,1:T(8,128)(2,1)} %bitcast.558, f32[2,4,512,512]{2,3,1,0:T(8,128)} %get-tuple-element.329, f32[2,4,512]{2,1,0:T(4,128)S(1)} %get-tuple-element.328), kind=kOutput, calls=%fused_computation.5 | convolution fusion | flops 549458432 | bytes 13254656 | tf_op jit(solution)/shard_map/sub | solution.py:539
  527.0 10.0 %collective-permute-done.82 = bf16[128,2048]{1,0:T(8,128)(2,1)} collective-permute-done((bf16[128,2048]{1,0:T(8,128)(2,1)}, bf16[128,2048]{1,0:T(8,128)(2,1)}, u32[]{:S(2)}, u32[]{:S(2)}) %collective-permute-start.82) | collective-permute-done | bytes 524320 | tf_op jit(solution)/shard_map/ppermute | solution.py:137
  548.0 3.9 convolution_multiply_fusion
  557.4 3.6 fusion.44
  563.0 5.6 fusion.45
  573.2 5.9 fusion.184.part
  604.9 12.7 %collective-permute-done.67 = bf16[128,2048]{1,0:T(8,128)(2,1)S(1)} collective-permute-done((bf16[128,2048]{1,0:T(8,128)(2,1)}, bf16[128,2048]{1,0:T(8,128)(2,1)S(1)}, u32[]{:S(2)}, u32[]{:S(2)}) %collective-permute-start.67) | collective-permute-done | bytes 524320 | tf_op jit(solution)/shard_map/ppermute | solution.py:75
  617.6 3.8 fusion.5
  624.3 3.5 collective-permute-start.70
  628.6 10.2 %collective-permute-done.70 = bf16[128,2048]{1,0:T(8,128)(2,1)S(1)} collective-permute-done((bf16[128,2048]{1,0:T(8,128)(2,1)S(1)}, bf16[128,2048]{1,0:T(8,128)(2,1)S(1)}, u32[]{:S(2)}, u32[]{:S(2)}) %collective-permute-start.70) | collective-permute-done | bytes 524320 | tf_op jit(solution)/shard_map/ppermute | solution.py:75
  638.9 3.5 collective-permute-done.73
  647.5 6.8 collective-permute-done.76
  657.7 3.7 fusion.22
  661.5 3.7 collective-permute-start.78
  669.1 7.5 convert_add_fusion.1
  683.3 10.4 %shard_map.239 = f32[2048,2048]{1,0:T(8,128)} custom-call(bf16[8,256,2048]{2,1,0:T(8,128)(2,1)} %bitcast.506), custom_call_target="tpu_custom_call" | custom-call | tf_op jit(solution)/shard_map/pallas_call | solution.py:339
  697.1 3.7 collective-permute-start.86
  704.7 4.6 shard_map.241
  715.4 19.2 %shard_map.240 = (f32[512,8192]{1,0:T(8,128)}, f32[512,8192]{1,0:T(8,128)}) custom-call(bf16[4,2,4,128,2048]{4,3,2,1,0:T(8,128)(2,1)} %bitcast.505), custom_call_target="tpu_custom_call" | custom-call | tf_op jit(solution)/shard_map/pallas_call | solution.py:325
  750.6 6.7 slice_convert_fusion
  (592 shorter events, 293.3 us)
Async XLA Ops:
  7.3 76.4 %all-gather.13.cloned.1.call-start = ((), (), s32[]{:S(2)}) async-start(), calls=%async_computation.2 | async-start | bytes 3538944 | tf_op jit(solution)/shard_map/all_gather | solution.py:401
  24.2 216.4 %all-gather.15.cloned.1.call-start = ((), (), s32[]{:S(2)}) async-start(), calls=%async_computation.3 | async-start | bytes 10485760 | tf_op jit(solution)/shard_map/all_gather | solution.py:462
  25.0 15.5 %collective-permute-start.1 = (bf16[128,2048]{1,0:T(8,128)(2,1)S(1)}, bf16[128,2048]{1,0:T(8,128)(2,1)}, u32[]{:S(2)}, u32[]{:S(2)}) collective-permute-start(bf16[128,2048]{1,0:T(8,128)(2,1)S(1)} %copy-done.16), channel_id=1, source_target_pairs={{0,1},{1,0},{2,3},{3,2},{4,5},{5,4},{6,7},{7,6},{8,9},{9,8},{10,11... | collective-permute-start | bytes 1572872 | tf_op jit(solution)/shard_map/ppermute | solution.py:75
  29.2 17.6 %collective-permute-start.9 = (bf16[1056]{0:T(1024)(128)(2,1)S(1)}, bf16[1056]{0:T(1024)(128)(2,1)S(1)}, u32[]{:S(2)}, u32[]{:S(2)}) collective-permute-start(bf16[1056]{0:T(1024)(128)(2,1)S(1)} %concatenate.123), channel_id=1, source_target_pairs={{0,3},{1,0},{2,1},{3,2},{4,7},{5,4},{6,5},{7,6},{8,11},{9,8},{10,9... | collective-permute-start | bytes 6344 | tf_op jit(solution)/shard_map/ppermute | solution.py:137
  30.1 16.7 %collective-permute-start.10 = (bf16[1056]{0:T(1024)(128)(2,1)S(1)}, bf16[1056]{0:T(1024)(128)(2,1)S(1)}, u32[]{:S(2)}, u32[]{:S(2)}) collective-permute-start(bf16[1056]{0:T(1024)(128)(2,1)S(1)} %concatenate.123), channel_id=1, source_target_pairs={{0,2},{1,3},{2,0},{3,1},{4,6},{5,7},{6,4},{7,5},{8,10},{9,11},{10,... | collective-permute-start | bytes 6344 | tf_op jit(solution)/shard_map/ppermute | solution.py:137
  30.7 16.1 %collective-permute-start.11 = (bf16[1056]{0:T(1024)(128)(2,1)S(1)}, bf16[1056]{0:T(1024)(128)(2,1)S(1)}, u32[]{:S(2)}, u32[]{:S(2)}) collective-permute-start(bf16[1056]{0:T(1024)(128)(2,1)S(1)} %concatenate.123), channel_id=1, source_target_pairs={{0,1},{1,2},{2,3},{3,0},{4,5},{5,6},{6,7},{7,4},{8,9},{9,10},{10,1... | collective-permute-start | bytes 6344 | tf_op jit(solution)/shard_map/ppermute | solution.py:137
  45.9 15.0 %collective-permute-start.7 = (bf16[128,2048]{1,0:T(8,128)(2,1)S(1)}, bf16[128,2048]{1,0:T(8,128)(2,1)}, u32[]{:S(2)}, u32[]{:S(2)}) collective-permute-start(bf16[128,2048]{1,0:T(8,128)(2,1)S(1)} %collective-permute-done), channel_id=1, source_target_pairs={{0,1},{1,0},{2,3},{3,2},{4,5},{5,4},{6,7},{7,6},{8,9},{9,8},{10,11... | collective-permute-start | bytes 1572872 | tf_op jit(solution)/shard_map/ppermute | solution.py:75
  47.6 21.7 %collective-permute-start.6 = (bf16[128,2048]{1,0:T(8,128)(2,1)}, bf16[128,2048]{1,0:T(8,128)(2,1)}, u32[]{:S(2)}, u32[]{:S(2)}) collective-permute-start(bf16[128,2048]{1,0:T(8,128)(2,1)} %collective-permute-done.5), channel_id=1, source_target_pairs={{0,1},{1,0},{2,3},{3,2},{4,5},{5,4},{6,7},{7,6},{8,9},{9,8},{10,11... | collective-permute-start | bytes 1572872 | tf_op jit(solution)/shard_map/ppermute | solution.py:75
  77.1 43.1 %collective-permute-start.14 = (bf16[128,2048]{1,0:T(8,128)(2,1)}, bf16[128,2048]{1,0:T(8,128)(2,1)}, u32[]{:S(2)}, u32[]{:S(2)}) collective-permute-start(bf16[128,2048]{1,0:T(8,128)(2,1)} %pad_maximum_fusion.9), channel_id=1, source_target_pairs={{0,3},{1,0},{2,1},{3,2},{4,7},{5,4},{6,5},{7,6},{8,11},{9,8},{10,9... | collective-permute-start | bytes 1572872 | tf_op jit(solution)/shard_map/ppermute | solution.py:137
  79.4 48.6 %collective-permute-start.15 = (bf16[128,2048]{1,0:T(8,128)(2,1)}, bf16[128,2048]{1,0:T(8,128)(2,1)}, u32[]{:S(2)}, u32[]{:S(2)}) collective-permute-start(bf16[128,2048]{1,0:T(8,128)(2,1)} %pad_maximum_fusion.10), channel_id=1, source_target_pairs={{0,2},{1,3},{2,0},{3,1},{4,6},{5,7},{6,4},{7,5},{8,10},{9,11},{10,... | collective-permute-start | bytes 1572872 | tf_op jit(solution)/shard_map/ppermute | solution.py:137
  82.8 45.2 %collective-permute-start.16 = (bf16[128,2048]{1,0:T(8,128)(2,1)}, bf16[128,2048]{1,0:T(8,128)(2,1)}, u32[]{:S(2)}, u32[]{:S(2)}) collective-permute-start(bf16[128,2048]{1,0:T(8,128)(2,1)} %pad_maximum_fusion.11), channel_id=1, source_target_pairs={{0,1},{1,2},{2,3},{3,0},{4,5},{5,6},{6,7},{7,4},{8,9},{9,10},{10,1... | collective-permute-start | bytes 1572872 | tf_op jit(solution)/shard_map/ppermute | solution.py:137
  109.5 21.8 %collective-permute-start.12 = (bf16[128,2048]{1,0:T(8,128)(2,1)S(1)}, bf16[128,2048]{1,0:T(8,128)(2,1)S(1)}, u32[]{:S(2)}, u32[]{:S(2)}) collective-permute-start(bf16[128,2048]{1,0:T(8,128)(2,1)S(1)} %get-tuple-element.255), channel_id=1, source_target_pairs={{0,1},{1,0},{2,3},{3,2},{4,5},{5,4},{6,7},{7,6},{8,9},{9,8},{10,11... | collective-permute-start | bytes 1572872 | tf_op jit(solution)/shard_map/ppermute | solution.py:75
  109.6 21.7 %collective-permute-start.13 = (bf16[128,2048]{1,0:T(8,128)(2,1)S(1)}, bf16[128,2048]{1,0:T(8,128)(2,1)S(1)}, u32[]{:S(2)}, u32[]{:S(2)}) collective-permute-start(bf16[128,2048]{1,0:T(8,128)(2,1)S(1)} %get-tuple-element.254), channel_id=1, source_target_pairs={{0,0},{1,2},{2,1},{3,3},{4,4},{5,6},{6,5},{7,7},{8,8},{9,10},{10,9... | collective-permute-start | bytes 1572872 | tf_op jit(solution)/shard_map/ppermute | solution.py:75
  139.6 433.6 %all-gather.17.cloned.1.call-start = ((), (), s32[]{:S(2)}) async-start(), calls=%async_computation.4 | async-start | bytes 9437184 | tf_op jit(solution)/shard_map/all_gather | solution.py:532
  142.3 15.3 %collective-permute-start.17 = (bf16[128,2048]{1,0:T(8,128)(2,1)}, bf16[128,2048]{1,0:T(8,128)(2,1)S(1)}, u32[]{:S(2)}, u32[]{:S(2)}) collective-permute-start(bf16[128,2048]{1,0:T(8,128)(2,1)} %get-tuple-element.253), channel_id=1, source_target_pairs={{0,1},{1,0},{2,3},{3,2},{4,5},{5,4},{6,7},{7,6},{8,9},{9,8},{10,11... | collective-permute-start | bytes 1572872 | tf_op jit(solution)/shard_map/ppermute | solution.py:75
  159.5 16.1 %collective-permute-start.19 = (bf16[128,2048]{1,0:T(8,128)(2,1)S(1)}, bf16[128,2048]{1,0:T(8,128)(2,1)S(1)}, u32[]{:S(2)}, u32[]{:S(2)}) collective-permute-start(bf16[128,2048]{1,0:T(8,128)(2,1)S(1)} %get-tuple-element.251), channel_id=1, source_target_pairs={{0,1},{1,0},{2,3},{3,2},{4,5},{5,4},{6,7},{7,6},{8,9},{9,8},{10,11... | collective-permute-start | bytes 1572872 | tf_op jit(solution)/shard_map/ppermute | solution.py:75
  176.4 13.7 %collective-permute-start.21 = (bf16[128,2048]{1,0:T(8,128)(2,1)S(1)}, bf16[128,2048]{1,0:T(8,128)(2,1)S(1)}, u32[]{:S(2)}, u32[]{:S(2)}) collective-permute-start(bf16[128,2048]{1,0:T(8,128)(2,1)S(1)} %copy-done.15), channel_id=1, source_target_pairs={{0,1},{1,0},{2,3},{3,2},{4,5},{5,4},{6,7},{7,6},{8,9},{9,8},{10,11... | collective-permute-start | bytes 1572872 | tf_op jit(solution)/shard_map/ppermute | solution.py:75
  190.1 14.5 %collective-permute-start.24 = (bf16[128,2048]{1,0:T(8,128)(2,1)}, bf16[128,2048]{1,0:T(8,128)(2,1)S(1)}, u32[]{:S(2)}, u32[]{:S(2)}) collective-permute-start(bf16[128,2048]{1,0:T(8,128)(2,1)} %get-tuple-element.117), channel_id=1, source_target_pairs={{0,1},{1,0},{2,3},{3,2},{4,5},{5,4},{6,7},{7,6},{8,9},{9,8},{10,11... | collective-permute-start | bytes 1572872 | tf_op jit(solution)/shard_map/ppermute | solution.py:75
  205.3 14.2 %collective-permute-start.27 = (bf16[128,2048]{1,0:T(8,128)(2,1)S(1)}, bf16[128,2048]{1,0:T(8,128)(2,1)S(1)}, u32[]{:S(2)}, u32[]{:S(2)}) collective-permute-start(bf16[128,2048]{1,0:T(8,128)(2,1)S(1)} %collective-permute-done.23), channel_id=1, source_target_pairs={{0,1},{1,0},{2,3},{3,2},{4,5},{5,4},{6,7},{7,6},{8,9},{9,8},{10,11... | collective-permute-start | bytes 1572872 | tf_op jit(solution)/shard_map/ppermute | solution.py:75
  209.1 19.7 %collective-permute-start.26 = (bf16[128,2048]{1,0:T(8,128)(2,1)S(1)}, bf16[128,2048]{1,0:T(8,128)(2,1)S(1)}, u32[]{:S(2)}, u32[]{:S(2)}) collective-permute-start(bf16[128,2048]{1,0:T(8,128)(2,1)S(1)} %collective-permute-done.25), channel_id=1, source_target_pairs={{0,1},{1,0},{2,3},{3,2},{4,5},{5,4},{6,7},{7,6},{8,9},{9,8},{10,11... | collective-permute-start | bytes 1572872 | tf_op jit(solution)/shard_map/ppermute | solution.py:75
  232.7 22.4 %collective-permute-start.30 = (bf16[128,2048]{1,0:T(8,128)(2,1)S(1)}, bf16[128,2048]{1,0:T(8,128)(2,1)}, u32[]{:S(2)}, u32[]{:S(2)}) collective-permute-start(bf16[128,2048]{1,0:T(8,128)(2,1)S(1)} %collective-permute-done.21), channel_id=1, source_target_pairs={{0,0},{1,2},{2,1},{3,3},{4,4},{5,6},{6,5},{7,7},{8,8},{9,10},{10,9... | collective-permute-start | bytes 1572872 | tf_op jit(solution)/shard_map/ppermute | solution.py:75
  234.2 20.9 %collective-permute-start.31 = (bf16[128,2048]{1,0:T(8,128)(2,1)}, bf16[128,2048]{1,0:T(8,128)(2,1)}, u32[]{:S(2)}, u32[]{:S(2)}) collective-permute-start(bf16[128,2048]{1,0:T(8,128)(2,1)} %collective-permute-done.22), channel_id=1, source_target_pairs={{0,1},{1,0},{2,3},{3,2},{4,5},{5,4},{6,7},{7,6},{8,9},{9,8},{10,11... | collective-permute-start | bytes 1572872 | tf_op jit(solution)/shard_map/ppermute | solution.py:75
  255.1 14.0 %collective-permute-start.32 = (bf16[128,2048]{1,0:T(8,128)(2,1)}, bf16[128,2048]{1,0:T(8,128)(2,1)S(1)}, u32[]{:S(2)}, u32[]{:S(2)}) collective-permute-start(bf16[128,2048]{1,0:T(8,128)(2,1)} %collective-permute-done.30), channel_id=1, source_target_pairs={{0,1},{1,0},{2,3},{3,2},{4,5},{5,4},{6,7},{7,6},{8,9},{9,8},{10,11... | collective-permute-start | bytes 1572872 | tf_op jit(solution)/shard_map/ppermute | solution.py:75
  255.8 13.3 %collective-permute-start.33 = (bf16[128,2048]{1,0:T(8,128)(2,1)}, bf16[128,2048]{1,0:T(8,128)(2,1)S(1)}, u32[]{:S(2)}, u32[]{:S(2)}) collective-permute-start(bf16[128,2048]{1,0:T(8,128)(2,1)} %collective-permute-done.31), channel_id=1, source_target_pairs={{0,0},{1,2},{2,1},{3,3},{4,4},{5,6},{6,5},{7,7},{8,8},{9,10},{10,9... | collective-permute-start | bytes 1572872 | tf_op jit(solution)/shard_map/ppermute | solution.py:75
  317.4 17.6 %collective-permute-start.37 = (bf16[512,2048]{1,0:T(8,128)(2,1)}, bf16[512,2048]{1,0:T(8,128)(2,1)S(1)}, u32[]{:S(2)}, u32[]{:S(2)}) collective-permute-start(bf16[512,2048]{1,0:T(8,128)(2,1)} %convolution_convert_fusion.5), channel_id=1, source_target_pairs={{0,4},{4,0},{1,5},{5,1},{2,6},{6,2},{3,7},{7,3},{8,12},{12,8},{9,1... | collective-permute-start | bytes 6291464 | tf_op jit(solution)/shard_map/ppermute | solution.py:63
  318.1 14.8 %collective-permute-start.36 = (bf16[2,64,2048]{2,1,0:T(8,128)(2,1)S(1)}, bf16[2,64,2048]{2,1,0:T(8,128)(2,1)S(1)}, u32[]{:S(2)}, u32[]{:S(2)}) collective-permute-start(bf16[2,64,2048]{2,1,0:T(8,128)(2,1)S(1)} %dynamic-slice_bitcast_fusion.17), channel_id=1, source_target_pairs={{0,16},{8,24},{16,0},{24,8},{1,17},{9,25},{17,1},{25,9},{2,18},{10... | collective-permute-start | bytes 1572872 | tf_op jit(solution)/shard_map/ppermute | solution.py:153
  319.9 14.8 %collective-permute-start.35 = (bf16[2,64,2048]{2,1,0:T(8,128)(2,1)S(1)}, bf16[2,64,2048]{2,1,0:T(8,128)(2,1)S(1)}, u32[]{:S(2)}, u32[]{:S(2)}) collective-permute-start(bf16[2,64,2048]{2,1,0:T(8,128)(2,1)S(1)} %dynamic-slice_bitcast_fusion.18), channel_id=1, source_target_pairs={{0,8},{8,0},{16,24},{24,16},{1,9},{9,1},{17,25},{25,17},{2,10},{10... | collective-permute-start | bytes 1572872 | tf_op jit(solution)/shard_map/ppermute | solution.py:153
  329.2 14.9 %collective-permute-start.39 = (bf16[2,64,2048]{2,1,0:T(8,128)(2,1)S(1)}, bf16[2,64,2048]{2,1,0:T(8,128)(2,1)S(1)}, u32[]{:S(2)}, u32[]{:S(2)}) collective-permute-start(bf16[2,64,2048]{2,1,0:T(8,128)(2,1)S(1)} %dynamic-slice_bitcast_fusion.15), channel_id=1, source_target_pairs={{0,16},{8,24},{16,0},{24,8},{1,17},{9,25},{17,1},{25,9},{2,18},{10... | collective-permute-start | bytes 1572872 | tf_op jit(solution)/shard_map/ppermute | solution.py:153
  330.5 14.7 %collective-permute-start.38 = (bf16[2,64,2048]{2,1,0:T(8,128)(2,1)S(1)}, bf16[2,64,2048]{2,1,0:T(8,128)(2,1)S(1)}, u32[]{:S(2)}, u32[]{:S(2)}) collective-permute-start(bf16[2,64,2048]{2,1,0:T(8,128)(2,1)S(1)} %dynamic-slice_bitcast_fusion.16), channel_id=1, source_target_pairs={{0,8},{8,0},{16,24},{24,16},{1,9},{9,1},{17,25},{25,17},{2,10},{10... | collective-permute-start | bytes 1572872 | tf_op jit(solution)/shard_map/ppermute | solution.py:153
  332.9 22.5 %collective-permute-start.43 = (bf16[2,128,1024]{2,1,0:T(8,128)(2,1)S(1)}, bf16[2,128,1024]{2,1,0:T(8,128)(2,1)S(1)}, u32[]{:S(2)}, u32[]{:S(2)}) collective-permute-start(bf16[2,128,1024]{2,1,0:T(8,128)(2,1)S(1)} %dynamic-slice_bitcast_fusion.13), channel_id=1, source_target_pairs={{0,16},{8,24},{16,0},{24,8},{1,17},{9,25},{17,1},{25,9},{2,18},{10... | collective-permute-start | bytes 1572872 | tf_op jit(solution)/shard_map/ppermute | solution.py:153
  345.4 15.1 %collective-permute-start.40 = (bf16[128,2048]{1,0:T(8,128)(2,1)S(1)}, bf16[128,2048]{1,0:T(8,128)(2,1)S(1)}, u32[]{:S(2)}, u32[]{:S(2)}) collective-permute-start(bf16[128,2048]{1,0:T(8,128)(2,1)S(1)} %get-tuple-element.245), channel_id=1, source_target_pairs={{0,1},{1,0},{2,3},{3,2},{4,5},{5,4},{6,7},{7,6},{8,9},{9,8},{10,11... | collective-permute-start | bytes 1572872 | tf_op jit(solution)/shard_map/ppermute | solution.py:75
  350.1 12.9 %collective-permute-start.42 = (bf16[2,128,1024]{2,1,0:T(8,128)(2,1)S(1)}, bf16[2,128,1024]{2,1,0:T(8,128)(2,1)S(1)}, u32[]{:S(2)}, u32[]{:S(2)}) collective-permute-start(bf16[2,128,1024]{2,1,0:T(8,128)(2,1)S(1)} %dynamic-slice_bitcast_fusion.14), channel_id=1, source_target_pairs={{0,8},{8,0},{16,24},{24,16},{1,9},{9,1},{17,25},{25,17},{2,10},{10... | collective-permute-start | bytes 1572872 | tf_op jit(solution)/shard_map/ppermute | solution.py:153
  351.1 17.4 %collective-permute-start.47 = (bf16[2,128,1024]{2,1,0:T(8,128)(2,1)S(1)}, bf16[2,128,1024]{2,1,0:T(8,128)(2,1)S(1)}, u32[]{:S(2)}, u32[]{:S(2)}) collective-permute-start(bf16[2,128,1024]{2,1,0:T(8,128)(2,1)S(1)} %dynamic-slice_bitcast_fusion.11), channel_id=1, source_target_pairs={{0,16},{8,24},{16,0},{24,8},{1,17},{9,25},{17,1},{25,9},{2,18},{10... | collective-permute-start | bytes 1572872 | tf_op jit(solution)/shard_map/ppermute | solution.py:153
  366.2 14.9 %collective-permute-start.46 = (bf16[2,128,1024]{2,1,0:T(8,128)(2,1)S(1)}, bf16[2,128,1024]{2,1,0:T(8,128)(2,1)S(1)}, u32[]{:S(2)}, u32[]{:S(2)}) collective-permute-start(bf16[2,128,1024]{2,1,0:T(8,128)(2,1)S(1)} %dynamic-slice_bitcast_fusion.12), channel_id=1, source_target_pairs={{0,8},{8,0},{16,24},{24,16},{1,9},{9,1},{17,25},{25,17},{2,10},{10... | collective-permute-start | bytes 1572872 | tf_op jit(solution)/shard_map/ppermute | solution.py:153
  367.4 21.8 %collective-permute-start.51 = (bf16[128,2048]{1,0:T(8,128)(2,1)S(1)}, bf16[128,2048]{1,0:T(8,128)(2,1)S(1)}, u32[]{:S(2)}, u32[]{:S(2)}) collective-permute-start(bf16[128,2048]{1,0:T(8,128)(2,1)S(1)} %fusion.121), channel_id=1, source_target_pairs={{0,8},{8,0},{16,24},{24,16},{1,9},{9,1},{17,25},{25,17},{2,10},{10... | collective-permute-start | bytes 1572872 | tf_op jit(solution)/shard_map/ppermute | solution.py:153
  396.7 280.6 %all-gather.9.cloned.1.call-start = ((), (), s32[]{:S(2)}) async-start(), calls=%async_computation | async-start | bytes 18874368 | tf_op jit(solution)/shard_map/all_gather | solution.py:541
  399.8 19.6 %collective-permute-start.53 = (bf16[2,128,1024]{2,1,0:T(8,128)(2,1)S(1)}, bf16[2,128,1024]{2,1,0:T(8,128)(2,1)S(1)}, u32[]{:S(2)}, u32[]{:S(2)}) collective-permute-start(bf16[2,128,1024]{2,1,0:T(8,128)(2,1)S(1)} %dynamic-slice_bitcast_fusion.9), channel_id=1, source_target_pairs={{0,16},{8,24},{16,0},{24,8},{1,17},{9,25},{17,1},{25,9},{2,18},{10... | collective-permute-start | bytes 1572872 | tf_op jit(solution)/shard_map/ppermute | solution.py:153
  401.7 20.0 %collective-permute-start.52 = (bf16[2,128,1024]{2,1,0:T(8,128)(2,1)S(1)}, bf16[2,128,1024]{2,1,0:T(8,128)(2,1)S(1)}, u32[]{:S(2)}, u32[]{:S(2)}) collective-permute-start(bf16[2,128,1024]{2,1,0:T(8,128)(2,1)S(1)} %dynamic-slice_bitcast_fusion.10), channel_id=1, source_target_pairs={{0,8},{8,0},{16,24},{24,16},{1,9},{9,1},{17,25},{25,17},{2,10},{10... | collective-permute-start | bytes 1572872 | tf_op jit(solution)/shard_map/ppermute | solution.py:153
  404.0 35.6 %collective-permute-start.57 = (bf16[2,128,1024]{2,1,0:T(8,128)(2,1)}, bf16[2,128,1024]{2,1,0:T(8,128)(2,1)}, u32[]{:S(2)}, u32[]{:S(2)}) collective-permute-start(bf16[2,128,1024]{2,1,0:T(8,128)(2,1)} %dynamic-slice_bitcast_fusion.7), channel_id=1, source_target_pairs={{0,16},{8,24},{16,0},{24,8},{1,17},{9,25},{17,1},{25,9},{2,18},{10... | collective-permute-start | bytes 1572872 | tf_op jit(solution)/shard_map/ppermute | solution.py:153
  432.0 14.4 %collective-permute-start.55 = (bf16[128,2048]{1,0:T(8,128)(2,1)}, bf16[128,2048]{1,0:T(8,128)(2,1)S(1)}, u32[]{:S(2)}, u32[]{:S(2)}) collective-permute-start(bf16[128,2048]{1,0:T(8,128)(2,1)} %get-tuple-element.155), channel_id=1, source_target_pairs={{0,1},{1,0},{2,3},{3,2},{4,5},{5,4},{6,7},{7,6},{8,9},{9,8},{10,11... | collective-permute-start | bytes 1572872 | tf_op jit(solution)/shard_map/ppermute | solution.py:75
  436.6 26.1 %collective-permute-start.56 = (bf16[2,128,1024]{2,1,0:T(8,128)(2,1)S(1)}, bf16[2,128,1024]{2,1,0:T(8,128)(2,1)S(1)}, u32[]{:S(2)}, u32[]{:S(2)}) collective-permute-start(bf16[2,128,1024]{2,1,0:T(8,128)(2,1)S(1)} %dynamic-slice_bitcast_fusion.8), channel_id=1, source_target_pairs={{0,8},{8,0},{16,24},{24,16},{1,9},{9,1},{17,25},{25,17},{2,10},{10... | collective-permute-start | bytes 1572872 | tf_op jit(solution)/shard_map/ppermute | solution.py:153
  439.5 33.3 %collective-permute-start.61 = (bf16[256,1024]{1,0:T(8,128)(2,1)S(1)}, bf16[256,1024]{1,0:T(8,128)(2,1)S(1)}, u32[]{:S(2)}, u32[]{:S(2)}) collective-permute-start(bf16[256,1024]{1,0:T(8,128)(2,1)S(1)} %fusion.113), channel_id=1, source_target_pairs={{0,8},{8,0},{16,24},{24,16},{1,9},{9,1},{17,25},{25,17},{2,10},{10... | collective-permute-start | bytes 1572872 | tf_op jit(solution)/shard_map/ppermute | solution.py:153
  467.5 19.9 %collective-permute-start.65 = (bf16[256,1024]{1,0:T(8,128)(2,1)}, bf16[256,1024]{1,0:T(8,128)(2,1)}, u32[]{:S(2)}, u32[]{:S(2)}) collective-permute-start(bf16[256,1024]{1,0:T(8,128)(2,1)} %fusion.105), channel_id=1, source_target_pairs={{0,8},{8,0},{16,24},{24,16},{1,9},{9,1},{17,25},{25,17},{2,10},{10... | collective-permute-start | bytes 1572872 | tf_op jit(solution)/shard_map/ppermute | solution.py:153
  478.3 24.0 %collective-permute-start.62 = (bf16[128,2048]{1,0:T(8,128)(2,1)}, bf16[128,2048]{1,0:T(8,128)(2,1)}, u32[]{:S(2)}, u32[]{:S(2)}) collective-permute-start(bf16[128,2048]{1,0:T(8,128)(2,1)} %collective-permute-done.58), channel_id=1, source_target_pairs={{0,1},{1,0},{2,3},{3,2},{4,5},{5,4},{6,7},{7,6},{8,9},{9,8},{10,11... | collective-permute-start | bytes 1572872 | tf_op jit(solution)/shard_map/ppermute | solution.py:75
  479.0 23.3 %collective-permute-start.63 = (bf16[128,2048]{1,0:T(8,128)(2,1)}, bf16[128,2048]{1,0:T(8,128)(2,1)}, u32[]{:S(2)}, u32[]{:S(2)}) collective-permute-start(bf16[128,2048]{1,0:T(8,128)(2,1)} %collective-permute-done.59), channel_id=1, source_target_pairs={{0,0},{1,2},{2,1},{3,3},{4,4},{5,6},{6,5},{7,7},{8,8},{9,10},{10,9... | collective-permute-start | bytes 1572872 | tf_op jit(solution)/shard_map/ppermute | solution.py:75
  485.2 17.0 %collective-permute-start.64 = (bf16[256,1024]{1,0:T(8,128)(2,1)}, bf16[256,1024]{1,0:T(8,128)(2,1)}, u32[]{:S(2)}, u32[]{:S(2)}) collective-permute-start(bf16[256,1024]{1,0:T(8,128)(2,1)} %fusion.109), channel_id=1, source_target_pairs={{0,16},{8,24},{16,0},{24,8},{1,17},{9,25},{17,1},{25,9},{2,18},{10... | collective-permute-start | bytes 1572872 | tf_op jit(solution)/shard_map/ppermute | solution.py:153
  507.8 19.2 %collective-permute-start.81 = (bf16[128,2048]{1,0:T(8,128)(2,1)}, bf16[128,2048]{1,0:T(8,128)(2,1)S(1)}, u32[]{:S(2)}, u32[]{:S(2)}) collective-permute-start(bf16[128,2048]{1,0:T(8,128)(2,1)} %get-tuple-element.268), channel_id=1, source_target_pairs={{0,3},{1,0},{2,1},{3,2},{4,7},{5,4},{6,5},{7,6},{8,11},{9,8},{10,9... | collective-permute-start | bytes 1572872 | tf_op jit(solution)/shard_map/ppermute | solution.py:137
  510.1 26.9 %collective-permute-start.82 = (bf16[128,2048]{1,0:T(8,128)(2,1)}, bf16[128,2048]{1,0:T(8,128)(2,1)}, u32[]{:S(2)}, u32[]{:S(2)}) collective-permute-start(bf16[128,2048]{1,0:T(8,128)(2,1)} %get-tuple-element.267), channel_id=1, source_target_pairs={{0,2},{1,3},{2,0},{3,1},{4,6},{5,7},{6,4},{7,5},{8,10},{9,11},{10,... | collective-permute-start | bytes 1572872 | tf_op jit(solution)/shard_map/ppermute | solution.py:137
  512.7 24.3 %collective-permute-start.83 = (bf16[128,2048]{1,0:T(8,128)(2,1)}, bf16[128,2048]{1,0:T(8,128)(2,1)}, u32[]{:S(2)}, u32[]{:S(2)}) collective-permute-start(bf16[128,2048]{1,0:T(8,128)(2,1)} %get-tuple-element.266), channel_id=1, source_target_pairs={{0,1},{1,2},{2,3},{3,0},{4,5},{5,6},{6,7},{7,4},{8,9},{9,10},{10,1... | collective-permute-start | bytes 1572872 | tf_op jit(solution)/shard_map/ppermute | solution.py:137
  543.1 207.4 %all-gather.11.cloned.1.call-start = ((), (), s32[]{:S(2)}) async-start(), calls=%async_computation.1 | async-start | bytes 5898240 | tf_op jit(solution)/shard_map/all_gather | solution.py:606
  600.3 17.2 %collective-permute-start.66 = (bf16[4,64,5120]{2,1,0:T(8,128)(2,1)}, bf16[4,64,5120]{2,1,0:T(8,128)(2,1)}, u32[]{:S(2)}, u32[]{:S(2)}) collective-permute-start(bf16[4,64,5120]{2,1,0:T(8,128)(2,1)} %dynamic-slice_bitcast_fusion), channel_id=1, source_target_pairs={{0,4},{4,0},{1,5},{5,1},{2,6},{6,2},{3,7},{7,3},{8,12},{12,8},{9,1... | collective-permute-start | bytes 7864328 | tf_op jit(solution)/shard_map/ppermute | solution.py:153
  603.0 14.5 %collective-permute-start.67 = (bf16[128,2048]{1,0:T(8,128)(2,1)}, bf16[128,2048]{1,0:T(8,128)(2,1)S(1)}, u32[]{:S(2)}, u32[]{:S(2)}) collective-permute-start(bf16[128,2048]{1,0:T(8,128)(2,1)} %get-tuple-element.235), channel_id=1, source_target_pairs={{0,1},{1,0},{2,3},{3,2},{4,5},{5,4},{6,7},{7,6},{8,9},{9,8},{10,11... | collective-permute-start | bytes 1572872 | tf_op jit(solution)/shard_map/ppermute | solution.py:75
  603.0 14.5 %collective-permute-start.68 = (bf16[128,2048]{1,0:T(8,128)(2,1)}, bf16[128,2048]{1,0:T(8,128)(2,1)S(1)}, u32[]{:S(2)}, u32[]{:S(2)}) collective-permute-start(bf16[128,2048]{1,0:T(8,128)(2,1)} %get-tuple-element.234), channel_id=1, source_target_pairs={{0,0},{1,2},{2,1},{3,3},{4,4},{5,6},{6,5},{7,7},{8,8},{9,10},{10,9... | collective-permute-start | bytes 1572872 | tf_op jit(solution)/shard_map/ppermute | solution.py:75
  621.6 20.8 %collective-permute-start.73 = (bf16[2,32,5120]{2,1,0:T(8,128)(2,1)S(1)}, bf16[2,32,5120]{2,1,0:T(8,128)(2,1)S(1)}, u32[]{:S(2)}, u32[]{:S(2)}) collective-permute-start(bf16[2,32,5120]{2,1,0:T(8,128)(2,1)S(1)} %dynamic-slice_bitcast_fusion.1), channel_id=1, source_target_pairs={{0,16},{8,24},{16,0},{24,8},{1,17},{9,25},{17,1},{25,9},{2,18},{10... | collective-permute-start | bytes 1966088 | tf_op jit(solution)/shard_map/ppermute | solution.py:153
  623.0 19.3 %collective-permute-start.69 = (bf16[2,32,5120]{2,1,0:T(8,128)(2,1)S(1)}, bf16[2,32,5120]{2,1,0:T(8,128)(2,1)S(1)}, u32[]{:S(2)}, u32[]{:S(2)}) collective-permute-start(bf16[2,32,5120]{2,1,0:T(8,128)(2,1)S(1)} %dynamic-slice_bitcast_fusion.2), channel_id=1, source_target_pairs={{0,8},{8,0},{16,24},{24,16},{1,9},{9,1},{17,25},{25,17},{2,10},{10... | collective-permute-start | bytes 1966088 | tf_op jit(solution)/shard_map/ppermute | solution.py:153
  624.3 14.6 %collective-permute-start.70 = (bf16[128,2048]{1,0:T(8,128)(2,1)S(1)}, bf16[128,2048]{1,0:T(8,128)(2,1)S(1)}, u32[]{:S(2)}, u32[]{:S(2)}) collective-permute-start(bf16[128,2048]{1,0:T(8,128)(2,1)S(1)} %get-tuple-element.233), channel_id=1, source_target_pairs={{0,1},{1,0},{2,3},{3,2},{4,5},{5,4},{6,7},{7,6},{8,9},{9,8},{10,11... | collective-permute-start | bytes 1572872 | tf_op jit(solution)/shard_map/ppermute | solution.py:75
  643.0 13.6 %collective-permute-start.74 = (bf16[128,2048]{1,0:T(8,128)(2,1)S(1)}, bf16[128,2048]{1,0:T(8,128)(2,1)S(1)}, u32[]{:S(2)}, u32[]{:S(2)}) collective-permute-start(bf16[128,2048]{1,0:T(8,128)(2,1)S(1)} %get-tuple-element.231), channel_id=1, source_target_pairs={{0,1},{1,0},{2,3},{3,2},{4,5},{5,4},{6,7},{7,6},{8,9},{9,8},{10,11... | collective-permute-start | bytes 1572872 | tf_op jit(solution)/shard_map/ppermute | solution.py:75
  661.5 15.2 %collective-permute-start.78 = (bf16[64,768]{1,0:T(8,128)(2,1)S(1)}, bf16[64,768]{1,0:T(8,128)(2,1)S(1)}, u32[]{:S(2)}, u32[]{:S(2)}) collective-permute-start(bf16[64,768]{1,0:T(8,128)(2,1)S(1)} %get-tuple-element.298), channel_id=1, source_target_pairs={{0,3},{1,0},{2,1},{3,2},{4,7},{5,4},{6,5},{7,6},{8,11},{9,8},{10,9... | collective-permute-start | bytes 294920 | tf_op jit(solution)/shard_map/ppermute | solution.py:137
  680.7 13.8 %collective-permute-start.84 = (bf16[128,2048]{1,0:T(8,128)(2,1)}, bf16[128,2048]{1,0:T(8,128)(2,1)S(1)}, u32[]{:S(2)}, u32[]{:S(2)}) collective-permute-start(bf16[128,2048]{1,0:T(8,128)(2,1)} %get-tuple-element.229), channel_id=1, source_target_pairs={{0,1},{1,0},{2,3},{3,2},{4,5},{5,4},{6,7},{7,6},{8,9},{9,8},{10,11... | collective-permute-start | bytes 1572872 | tf_op jit(solution)/shard_map/ppermute | solution.py:75
  697.1 37.5 %collective-permute-start.86 = (bf16[128,2048]{1,0:T(8,128)(2,1)}, bf16[128,2048]{1,0:T(8,128)(2,1)S(1)}, u32[]{:S(2)}, u32[]{:S(2)}) collective-permute-start(bf16[128,2048]{1,0:T(8,128)(2,1)} %get-tuple-element.227), channel_id=1, source_target_pairs={{0,1},{1,0},{2,3},{3,2},{4,5},{5,4},{6,7},{7,6},{8,9},{9,8},{10,11... | collective-permute-start | bytes 1572872 | tf_op jit(solution)/shard_map/ppermute | solution.py:75
  700.8 33.8 %collective-permute-start.87 = (bf16[128,2048]{1,0:T(8,128)(2,1)}, bf16[128,2048]{1,0:T(8,128)(2,1)S(1)}, u32[]{:S(2)}, u32[]{:S(2)}) collective-permute-start(bf16[128,2048]{1,0:T(8,128)(2,1)} %get-tuple-element.226), channel_id=1, source_target_pairs={{0,0},{1,2},{2,1},{3,3},{4,4},{5,6},{6,5},{7,7},{8,8},{9,10},{10,9... | collective-permute-start | bytes 1572872 | tf_op jit(solution)/shard_map/ppermute | solution.py:75
  710.8 26.6 %collective-permute-start.90 = (f32[1056]{0:T(1024)S(1)}, f32[1056]{0:T(1024)S(1)}, u32[]{:S(2)}, u32[]{:S(2)}) collective-permute-start(f32[1056]{0:T(1024)S(1)} %get-tuple-element.191), channel_id=1, source_target_pairs={{0,1},{1,2},{2,3},{3,0},{4,5},{5,6},{6,7},{7,4},{8,9},{9,10},{10,1... | collective-permute-start | bytes 12680 | tf_op jit(solution)/shard_map/ppermute | solution.py:210
  712.5 24.9 %collective-permute-start.91 = (f32[1056]{0:T(1024)S(1)}, f32[1056]{0:T(1024)S(1)}, u32[]{:S(2)}, u32[]{:S(2)}) collective-permute-start(f32[1056]{0:T(1024)S(1)} %get-tuple-element.193), channel_id=1, source_target_pairs={{0,2},{1,3},{2,0},{3,1},{4,6},{5,7},{6,4},{7,5},{8,10},{9,11},{10,... | collective-permute-start | bytes 12680 | tf_op jit(solution)/shard_map/ppermute | solution.py:210
  713.8 23.6 %collective-permute-start.92 = (f32[1056]{0:T(1024)S(1)}, f32[1056]{0:T(1024)S(1)}, u32[]{:S(2)}, u32[]{:S(2)}) collective-permute-start(f32[1056]{0:T(1024)S(1)} %get-tuple-element.192), channel_id=1, source_target_pairs={{0,3},{1,0},{2,1},{3,2},{4,7},{5,4},{6,5},{7,6},{8,11},{9,8},{10,9... | collective-permute-start | bytes 12680 | tf_op jit(solution)/shard_map/ppermute | solution.py:210
  (125 other events, 2004.3 us)
Sparse Core Ops, SparseCore 0:
  24.3 32.2 all-gather.12
  139.7 90.1 all-gather.14
  396.9 74.0 all-gather.16
  543.2 91.7 all-gather.8
  678.4 39.9 all-gather.10

commit v4 on v3

v4 whole, which is shorter than its diff:
```python
import functools

import jax
import jax.numpy as jnp
from jax import lax
from jax.experimental import pallas as pl
from jax.experimental.pallas import tpu as pltpu
from jax.sharding import Mesh, PartitionSpec as P

HEAD_SIZE = 64
EPSILON = 1e-05
THETA_BASE = 1000000.0
NEG_FILL = -1e30
LOG2E = 1.4426950408889634
BF = jnp.bfloat16
F32 = jnp.float32
PLANE = ("chip", "core")


def mm(a, b):
    return jnp.dot(a, b, preferred_element_type=F32)


def mm_last(a, b):
    return lax.dot_general(a, b, (((1,), (1,)), ((), ())), preferred_element_type=F32)


def mm_first(a, b):
    return lax.dot_general(a, b, (((0,), (0,)), ((), ())), preferred_element_type=F32)


def swap_cores(a):
    return lax.ppermute(a, "core", [(0, 1), (1, 0)])


def exchanges():
    count = lax.axis_size("fsdp")
    even = [(i, i ^ 1) for i in range(count)]
    odd = [(0, 0)] + [(i, ((i - 1) ^ 1) + 1) for i in range(1, count - 1)] + [(count - 1, count - 1)]
    return even, odd


def line_step(first, second):
    even, odd = exchanges()
    return lax.ppermute(first, "fsdp", even), lax.ppermute(second, "fsdp", odd)


def line_steps(own, ahead_of={}, begun=None, turn=None):
    steps = []
    first, second = own, own
    for t in range(lax.axis_size("fsdp") - 1):
        if t in ahead_of:
            first, second = after((first, second), ahead_of[t])
        if t and turn:
            first, second = after((first, second), turn((first, second)))
        if t == 0 and begun:
            by_even, by_odd = begun
        else:
            by_even, by_odd = line_step(first, second)
        steps.append((by_even, by_odd))
        first, second = by_odd, by_even
    return steps


def line_pieces(own, steps):
    count = lax.axis_size("fsdp")
    mine = lax.axis_index("fsdp")
    is_even = mine % 2 == 0
    pieces = [own]
    for d in range(1, count):
        below, above = steps[d - 1], steps[count - d - 1]
        from_below = jnp.where(is_even, below[1], below[0])
        from_above = jnp.where(is_even, above[0], above[1])
        pieces.append(jnp.where(mine >= d, from_below, from_above))
    return jnp.concatenate(pieces, axis=0)


def line_scatter(parts, ahead_of=None):
    count = lax.axis_size("fsdp")
    mine = lax.axis_index("fsdp")
    is_even = mine % 2 == 0
    is_end = (mine == 0) | (mine == count - 1)
    by_even = by_odd = None
    for t in range(count - 1):
        up = jnp.where(is_even, t + 1, count - 1 - t)
        first = lax.dynamic_index_in_dim(parts, up, keepdims=False)
        second = lax.dynamic_index_in_dim(parts, count - up, keepdims=False)
        if t:
            if ahead_of:
                by_even, by_odd = after((by_even, by_odd), ahead_of(t, (by_even, by_odd)))
            first, second = first + by_odd.astype(F32), second + by_even.astype(F32)
        second = jnp.where(is_end, 0.0, second)
        by_even, by_odd = line_step(first.astype(BF), second.astype(BF))
    return by_even, by_odd


def absolute(ring):
    count = len(ring)
    mine = lax.axis_index("fsdp")
    out = jnp.zeros((count, *ring[0].shape), ring[0].dtype)
    for e, piece in enumerate(ring):
        out = lax.dynamic_update_index_in_dim(out, piece, (mine + e) % count, 0)
    return out


def exchange_line(piece_for):
    count = lax.axis_size("fsdp")
    mine = lax.axis_index("fsdp")
    return [piece_for(mine)] + [
        lax.ppermute(
            piece_for((mine - e) % count),
            "fsdp",
            [(i, (i - e) % count) for i in range(count)],
        )
        for e in range(1, count)
    ]


def add_low(a, b):
    return (a.astype(F32) + b.astype(F32)).astype(BF)


def halve(blocks, axis, name, bit, pin=()):
    mybit = (lax.axis_index(name) >> bit) & 1
    pairs = [(i, i ^ (1 << bit)) for i in range(lax.axis_size(name))]
    got = lax.ppermute(
        lax.dynamic_index_in_dim(blocks, 1 - mybit, axis, keepdims=False), name, pairs
    )
    got = after(got, pin)
    return add_low(lax.dynamic_index_in_dim(blocks, mybit, axis, keepdims=False), got)


def chip_halves(terms):
    chips, rows, cols = terms.shape
    bits = chips.bit_length() - 1
    return [
        terms[:, g * rows // 2 : (g + 1) * rows // 2].reshape([2] * bits + [rows // 2, cols])
        for g in range(2)
    ]


def chip_stage(halves, step, pin=(), lead=(0, 0)):
    bits = lax.axis_size("chip").bit_length() - 1
    out = []
    for g in range(2):
        done = [(g + k) % bits for k in range(step)]
        left = [b for b in range(bits - 1, -1, -1) if b not in done]
        bit = (g + step) % bits
        out.append(halve(halves[g], lead[g] + left.index(bit), "chip", bit, pin))
    return out


def chip_rest(halves, step, pin=(), lead=(0, 0)):
    for k in range(step, lax.axis_size("chip").bit_length() - 1):
        halves = chip_stage(halves, k, pin, lead)
    return halves


def after(value, *others):
    return lax.optimization_barrier((value, *others))[0]


def gather_small(own):
    return absolute(exchange_line(lambda j: own))


def small_line(rows, pin):
    count = lax.axis_size("fsdp")
    mine = lax.axis_index("fsdp")
    got = [
        lax.ppermute(
            lax.dynamic_index_in_dim(rows, (mine + d) % count, keepdims=False),
            "fsdp",
            [(i, (i + d) % count) for i in range(count)],
        )
        for d in range(1, count)
    ]
    return sum(after(got, pin), lax.dynamic_index_in_dim(rows, mine, keepdims=False))


def small_chips(total, pin):
    chips = lax.axis_size("chip")
    got = [
        lax.ppermute(total, "chip", [(i, i ^ d) for i in range(chips)]) for d in range(1, chips)
    ]
    return sum(after(got, pin), total)


def split_mean(values, block):
    high = values.astype(BF)
    low = (values - high.astype(F32)).astype(BF)
    return mm(high, block) + mm(low, block)


def swap_pairs(values):
    lane = lax.broadcasted_iota(jnp.int32, values.shape, 1)
    half = HEAD_SIZE // 2
    lanes = values.shape[1]
    return jnp.where(
        lane % HEAD_SIZE < half,
        pltpu.roll(values, lanes - half, 1),
        pltpu.roll(values, half, 1),
    )


def head_unit(pre, block):
    inverse = lax.rsqrt(split_mean(pre * pre, block) + EPSILON)
    return pre * inverse, inverse


def turn_heads(values, cosine, sine):
    return values * cosine + swap_pairs(values) * sine


def turn_back(values, cosine, sine):
    return values * cosine - swap_pairs(values) * sine


def head_grad(grad, unit, inverse, gain, block):
    scaled = grad * gain
    return inverse * (scaled - unit * split_mean(scaled * unit, block))


def spread(values, source, seq, rows):
    lanes = values.shape[1]
    a = lax.broadcasted_iota(jnp.int32, (lanes, 2 * HEAD_SIZE), 0)
    b = lax.broadcasted_iota(jnp.int32, (lanes, 2 * HEAD_SIZE), 1)
    for side in range(2):
        move = (a - source * HEAD_SIZE == b - side * HEAD_SIZE) & (b // HEAD_SIZE == side)
        rows[side * seq : (side + 1) * seq, :] = mm(values, move.astype(BF)).astype(BF)


def load_heads(keys, vals, cosine, sine, key_gain, block, kv, keys_at, vals_at):
    seq = keys.shape[0]
    unit, _ = head_unit(keys[...], block[...])
    turned = turn_heads(unit * key_gain[...], cosine[...], sine[...]).astype(BF)
    low = vals[...].astype(BF)
    for n in range(kv):
        spread(turned, n, seq, keys_at.at[n])
        spread(low, n if kv == 2 else 1, seq, vals_at.at[n])


def attend_kernel(
    kv, each, scale, pre, keys, vals, bias, cosine, sine, cos_own, sin_own, query_gain, key_gain,
    block, out, inverse, keys_at, vals_at,
):
    j, i = pl.program_id(0), pl.program_id(1)
    seq = keys.shape[0]

    @pl.when((j == 0) & (i == 0))
    def _():
        load_heads(keys, vals, cosine, sine, key_gain, block, kv, keys_at, vals_at)

    unit, _ = head_unit(pre[...], block[...])
    query = turn_heads(unit * query_gain[...], cos_own[...], sin_own[...]).astype(BF)
    head = j // each
    scores = mm_last(query, keys_at[head]) * (scale * LOG2E)
    side = lax.broadcasted_iota(jnp.int32, (2 * seq, 2 * HEAD_SIZE), 0) // seq
    lane = lax.broadcasted_iota(jnp.int32, (2 * seq, 2 * HEAD_SIZE), 1) // HEAD_SIZE
    ones = (side == lane).astype(BF)
    allowed = bias[...]
    expo = jnp.exp2(
        jnp.concatenate([scores[:, :seq] + allowed, scores[:, seq:] + allowed], axis=1)
    ).astype(BF)
    inv = 1.0 / mm(expo, ones)
    out[...] = (mm(expo, vals_at[head]) * inv).astype(BF)
    inverse[...] = inv


def attend_back_kernel(
    kv, each, scale, pre, keys, vals, bias, cosine, sine, cos_own, sin_own, query_gain, key_gain,
    block, out, inverse, grad, grad_proj, query_sum, key_sum, keys_at, vals_at, key_acc, val_acc,
):
    j, i = pl.program_id(0), pl.program_id(1)
    seq = keys.shape[0]
    rows = pre.shape[0]
    two = 2 * HEAD_SIZE

    @pl.when((j == 0) & (i == 0))
    def _():
        load_heads(keys, vals, cosine, sine, key_gain, block, kv, keys_at, vals_at)
        key_acc[...] = jnp.zeros_like(key_acc)
        val_acc[...] = jnp.zeros_like(val_acc)
        query_sum[...] = jnp.zeros_like(query_sum)

    unit, inv_unit = head_unit(pre[...], block[...])
    query = turn_heads(unit * query_gain[...], cos_own[...], sin_own[...]).astype(BF)
    head = j // each
    keys_of, vals_of = keys_at[head], vals_at[head]
    scores = mm_last(query, keys_of) * (scale * LOG2E)
    low = grad[...]
    gprobs = mm_last(low, vals_of)
    product = low.astype(F32) * out[...].astype(F32)
    delta = split_mean(product, block[...]) * HEAD_SIZE
    inv = inverse[...]
    allowed = bias[...]
    probs, gscores = [], []
    for side in range(2):
        part = slice(side * seq, (side + 1) * seq)
        at = side * HEAD_SIZE
        p = jnp.exp2(scores[:, part] + allowed) * inv[:, at : at + 1]
        probs.append(p.astype(BF))
        gscores.append((p * (gprobs[:, part] - delta[:, at : at + 1])).astype(BF))
    probs = jnp.concatenate(probs, axis=1)
    gscores = jnp.concatenate(gscores, axis=1)
    key_acc[head] += mm_first(gscores, query)
    val_acc[head] += mm_first(probs, low)
    back = turn_back(mm(gscores, keys_of) * scale, cos_own[...], sin_own[...])
    query_sum[...] += jnp.sum(back * unit, axis=0, keepdims=True)
    grad_proj[pl.ds(pl.multiple_of(i * rows, rows), rows), pl.ds(pl.multiple_of(j * two, two), two)] = (
        head_grad(back, unit, inv_unit, query_gain[...], block[...]).astype(BF)
    )

    @pl.when((j == pl.num_programs(0) - 1) & (i == pl.num_programs(1) - 1))
    def _():
        lane = lax.broadcasted_iota(jnp.int32, (seq, two), 1)

        def fold(acc, n):
            both = jnp.where(lane < HEAD_SIZE, acc[n, :seq, :], acc[n, seq:, :])
            return both + pltpu.roll(both, HEAD_SIZE, 1)

        key_tile = fold(key_acc, 0) * scale
        val_tile = fold(val_acc, 0)
        if kv == 2:
            key_tile = jnp.where(lane < HEAD_SIZE, key_tile, fold(key_acc, 1) * scale)
            val_tile = jnp.where(lane < HEAD_SIZE, val_tile, fold(val_acc, 1))
        unit_k, inv_k = head_unit(keys[...], block[...])
        back_k = turn_back(key_tile, cosine[...], sine[...])
        key_sum[...] = jnp.sum(back_k * unit_k, axis=0, keepdims=True)
        key_low = head_grad(back_k, unit_k, inv_k, key_gain[...], block[...])
        start = grad_proj.shape[1] - kv * two
        if kv == 2:
            grad_proj[:, start : start + two] = key_low.astype(BF)
            grad_proj[:, start + two :] = val_tile.astype(BF)
        else:
            grad_proj[:, start:] = jnp.where(lane < HEAD_SIZE, key_low, val_tile).astype(BF)


def attention_call(pre, bias, cosine, sine, query_gain, key_gain, kv, more=None):
    seq, cols = pre.shape
    two = 2 * HEAD_SIZE
    q_cols = cols - kv * two
    tiles = q_cols // two
    each = tiles // kv
    rows = min(256, seq)
    lane = jnp.arange(two) // HEAD_SIZE
    block = jnp.where(lane[:, None] == lane[None, :], 1.0 / HEAD_SIZE, 0.0).astype(BF)
    own = pl.BlockSpec((rows, two), lambda j, i: (i, j))
    here = pl.BlockSpec((rows, two), lambda j, i: (i, 0))
    whole = pl.BlockSpec((seq, two), lambda j, i: (0, 0))
    row = pl.BlockSpec((1, two), lambda j, i: (0, 0))
    key_tile = pl.BlockSpec((seq, two), lambda j, i: (0, tiles))
    val_tile = pl.BlockSpec((seq, two), lambda j, i: (0, tiles + kv - 1))
    in_specs = [
        own, key_tile, val_tile, pl.BlockSpec((rows, seq), lambda j, i: (i, 0)), whole, whole,
        here, here, row, row, pl.BlockSpec((two, two), lambda j, i: (0, 0)),
    ]
    twice = [jnp.concatenate([g, g]).reshape(1, two) for g in (query_gain, key_gain)]
    args = [pre, pre, pre, bias, cosine, sine, cosine, sine, *twice, block]
    heads = pltpu.VMEM((kv, 2 * seq, two), BF)
    params = pltpu.CompilerParams(vmem_limit_bytes=48 * 2**20)
    grid = (tiles, seq // rows)
    scale = HEAD_SIZE ** (-0.5)
    if more is None:
        return pl.pallas_call(
            functools.partial(attend_kernel, kv, each, scale),
            grid=grid,
            in_specs=in_specs,
            out_specs=[own, own],
            out_shape=[
                jax.ShapeDtypeStruct((seq, q_cols), BF),
                jax.ShapeDtypeStruct((seq, q_cols), F32),
            ],
            scratch_shapes=[heads, heads],
            compiler_params=params,
        )(*args)
    sums = pltpu.VMEM((kv, 2 * seq, two), F32)
    return pl.pallas_call(
        functools.partial(attend_back_kernel, kv, each, scale),
        grid=grid,
        in_specs=in_specs + [own, own, own],
        out_specs=[pl.BlockSpec((seq, cols), lambda j, i: (0, 0)), row, row],
        out_shape=[
            jax.ShapeDtypeStruct((seq, cols), BF),
            jax.ShapeDtypeStruct((1, two), F32),
            jax.ShapeDtypeStruct((1, two), F32),
        ],
        scratch_shapes=[heads, heads, sums, sums],
        compiler_params=params,
    )(*args, *more)


def pair_tables(positions):
    half = HEAD_SIZE // 2
    inverse = THETA_BASE ** (-(jnp.arange(half, dtype=F32) * 2.0) / HEAD_SIZE)
    angles = positions.astype(F32)[:, None] * inverse[None, :]
    cosine, sine = jnp.cos(angles), jnp.sin(angles)
    return jnp.tile(cosine, (1, 4)), jnp.concatenate([-sine, sine, -sine, sine], axis=1)


def lanes(width, chips, count):
    part = width // chips // count
    return [
        (slice((z * chips + c) * part, (z * chips + c + 1) * part),
         slice((c * count + z) * part, (c * count + z + 1) * part))
        for z in range(count)
        for c in range(chips)
    ]


def inverse_root(wide):
    return lax.rsqrt(jnp.mean(wide * wide, axis=-1, keepdims=True) + EPSILON)


def norm_forward(chips, count, own, part, right, left, gain, hidden, normed):
    wide = own[...].astype(F32) + part[0] + right[...].astype(F32) + left[...].astype(F32)
    hidden[...] = wide
    low = (wide * inverse_root(wide) * gain[...]).astype(BF)
    for here, there in lanes(wide.shape[1], chips, count):
        normed[:, there] = low[:, here]


def norm_backward(chips, count, part, right, left, wide, base, gain, grad, low, total, scratch):
    summed = part[0] + right[...].astype(F32) + left[...].astype(F32)
    if chips:
        for here, there in lanes(summed.shape[1], chips, count):
            scratch[:, here] = summed[:, there]
        summed = scratch[...]
    values = wide[...].astype(F32)
    inverse = inverse_root(values)
    unit = values * inverse
    sums = jnp.sum(summed * unit, axis=0, keepdims=True)

    @pl.when(pl.program_id(0) == 0)
    def _():
        total[...] = sums

    @pl.when(pl.program_id(0) > 0)
    def _():
        total[...] += sums

    scaled = summed * gain[...]
    out = base[...].astype(F32) + inverse * (
        scaled - unit * jnp.mean(scaled * unit, axis=-1, keepdims=True)
    )
    grad[...] = out
    low[...] = out.astype(BF)


def row_specs(tok, width):
    step = min(32, tok)
    block = pl.BlockSpec((step, width), lambda i: (i, 0))
    first = pl.BlockSpec((1, step, width), lambda i: (0, i, 0))
    row = pl.BlockSpec((1, width), lambda i: (0, 0))
    return tok // step, step, block, first, row


def forward_norm(own, parts, right, left, gain, chips, count):
    tok, width = own.shape
    grid, _, block, first, row = row_specs(tok, width)
    return pl.pallas_call(
        functools.partial(norm_forward, chips, count),
        grid=(grid,),
        in_specs=[block, first, block, block, row],
        out_specs=[block, block],
        out_shape=[
            jax.ShapeDtypeStruct((tok, width), F32),
            jax.ShapeDtypeStruct((tok, width), BF),
        ],
    )(own, parts, right, left, gain.reshape(1, width))


def backward_norm(parts, right, left, wide, base, gain, chips, count):
    tok, width = wide.shape
    grid, step, block, first, row = row_specs(tok, width)
    return pl.pallas_call(
        functools.partial(norm_backward, chips, count),
        grid=(grid,),
        in_specs=[first, block, block, block, block, row],
        out_specs=[block, block, row],
        out_shape=[
            jax.ShapeDtypeStruct((tok, width), F32),
            jax.ShapeDtypeStruct((tok, width), BF),
            jax.ShapeDtypeStruct((1, width), F32),
        ],
        scratch_shapes=[pltpu.VMEM((step, width), F32)],
    )(parts, right, left, wide, base, gain.reshape(1, width))


def cast_pair(own, out):
    _, cores, count, _, _ = own.shape
    half = out.shape[1] // cores // count
    for j in range(count):
        for k in range(cores):
            at = (j * cores + k) * half
            out[:, at : at + half] = own[0, k, j].astype(F32)


def place_pair(own, which, chips, count, part, half):
    step = min(64, part)
    own = own.reshape(chips, 2, count, part, 2 * half)
    cols = count * 2 * half
    return pl.pallas_call(
        cast_pair,
        grid=(chips, part // step),
        in_specs=[pl.BlockSpec((1, 2, count, step, half), lambda c, r: (c, 0, 0, r, which))],
        out_specs=pl.BlockSpec((step, cols), lambda c, r: (c * (part // step) + r, 0)),
        out_shape=jax.ShapeDtypeStruct((chips * part, cols), F32),
    )(own)


def cast_columns(_, one, two, *outs):
    half = pl.num_programs(0) // 2
    for own, mine in ((one, pl.program_id(0) < half), (two, pl.program_id(0) >= half)):

        @pl.when(mine)
        def _(own=own):
            at = 0
            for out in outs:
                out[...] = own[:, at : at + out.shape[1]].astype(F32)
                at += out.shape[1]


def place_columns(order, one, two, widths):
    blocks = order.shape[0]
    rows, cols = one.shape
    half = blocks // 2
    step = rows // half
    return pl.pallas_call(
        cast_columns,
        grid_spec=pltpu.PrefetchScalarGridSpec(
            num_scalar_prefetch=1,
            grid=(blocks,),
            in_specs=[
                pl.BlockSpec((step, cols), lambda r, order: (jnp.minimum(r, half - 1), 0)),
                pl.BlockSpec((step, cols), lambda r, order: (jnp.maximum(r - half, 0), 0)),
            ],
            out_specs=[pl.BlockSpec((step, w), lambda r, order: (order[r], 0)) for w in widths],
        ),
        out_shape=[jax.ShapeDtypeStruct((2 * rows, w), F32) for w in widths],
    )(order, one, two)


def gather_stage(halves, step, pin=()):
    chips = lax.axis_size("chip")
    bits = chips.bit_length() - 1
    out = []
    for g, half in enumerate(halves):
        bit = (g + step) % bits
        got = lax.ppermute(half, "chip", [(i, i ^ (1 << bit)) for i in range(chips)])
        out.append(jnp.concatenate([half, after(got, pin)], axis=0))
    return out


def gathered_order(g):
    chips = lax.axis_size("chip")
    bits = chips.bit_length() - 1
    chip, core = lax.axis_index("chip"), lax.axis_index("core")
    away = [0]
    for step in range(bits):
        away += [a ^ (1 << ((g + step) % bits)) for a in away]
    places = [(chip ^ a) * 2 + (core ^ k) for k in range(2) for a in away]
    return jnp.stack(places).astype(jnp.int32)


def cast_down(own, out):
    out[...] = own[0].astype(F32)


def place_down(own, chips, part, width):
    return pl.pallas_call(
        cast_down,
        grid=(2, chips),
        in_specs=[pl.BlockSpec((1, part, width), lambda k, c: (c * 2 + k, 0, 0))],
        out_specs=pl.BlockSpec((part, width), lambda k, c: (k * chips + c, 0)),
        out_shape=jax.ShapeDtypeStruct((2 * chips * part, width), F32),
    )(own)


def shards(
    inputs,
    doc_lengths,
    attn_gain,
    query_weight,
    key_projection,
    value_projection,
    query_gain,
    key_norm_gain,
    out_weight,
    ffn_gain,
    gate_weight,
    up_weight,
    down_weight,
    cotangent,
):
    tok, width = inputs.shape
    count = lax.axis_size("fsdp")
    chips = lax.axis_size("chip")
    rep = chips * 2
    mine = lax.axis_index("fsdp")
    chip = lax.axis_index("chip")
    core = lax.axis_index("core")
    seq = tok * count
    hd = HEAD_SIZE
    rows = query_weight.shape[0]
    q_cols = query_weight.shape[1] // count
    kv_cols = key_projection.shape[1] // count
    ff = gate_weight.shape[1]
    ff_own = ff // count // 2

    share = rows // rep
    at = (chip * 2 + core) * share

    def proj_piece(j):
        return jnp.concatenate(
            [
                lax.dynamic_slice(w, (at, j * wide), (share, wide))
                for w, wide in (
                    (query_weight, q_cols),
                    (key_projection, kv_cols),
                    (value_projection, kv_cols),
                )
            ],
            axis=1,
        )

    proj_ring = exchange_line(proj_piece)
    begun = line_step(inputs, inputs)
    proj_own = absolute(after(proj_ring, begun))
    x_steps = line_steps(inputs, {2: proj_own}, begun)
    x_all = line_pieces(inputs, x_steps)
    proj = lax.all_gather(proj_own, PLANE, axis=0)
    proj = proj.transpose(1, 0, 2, 3).reshape(width, q_cols + 2 * kv_cols)

    gains = jnp.concatenate([attn_gain, ffn_gain, query_gain, key_norm_gain])
    gains = gather_small(after(gains, x_steps[0]))
    gains = gains.astype(F32)
    gain_one = gains[:, :rows].reshape(-1)
    gain_two = gains[:, rows : 2 * rows].reshape(-1)
    small = hd // count
    gain_query = gains[:, 2 * rows : 2 * rows + small].reshape(-1)
    gain_key = gains[:, 2 * rows + small :].reshape(-1)

    part = rows // chips
    gate_up = after((gate_weight, up_weight), x_steps[-1])

    def pair_piece(j):
        return jnp.concatenate(
            [
                lax.dynamic_slice(w, (chip * part, (j * 2 + core) * ff_own), (part, ff_own))
                for w in gate_up
            ],
            axis=1,
        )

    pair_ring = exchange_line(pair_piece)

    order = (mine - jnp.arange(count, dtype=jnp.int32)) % count
    positions = (order[:, None] * tok + jnp.arange(tok, dtype=jnp.int32)[None, :]).reshape(-1)
    lengths = after(doc_lengths, x_steps[1])[0]
    docs = lengths.shape[0]
    upto = jnp.arange(docs)[None, :] <= jnp.arange(docs)[:, None]
    ends = jnp.sum(jnp.where(upto, lengths[None, :], 0), axis=1)
    segment = jnp.sum((positions[:, None] >= ends[None, :]).astype(jnp.int32), axis=1)
    allowed = (segment[:, None] == segment[None, :]) & (positions[None, :] <= positions[:, None])
    bias = jnp.where(allowed, 0.0, NEG_FILL).astype(F32)
    tables = pair_tables(positions)

    wide = x_all.astype(F32)
    normed_one = (wide * inverse_root(wide) * gain_one).astype(BF)
    kv_heads = kv_cols // hd
    core_args = (mm(normed_one, proj), bias, *tables, gain_query, gain_key, kv_heads)
    attended, inverse_sums = attention_call(*core_args)
    out_part = mm(attended, out_weight).reshape(count, tok, width)
    stage = {}

    def slices(t, sides):
        if t == 1:
            stage["slices"] = absolute(after(pair_ring, sides))
            return stage["slices"]
        return ()

    sides = line_scatter(out_part, slices)
    pair = lax.all_gather(stage["slices"], "chip", axis=0)
    pair = pair.reshape(width, 2 * ff_own)
    hidden_one, normed_own = forward_norm(inputs, out_part, *sides, gain_two, chips, count)

    cot_begun = line_step(*(after(cotangent, sides),) * 2)
    two_steps = line_steps(after(normed_own, cot_begun))
    normed_two = line_pieces(normed_own, two_steps)
    normed_two = jnp.concatenate([normed_two, swap_cores(normed_two)], axis=0)
    down_own = lax.dynamic_slice_in_dim(down_weight, core * ff_own, ff_own)
    both = mm(normed_two, pair)
    cot_steps = line_steps(cotangent, {1: two_steps[-1], count - 2: both}, cot_begun)
    cot_own = line_pieces(cotangent, cot_steps)
    cot_all = jnp.concatenate([cot_own, swap_cores(cot_own)], axis=0)
    grad_hidden = mm_last(cot_all, down_own)
    gate_pre, upward = both[:, :ff_own], both[:, ff_own:]
    sigmoid = jax.nn.sigmoid(gate_pre)
    silu = gate_pre * sigmoid
    hidden = (silu * upward).astype(BF)
    grad_gate = (grad_hidden * upward * sigmoid * (1.0 + gate_pre * (1.0 - sigmoid))).astype(BF)
    grad_up = (grad_hidden * silu).astype(BF)
    grad_both = jnp.concatenate([grad_gate, grad_up], axis=1)

    down_part = mm_first(hidden, cot_all).astype(BF)
    down_sum = lax.psum_scatter(down_part, "chip", scatter_dimension=0, tiled=True)
    out_other = mm(after(hidden[seq:], down_part), down_own).astype(BF)
    other = mm_last(after(grad_both[seq:], out_other), pair).astype(BF)
    out_terms = mm(after(hidden[:seq], other), down_own) + swap_cores(out_other).astype(F32)
    out_terms = out_terms.reshape(count, tok, width)
    pair_part = mm_first(normed_two, after(grad_both, out_terms)).astype(BF)
    pair_sum = lax.psum_scatter(pair_part, "chip", scatter_dimension=0, tiled=True)
    own = after(grad_both[:seq], pair_part)
    two_terms = mm_last(own, pair) + swap_cores(other).astype(F32)
    two_terms = two_terms.reshape(count, tok, width)
    sides = line_scatter(out_terms, lambda t, _: pair_part if t == 1 else two_terms)
    output = (
        hidden_one + out_terms[0] + sides[0].astype(F32) + sides[1].astype(F32)
    ).astype(BF)
    sides = line_scatter(two_terms)
    grad_hidden_one, grad_low, gain_two_sum = backward_norm(
        two_terms, *sides, hidden_one, cotangent, gain_two, chips, count
    )
    grad_attn = line_pieces(grad_low, line_steps(grad_low))

    grad_att = mm_last(grad_attn, out_weight).astype(BF)
    out_term = mm_first(attended, grad_attn).astype(BF)
    grad_att = after(grad_att, out_term)
    down_all = lax.all_gather(after(down_sum, grad_att), PLANE, axis=0)
    pair_sum = after(pair_sum, grad_att)
    rings = [
        exchange_line(
            lambda j, w=w: lax.dynamic_slice(pair_sum, (j * part, w * ff_own), (part, ff_own))
        )
        for w in range(2)
    ]
    grad_proj, query_sum, key_sum = attention_call(
        *core_args, more=(attended, inverse_sums, grad_att)
    )
    query_gain_sum = query_sum[0, :hd] + query_sum[0, hd:]
    key_gain_sum = key_sum[0, :hd] + (key_sum[0, hd:] if kv_heads == 2 else 0.0)
    proj_part = mm_first(normed_one, grad_proj).astype(BF)
    one_part = mm_last(after(grad_proj, proj_part), proj).reshape(count, tok, width)
    bits = chips.bit_length() - 1
    cols = q_cols + 2 * kv_cols
    att_terms = [proj_part.reshape(count, chips, 2, share, cols), out_term.reshape(chips, 2, share, -1)]

    def att_cores(pin):
        out = [halve(x, 2 - g, "core", 0, pin) for g, x in enumerate(att_terms)]
        return [
            out[0].reshape([count] + [2] * bits + [share, cols]),
            out[1].reshape([2] * bits + [share, width]),
        ]

    att_sum = att_cores(one_part)
    ffn_sum = jnp.concatenate([absolute(after(ring, att_sum)) for ring in rings], axis=2)
    ffn_all = lax.all_gather(ffn_sum.reshape(count * part, 2 * ff_own), PLANE, axis=0)

    def att_stages(t, sides):
        if t > 2:
            return ()
        stage["att"] = chip_stage(stage.get("att", att_sum), t - 1, sides, (1, 0))
        return (stage["att"], down_grad) if t == 2 else stage["att"]

    down_grad = place_down(down_all, chips, ff_own // chips, width)
    sides = line_scatter(after(one_part, ffn_sum), att_stages)
    _, input_grad, gain_one_sum = backward_norm(
        one_part, *sides, inputs, grad_hidden_one, gain_one, 0, count
    )

    sums = jnp.concatenate(
        [
            v.reshape(count, -1)
            for v in (gain_one_sum, gain_two_sum, query_gain_sum, key_gain_sum)
        ],
        axis=1,
    )

    att_sum = chip_rest(stage["att"], 2, sides, (1, 0))
    ring = exchange_line(lambda j: lax.dynamic_index_in_dim(att_sum[0], j, keepdims=False))
    cuts = ((0, q_cols), (q_cols, q_cols + kv_cols), (q_cols + kv_cols, cols))
    got = absolute(after(ring, input_grad))
    columns = [[got[j, :, a:b] for j in range(count)] for a, b in cuts]
    att_all = [
        jnp.concatenate(columns[0] + columns[1], axis=1),
        jnp.concatenate(columns[2] + [att_sum[1]], axis=1),
    ]
    sums = small_line(sums, att_all)
    for step in range(bits):
        att_all = gather_stage(att_all, step, sums)
        if step == 0:
            sums = sums + after(swap_cores(sums), att_all)
    sums = small_chips(sums, att_all)
    gate_grad, up_grad = (place_pair(ffn_all, w, chips, count, part, ff_own) for w in range(2))
    others = after([swap_cores(a) for a in att_all], gate_grad, up_grad)
    query_grad, key_grad = place_columns(
        gathered_order(0), att_all[0], others[0], (q_cols * count, kv_cols * count)
    )
    value_grad, out_grad = place_columns(
        gathered_order(1), att_all[1], others[1], (kv_cols * count, width)
    )
    return (
        output,
        input_grad,
        sums[:rows],
        query_grad,
        key_grad,
        value_grad,
        sums[2 * rows : 2 * rows + small],
        sums[2 * rows + small :],
        out_grad,
        sums[rows : 2 * rows],
        gate_grad,
        up_grad,
        down_grad,
    )


def solution(mesh):
    chips, count = mesh.shape["rep"] // 2, mesh.shape["fsdp"]
    split = Mesh(mesh.devices.reshape(chips, 2, count), ("chip", "core", "fsdp"))
    tokens, reps, fsdp = (*PLANE, "fsdp"), PLANE, "fsdp"
    in_specs = (
        P(tokens, None),
        P(reps, None),
        P(fsdp),
        P(fsdp, None),
        P(fsdp, None),
        P(fsdp, None),
        P(fsdp),
        P(fsdp),
        P(fsdp, None),
        P(fsdp),
        P(fsdp, None),
        P(fsdp, None),
        P(fsdp, None),
        P(tokens, None),
    )
    out_specs = (
        P(tokens, None),
        P(tokens, None),
        P(fsdp),
        P(fsdp, None),
        P(fsdp, None),
        P(fsdp, None),
        P(fsdp),
        P(fsdp),
        P(fsdp, None),
        P(fsdp),
        P(fsdp, None),
        P(fsdp, None),
        P(fsdp, None),
    )
    return jax.shard_map(
        shards, mesh=split, in_specs=in_specs, out_specs=out_specs, check_vma=False
    )
```

time: 780 us -> 738 us (0.946)
  Pallas kernels: 42.8 us -> 82.8 us
  matrix products: 124 us -> 92.1 us
  local copies, waits for them, and re-layouts: 86.9 us -> 56.2 us
  waiting for transfers between devices: 235 us -> 213 us
  starting transfers between devices: 184 us -> 199 us
  other arithmetic: 78.3 us -> 65.2 us
    ppermute x23 -> x6, waiting for transfers between devices: 66.8 us -> 4.07 us  [halve(): lax.ppermute(lax.dynamic_index_in_dim(blocks, 1 - mybit, axis, keepdims=F...]
    ppermute x15 -> x18, waiting for transfers between devices: 25.7 us -> 66.3 us  [exchange_line(): lax.ppermute(piece_for((mine - e) % count), 'fsdp', [(i, (i - e) % count)...]
    pallas_call x0 -> x4, Pallas kernels: none -> 38 us  [the longest x1 15.8 us: attention_call(): pl.pallas_call(functools.partial(attend_back_kernel, kv, each, scale), gr...]
    slice x21 -> x1, local copies, waits for them, and re-layouts: 20.6 us -> 1.71 us  [shards(): hidden[:seq]]
    sub x2 -> x0, matrix products: 18 us -> none  [the longest x1 10.4 us: shards(): grad_scores = (probs * (grad_probs - delta)).astype(BF)]
    ppermute x24, starting transfers between devices: 71 us -> 88.9 us  [line_step(): lax.ppermute(first, 'fsdp', even)]
    dot_general x4 -> x0, matrix products: 17.3 us -> none  [the longest x1 5.59 us: shards(): jnp.einsum('ngts,tngd->snd', probs_low, grad_att, preferred_element_type=...]
    ppermute x23 -> x6, starting transfers between devices: 24.1 us -> 8.47 us  [halve(): lax.ppermute(lax.dynamic_index_in_dim(blocks, 1 - mybit, axis, keepdims=F...]
  transfers between devices with their start and end apart: 101 -> 95, of which waited for: 46 -> 24; matrix products, arithmetic and copies ran while one was open for 28% -> 22% of each run, Pallas kernels for 6% -> 9%
where the time goes in v4:
time: 738 us; the launch traced here: 725 us
  waiting for transfers between devices  213 us (29%)
  starting transfers between devices  199 us (27%)
  matrix products  92.1 us (12%)
  Pallas kernels  82.8 us (11%)
  other arithmetic  65.2 us (9%)
  local copies, waits for them, and re-layouts  56.2 us (8%)
  between operations  15.8 us (2%)
    ppermute x24, waiting for transfers between devices, line_step(): lax.ppermute(first, 'fsdp', even)  122 us
    ppermute x24, starting transfers between devices, line_step(): lax.ppermute(first, 'fsdp', even)  88.9 us
    ppermute x18, waiting for transfers between devices, exchange_line(): lax.ppermute(piece_for((mine - e) % count), 'fsdp', [(i, (i - e) % count)...  66.3 us
    ppermute x24, starting transfers between devices, line_step(): lax.ppermute(second, 'fsdp', odd)  58.6 us
    dot_general x5, matrix products, mm_last(): lax.dot_general(a, b, (((1,), (1,)), ((), ())), preferred_element_type=F32)  39.6 us
    ppermute x18, starting transfers between devices, exchange_line(): lax.ppermute(piece_for((mine - e) % count), 'fsdp', [(i, (i - e) % count)...  28.7 us
    dot_general x5, matrix products, mm(): return jnp.dot(a, b, preferred_element_type=F32)  28 us
    dot_general x4, matrix products, mm_first(): lax.dot_general(a, b, (((0,), (0,)), ((), ())), preferred_element_type=F32)  24.5 us
  transfers between devices with their start and end apart: 95, of which 24 were waited for; matrix products, arithmetic and copies ran while one was open for 22% of the time, Pallas kernels for 9%

profile of v4, /device:TPU:0, one launch (start us, length us, event | category | flops | bytes accessed | tf_op | source)
XLA Modules:
  0.0 724.5 jit_solution(14373822609746825225)
XLA Ops:
  10.3 5.4 collective-permute-start
  21.0 13.1 %collective-permute-done.5 = bf16[64,768]{1,0:T(8,128)(2,1)S(1)} collective-permute-done((bf16[64,768]{1,0:T(8,128)(2,1)S(1)}, bf16[64,768]{1,0:T(8,128)(2,1)S(1)}, u32[]{:S(2)}, u32[]{:S(2)}) %collective-permute-start.5) | collective-permute-done | bytes 98336 | tf_op jit(solution)/shard_map/ppermute | solution.py:110
  49.8 9.0 %collective-permute-done.3 = bf16[128,2048]{1,0:T(8,128)(2,1)} collective-permute-done((bf16[128,2048]{1,0:T(8,128)(2,1)}, bf16[128,2048]{1,0:T(8,128)(2,1)}, u32[]{:S(2)}, u32[]{:S(2)}) %collective-permute-start.3) | collective-permute-done | bytes 524320 | tf_op jit(solution)/shard_map/ppermute | solution.py:45
  64.1 5.4 collective-permute-done.7
  88.4 7.8 %shard_map.237 = (bf16[512,512]{1,0:T(8,128)(2,1)S(1)}, f32[512,512]{1,0:T(8,128)S(1)}) custom-call(f32[512,768]{1,0:T(8,128)S(1)} %fusion.41.pre.keys.vals, f32[512,768]{1,0:T(8,128)S(1)} %fusion.41.pre.keys.vals, f32[512,768]{1,0:T(8,128)S(1)} %fusion.41.pre.keys.vals, f32[512,512]{1,0:T(8,128)S(1)} %and_select_fusion.bias, f32[512,128]{1,0:T(8,128)S(1)} %copy-done.3, ...), custom_call_target="tpu_custom_call" | custom-call | tf_op jit(solution)/shard_map/pallas_call | solution.py:365
  100.6 25.0 %collective-permute-done.15 = bf16[128,2048]{1,0:T(8,128)(2,1)} collective-permute-done((bf16[128,2048]{1,0:T(8,128)(2,1)}, bf16[128,2048]{1,0:T(8,128)(2,1)}, u32[]{:S(2)}, u32[]{:S(2)}) %collective-permute-start.15) | collective-permute-done | bytes 524320 | tf_op jit(solution)/shard_map/ppermute | solution.py:110
  136.6 5.4 collective-permute-start.18
  141.9 3.8 collective-permute-start.17
  145.7 12.1 %collective-permute-done.17 = bf16[128,2048]{1,0:T(8,128)(2,1)} collective-permute-done((bf16[128,2048]{1,0:T(8,128)(2,1)}, bf16[128,2048]{1,0:T(8,128)(2,1)}, u32[]{:S(2)}, u32[]{:S(2)}) %collective-permute-start.17) | collective-permute-done | bytes 524320 | tf_op jit(solution)/shard_map/ppermute | solution.py:45
  160.7 3.3 collective-permute-start.19
  164.0 10.9 %collective-permute-done.19.right = bf16[128,2048]{1,0:T(8,128)(2,1)S(1)} collective-permute-done((bf16[128,2048]{1,0:T(8,128)(2,1)S(1)}, bf16[128,2048]{1,0:T(8,128)(2,1)S(1)}, u32[]{:S(2)}, u32[]{:S(2)}) %collective-permute-start.19) | collective-permute-done | bytes 524320 | tf_op jit(solution)/shard_map/ppermute | solution.py:45
  174.9 5.4 collective-permute-start.22
  180.9 3.8 shard_map.238
  184.8 7.9 %collective-permute-done.21 = bf16[128,2048]{1,0:T(8,128)(2,1)} collective-permute-done((bf16[128,2048]{1,0:T(8,128)(2,1)}, bf16[128,2048]{1,0:T(8,128)(2,1)}, u32[]{:S(2)}, u32[]{:S(2)}) %collective-permute-start.21) | collective-permute-done | bytes 524320 | tf_op jit(solution)/shard_map/ppermute | solution.py:45
  194.7 9.4 %collective-permute-done.24 = bf16[128,2048]{1,0:T(8,128)(2,1)S(1)} collective-permute-done((bf16[128,2048]{1,0:T(8,128)(2,1)}, bf16[128,2048]{1,0:T(8,128)(2,1)S(1)}, u32[]{:S(2)}, u32[]{:S(2)}) %collective-permute-start.24) | collective-permute-done | bytes 524320 | tf_op jit(solution)/shard_map/ppermute | solution.py:45
  204.7 4.7 collective-permute-start.27
  209.4 9.5 %collective-permute-start.26 = (bf16[128,2048]{1,0:T(8,128)(2,1)S(1)}, bf16[128,2048]{1,0:T(8,128)(2,1)S(1)}, u32[]{:S(2)}, u32[]{:S(2)}) collective-permute-start(bf16[128,2048]{1,0:T(8,128)(2,1)S(1)} %collective-permute-done.25), channel_id=1, source_target_pairs={{0,1},{1,0},{2,3},{3,2},{4,5},{5,4},{6,7},{7,6},{8,9},{9,8},{10,11... | collective-permute-start | bytes 1572872 | tf_op jit(solution)/shard_map/ppermute | solution.py:45
  221.6 7.1 collective-permute-done.26
  232.6 5.4 collective-permute-start.30
  240.8 14.5 %fusion.79 = f32[1024,2048]{1,0:T(8,128)} fusion(bf16[1024,2048]{1,0:T(8,128)(2,1)} %constant_dynamic-update-slice_fusion, bf16[2048,2048]{1,0:T(8,128)(2,1)} %bitcast.295), kind=kOutput, calls=%fused_computation.252 | convolution fusion | flops 8589934592 | bytes 20971520 | tf_op jit(solution)/shard_map/dot_general | solution.py:21
  259.2 10.1 %collective-permute-done.32 = bf16[128,2048]{1,0:T(8,128)(2,1)S(1)} collective-permute-done((bf16[128,2048]{1,0:T(8,128)(2,1)}, bf16[128,2048]{1,0:T(8,128)(2,1)S(1)}, u32[]{:S(2)}, u32[]{:S(2)}) %collective-permute-start.32) | collective-permute-done | bytes 524320 | tf_op jit(solution)/shard_map/ppermute | solution.py:45
  278.1 4.5 collective-permute-done.34
  282.6 3.2 constant_dynamic-update-slice_fusion.5
  285.8 14.1 %multiply_convert_fusion = (bf16[1024,1024]{1,0:T(8,128)(2,1)}, bf16[1024,1024]{1,0:T(8,128)(2,1)}, bf16[1024,1024]{1,0:T(8,128)(2,1)S(1)}) fusion(f32[1024,2048]{1,0:T(8,128)} %fusion.79, bf16[1024,2048]{1,0:T(8,128)(2,1)} %constant_dynamic-update-slice_fusion.5, bf16[2048,2048]{1,0:T(8,128)(2,1)} %param.26, s32[]{:T(128)S(6)} %select_n.652), kind=kOutput, calls=%fused_computation.13 | convolution fusion | flops 4310695936 | bytes 23068676 | tf_op jit(solution)/shard_map/dot_general | solution.py:25
  301.2 6.2 convolution_convert_fusion.1
  309.4 6.0 fusion.13
  317.1 9.6 %convolution_convert_fusion.4 = bf16[512,2048]{1,0:T(8,128)(2,1)} fusion(bf16[512,2048]{1,0:T(8,128)(2,1)S(1)} %get-tuple-element.130, bf16[2048,2048]{1,0:T(8,128)(2,1)} %bitcast.296), kind=kOutput, calls=%fused_computation.30 | convolution fusion | flops 4296015872 | bytes 12582912 | tf_op jit(solution)/shard_map/dot_general | solution.py:25
  327.2 4.4 convert_add_fusion.1
  331.6 13.4 %convolution_convert_fusion = bf16[2048,2048]{1,0:T(8,128)(2,1)} fusion(bf16[1024,2048]{1,0:T(8,128)(2,1)} %constant_dynamic-update-slice_fusion, bf16[1024,2048]{1,0:T(8,128)(2,1)S(1)} %pad_maximum_fusion), kind=kOutput, calls=%fused_computation | convolution fusion | flops 8594128896 | bytes 16777216 | tf_op jit(solution)/shard_map/dot_general | solution.py:29
  346.0 4.0 collective-permute-done.40
  350.0 7.6 %convert_add_fusion = f32[512,2048]{1,0:T(8,128)S(1)} fusion(bf16[512,2048]{1,0:T(8,128)(2,1)S(1)} %collective-permute-done.40, bf16[512,2048]{1,0:T(8,128)(2,1)} %get-tuple-element.135, bf16[2048,2048]{1,0:T(8,128)(2,1)} %bitcast.297), kind=kOutput, calls=%fused_computation.11 | convolution fusion | flops 4297064448 | bytes 16777216 | tf_op jit(solution)/shard_map/dot_general | solution.py:25
  358.5 6.1 collective-permute-start.43
  364.6 12.2 %collective-permute-done.43 = bf16[128,2048]{1,0:T(8,128)(2,1)S(1)} collective-permute-done((bf16[128,2048]{1,0:T(8,128)(2,1)S(1)}, bf16[128,2048]{1,0:T(8,128)(2,1)S(1)}, u32[]{:S(2)}, u32[]{:S(2)}) %collective-permute-start.43) | collective-permute-done | bytes 524320 | tf_op jit(solution)/shard_map/ppermute | solution.py:45
  379.5 11.0 %collective-permute-done.47 = bf16[128,2048]{1,0:T(8,128)(2,1)S(1)} collective-permute-done((bf16[128,2048]{1,0:T(8,128)(2,1)S(1)}, bf16[128,2048]{1,0:T(8,128)(2,1)S(1)}, u32[]{:S(2)}, u32[]{:S(2)}) %collective-permute-start.47) | collective-permute-done | bytes 524320 | tf_op jit(solution)/shard_map/ppermute | solution.py:45
  391.6 6.0 collective-permute-start.45
  397.6 10.3 %collective-permute-done.45.right = bf16[128,2048]{1,0:T(8,128)(2,1)S(1)} collective-permute-done((bf16[128,2048]{1,0:T(8,128)(2,1)S(1)}, bf16[128,2048]{1,0:T(8,128)(2,1)S(1)}, u32[]{:S(2)}, u32[]{:S(2)}) %collective-permute-start.45) | collective-permute-done | bytes 524320 | tf_op jit(solution)/shard_map/ppermute | solution.py:45
  408.7 4.8 shard_map.239
  417.0 8.2 %collective-permute-done.50 = bf16[128,2048]{1,0:T(8,128)(2,1)S(1)} collective-permute-done((bf16[128,2048]{1,0:T(8,128)(2,1)}, bf16[128,2048]{1,0:T(8,128)(2,1)S(1)}, u32[]{:S(2)}, u32[]{:S(2)}) %collective-permute-start.50) | collective-permute-done | bytes 524320 | tf_op jit(solution)/shard_map/ppermute | solution.py:45
  425.9 4.1 collective-permute-start.53
  430.0 10.2 %collective-permute-start.52 = (bf16[128,2048]{1,0:T(8,128)(2,1)S(1)}, bf16[128,2048]{1,0:T(8,128)(2,1)S(1)}, u32[]{:S(2)}, u32[]{:S(2)}) collective-permute-start(bf16[128,2048]{1,0:T(8,128)(2,1)S(1)} %collective-permute-done.51), channel_id=1, source_target_pairs={{0,1},{1,0},{2,3},{3,2},{4,5},{5,4},{6,7},{7,6},{8,9},{9,8},{10,11... | collective-permute-start | bytes 1572872 | tf_op jit(solution)/shard_map/ppermute | solution.py:45
  441.0 8.8 %collective-permute-done.52 = bf16[128,2048]{1,0:T(8,128)(2,1)S(1)} collective-permute-done((bf16[128,2048]{1,0:T(8,128)(2,1)S(1)}, bf16[128,2048]{1,0:T(8,128)(2,1)S(1)}, u32[]{:S(2)}, u32[]{:S(2)}) %collective-permute-start.52) | collective-permute-done | bytes 524320 | tf_op jit(solution)/shard_map/ppermute | solution.py:45
  460.6 15.8 %shard_map.240 = (bf16[512,768]{1,0:T(8,128)(2,1)S(1)}, f32[1,128]{1,0:T(1,128)S(1)}, f32[1,128]{1,0:T(1,128)S(1)}) custom-call(f32[512,768]{1,0:T(8,128)S(1)} %copy-done.2, f32[512,768]{1,0:T(8,128)S(1)} %copy-done.2, f32[512,768]{1,0:T(8,128)S(1)} %copy-done.2, f32[512,512]{1,0:T(8,128)S(1)} %and_select_fusion.bias, f32[512,128]{1,0:T(8,128)S(1)} %copy-done.4, ...), custom_call_target="tpu_custom_call" | custom-call | tf_op jit(solution)/shard_map/pallas_call | solution.py:378
  482.4 6.1 fusion.80.part
  490.3 4.0 collective-permute-start.62
  496.9 3.2 collective-permute-start.60
  506.1 12.6 %collective-permute-done.61 = bf16[128,1024]{1,0:T(8,128)(2,1)S(1)} collective-permute-done((bf16[128,1024]{1,0:T(8,128)(2,1)S(1)}, bf16[128,1024]{1,0:T(8,128)(2,1)S(1)}, u32[]{:S(2)}, u32[]{:S(2)}) %collective-permute-start.61) | collective-permute-done | bytes 262176 | tf_op jit(solution)/shard_map/ppermute | solution.py:110
  518.7 15.5 %collective-permute-done.56 = bf16[128,1024]{1,0:T(8,128)(2,1)S(1)} collective-permute-done((bf16[128,1024]{1,0:T(8,128)(2,1)S(1)}, bf16[128,1024]{1,0:T(8,128)(2,1)S(1)}, u32[]{:S(2)}, u32[]{:S(2)}) %collective-permute-start.56) | collective-permute-done | bytes 262176 | tf_op jit(solution)/shard_map/ppermute | solution.py:110
  545.7 5.4 collective-permute-start.64
  558.2 8.6 %collective-permute-start.36 = (bf16[128,2048]{1,0:T(8,128)(2,1)}, bf16[128,2048]{1,0:T(8,128)(2,1)}, u32[]{:S(2)}, u32[]{:S(2)}) collective-permute-start(bf16[128,2048]{1,0:T(8,128)(2,1)} %get-tuple-element.237), channel_id=1, source_target_pairs={{0,1},{1,0},{2,3},{3,2},{4,5},{5,4},{6,7},{7,6},{8,9},{9,8},{10,11... | collective-permute-start | bytes 1572872 | tf_op jit(solution)/shard_map/ppermute | solution.py:45
  574.5 7.6 %collective-permute-start.67 = (bf16[128,2048]{1,0:T(8,128)(2,1)}, bf16[128,2048]{1,0:T(8,128)(2,1)}, u32[]{:S(2)}, u32[]{:S(2)}) collective-permute-start(bf16[128,2048]{1,0:T(8,128)(2,1)} %get-tuple-element.221), channel_id=1, source_target_pairs={{0,1},{1,0},{2,3},{3,2},{4,5},{5,4},{6,7},{7,6},{8,9},{9,8},{10,11... | collective-permute-start | bytes 1572872 | tf_op jit(solution)/shard_map/ppermute | solution.py:45
  587.4 4.1 collective-permute-done.70
  593.7 10.9 %shard_map.241 = f32[2048,2048]{1,0:T(8,128)} custom-call(bf16[8,256,2048]{2,1,0:T(8,128)(2,1)} %bitcast.272), custom_call_target="tpu_custom_call" | custom-call | tf_op jit(solution)/shard_map/pallas_call | solution.py:571
  609.3 3.5 collective-permute-start.71
  621.5 5.6 collective-permute-start.39
  627.1 5.0 collective-permute-start.38
  632.1 4.5 shard_map.242
  646.6 3.1 collective-permute-done.74
  653.7 3.1 fusion.35
  656.8 5.4 collective-permute-start.42
  662.2 6.8 collective-permute-done.86
  682.3 10.4 %shard_map.244 = f32[512,8192]{1,0:T(8,128)} custom-call(bf16[4,2,4,128,2048]{4,3,2,1,0:T(8,128)(2,1)} %bitcast.264), custom_call_target="tpu_custom_call" | custom-call | tf_op jit(solution)/shard_map/pallas_call | solution.py:503
  692.7 10.4 %shard_map.243 = f32[512,8192]{1,0:T(8,128)} custom-call(bf16[4,2,4,128,2048]{4,3,2,1,0:T(8,128)(2,1)} %bitcast.265), custom_call_target="tpu_custom_call" | custom-call | tf_op jit(solution)/shard_map/pallas_call | solution.py:503
  703.1 7.2 shard_map.245
  710.3 7.2 shard_map.246
  (423 shorter events, 209.2 us)
Async XLA Ops:
  7.2 76.9 %all-gather.10.cloned.1.call-start = ((), (), s32[]{:S(2)}) async-start(), calls=%async_computation.5 | async-start | bytes 3538944 | tf_op jit(solution)/shard_map/all_gather | solution.py:632
  7.2 26.8 %collective-permute-start.1 = (bf16[128,2048]{1,0:T(8,128)(2,1)}, bf16[128,2048]{1,0:T(8,128)(2,1)S(1)}, u32[]{:S(2)}, u32[]{:S(2)}) collective-permute-start(bf16[128,2048]{1,0:T(8,128)(2,1)} %wide.1), channel_id=1, source_target_pairs={{0,1},{1,0},{2,3},{3,2},{4,5},{5,4},{6,7},{7,6},{8,9},{9,8},{10,11... | collective-permute-start | bytes 1572872 | tf_op jit(solution)/shard_map/ppermute | solution.py:45
  10.3 23.7 %collective-permute-start = (bf16[128,2048]{1,0:T(8,128)(2,1)}, bf16[128,2048]{1,0:T(8,128)(2,1)}, u32[]{:S(2)}, u32[]{:S(2)}) collective-permute-start(bf16[128,2048]{1,0:T(8,128)(2,1)} %wide.1), channel_id=1, source_target_pairs={{0,0},{1,2},{2,1},{3,3},{4,4},{5,6},{6,5},{7,7},{8,8},{9,10},{10,9... | collective-permute-start | bytes 1572872 | tf_op jit(solution)/shard_map/ppermute | solution.py:45
  17.6 16.5 %collective-permute-start.5 = (bf16[64,768]{1,0:T(8,128)(2,1)S(1)}, bf16[64,768]{1,0:T(8,128)(2,1)S(1)}, u32[]{:S(2)}, u32[]{:S(2)}) collective-permute-start(bf16[64,768]{1,0:T(8,128)(2,1)S(1)} %pad_maximum_fusion.19), channel_id=1, source_target_pairs={{0,2},{1,3},{2,0},{3,1},{4,6},{5,7},{6,4},{7,5},{8,10},{9,11},{10,... | collective-permute-start | bytes 294920 | tf_op jit(solution)/shard_map/ppermute | solution.py:110
  17.7 16.4 %collective-permute-start.4 = (bf16[64,768]{1,0:T(8,128)(2,1)S(1)}, bf16[64,768]{1,0:T(8,128)(2,1)S(1)}, u32[]{:S(2)}, u32[]{:S(2)}) collective-permute-start(bf16[64,768]{1,0:T(8,128)(2,1)S(1)} %pad_maximum_fusion.18), channel_id=1, source_target_pairs={{0,3},{1,0},{2,1},{3,2},{4,7},{5,4},{6,5},{7,6},{8,11},{9,8},{10,9... | collective-permute-start | bytes 294920 | tf_op jit(solution)/shard_map/ppermute | solution.py:110
  20.3 13.7 %collective-permute-start.6 = (bf16[64,768]{1,0:T(8,128)(2,1)S(1)}, bf16[64,768]{1,0:T(8,128)(2,1)S(1)}, u32[]{:S(2)}, u32[]{:S(2)}) collective-permute-start(bf16[64,768]{1,0:T(8,128)(2,1)S(1)} %pad_maximum_fusion.20), channel_id=1, source_target_pairs={{0,1},{1,2},{2,3},{3,0},{4,5},{5,6},{6,7},{7,4},{8,9},{9,10},{10,1... | collective-permute-start | bytes 294920 | tf_op jit(solution)/shard_map/ppermute | solution.py:110
  35.0 205.8 %all-gather.12.cloned.1.call-start = ((), (), s32[]{:S(2)}) async-start(), calls=%async_computation.6 | async-start | bytes 10485760 | tf_op jit(solution)/shard_map/all_gather | solution.py:684
  46.7 12.1 %collective-permute-start.3 = (bf16[128,2048]{1,0:T(8,128)(2,1)}, bf16[128,2048]{1,0:T(8,128)(2,1)}, u32[]{:S(2)}, u32[]{:S(2)}) collective-permute-start(bf16[128,2048]{1,0:T(8,128)(2,1)} %collective-permute-done), channel_id=1, source_target_pairs={{0,1},{1,0},{2,3},{3,2},{4,5},{5,4},{6,7},{7,6},{8,9},{9,8},{10,11... | collective-permute-start | bytes 1572872 | tf_op jit(solution)/shard_map/ppermute | solution.py:45
  74.4 26.2 %collective-permute-start.14 = (bf16[128,2048]{1,0:T(8,128)(2,1)}, bf16[128,2048]{1,0:T(8,128)(2,1)}, u32[]{:S(2)}, u32[]{:S(2)}) collective-permute-start(bf16[128,2048]{1,0:T(8,128)(2,1)} %pad_maximum_fusion.11), channel_id=1, source_target_pairs={{0,3},{1,0},{2,1},{3,2},{4,7},{5,4},{6,5},{7,6},{8,11},{9,8},{10,9... | collective-permute-start | bytes 1572872 | tf_op jit(solution)/shard_map/ppermute | solution.py:110
  77.6 48.1 %collective-permute-start.15 = (bf16[128,2048]{1,0:T(8,128)(2,1)}, bf16[128,2048]{1,0:T(8,128)(2,1)}, u32[]{:S(2)}, u32[]{:S(2)}) collective-permute-start(bf16[128,2048]{1,0:T(8,128)(2,1)} %pad_maximum_fusion.12), channel_id=1, source_target_pairs={{0,2},{1,3},{2,0},{3,1},{4,6},{5,7},{6,4},{7,5},{8,10},{9,11},{10,... | collective-permute-start | bytes 1572872 | tf_op jit(solution)/shard_map/ppermute | solution.py:110
  80.7 45.0 %collective-permute-start.16 = (bf16[128,2048]{1,0:T(8,128)(2,1)}, bf16[128,2048]{1,0:T(8,128)(2,1)}, u32[]{:S(2)}, u32[]{:S(2)}) collective-permute-start(bf16[128,2048]{1,0:T(8,128)(2,1)} %pad_maximum_fusion.13), channel_id=1, source_target_pairs={{0,1},{1,2},{2,3},{3,0},{4,5},{5,6},{6,7},{7,4},{8,9},{9,10},{10,1... | collective-permute-start | bytes 1572872 | tf_op jit(solution)/shard_map/ppermute | solution.py:110
  97.8 27.9 %collective-permute-start.13 = (bf16[128,2048]{1,0:T(8,128)(2,1)S(1)}, bf16[128,2048]{1,0:T(8,128)(2,1)}, u32[]{:S(2)}, u32[]{:S(2)}) collective-permute-start(bf16[128,2048]{1,0:T(8,128)(2,1)S(1)} %get-tuple-element.242), channel_id=1, source_target_pairs={{0,0},{1,2},{2,1},{3,3},{4,4},{5,6},{6,5},{7,7},{8,8},{9,10},{10,9... | collective-permute-start | bytes 1572872 | tf_op jit(solution)/shard_map/ppermute | solution.py:45
  99.8 25.9 %collective-permute-start.12 = (bf16[128,2048]{1,0:T(8,128)(2,1)S(1)}, bf16[128,2048]{1,0:T(8,128)(2,1)}, u32[]{:S(2)}, u32[]{:S(2)}) collective-permute-start(bf16[128,2048]{1,0:T(8,128)(2,1)S(1)} %get-tuple-element.243), channel_id=1, source_target_pairs={{0,1},{1,0},{2,3},{3,2},{4,5},{5,4},{6,7},{7,6},{8,9},{9,8},{10,11... | collective-permute-start | bytes 1572872 | tf_op jit(solution)/shard_map/ppermute | solution.py:45
  133.8 320.9 %reduce-scatter.5.cloned.1.call-start = ((), (), s32[]{:S(2)}) async-start(), calls=%async_computation.3 | async-start | bytes 5242880 | tf_op jit(solution)/shard_map/reduce_scatter | solution.py:707
  141.9 15.9 %collective-permute-start.17 = (bf16[128,2048]{1,0:T(8,128)(2,1)}, bf16[128,2048]{1,0:T(8,128)(2,1)}, u32[]{:S(2)}, u32[]{:S(2)}) collective-permute-start(bf16[128,2048]{1,0:T(8,128)(2,1)} %get-tuple-element.241), channel_id=1, source_target_pairs={{0,1},{1,0},{2,3},{3,2},{4,5},{5,4},{6,7},{7,6},{8,9},{9,8},{10,11... | collective-permute-start | bytes 1572872 | tf_op jit(solution)/shard_map/ppermute | solution.py:45
  160.7 14.2 %collective-permute-start.19 = (bf16[128,2048]{1,0:T(8,128)(2,1)S(1)}, bf16[128,2048]{1,0:T(8,128)(2,1)S(1)}, u32[]{:S(2)}, u32[]{:S(2)}) collective-permute-start(bf16[128,2048]{1,0:T(8,128)(2,1)S(1)} %get-tuple-element.239), channel_id=1, source_target_pairs={{0,1},{1,0},{2,3},{3,2},{4,5},{5,4},{6,7},{7,6},{8,9},{9,8},{10,11... | collective-permute-start | bytes 1572872 | tf_op jit(solution)/shard_map/ppermute | solution.py:45
  180.3 12.4 %collective-permute-start.21 = (bf16[128,2048]{1,0:T(8,128)(2,1)}, bf16[128,2048]{1,0:T(8,128)(2,1)}, u32[]{:S(2)}, u32[]{:S(2)}) collective-permute-start(bf16[128,2048]{1,0:T(8,128)(2,1)} %base.1), channel_id=1, source_target_pairs={{0,1},{1,0},{2,3},{3,2},{4,5},{5,4},{6,7},{7,6},{8,9},{9,8},{10,11... | collective-permute-start | bytes 1572872 | tf_op jit(solution)/shard_map/ppermute | solution.py:45
  193.0 11.7 %collective-permute-start.23 = (bf16[128,2048]{1,0:T(8,128)(2,1)}, bf16[128,2048]{1,0:T(8,128)(2,1)S(1)}, u32[]{:S(2)}, u32[]{:S(2)}) collective-permute-start(bf16[128,2048]{1,0:T(8,128)(2,1)} %get-tuple-element.124), channel_id=1, source_target_pairs={{0,0},{1,2},{2,1},{3,3},{4,4},{5,6},{6,5},{7,7},{8,8},{9,10},{10,9... | collective-permute-start | bytes 1572872 | tf_op jit(solution)/shard_map/ppermute | solution.py:45
  204.7 14.2 %collective-permute-start.27 = (bf16[128,2048]{1,0:T(8,128)(2,1)S(1)}, bf16[128,2048]{1,0:T(8,128)(2,1)S(1)}, u32[]{:S(2)}, u32[]{:S(2)}) collective-permute-start(bf16[128,2048]{1,0:T(8,128)(2,1)S(1)} %collective-permute-done.23), channel_id=1, source_target_pairs={{0,1},{1,0},{2,3},{3,2},{4,5},{5,4},{6,7},{7,6},{8,9},{9,8},{10,11... | collective-permute-start | bytes 1572872 | tf_op jit(solution)/shard_map/ppermute | solution.py:45
  209.4 19.3 %collective-permute-start.26 = (bf16[128,2048]{1,0:T(8,128)(2,1)S(1)}, bf16[128,2048]{1,0:T(8,128)(2,1)S(1)}, u32[]{:S(2)}, u32[]{:S(2)}) collective-permute-start(bf16[128,2048]{1,0:T(8,128)(2,1)S(1)} %collective-permute-done.25), channel_id=1, source_target_pairs={{0,1},{1,0},{2,3},{3,2},{4,5},{5,4},{6,7},{7,6},{8,9},{9,8},{10,11... | collective-permute-start | bytes 1572872 | tf_op jit(solution)/shard_map/ppermute | solution.py:45
  232.6 22.6 %collective-permute-start.30 = (bf16[128,2048]{1,0:T(8,128)(2,1)}, bf16[128,2048]{1,0:T(8,128)(2,1)}, u32[]{:S(2)}, u32[]{:S(2)}) collective-permute-start(bf16[128,2048]{1,0:T(8,128)(2,1)} %collective-permute-done.21), channel_id=1, source_target_pairs={{0,0},{1,2},{2,1},{3,3},{4,4},{5,6},{6,5},{7,7},{8,8},{9,10},{10,9... | collective-permute-start | bytes 1572872 | tf_op jit(solution)/shard_map/ppermute | solution.py:45
  238.0 17.3 %collective-permute-start.31 = (bf16[128,2048]{1,0:T(8,128)(2,1)}, bf16[128,2048]{1,0:T(8,128)(2,1)}, u32[]{:S(2)}, u32[]{:S(2)}) collective-permute-start(bf16[128,2048]{1,0:T(8,128)(2,1)} %collective-permute-done.22), channel_id=1, source_target_pairs={{0,1},{1,0},{2,3},{3,2},{4,5},{5,4},{6,7},{7,6},{8,9},{9,8},{10,11... | collective-permute-start | bytes 1572872 | tf_op jit(solution)/shard_map/ppermute | solution.py:45
  255.3 14.0 %collective-permute-start.32 = (bf16[128,2048]{1,0:T(8,128)(2,1)}, bf16[128,2048]{1,0:T(8,128)(2,1)S(1)}, u32[]{:S(2)}, u32[]{:S(2)}) collective-permute-start(bf16[128,2048]{1,0:T(8,128)(2,1)} %collective-permute-done.30), channel_id=1, source_target_pairs={{0,1},{1,0},{2,3},{3,2},{4,5},{5,4},{6,7},{7,6},{8,9},{9,8},{10,11... | collective-permute-start | bytes 1572872 | tf_op jit(solution)/shard_map/ppermute | solution.py:45
  256.4 12.9 %collective-permute-start.33 = (bf16[128,2048]{1,0:T(8,128)(2,1)}, bf16[128,2048]{1,0:T(8,128)(2,1)S(1)}, u32[]{:S(2)}, u32[]{:S(2)}) collective-permute-start(bf16[128,2048]{1,0:T(8,128)(2,1)} %collective-permute-done.31), channel_id=1, source_target_pairs={{0,0},{1,2},{2,1},{3,3},{4,4},{5,6},{6,5},{7,7},{8,8},{9,10},{10,9... | collective-permute-start | bytes 1572872 | tf_op jit(solution)/shard_map/ppermute | solution.py:45
  307.4 181.0 %reduce-scatter.3.cloned.1.call-start = ((), (), s32[]{:S(2)}) async-start(), calls=%async_computation.2 | async-start | bytes 10485760 | tf_op jit(solution)/shard_map/reduce_scatter | solution.py:713
  345.0 248.7 %all-gather.14.cloned.1.call-start = ((), (), s32[]{:S(2)}) async-start(), calls=%async_computation.7 | async-start | bytes 9437184 | tf_op jit(solution)/shard_map/all_gather | solution.py:730
  358.5 18.3 %collective-permute-start.43 = (bf16[128,2048]{1,0:T(8,128)(2,1)S(1)}, bf16[128,2048]{1,0:T(8,128)(2,1)S(1)}, u32[]{:S(2)}, u32[]{:S(2)}) collective-permute-start(bf16[128,2048]{1,0:T(8,128)(2,1)S(1)} %get-tuple-element.229), channel_id=1, source_target_pairs={{0,1},{1,0},{2,3},{3,2},{4,5},{5,4},{6,7},{7,6},{8,9},{9,8},{10,11... | collective-permute-start | bytes 1572872 | tf_op jit(solution)/shard_map/ppermute | solution.py:45
  377.0 13.5 %collective-permute-start.47 = (bf16[128,2048]{1,0:T(8,128)(2,1)S(1)}, bf16[128,2048]{1,0:T(8,128)(2,1)S(1)}, u32[]{:S(2)}, u32[]{:S(2)}) collective-permute-start(bf16[128,2048]{1,0:T(8,128)(2,1)S(1)} %get-tuple-element.226), channel_id=1, source_target_pairs={{0,1},{1,0},{2,3},{3,2},{4,5},{5,4},{6,7},{7,6},{8,9},{9,8},{10,11... | collective-permute-start | bytes 1572872 | tf_op jit(solution)/shard_map/ppermute | solution.py:45
  378.8 11.7 %collective-permute-start.44 = (bf16[128,2048]{1,0:T(8,128)(2,1)S(1)}, bf16[128,2048]{1,0:T(8,128)(2,1)S(1)}, u32[]{:S(2)}, u32[]{:S(2)}) collective-permute-start(bf16[128,2048]{1,0:T(8,128)(2,1)S(1)} %get-tuple-element.227), channel_id=1, source_target_pairs={{0,0},{1,2},{2,1},{3,3},{4,4},{5,6},{6,5},{7,7},{8,8},{9,10},{10,9... | collective-permute-start | bytes 1572872 | tf_op jit(solution)/shard_map/ppermute | solution.py:45
  391.6 16.3 %collective-permute-start.45 = (bf16[128,2048]{1,0:T(8,128)(2,1)S(1)}, bf16[128,2048]{1,0:T(8,128)(2,1)S(1)}, u32[]{:S(2)}, u32[]{:S(2)}) collective-permute-start(bf16[128,2048]{1,0:T(8,128)(2,1)S(1)} %get-tuple-element.225), channel_id=1, source_target_pairs={{0,1},{1,0},{2,3},{3,2},{4,5},{5,4},{6,7},{7,6},{8,9},{9,8},{10,11... | collective-permute-start | bytes 1572872 | tf_op jit(solution)/shard_map/ppermute | solution.py:45
  425.9 14.3 %collective-permute-start.53 = (bf16[128,2048]{1,0:T(8,128)(2,1)S(1)}, bf16[128,2048]{1,0:T(8,128)(2,1)S(1)}, u32[]{:S(2)}, u32[]{:S(2)}) collective-permute-start(bf16[128,2048]{1,0:T(8,128)(2,1)S(1)} %collective-permute-done.49), channel_id=1, source_target_pairs={{0,1},{1,0},{2,3},{3,2},{4,5},{5,4},{6,7},{7,6},{8,9},{9,8},{10,11... | collective-permute-start | bytes 1572872 | tf_op jit(solution)/shard_map/ppermute | solution.py:45
  430.0 19.8 %collective-permute-start.52 = (bf16[128,2048]{1,0:T(8,128)(2,1)S(1)}, bf16[128,2048]{1,0:T(8,128)(2,1)S(1)}, u32[]{:S(2)}, u32[]{:S(2)}) collective-permute-start(bf16[128,2048]{1,0:T(8,128)(2,1)S(1)} %collective-permute-done.51), channel_id=1, source_target_pairs={{0,1},{1,0},{2,3},{3,2},{4,5},{5,4},{6,7},{7,6},{8,9},{9,8},{10,11... | collective-permute-start | bytes 1572872 | tf_op jit(solution)/shard_map/ppermute | solution.py:45
  454.7 227.6 %all-gather.8.cloned.1.call-start = ((), (), s32[]{:S(2)}) async-start(), calls=%async_computation.4 | async-start | bytes 18874368 | tf_op jit(solution)/shard_map/all_gather | solution.py:758
  476.5 11.9 %collective-permute-start.59 = (bf16[4,64,2048]{2,1,0:T(8,128)(2,1)S(1)}, bf16[4,64,2048]{2,1,0:T(8,128)(2,1)}, u32[]{:S(2)}, u32[]{:S(2)}) collective-permute-start(bf16[4,64,2048]{2,1,0:T(8,128)(2,1)S(1)} %dynamic-slice_bitcast_fusion.1), channel_id=1, source_target_pairs={{0,4},{4,0},{1,5},{5,1},{2,6},{6,2},{3,7},{7,3},{8,12},{12,8},{9,1... | collective-permute-start | bytes 3145736 | tf_op jit(solution)/shard_map/ppermute | solution.py:126
  481.9 14.3 %collective-permute-start.58 = (bf16[4,4,64,768]{3,2,1,0:T(8,128)(2,1)}, bf16[4,4,64,768]{3,2,1,0:T(8,128)(2,1)}, u32[]{:S(2)}, u32[]{:S(2)}) collective-permute-start(bf16[4,4,64,768]{3,2,1,0:T(8,128)(2,1)} %dynamic-slice_bitcast_fusion), channel_id=1, source_target_pairs={{0,4},{4,0},{1,5},{5,1},{2,6},{6,2},{3,7},{7,3},{8,12},{12,8},{9,1... | collective-permute-start | bytes 4718600 | tf_op jit(solution)/shard_map/ppermute | solution.py:126
  490.3 11.8 %collective-permute-start.62 = (bf16[128,1024]{1,0:T(8,128)(2,1)S(1)}, bf16[128,1024]{1,0:T(8,128)(2,1)S(1)}, u32[]{:S(2)}, u32[]{:S(2)}) collective-permute-start(bf16[128,1024]{1,0:T(8,128)(2,1)S(1)} %get-tuple-element.245), channel_id=1, source_target_pairs={{0,1},{1,2},{2,3},{3,0},{4,5},{5,6},{6,7},{7,4},{8,9},{9,10},{10,1... | collective-permute-start | bytes 786440 | tf_op jit(solution)/shard_map/ppermute | solution.py:110
  496.2 22.5 %collective-permute-start.57 = (bf16[128,1024]{1,0:T(8,128)(2,1)S(1)}, bf16[128,1024]{1,0:T(8,128)(2,1)S(1)}, u32[]{:S(2)}, u32[]{:S(2)}) collective-permute-start(bf16[128,1024]{1,0:T(8,128)(2,1)S(1)} %get-tuple-element.244), channel_id=1, source_target_pairs={{0,1},{1,2},{2,3},{3,0},{4,5},{5,6},{6,7},{7,4},{8,9},{9,10},{10,1... | collective-permute-start | bytes 786440 | tf_op jit(solution)/shard_map/ppermute | solution.py:110
  496.9 21.8 %collective-permute-start.61 = (bf16[128,1024]{1,0:T(8,128)(2,1)S(1)}, bf16[128,1024]{1,0:T(8,128)(2,1)S(1)}, u32[]{:S(2)}, u32[]{:S(2)}) collective-permute-start(bf16[128,1024]{1,0:T(8,128)(2,1)S(1)} %get-tuple-element.246), channel_id=1, source_target_pairs={{0,2},{1,3},{2,0},{3,1},{4,6},{5,7},{6,4},{7,5},{8,10},{9,11},{10,... | collective-permute-start | bytes 786440 | tf_op jit(solution)/shard_map/ppermute | solution.py:110
  496.9 21.8 %collective-permute-start.60 = (bf16[128,1024]{1,0:T(8,128)(2,1)S(1)}, bf16[128,1024]{1,0:T(8,128)(2,1)S(1)}, u32[]{:S(2)}, u32[]{:S(2)}) collective-permute-start(bf16[128,1024]{1,0:T(8,128)(2,1)S(1)} %get-tuple-element.247), channel_id=1, source_target_pairs={{0,3},{1,0},{2,1},{3,2},{4,7},{5,4},{6,5},{7,6},{8,11},{9,8},{10,9... | collective-permute-start | bytes 786440 | tf_op jit(solution)/shard_map/ppermute | solution.py:110
  500.1 34.1 %collective-permute-start.56 = (bf16[128,1024]{1,0:T(8,128)(2,1)S(1)}, bf16[128,1024]{1,0:T(8,128)(2,1)S(1)}, u32[]{:S(2)}, u32[]{:S(2)}) collective-permute-start(bf16[128,1024]{1,0:T(8,128)(2,1)S(1)} %get-tuple-element.249), channel_id=1, source_target_pairs={{0,2},{1,3},{2,0},{3,1},{4,6},{5,7},{6,4},{7,5},{8,10},{9,11},{10,... | collective-permute-start | bytes 786440 | tf_op jit(solution)/shard_map/ppermute | solution.py:110
  502.1 32.1 %collective-permute-start.55 = (bf16[128,1024]{1,0:T(8,128)(2,1)S(1)}, bf16[128,1024]{1,0:T(8,128)(2,1)S(1)}, u32[]{:S(2)}, u32[]{:S(2)}) collective-permute-start(bf16[128,1024]{1,0:T(8,128)(2,1)S(1)} %get-tuple-element.250), channel_id=1, source_target_pairs={{0,3},{1,0},{2,1},{3,2},{4,7},{5,4},{6,5},{7,6},{8,11},{9,8},{10,9... | collective-permute-start | bytes 786440 | tf_op jit(solution)/shard_map/ppermute | solution.py:110
  538.3 28.5 %collective-permute-start.65 = (bf16[4,2,64,768]{3,2,1,0:T(8,128)(2,1)}, bf16[4,2,64,768]{3,2,1,0:T(8,128)(2,1)}, u32[]{:S(2)}, u32[]{:S(2)}) collective-permute-start(bf16[4,2,64,768]{3,2,1,0:T(8,128)(2,1)} %dynamic-slice_bitcast_fusion.2), channel_id=1, source_target_pairs={{0,8},{8,0},{16,24},{24,16},{1,9},{9,1},{17,25},{25,17},{2,10},{10... | collective-permute-start | bytes 2359304 | tf_op jit(solution)/shard_map/ppermute | solution.py:126
  540.6 17.5 %collective-permute-start.66 = (bf16[2,64,2048]{2,1,0:T(8,128)(2,1)}, bf16[2,64,2048]{2,1,0:T(8,128)(2,1)}, u32[]{:S(2)}, u32[]{:S(2)}) collective-permute-start(bf16[2,64,2048]{2,1,0:T(8,128)(2,1)} %dynamic-slice_bitcast_fusion.3), channel_id=1, source_target_pairs={{0,16},{8,24},{16,0},{24,8},{1,17},{9,25},{17,1},{25,9},{2,18},{10... | collective-permute-start | bytes 1572872 | tf_op jit(solution)/shard_map/ppermute | solution.py:126
  545.7 21.1 %collective-permute-start.64 = (bf16[128,2048]{1,0:T(8,128)(2,1)}, bf16[128,2048]{1,0:T(8,128)(2,1)}, u32[]{:S(2)}, u32[]{:S(2)}) collective-permute-start(bf16[128,2048]{1,0:T(8,128)(2,1)} %get-tuple-element.222), channel_id=1, source_target_pairs={{0,0},{1,2},{2,1},{3,3},{4,4},{5,6},{6,5},{7,7},{8,8},{9,10},{10,9... | collective-permute-start | bytes 1572872 | tf_op jit(solution)/shard_map/ppermute | solution.py:45
  551.1 15.7 %collective-permute-start.63 = (bf16[128,2048]{1,0:T(8,128)(2,1)}, bf16[128,2048]{1,0:T(8,128)(2,1)}, u32[]{:S(2)}, u32[]{:S(2)}) collective-permute-start(bf16[128,2048]{1,0:T(8,128)(2,1)} %get-tuple-element.223), channel_id=1, source_target_pairs={{0,1},{1,0},{2,3},{3,2},{4,5},{5,4},{6,7},{7,6},{8,9},{9,8},{10,11... | collective-permute-start | bytes 1572872 | tf_op jit(solution)/shard_map/ppermute | solution.py:45
  556.7 27.6 %collective-permute-start.37 = (bf16[128,2048]{1,0:T(8,128)(2,1)S(1)}, bf16[128,2048]{1,0:T(8,128)(2,1)}, u32[]{:S(2)}, u32[]{:S(2)}) collective-permute-start(bf16[128,2048]{1,0:T(8,128)(2,1)S(1)} %get-tuple-element.236), channel_id=1, source_target_pairs={{0,0},{1,2},{2,1},{3,3},{4,4},{5,6},{6,5},{7,7},{8,8},{9,10},{10,9... | collective-permute-start | bytes 1572872 | tf_op jit(solution)/shard_map/ppermute | solution.py:45
  558.2 29.3 %collective-permute-start.36 = (bf16[128,2048]{1,0:T(8,128)(2,1)}, bf16[128,2048]{1,0:T(8,128)(2,1)}, u32[]{:S(2)}, u32[]{:S(2)}) collective-permute-start(bf16[128,2048]{1,0:T(8,128)(2,1)} %get-tuple-element.237), channel_id=1, source_target_pairs={{0,1},{1,0},{2,3},{3,2},{4,5},{5,4},{6,7},{7,6},{8,9},{9,8},{10,11... | collective-permute-start | bytes 1572872 | tf_op jit(solution)/shard_map/ppermute | solution.py:45
  572.8 18.7 %collective-permute-start.68 = (bf16[128,2048]{1,0:T(8,128)(2,1)}, bf16[128,2048]{1,0:T(8,128)(2,1)S(1)}, u32[]{:S(2)}, u32[]{:S(2)}) collective-permute-start(bf16[128,2048]{1,0:T(8,128)(2,1)} %get-tuple-element.220), channel_id=1, source_target_pairs={{0,0},{1,2},{2,1},{3,3},{4,4},{5,6},{6,5},{7,7},{8,8},{9,10},{10,9... | collective-permute-start | bytes 1572872 | tf_op jit(solution)/shard_map/ppermute | solution.py:45
  574.5 17.0 %collective-permute-start.67 = (bf16[128,2048]{1,0:T(8,128)(2,1)}, bf16[128,2048]{1,0:T(8,128)(2,1)}, u32[]{:S(2)}, u32[]{:S(2)}) collective-permute-start(bf16[128,2048]{1,0:T(8,128)(2,1)} %get-tuple-element.221), channel_id=1, source_target_pairs={{0,1},{1,0},{2,3},{3,2},{4,5},{5,4},{6,7},{7,6},{8,9},{9,8},{10,11... | collective-permute-start | bytes 1572872 | tf_op jit(solution)/shard_map/ppermute | solution.py:45
  607.6 13.9 %collective-permute-start.72 = (bf16[128,2048]{1,0:T(8,128)(2,1)}, bf16[128,2048]{1,0:T(8,128)(2,1)S(1)}, u32[]{:S(2)}, u32[]{:S(2)}) collective-permute-start(bf16[128,2048]{1,0:T(8,128)(2,1)} %get-tuple-element.218), channel_id=1, source_target_pairs={{0,0},{1,2},{2,1},{3,3},{4,4},{5,6},{6,5},{7,7},{8,8},{9,10},{10,9... | collective-permute-start | bytes 1572872 | tf_op jit(solution)/shard_map/ppermute | solution.py:45
  609.3 17.8 %collective-permute-start.71 = (bf16[128,2048]{1,0:T(8,128)(2,1)}, bf16[128,2048]{1,0:T(8,128)(2,1)}, u32[]{:S(2)}, u32[]{:S(2)}) collective-permute-start(bf16[128,2048]{1,0:T(8,128)(2,1)} %get-tuple-element.219), channel_id=1, source_target_pairs={{0,1},{1,0},{2,3},{3,2},{4,5},{5,4},{6,7},{7,6},{8,9},{9,8},{10,11... | collective-permute-start | bytes 1572872 | tf_op jit(solution)/shard_map/ppermute | solution.py:45
  617.5 19.1 %collective-permute-start.78 = (bf16[64,768]{1,0:T(8,128)(2,1)}, bf16[64,768]{1,0:T(8,128)(2,1)S(1)}, u32[]{:S(2)}, u32[]{:S(2)}) collective-permute-start(bf16[64,768]{1,0:T(8,128)(2,1)} %get-tuple-element.278), channel_id=1, source_target_pairs={{0,1},{1,2},{2,3},{3,0},{4,5},{5,6},{6,7},{7,4},{8,9},{9,10},{10,1... | collective-permute-start | bytes 294920 | tf_op jit(solution)/shard_map/ppermute | solution.py:110
  617.5 19.1 %collective-permute-start.77 = (bf16[64,768]{1,0:T(8,128)(2,1)}, bf16[64,768]{1,0:T(8,128)(2,1)S(1)}, u32[]{:S(2)}, u32[]{:S(2)}) collective-permute-start(bf16[64,768]{1,0:T(8,128)(2,1)} %get-tuple-element.279), channel_id=1, source_target_pairs={{0,2},{1,3},{2,0},{3,1},{4,6},{5,7},{6,4},{7,5},{8,10},{9,11},{10,... | collective-permute-start | bytes 294920 | tf_op jit(solution)/shard_map/ppermute | solution.py:110
  618.9 17.7 %collective-permute-start.76 = (bf16[64,768]{1,0:T(8,128)(2,1)S(1)}, bf16[64,768]{1,0:T(8,128)(2,1)S(1)}, u32[]{:S(2)}, u32[]{:S(2)}) collective-permute-start(bf16[64,768]{1,0:T(8,128)(2,1)S(1)} %get-tuple-element.280), channel_id=1, source_target_pairs={{0,3},{1,0},{2,1},{3,2},{4,7},{5,4},{6,5},{7,6},{8,11},{9,8},{10,9... | collective-permute-start | bytes 294920 | tf_op jit(solution)/shard_map/ppermute | solution.py:110
  621.5 23.6 %collective-permute-start.39 = (bf16[128,2048]{1,0:T(8,128)(2,1)}, bf16[128,2048]{1,0:T(8,128)(2,1)}, u32[]{:S(2)}, u32[]{:S(2)}) collective-permute-start(bf16[128,2048]{1,0:T(8,128)(2,1)} %get-tuple-element.234), channel_id=1, source_target_pairs={{0,0},{1,2},{2,1},{3,3},{4,4},{5,6},{6,5},{7,7},{8,8},{9,10},{10,9... | collective-permute-start | bytes 1572872 | tf_op jit(solution)/shard_map/ppermute | solution.py:45
  627.1 18.1 %collective-permute-start.38 = (bf16[128,2048]{1,0:T(8,128)(2,1)}, bf16[128,2048]{1,0:T(8,128)(2,1)}, u32[]{:S(2)}, u32[]{:S(2)}) collective-permute-start(bf16[128,2048]{1,0:T(8,128)(2,1)} %get-tuple-element.235), channel_id=1, source_target_pairs={{0,1},{1,0},{2,3},{3,2},{4,5},{5,4},{6,7},{7,6},{8,9},{9,8},{10,11... | collective-permute-start | bytes 1572872 | tf_op jit(solution)/shard_map/ppermute | solution.py:45
  636.9 13.8 %collective-permute-start.81 = (bf16[64,2560]{1,0:T(8,128)(2,1)S(1)}, bf16[64,2560]{1,0:T(8,128)(2,1)}, u32[]{:S(2)}, u32[]{:S(2)}) collective-permute-start(bf16[64,2560]{1,0:T(8,128)(2,1)S(1)} %constant_dynamic-update-slice_fusion.14), channel_id=1, source_target_pairs={{0,16},{8,24},{16,0},{24,8},{1,17},{9,25},{17,1},{25,9},{2,18},{10... | collective-permute-start | bytes 983048 | tf_op jit(solution)/shard_map/ppermute | solution.py:550
  638.6 12.1 %collective-permute-start.80 = (bf16[64,2560]{1,0:T(8,128)(2,1)S(1)}, bf16[64,2560]{1,0:T(8,128)(2,1)S(1)}, u32[]{:S(2)}, u32[]{:S(2)}) collective-permute-start(bf16[64,2560]{1,0:T(8,128)(2,1)S(1)} %get-tuple-element.271), channel_id=1, source_target_pairs={{0,8},{8,0},{16,24},{24,16},{1,9},{9,1},{17,25},{25,17},{2,10},{10... | collective-permute-start | bytes 983048 | tf_op jit(solution)/shard_map/ppermute | solution.py:550
  651.9 17.2 %collective-permute-start.86 = (bf16[128,2560]{1,0:T(8,128)(2,1)S(1)}, bf16[128,2560]{1,0:T(8,128)(2,1)S(1)}, u32[]{:S(2)}, u32[]{:S(2)}) collective-permute-start(bf16[128,2560]{1,0:T(8,128)(2,1)S(1)} %pad_maximum_fusion.9), channel_id=1, source_target_pairs={{0,8},{8,0},{16,24},{24,16},{1,9},{9,1},{17,25},{25,17},{2,10},{10... | collective-permute-start | bytes 1966088 | tf_op jit(solution)/shard_map/ppermute | solution.py:550
  652.0 18.2 %collective-permute-start.85 = (bf16[128,2560]{1,0:T(8,128)(2,1)S(1)}, bf16[128,2560]{1,0:T(8,128)(2,1)S(1)}, u32[]{:S(2)}, u32[]{:S(2)}) collective-permute-start(bf16[128,2560]{1,0:T(8,128)(2,1)S(1)} %pad_maximum_fusion.8), channel_id=1, source_target_pairs={{0,16},{8,24},{16,0},{24,8},{1,17},{9,25},{17,1},{25,9},{2,18},{10... | collective-permute-start | bytes 1966088 | tf_op jit(solution)/shard_map/ppermute | solution.py:550
  656.8 19.1 %collective-permute-start.41 = (bf16[128,2048]{1,0:T(8,128)(2,1)}, bf16[128,2048]{1,0:T(8,128)(2,1)}, u32[]{:S(2)}, u32[]{:S(2)}) collective-permute-start(bf16[128,2048]{1,0:T(8,128)(2,1)} %get-tuple-element.230), channel_id=1, source_target_pairs={{0,1},{1,0},{2,3},{3,2},{4,5},{5,4},{6,7},{7,6},{8,9},{9,8},{10,11... | collective-permute-start | bytes 1572872 | tf_op jit(solution)/shard_map/ppermute | solution.py:45
  656.8 19.7 %collective-permute-start.42 = (bf16[128,2048]{1,0:T(8,128)(2,1)}, bf16[128,2048]{1,0:T(8,128)(2,1)}, u32[]{:S(2)}, u32[]{:S(2)}) collective-permute-start(bf16[128,2048]{1,0:T(8,128)(2,1)} %get-tuple-element.231), channel_id=1, source_target_pairs={{0,0},{1,2},{2,1},{3,3},{4,4},{5,6},{6,5},{7,7},{8,8},{9,10},{10,9... | collective-permute-start | bytes 1572872 | tf_op jit(solution)/shard_map/ppermute | solution.py:45
  672.9 30.2 %collective-permute-start.87 = (bf16[256,2560]{1,0:T(8,128)(2,1)}, bf16[256,2560]{1,0:T(8,128)(2,1)}, u32[]{:S(2)}, u32[]{:S(2)}) collective-permute-start(bf16[256,2560]{1,0:T(8,128)(2,1)} %pad_maximum_fusion.6.one), channel_id=1, source_target_pairs={{0,4},{4,0},{1,5},{5,1},{2,6},{6,2},{3,7},{7,3},{8,12},{12,8},{9,1... | collective-permute-start | bytes 3932168 | tf_op jit(solution)/shard_map/ppermute | solution.py:33
  672.9 30.2 %collective-permute-start.88 = (bf16[256,2560]{1,0:T(8,128)(2,1)S(1)}, bf16[256,2560]{1,0:T(8,128)(2,1)}, u32[]{:S(2)}, u32[]{:S(2)}) collective-permute-start(bf16[256,2560]{1,0:T(8,128)(2,1)S(1)} %pad_maximum_fusion.7.one), channel_id=1, source_target_pairs={{0,4},{4,0},{1,5},{5,1},{2,6},{6,2},{3,7},{7,3},{8,12},{12,8},{9,1... | collective-permute-start | bytes 3932168 | tf_op jit(solution)/shard_map/ppermute | solution.py:33
  (89 other events, 989.0 us)
Sparse Core Ops, SparseCore 0:
  35.1 32.7 all-gather.9
  133.9 91.8 all-gather.11
  307.6 54.1 reduce-scatter.4
  365.5 86.3 reduce-scatter.2
  454.8 55.9 all-gather.13
  536.3 112.0 all-gather.7

commit v5 on v4

--- a/solution.py
+++ b/solution.py
@@ -342,7 +342,7 @@
     q_cols = cols - kv * two
     tiles = q_cols // two
     each = tiles // kv
-    rows = min(256, seq)
+    rows = min(512, seq)
     lane = jnp.arange(two) // HEAD_SIZE
     block = jnp.where(lane[:, None] == lane[None, :], 1.0 / HEAD_SIZE, 0.0).astype(BF)
     own = pl.BlockSpec((rows, two), lambda j, i: (i, j))
@@ -633,7 +633,7 @@
     proj = proj.transpose(1, 0, 2, 3).reshape(width, q_cols + 2 * kv_cols)
 
     gains = jnp.concatenate([attn_gain, ffn_gain, query_gain, key_norm_gain])
-    gains = gather_small(after(gains, x_steps[0]))
+    gains = gather_small(after(gains, x_steps[1]))
     gains = gains.astype(F32)
     gain_one = gains[:, :rows].reshape(-1)
     gain_two = gains[:, rows : 2 * rows].reshape(-1)
@@ -787,13 +787,14 @@
         jnp.concatenate(columns[2] + [att_sum[1]], axis=1),
     ]
     sums = small_line(sums, att_all)
+    gate_grad, up_grad = (place_pair(ffn_all, w, chips, count, part, ff_own) for w in range(2))
     for step in range(bits):
-        att_all = gather_stage(att_all, step, sums)
+        last = step == bits - 1
+        att_all = gather_stage(att_all, step, (gate_grad, up_grad) if last else sums)
         if step == 0:
             sums = sums + after(swap_cores(sums), att_all)
     sums = small_chips(sums, att_all)
-    gate_grad, up_grad = (place_pair(ffn_all, w, chips, count, part, ff_own) for w in range(2))
-    others = after([swap_cores(a) for a in att_all], gate_grad, up_grad)
+    others = [swap_cores(a) for a in att_all]
     query_grad, key_grad = place_columns(
         gathered_order(0), att_all[0], others[0], (q_cols * count, kv_cols * count)
     )

time: 738 us -> 731 us (level)
    ppermute x24, starting transfers between devices: 58.6 us -> 66.4 us  [line_step(): lax.ppermute(second, 'fsdp', odd)]
    unnamed x130 -> x134, local copies, waits for them, and re-layouts: 17.8 us -> 17.7 us
  transfers between devices with their start and end apart: 95 -> 95, of which waited for: 24 -> 25; matrix products, arithmetic and copies ran while one was open for 22% -> 23% of each run, Pallas kernels for 9% -> 10%
where the time goes in v5:
time: 731 us; the launch traced here: 716 us
  waiting for transfers between devices  207 us (28%)
  starting transfers between devices  202 us (28%)
  matrix products  92.7 us (13%)
  Pallas kernels  77.1 us (11%)
  other arithmetic  68.5 us (9%)
  local copies, waits for them, and re-layouts  52.7 us (7%)
  between operations  16.2 us (2%)
    ppermute x24, waiting for transfers between devices, line_step(): lax.ppermute(first, 'fsdp', even)  117 us
    ppermute x24, starting transfers between devices, line_step(): lax.ppermute(first, 'fsdp', even)  86.3 us
    ppermute x18, waiting for transfers between devices, exchange_line(): lax.ppermute(piece_for((mine - e) % count), 'fsdp', [(i, (i - e) % count)...  69.5 us
    ppermute x24, starting transfers between devices, line_step(): lax.ppermute(second, 'fsdp', odd)  66.4 us
    dot_general x5, matrix products, mm_last(): lax.dot_general(a, b, (((1,), (1,)), ((), ())), preferred_element_type=F32)  40.2 us
    dot_general x5, matrix products, mm(): return jnp.dot(a, b, preferred_element_type=F32)  28 us
    ppermute x18, starting transfers between devices, exchange_line(): lax.ppermute(piece_for((mine - e) % count), 'fsdp', [(i, (i - e) % count)...  25.4 us
    dot_general x4, matrix products, mm_first(): lax.dot_general(a, b, (((0,), (0,)), ((), ())), preferred_element_type=F32)  24.5 us
  transfers between devices with their start and end apart: 95, of which 25 were waited for; matrix products, arithmetic and copies ran while one was open for 23% of the time, Pallas kernels for 10%

profile of v5, /device:TPU:0, one launch (start us, length us, event | category | flops | bytes accessed | tf_op | source)
XLA Modules:
  0.0 716.5 jit_solution(723862271903979177)
XLA Ops:
  7.3 3.1 collective-permute-start.1
  10.4 5.4 collective-permute-start
  21.0 13.1 %collective-permute-done.5 = bf16[64,768]{1,0:T(8,128)(2,1)S(1)} collective-permute-done((bf16[64,768]{1,0:T(8,128)(2,1)S(1)}, bf16[64,768]{1,0:T(8,128)(2,1)S(1)}, u32[]{:S(2)}, u32[]{:S(2)}) %collective-permute-start.5) | collective-permute-done | bytes 98336 | tf_op jit(solution)/shard_map/ppermute | solution.py:110
  35.2 5.4 collective-permute-start.2
  43.1 9.2 %collective-permute-done.3 = bf16[128,2048]{1,0:T(8,128)(2,1)} collective-permute-done((bf16[128,2048]{1,0:T(8,128)(2,1)}, bf16[128,2048]{1,0:T(8,128)(2,1)}, u32[]{:S(2)}, u32[]{:S(2)}) %collective-permute-start.3) | collective-permute-done | bytes 524320 | tf_op jit(solution)/shard_map/ppermute | solution.py:45
  57.2 5.4 collective-permute-start.8
  85.7 6.1 shard_map.237
  96.7 26.0 %collective-permute-done.15 = bf16[128,2048]{1,0:T(8,128)(2,1)} collective-permute-done((bf16[128,2048]{1,0:T(8,128)(2,1)}, bf16[128,2048]{1,0:T(8,128)(2,1)}, u32[]{:S(2)}, u32[]{:S(2)}) %collective-permute-start.15) | collective-permute-done | bytes 524320 | tf_op jit(solution)/shard_map/ppermute | solution.py:110
  133.5 5.4 collective-permute-start.18
  138.9 3.9 collective-permute-start.17
  142.8 12.1 %collective-permute-done.17 = bf16[128,2048]{1,0:T(8,128)(2,1)} collective-permute-done((bf16[128,2048]{1,0:T(8,128)(2,1)}, bf16[128,2048]{1,0:T(8,128)(2,1)}, u32[]{:S(2)}, u32[]{:S(2)}) %collective-permute-start.17) | collective-permute-done | bytes 524320 | tf_op jit(solution)/shard_map/ppermute | solution.py:45
  157.8 3.3 collective-permute-start.19
  161.1 10.9 %collective-permute-done.19.right = bf16[128,2048]{1,0:T(8,128)(2,1)S(1)} collective-permute-done((bf16[128,2048]{1,0:T(8,128)(2,1)S(1)}, bf16[128,2048]{1,0:T(8,128)(2,1)S(1)}, u32[]{:S(2)}, u32[]{:S(2)}) %collective-permute-start.19) | collective-permute-done | bytes 524320 | tf_op jit(solution)/shard_map/ppermute | solution.py:45
  172.0 5.4 collective-permute-start.22
  178.0 3.9 shard_map.238
  181.9 7.9 %collective-permute-done.21 = bf16[128,2048]{1,0:T(8,128)(2,1)} collective-permute-done((bf16[128,2048]{1,0:T(8,128)(2,1)}, bf16[128,2048]{1,0:T(8,128)(2,1)}, u32[]{:S(2)}, u32[]{:S(2)}) %collective-permute-start.21) | collective-permute-done | bytes 524320 | tf_op jit(solution)/shard_map/ppermute | solution.py:45
  191.7 9.4 %collective-permute-done.24 = bf16[128,2048]{1,0:T(8,128)(2,1)S(1)} collective-permute-done((bf16[128,2048]{1,0:T(8,128)(2,1)}, bf16[128,2048]{1,0:T(8,128)(2,1)S(1)}, u32[]{:S(2)}, u32[]{:S(2)}) %collective-permute-start.24) | collective-permute-done | bytes 524320 | tf_op jit(solution)/shard_map/ppermute | solution.py:45
  202.1 4.3 collective-permute-start.27
  206.5 9.5 %collective-permute-start.26 = (bf16[128,2048]{1,0:T(8,128)(2,1)S(1)}, bf16[128,2048]{1,0:T(8,128)(2,1)S(1)}, u32[]{:S(2)}, u32[]{:S(2)}) collective-permute-start(bf16[128,2048]{1,0:T(8,128)(2,1)S(1)} %collective-permute-done.25), channel_id=1, source_target_pairs={{0,1},{1,0},{2,3},{3,2},{4,5},{5,4},{6,7},{7,6},{8,9},{9,8},{10,11... | collective-permute-start | bytes 1572872 | tf_op jit(solution)/shard_map/ppermute | solution.py:45
  218.5 7.3 %collective-permute-done.26 = bf16[128,2048]{1,0:T(8,128)(2,1)S(1)} collective-permute-done((bf16[128,2048]{1,0:T(8,128)(2,1)S(1)}, bf16[128,2048]{1,0:T(8,128)(2,1)S(1)}, u32[]{:S(2)}, u32[]{:S(2)}) %collective-permute-start.26) | collective-permute-done | bytes 524320 | tf_op jit(solution)/shard_map/ppermute | solution.py:45
  229.7 5.4 collective-permute-start.30
  237.9 14.5 %fusion.79 = f32[1024,2048]{1,0:T(8,128)} fusion(bf16[1024,2048]{1,0:T(8,128)(2,1)} %constant_dynamic-update-slice_fusion, bf16[2048,2048]{1,0:T(8,128)(2,1)} %bitcast.295), kind=kOutput, calls=%fused_computation.252 | convolution fusion | flops 8589934592 | bytes 20971520 | tf_op jit(solution)/shard_map/dot_general | solution.py:21
  256.3 10.1 %collective-permute-done.32 = bf16[128,2048]{1,0:T(8,128)(2,1)S(1)} collective-permute-done((bf16[128,2048]{1,0:T(8,128)(2,1)}, bf16[128,2048]{1,0:T(8,128)(2,1)S(1)}, u32[]{:S(2)}, u32[]{:S(2)}) %collective-permute-start.32) | collective-permute-done | bytes 524320 | tf_op jit(solution)/shard_map/ppermute | solution.py:45
  275.2 4.5 collective-permute-done.34
  279.7 3.2 constant_dynamic-update-slice_fusion.5
  282.9 14.1 %multiply_convert_fusion = (bf16[1024,1024]{1,0:T(8,128)(2,1)}, bf16[1024,1024]{1,0:T(8,128)(2,1)}, bf16[1024,1024]{1,0:T(8,128)(2,1)S(1)}) fusion(f32[1024,2048]{1,0:T(8,128)} %fusion.79, bf16[1024,2048]{1,0:T(8,128)(2,1)} %constant_dynamic-update-slice_fusion.5, bf16[2048,2048]{1,0:T(8,128)(2,1)} %param.26, s32[]{:T(128)S(6)} %select_n.652), kind=kOutput, calls=%fused_computation.13 | convolution fusion | flops 4310695936 | bytes 23068676 | tf_op jit(solution)/shard_map/dot_general | solution.py:25
  298.2 6.2 convolution_convert_fusion.1
  306.4 6.0 fusion.13
  314.1 9.7 %convolution_convert_fusion.4 = bf16[512,2048]{1,0:T(8,128)(2,1)} fusion(bf16[512,2048]{1,0:T(8,128)(2,1)S(1)} %get-tuple-element.128, bf16[2048,2048]{1,0:T(8,128)(2,1)} %bitcast.296), kind=kOutput, calls=%fused_computation.30 | convolution fusion | flops 4296015872 | bytes 12582912 | tf_op jit(solution)/shard_map/dot_general | solution.py:25
  324.2 4.4 convert_add_fusion.1
  328.6 13.4 %convolution_convert_fusion = bf16[2048,2048]{1,0:T(8,128)(2,1)} fusion(bf16[1024,2048]{1,0:T(8,128)(2,1)} %constant_dynamic-update-slice_fusion, bf16[1024,2048]{1,0:T(8,128)(2,1)S(1)} %pad_maximum_fusion), kind=kOutput, calls=%fused_computation | convolution fusion | flops 8594128896 | bytes 16777216 | tf_op jit(solution)/shard_map/dot_general | solution.py:29
  342.8 4.0 collective-permute-done.40
  346.8 7.6 %convert_add_fusion = f32[512,2048]{1,0:T(8,128)S(1)} fusion(bf16[512,2048]{1,0:T(8,128)(2,1)S(1)} %collective-permute-done.40, bf16[512,2048]{1,0:T(8,128)(2,1)} %get-tuple-element.133, bf16[2048,2048]{1,0:T(8,128)(2,1)} %bitcast.297), kind=kOutput, calls=%fused_computation.11 | convolution fusion | flops 4297064448 | bytes 16777216 | tf_op jit(solution)/shard_map/dot_general | solution.py:25
  355.3 6.1 collective-permute-start.43
  361.4 12.2 %collective-permute-done.43 = bf16[128,2048]{1,0:T(8,128)(2,1)S(1)} collective-permute-done((bf16[128,2048]{1,0:T(8,128)(2,1)S(1)}, bf16[128,2048]{1,0:T(8,128)(2,1)S(1)}, u32[]{:S(2)}, u32[]{:S(2)}) %collective-permute-start.43) | collective-permute-done | bytes 524320 | tf_op jit(solution)/shard_map/ppermute | solution.py:45
  376.3 11.1 %collective-permute-done.47 = bf16[128,2048]{1,0:T(8,128)(2,1)S(1)} collective-permute-done((bf16[128,2048]{1,0:T(8,128)(2,1)S(1)}, bf16[128,2048]{1,0:T(8,128)(2,1)S(1)}, u32[]{:S(2)}, u32[]{:S(2)}) %collective-permute-start.47) | collective-permute-done | bytes 524320 | tf_op jit(solution)/shard_map/ppermute | solution.py:45
  388.4 5.8 collective-permute-start.45
  394.3 10.2 %collective-permute-done.45.right = bf16[128,2048]{1,0:T(8,128)(2,1)S(1)} collective-permute-done((bf16[128,2048]{1,0:T(8,128)(2,1)S(1)}, bf16[128,2048]{1,0:T(8,128)(2,1)S(1)}, u32[]{:S(2)}, u32[]{:S(2)}) %collective-permute-start.45) | collective-permute-done | bytes 524320 | tf_op jit(solution)/shard_map/ppermute | solution.py:45
  405.3 4.6 shard_map.239
  413.8 8.3 %collective-permute-done.50 = bf16[128,2048]{1,0:T(8,128)(2,1)S(1)} collective-permute-done((bf16[128,2048]{1,0:T(8,128)(2,1)}, bf16[128,2048]{1,0:T(8,128)(2,1)S(1)}, u32[]{:S(2)}, u32[]{:S(2)}) %collective-permute-start.50) | collective-permute-done | bytes 524320 | tf_op jit(solution)/shard_map/ppermute | solution.py:45
  422.8 3.9 collective-permute-start.53
  426.7 10.4 %collective-permute-start.52 = (bf16[128,2048]{1,0:T(8,128)(2,1)S(1)}, bf16[128,2048]{1,0:T(8,128)(2,1)S(1)}, u32[]{:S(2)}, u32[]{:S(2)}) collective-permute-start(bf16[128,2048]{1,0:T(8,128)(2,1)S(1)} %collective-permute-done.51), channel_id=1, source_target_pairs={{0,1},{1,0},{2,3},{3,2},{4,5},{5,4},{6,7},{7,6},{8,9},{9,8},{10,11... | collective-permute-start | bytes 1572872 | tf_op jit(solution)/shard_map/ppermute | solution.py:45
  437.9 8.7 %collective-permute-done.52 = bf16[128,2048]{1,0:T(8,128)(2,1)S(1)} collective-permute-done((bf16[128,2048]{1,0:T(8,128)(2,1)S(1)}, bf16[128,2048]{1,0:T(8,128)(2,1)S(1)}, u32[]{:S(2)}, u32[]{:S(2)}) %collective-permute-start.52) | collective-permute-done | bytes 524320 | tf_op jit(solution)/shard_map/ppermute | solution.py:45
  457.5 12.6 %shard_map.240 = (bf16[512,768]{1,0:T(8,128)(2,1)S(1)}, f32[1,128]{1,0:T(1,128)S(1)}, f32[1,128]{1,0:T(1,128)S(1)}) custom-call(f32[512,768]{1,0:T(8,128)S(1)} %copy-done.2, f32[512,768]{1,0:T(8,128)S(1)} %copy-done.2, f32[512,768]{1,0:T(8,128)S(1)} %copy-done.2, f32[512,512]{1,0:T(8,128)S(1)} %and_select_fusion.bias, f32[512,128]{1,0:T(8,128)S(1)} %copy.64.cosine.cos_own, ...), custom_call_target="tpu_custom_call" | custom-call | tf_op jit(solution)/shard_map/pallas_call | solution.py:378
  476.0 6.7 fusion.80.part
  496.1 3.0 fusion.10
  499.1 13.5 %collective-permute-done.61 = bf16[128,1024]{1,0:T(8,128)(2,1)S(1)} collective-permute-done((bf16[128,1024]{1,0:T(8,128)(2,1)S(1)}, bf16[128,1024]{1,0:T(8,128)(2,1)S(1)}, u32[]{:S(2)}, u32[]{:S(2)}) %collective-permute-start.61) | collective-permute-done | bytes 262176 | tf_op jit(solution)/shard_map/ppermute | solution.py:110
  512.6 15.9 %collective-permute-done.56 = bf16[128,1024]{1,0:T(8,128)(2,1)S(1)} collective-permute-done((bf16[128,1024]{1,0:T(8,128)(2,1)S(1)}, bf16[128,1024]{1,0:T(8,128)(2,1)S(1)}, u32[]{:S(2)}, u32[]{:S(2)}) %collective-permute-start.56) | collective-permute-done | bytes 262176 | tf_op jit(solution)/shard_map/ppermute | solution.py:110
  539.6 5.4 collective-permute-start.64
  551.9 10.3 %collective-permute-start.36 = (bf16[128,2048]{1,0:T(8,128)(2,1)}, bf16[128,2048]{1,0:T(8,128)(2,1)}, u32[]{:S(2)}, u32[]{:S(2)}) collective-permute-start(bf16[128,2048]{1,0:T(8,128)(2,1)} %get-tuple-element.233), channel_id=1, source_target_pairs={{0,1},{1,0},{2,3},{3,2},{4,5},{5,4},{6,7},{7,6},{8,9},{9,8},{10,11... | collective-permute-start | bytes 1572872 | tf_op jit(solution)/shard_map/ppermute | solution.py:45
  565.3 2.9 fusion.28
  569.9 6.9 collective-permute-start.67
  582.9 5.3 collective-permute-done.70
  590.4 10.3 %shard_map.241 = f32[2048,2048]{1,0:T(8,128)} custom-call(bf16[8,256,2048]{2,1,0:T(8,128)(2,1)} %bitcast.272), custom_call_target="tpu_custom_call" | custom-call | tf_op jit(solution)/shard_map/pallas_call | solution.py:571
  600.8 3.0 fusion.25
  616.7 5.4 collective-permute-start.39
  622.1 4.6 collective-permute-start.38
  626.6 4.5 shard_map.242
  650.8 3.1 fusion.35
  653.9 5.4 collective-permute-start.42
  659.3 10.4 %shard_map.244 = f32[512,8192]{1,0:T(8,128)} custom-call(bf16[4,2,4,128,2048]{4,3,2,1,0:T(8,128)(2,1)} %bitcast.264), custom_call_target="tpu_custom_call" | custom-call | tf_op jit(solution)/shard_map/pallas_call | solution.py:503
  669.7 10.4 %shard_map.243 = f32[512,8192]{1,0:T(8,128)} custom-call(bf16[4,2,4,128,2048]{4,3,2,1,0:T(8,128)(2,1)} %bitcast.265), custom_call_target="tpu_custom_call" | custom-call | tf_op jit(solution)/shard_map/pallas_call | solution.py:503
  694.7 7.2 %shard_map.246 = (f32[512,512]{1,0:T(8,128)}, f32[512,2048]{1,0:T(8,128)}) custom-call(s32[8]{0:T(128)} %stack.47._, bf16[256,2560]{1,0:T(8,128)(2,1)} %copy-done.16, bf16[256,2560]{1,0:T(8,128)(2,1)} %collective-permute-done.88.two), custom_call_target="tpu_custom_call" | custom-call | tf_op jit(solution)/shard_map/pallas_call | solution.py:529
  701.9 7.2 %shard_map.245 = (f32[512,2048]{1,0:T(8,128)}, f32[512,512]{1,0:T(8,128)}) custom-call(s32[8]{0:T(128)} %stack.46._, bf16[256,2560]{1,0:T(8,128)(2,1)} %pad_maximum_fusion.6.one, bf16[256,2560]{1,0:T(8,128)(2,1)} %collective-permute-done.87.two), custom_call_target="tpu_custom_call" | custom-call | tf_op jit(solution)/shard_map/pallas_call | solution.py:529
  (427 shorter events, 205.5 us)
Async XLA Ops:
  7.2 74.1 %all-gather.10.cloned.1.call-start = ((), (), s32[]{:S(2)}) async-start(), calls=%async_computation.5 | async-start | bytes 3538944 | tf_op jit(solution)/shard_map/all_gather | solution.py:632
  7.3 26.8 %collective-permute-start.1 = (bf16[128,2048]{1,0:T(8,128)(2,1)}, bf16[128,2048]{1,0:T(8,128)(2,1)}, u32[]{:S(2)}, u32[]{:S(2)}) collective-permute-start(bf16[128,2048]{1,0:T(8,128)(2,1)} %wide.1), channel_id=1, source_target_pairs={{0,1},{1,0},{2,3},{3,2},{4,5},{5,4},{6,7},{7,6},{8,9},{9,8},{10,11... | collective-permute-start | bytes 1572872 | tf_op jit(solution)/shard_map/ppermute | solution.py:45
  10.4 23.7 %collective-permute-start = (bf16[128,2048]{1,0:T(8,128)(2,1)}, bf16[128,2048]{1,0:T(8,128)(2,1)}, u32[]{:S(2)}, u32[]{:S(2)}) collective-permute-start(bf16[128,2048]{1,0:T(8,128)(2,1)} %wide.1), channel_id=1, source_target_pairs={{0,0},{1,2},{2,1},{3,3},{4,4},{5,6},{6,5},{7,7},{8,8},{9,10},{10,9... | collective-permute-start | bytes 1572872 | tf_op jit(solution)/shard_map/ppermute | solution.py:45
  17.6 16.5 %collective-permute-start.5 = (bf16[64,768]{1,0:T(8,128)(2,1)S(1)}, bf16[64,768]{1,0:T(8,128)(2,1)S(1)}, u32[]{:S(2)}, u32[]{:S(2)}) collective-permute-start(bf16[64,768]{1,0:T(8,128)(2,1)S(1)} %pad_maximum_fusion.19), channel_id=1, source_target_pairs={{0,2},{1,3},{2,0},{3,1},{4,6},{5,7},{6,4},{7,5},{8,10},{9,11},{10,... | collective-permute-start | bytes 294920 | tf_op jit(solution)/shard_map/ppermute | solution.py:110
  17.7 16.4 %collective-permute-start.4 = (bf16[64,768]{1,0:T(8,128)(2,1)S(1)}, bf16[64,768]{1,0:T(8,128)(2,1)S(1)}, u32[]{:S(2)}, u32[]{:S(2)}) collective-permute-start(bf16[64,768]{1,0:T(8,128)(2,1)S(1)} %pad_maximum_fusion.18), channel_id=1, source_target_pairs={{0,3},{1,0},{2,1},{3,2},{4,7},{5,4},{6,5},{7,6},{8,11},{9,8},{10,9... | collective-permute-start | bytes 294920 | tf_op jit(solution)/shard_map/ppermute | solution.py:110
  20.4 13.7 %collective-permute-start.6 = (bf16[64,768]{1,0:T(8,128)(2,1)S(1)}, bf16[64,768]{1,0:T(8,128)(2,1)S(1)}, u32[]{:S(2)}, u32[]{:S(2)}) collective-permute-start(bf16[64,768]{1,0:T(8,128)(2,1)S(1)} %pad_maximum_fusion.20), channel_id=1, source_target_pairs={{0,1},{1,2},{2,3},{3,0},{4,5},{5,6},{6,7},{7,4},{8,9},{9,10},{10,1... | collective-permute-start | bytes 294920 | tf_op jit(solution)/shard_map/ppermute | solution.py:110
  35.0 202.9 %all-gather.12.cloned.1.call-start = ((), (), s32[]{:S(2)}) async-start(), calls=%async_computation.6 | async-start | bytes 10485760 | tf_op jit(solution)/shard_map/all_gather | solution.py:684
  40.5 11.8 %collective-permute-start.3 = (bf16[128,2048]{1,0:T(8,128)(2,1)}, bf16[128,2048]{1,0:T(8,128)(2,1)}, u32[]{:S(2)}, u32[]{:S(2)}) collective-permute-start(bf16[128,2048]{1,0:T(8,128)(2,1)} %collective-permute-done), channel_id=1, source_target_pairs={{0,1},{1,0},{2,3},{3,2},{4,5},{5,4},{6,7},{7,6},{8,9},{9,8},{10,11... | collective-permute-start | bytes 1572872 | tf_op jit(solution)/shard_map/ppermute | solution.py:45
  52.3 13.1 %collective-permute-start.11 = (bf16[1056]{0:T(1024)(128)(2,1)S(1)}, bf16[1056]{0:T(1024)(128)(2,1)S(1)}, u32[]{:S(2)}, u32[]{:S(2)}) collective-permute-start(bf16[1056]{0:T(1024)(128)(2,1)S(1)} %concatenate.92), channel_id=1, source_target_pairs={{0,1},{1,2},{2,3},{3,0},{4,5},{5,6},{6,7},{7,4},{8,9},{9,10},{10,1... | collective-permute-start | bytes 6344 | tf_op jit(solution)/shard_map/ppermute | solution.py:110
  52.7 12.5 %collective-permute-start.10 = (bf16[1056]{0:T(1024)(128)(2,1)S(1)}, bf16[1056]{0:T(1024)(128)(2,1)S(1)}, u32[]{:S(2)}, u32[]{:S(2)}) collective-permute-start(bf16[1056]{0:T(1024)(128)(2,1)S(1)} %concatenate.92), channel_id=1, source_target_pairs={{0,2},{1,3},{2,0},{3,1},{4,6},{5,7},{6,4},{7,5},{8,10},{9,11},{10,... | collective-permute-start | bytes 6344 | tf_op jit(solution)/shard_map/ppermute | solution.py:110
  71.5 25.2 %collective-permute-start.14 = (bf16[128,2048]{1,0:T(8,128)(2,1)}, bf16[128,2048]{1,0:T(8,128)(2,1)}, u32[]{:S(2)}, u32[]{:S(2)}) collective-permute-start(bf16[128,2048]{1,0:T(8,128)(2,1)} %pad_maximum_fusion.11), channel_id=1, source_target_pairs={{0,3},{1,0},{2,1},{3,2},{4,7},{5,4},{6,5},{7,6},{8,11},{9,8},{10,9... | collective-permute-start | bytes 1572872 | tf_op jit(solution)/shard_map/ppermute | solution.py:110
  74.5 48.2 %collective-permute-start.15 = (bf16[128,2048]{1,0:T(8,128)(2,1)}, bf16[128,2048]{1,0:T(8,128)(2,1)}, u32[]{:S(2)}, u32[]{:S(2)}) collective-permute-start(bf16[128,2048]{1,0:T(8,128)(2,1)} %pad_maximum_fusion.12), channel_id=1, source_target_pairs={{0,2},{1,3},{2,0},{3,1},{4,6},{5,7},{6,4},{7,5},{8,10},{9,11},{10,... | collective-permute-start | bytes 1572872 | tf_op jit(solution)/shard_map/ppermute | solution.py:110
  78.1 44.6 %collective-permute-start.16 = (bf16[128,2048]{1,0:T(8,128)(2,1)}, bf16[128,2048]{1,0:T(8,128)(2,1)}, u32[]{:S(2)}, u32[]{:S(2)}) collective-permute-start(bf16[128,2048]{1,0:T(8,128)(2,1)} %pad_maximum_fusion.13), channel_id=1, source_target_pairs={{0,1},{1,2},{2,3},{3,0},{4,5},{5,6},{6,7},{7,4},{8,9},{9,10},{10,1... | collective-permute-start | bytes 1572872 | tf_op jit(solution)/shard_map/ppermute | solution.py:110
  93.3 29.3 %collective-permute-start.13 = (bf16[128,2048]{1,0:T(8,128)(2,1)S(1)}, bf16[128,2048]{1,0:T(8,128)(2,1)}, u32[]{:S(2)}, u32[]{:S(2)}) collective-permute-start(bf16[128,2048]{1,0:T(8,128)(2,1)S(1)} %get-tuple-element.238), channel_id=1, source_target_pairs={{0,0},{1,2},{2,1},{3,3},{4,4},{5,6},{6,5},{7,7},{8,8},{9,10},{10,9... | collective-permute-start | bytes 1572872 | tf_op jit(solution)/shard_map/ppermute | solution.py:45
  95.3 27.3 %collective-permute-start.12 = (bf16[128,2048]{1,0:T(8,128)(2,1)S(1)}, bf16[128,2048]{1,0:T(8,128)(2,1)}, u32[]{:S(2)}, u32[]{:S(2)}) collective-permute-start(bf16[128,2048]{1,0:T(8,128)(2,1)S(1)} %get-tuple-element.239), channel_id=1, source_target_pairs={{0,1},{1,0},{2,3},{3,2},{4,5},{5,4},{6,7},{7,6},{8,9},{9,8},{10,11... | collective-permute-start | bytes 1572872 | tf_op jit(solution)/shard_map/ppermute | solution.py:45
  130.7 320.7 %reduce-scatter.5.cloned.1.call-start = ((), (), s32[]{:S(2)}) async-start(), calls=%async_computation.3 | async-start | bytes 5242880 | tf_op jit(solution)/shard_map/reduce_scatter | solution.py:707
  138.9 16.0 %collective-permute-start.17 = (bf16[128,2048]{1,0:T(8,128)(2,1)}, bf16[128,2048]{1,0:T(8,128)(2,1)}, u32[]{:S(2)}, u32[]{:S(2)}) collective-permute-start(bf16[128,2048]{1,0:T(8,128)(2,1)} %get-tuple-element.237), channel_id=1, source_target_pairs={{0,1},{1,0},{2,3},{3,2},{4,5},{5,4},{6,7},{7,6},{8,9},{9,8},{10,11... | collective-permute-start | bytes 1572872 | tf_op jit(solution)/shard_map/ppermute | solution.py:45
  157.8 14.2 %collective-permute-start.19 = (bf16[128,2048]{1,0:T(8,128)(2,1)S(1)}, bf16[128,2048]{1,0:T(8,128)(2,1)S(1)}, u32[]{:S(2)}, u32[]{:S(2)}) collective-permute-start(bf16[128,2048]{1,0:T(8,128)(2,1)S(1)} %get-tuple-element.235), channel_id=1, source_target_pairs={{0,1},{1,0},{2,3},{3,2},{4,5},{5,4},{6,7},{7,6},{8,9},{9,8},{10,11... | collective-permute-start | bytes 1572872 | tf_op jit(solution)/shard_map/ppermute | solution.py:45
  177.4 12.4 %collective-permute-start.21 = (bf16[128,2048]{1,0:T(8,128)(2,1)}, bf16[128,2048]{1,0:T(8,128)(2,1)}, u32[]{:S(2)}, u32[]{:S(2)}) collective-permute-start(bf16[128,2048]{1,0:T(8,128)(2,1)} %base.1), channel_id=1, source_target_pairs={{0,1},{1,0},{2,3},{3,2},{4,5},{5,4},{6,7},{7,6},{8,9},{9,8},{10,11... | collective-permute-start | bytes 1572872 | tf_op jit(solution)/shard_map/ppermute | solution.py:45
  190.0 12.1 %collective-permute-start.23 = (bf16[128,2048]{1,0:T(8,128)(2,1)}, bf16[128,2048]{1,0:T(8,128)(2,1)S(1)}, u32[]{:S(2)}, u32[]{:S(2)}) collective-permute-start(bf16[128,2048]{1,0:T(8,128)(2,1)} %get-tuple-element.122), channel_id=1, source_target_pairs={{0,0},{1,2},{2,1},{3,3},{4,4},{5,6},{6,5},{7,7},{8,8},{9,10},{10,9... | collective-permute-start | bytes 1572872 | tf_op jit(solution)/shard_map/ppermute | solution.py:45
  202.1 13.8 %collective-permute-start.27 = (bf16[128,2048]{1,0:T(8,128)(2,1)S(1)}, bf16[128,2048]{1,0:T(8,128)(2,1)S(1)}, u32[]{:S(2)}, u32[]{:S(2)}) collective-permute-start(bf16[128,2048]{1,0:T(8,128)(2,1)S(1)} %collective-permute-done.23), channel_id=1, source_target_pairs={{0,1},{1,0},{2,3},{3,2},{4,5},{5,4},{6,7},{7,6},{8,9},{9,8},{10,11... | collective-permute-start | bytes 1572872 | tf_op jit(solution)/shard_map/ppermute | solution.py:45
  206.5 19.3 %collective-permute-start.26 = (bf16[128,2048]{1,0:T(8,128)(2,1)S(1)}, bf16[128,2048]{1,0:T(8,128)(2,1)S(1)}, u32[]{:S(2)}, u32[]{:S(2)}) collective-permute-start(bf16[128,2048]{1,0:T(8,128)(2,1)S(1)} %collective-permute-done.25), channel_id=1, source_target_pairs={{0,1},{1,0},{2,3},{3,2},{4,5},{5,4},{6,7},{7,6},{8,9},{9,8},{10,11... | collective-permute-start | bytes 1572872 | tf_op jit(solution)/shard_map/ppermute | solution.py:45
  229.7 22.6 %collective-permute-start.30 = (bf16[128,2048]{1,0:T(8,128)(2,1)}, bf16[128,2048]{1,0:T(8,128)(2,1)}, u32[]{:S(2)}, u32[]{:S(2)}) collective-permute-start(bf16[128,2048]{1,0:T(8,128)(2,1)} %collective-permute-done.21), channel_id=1, source_target_pairs={{0,0},{1,2},{2,1},{3,3},{4,4},{5,6},{6,5},{7,7},{8,8},{9,10},{10,9... | collective-permute-start | bytes 1572872 | tf_op jit(solution)/shard_map/ppermute | solution.py:45
  235.1 17.2 %collective-permute-start.31 = (bf16[128,2048]{1,0:T(8,128)(2,1)}, bf16[128,2048]{1,0:T(8,128)(2,1)}, u32[]{:S(2)}, u32[]{:S(2)}) collective-permute-start(bf16[128,2048]{1,0:T(8,128)(2,1)} %collective-permute-done.22), channel_id=1, source_target_pairs={{0,1},{1,0},{2,3},{3,2},{4,5},{5,4},{6,7},{7,6},{8,9},{9,8},{10,11... | collective-permute-start | bytes 1572872 | tf_op jit(solution)/shard_map/ppermute | solution.py:45
  252.3 14.0 %collective-permute-start.32 = (bf16[128,2048]{1,0:T(8,128)(2,1)}, bf16[128,2048]{1,0:T(8,128)(2,1)S(1)}, u32[]{:S(2)}, u32[]{:S(2)}) collective-permute-start(bf16[128,2048]{1,0:T(8,128)(2,1)} %collective-permute-done.30), channel_id=1, source_target_pairs={{0,1},{1,0},{2,3},{3,2},{4,5},{5,4},{6,7},{7,6},{8,9},{9,8},{10,11... | collective-permute-start | bytes 1572872 | tf_op jit(solution)/shard_map/ppermute | solution.py:45
  253.5 12.9 %collective-permute-start.33 = (bf16[128,2048]{1,0:T(8,128)(2,1)}, bf16[128,2048]{1,0:T(8,128)(2,1)S(1)}, u32[]{:S(2)}, u32[]{:S(2)}) collective-permute-start(bf16[128,2048]{1,0:T(8,128)(2,1)} %collective-permute-done.31), channel_id=1, source_target_pairs={{0,0},{1,2},{2,1},{3,3},{4,4},{5,6},{6,5},{7,7},{8,8},{9,10},{10,9... | collective-permute-start | bytes 1572872 | tf_op jit(solution)/shard_map/ppermute | solution.py:45
  304.5 178.2 %reduce-scatter.3.cloned.1.call-start = ((), (), s32[]{:S(2)}) async-start(), calls=%async_computation.2 | async-start | bytes 10485760 | tf_op jit(solution)/shard_map/reduce_scatter | solution.py:713
  342.1 248.4 %all-gather.14.cloned.1.call-start = ((), (), s32[]{:S(2)}) async-start(), calls=%async_computation.7 | async-start | bytes 9437184 | tf_op jit(solution)/shard_map/all_gather | solution.py:730
  355.3 18.3 %collective-permute-start.43 = (bf16[128,2048]{1,0:T(8,128)(2,1)S(1)}, bf16[128,2048]{1,0:T(8,128)(2,1)S(1)}, u32[]{:S(2)}, u32[]{:S(2)}) collective-permute-start(bf16[128,2048]{1,0:T(8,128)(2,1)S(1)} %get-tuple-element.225), channel_id=1, source_target_pairs={{0,1},{1,0},{2,3},{3,2},{4,5},{5,4},{6,7},{7,6},{8,9},{9,8},{10,11... | collective-permute-start | bytes 1572872 | tf_op jit(solution)/shard_map/ppermute | solution.py:45
  373.8 13.6 %collective-permute-start.47 = (bf16[128,2048]{1,0:T(8,128)(2,1)S(1)}, bf16[128,2048]{1,0:T(8,128)(2,1)S(1)}, u32[]{:S(2)}, u32[]{:S(2)}) collective-permute-start(bf16[128,2048]{1,0:T(8,128)(2,1)S(1)} %get-tuple-element.222), channel_id=1, source_target_pairs={{0,1},{1,0},{2,3},{3,2},{4,5},{5,4},{6,7},{7,6},{8,9},{9,8},{10,11... | collective-permute-start | bytes 1572872 | tf_op jit(solution)/shard_map/ppermute | solution.py:45
  388.4 16.1 %collective-permute-start.45 = (bf16[128,2048]{1,0:T(8,128)(2,1)S(1)}, bf16[128,2048]{1,0:T(8,128)(2,1)S(1)}, u32[]{:S(2)}, u32[]{:S(2)}) collective-permute-start(bf16[128,2048]{1,0:T(8,128)(2,1)S(1)} %get-tuple-element.221), channel_id=1, source_target_pairs={{0,1},{1,0},{2,3},{3,2},{4,5},{5,4},{6,7},{7,6},{8,9},{9,8},{10,11... | collective-permute-start | bytes 1572872 | tf_op jit(solution)/shard_map/ppermute | solution.py:45
  409.9 12.2 %collective-permute-start.50 = (bf16[128,2048]{1,0:T(8,128)(2,1)}, bf16[128,2048]{1,0:T(8,128)(2,1)S(1)}, u32[]{:S(2)}, u32[]{:S(2)}) collective-permute-start(bf16[128,2048]{1,0:T(8,128)(2,1)} %get-tuple-element.137), channel_id=1, source_target_pairs={{0,1},{1,0},{2,3},{3,2},{4,5},{5,4},{6,7},{7,6},{8,9},{9,8},{10,11... | collective-permute-start | bytes 1572872 | tf_op jit(solution)/shard_map/ppermute | solution.py:45
  422.8 14.3 %collective-permute-start.53 = (bf16[128,2048]{1,0:T(8,128)(2,1)S(1)}, bf16[128,2048]{1,0:T(8,128)(2,1)S(1)}, u32[]{:S(2)}, u32[]{:S(2)}) collective-permute-start(bf16[128,2048]{1,0:T(8,128)(2,1)S(1)} %collective-permute-done.49), channel_id=1, source_target_pairs={{0,1},{1,0},{2,3},{3,2},{4,5},{5,4},{6,7},{7,6},{8,9},{9,8},{10,11... | collective-permute-start | bytes 1572872 | tf_op jit(solution)/shard_map/ppermute | solution.py:45
  426.7 19.8 %collective-permute-start.52 = (bf16[128,2048]{1,0:T(8,128)(2,1)S(1)}, bf16[128,2048]{1,0:T(8,128)(2,1)S(1)}, u32[]{:S(2)}, u32[]{:S(2)}) collective-permute-start(bf16[128,2048]{1,0:T(8,128)(2,1)S(1)} %collective-permute-done.51), channel_id=1, source_target_pairs={{0,1},{1,0},{2,3},{3,2},{4,5},{5,4},{6,7},{7,6},{8,9},{9,8},{10,11... | collective-permute-start | bytes 1572872 | tf_op jit(solution)/shard_map/ppermute | solution.py:45
  451.5 207.8 %all-gather.8.cloned.1.call-start = ((), (), s32[]{:S(2)}) async-start(), calls=%async_computation.4 | async-start | bytes 18874368 | tf_op jit(solution)/shard_map/all_gather | solution.py:758
  470.2 12.5 %collective-permute-start.59 = (bf16[4,64,2048]{2,1,0:T(8,128)(2,1)S(1)}, bf16[4,64,2048]{2,1,0:T(8,128)(2,1)}, u32[]{:S(2)}, u32[]{:S(2)}) collective-permute-start(bf16[4,64,2048]{2,1,0:T(8,128)(2,1)S(1)} %dynamic-slice_bitcast_fusion.1), channel_id=1, source_target_pairs={{0,4},{4,0},{1,5},{5,1},{2,6},{6,2},{3,7},{7,3},{8,12},{12,8},{9,1... | collective-permute-start | bytes 3145736 | tf_op jit(solution)/shard_map/ppermute | solution.py:126
  475.5 13.3 %collective-permute-start.58 = (bf16[4,4,64,768]{3,2,1,0:T(8,128)(2,1)}, bf16[4,4,64,768]{3,2,1,0:T(8,128)(2,1)}, u32[]{:S(2)}, u32[]{:S(2)}) collective-permute-start(bf16[4,4,64,768]{3,2,1,0:T(8,128)(2,1)} %dynamic-slice_bitcast_fusion), channel_id=1, source_target_pairs={{0,4},{4,0},{1,5},{5,1},{2,6},{6,2},{3,7},{7,3},{8,12},{12,8},{9,1... | collective-permute-start | bytes 4718600 | tf_op jit(solution)/shard_map/ppermute | solution.py:126
  488.9 23.8 %collective-permute-start.57 = (bf16[128,1024]{1,0:T(8,128)(2,1)S(1)}, bf16[128,1024]{1,0:T(8,128)(2,1)S(1)}, u32[]{:S(2)}, u32[]{:S(2)}) collective-permute-start(bf16[128,1024]{1,0:T(8,128)(2,1)S(1)} %get-tuple-element.240), channel_id=1, source_target_pairs={{0,1},{1,2},{2,3},{3,0},{4,5},{5,6},{6,7},{7,4},{8,9},{9,10},{10,1... | collective-permute-start | bytes 786440 | tf_op jit(solution)/shard_map/ppermute | solution.py:110
  490.1 22.5 %collective-permute-start.61 = (bf16[128,1024]{1,0:T(8,128)(2,1)S(1)}, bf16[128,1024]{1,0:T(8,128)(2,1)S(1)}, u32[]{:S(2)}, u32[]{:S(2)}) collective-permute-start(bf16[128,1024]{1,0:T(8,128)(2,1)S(1)} %get-tuple-element.242), channel_id=1, source_target_pairs={{0,2},{1,3},{2,0},{3,1},{4,6},{5,7},{6,4},{7,5},{8,10},{9,11},{10,... | collective-permute-start | bytes 786440 | tf_op jit(solution)/shard_map/ppermute | solution.py:110
  491.0 21.6 %collective-permute-start.60 = (bf16[128,1024]{1,0:T(8,128)(2,1)S(1)}, bf16[128,1024]{1,0:T(8,128)(2,1)S(1)}, u32[]{:S(2)}, u32[]{:S(2)}) collective-permute-start(bf16[128,1024]{1,0:T(8,128)(2,1)S(1)} %get-tuple-element.243), channel_id=1, source_target_pairs={{0,3},{1,0},{2,1},{3,2},{4,7},{5,4},{6,5},{7,6},{8,11},{9,8},{10,9... | collective-permute-start | bytes 786440 | tf_op jit(solution)/shard_map/ppermute | solution.py:110
  492.7 35.8 %collective-permute-start.56 = (bf16[128,1024]{1,0:T(8,128)(2,1)S(1)}, bf16[128,1024]{1,0:T(8,128)(2,1)S(1)}, u32[]{:S(2)}, u32[]{:S(2)}) collective-permute-start(bf16[128,1024]{1,0:T(8,128)(2,1)S(1)} %get-tuple-element.245), channel_id=1, source_target_pairs={{0,2},{1,3},{2,0},{3,1},{4,6},{5,7},{6,4},{7,5},{8,10},{9,11},{10,... | collective-permute-start | bytes 786440 | tf_op jit(solution)/shard_map/ppermute | solution.py:110
  495.8 32.7 %collective-permute-start.55 = (bf16[128,1024]{1,0:T(8,128)(2,1)S(1)}, bf16[128,1024]{1,0:T(8,128)(2,1)S(1)}, u32[]{:S(2)}, u32[]{:S(2)}) collective-permute-start(bf16[128,1024]{1,0:T(8,128)(2,1)S(1)} %get-tuple-element.246), channel_id=1, source_target_pairs={{0,3},{1,0},{2,1},{3,2},{4,7},{5,4},{6,5},{7,6},{8,11},{9,8},{10,9... | collective-permute-start | bytes 786440 | tf_op jit(solution)/shard_map/ppermute | solution.py:110
  532.6 29.6 %collective-permute-start.65 = (bf16[4,2,64,768]{3,2,1,0:T(8,128)(2,1)}, bf16[4,2,64,768]{3,2,1,0:T(8,128)(2,1)}, u32[]{:S(2)}, u32[]{:S(2)}) collective-permute-start(bf16[4,2,64,768]{3,2,1,0:T(8,128)(2,1)} %dynamic-slice_bitcast_fusion.2), channel_id=1, source_target_pairs={{0,8},{8,0},{16,24},{24,16},{1,9},{9,1},{17,25},{25,17},{2,10},{10... | collective-permute-start | bytes 2359304 | tf_op jit(solution)/shard_map/ppermute | solution.py:126
  535.1 16.7 %collective-permute-start.66 = (bf16[2,64,2048]{2,1,0:T(8,128)(2,1)}, bf16[2,64,2048]{2,1,0:T(8,128)(2,1)}, u32[]{:S(2)}, u32[]{:S(2)}) collective-permute-start(bf16[2,64,2048]{2,1,0:T(8,128)(2,1)} %dynamic-slice_bitcast_fusion.3), channel_id=1, source_target_pairs={{0,16},{8,24},{16,0},{24,8},{1,17},{9,25},{17,1},{25,9},{2,18},{10... | collective-permute-start | bytes 1572872 | tf_op jit(solution)/shard_map/ppermute | solution.py:126
  539.6 22.6 %collective-permute-start.64 = (bf16[128,2048]{1,0:T(8,128)(2,1)}, bf16[128,2048]{1,0:T(8,128)(2,1)}, u32[]{:S(2)}, u32[]{:S(2)}) collective-permute-start(bf16[128,2048]{1,0:T(8,128)(2,1)} %get-tuple-element.218), channel_id=1, source_target_pairs={{0,0},{1,2},{2,1},{3,3},{4,4},{5,6},{6,5},{7,7},{8,8},{9,10},{10,9... | collective-permute-start | bytes 1572872 | tf_op jit(solution)/shard_map/ppermute | solution.py:45
  545.1 17.2 %collective-permute-start.63 = (bf16[128,2048]{1,0:T(8,128)(2,1)}, bf16[128,2048]{1,0:T(8,128)(2,1)}, u32[]{:S(2)}, u32[]{:S(2)}) collective-permute-start(bf16[128,2048]{1,0:T(8,128)(2,1)} %get-tuple-element.219), channel_id=1, source_target_pairs={{0,1},{1,0},{2,3},{3,2},{4,5},{5,4},{6,7},{7,6},{8,9},{9,8},{10,11... | collective-permute-start | bytes 1572872 | tf_op jit(solution)/shard_map/ppermute | solution.py:45
  550.5 29.4 %collective-permute-start.37 = (bf16[128,2048]{1,0:T(8,128)(2,1)S(1)}, bf16[128,2048]{1,0:T(8,128)(2,1)}, u32[]{:S(2)}, u32[]{:S(2)}) collective-permute-start(bf16[128,2048]{1,0:T(8,128)(2,1)S(1)} %get-tuple-element.232), channel_id=1, source_target_pairs={{0,0},{1,2},{2,1},{3,3},{4,4},{5,6},{6,5},{7,7},{8,8},{9,10},{10,9... | collective-permute-start | bytes 1572872 | tf_op jit(solution)/shard_map/ppermute | solution.py:45
  551.9 31.0 %collective-permute-start.36 = (bf16[128,2048]{1,0:T(8,128)(2,1)}, bf16[128,2048]{1,0:T(8,128)(2,1)}, u32[]{:S(2)}, u32[]{:S(2)}) collective-permute-start(bf16[128,2048]{1,0:T(8,128)(2,1)} %get-tuple-element.233), channel_id=1, source_target_pairs={{0,1},{1,0},{2,3},{3,2},{4,5},{5,4},{6,7},{7,6},{8,9},{9,8},{10,11... | collective-permute-start | bytes 1572872 | tf_op jit(solution)/shard_map/ppermute | solution.py:45
  568.2 20.0 %collective-permute-start.68 = (bf16[128,2048]{1,0:T(8,128)(2,1)}, bf16[128,2048]{1,0:T(8,128)(2,1)S(1)}, u32[]{:S(2)}, u32[]{:S(2)}) collective-permute-start(bf16[128,2048]{1,0:T(8,128)(2,1)} %get-tuple-element.216), channel_id=1, source_target_pairs={{0,0},{1,2},{2,1},{3,3},{4,4},{5,6},{6,5},{7,7},{8,8},{9,10},{10,9... | collective-permute-start | bytes 1572872 | tf_op jit(solution)/shard_map/ppermute | solution.py:45
  569.9 18.3 %collective-permute-start.67 = (bf16[128,2048]{1,0:T(8,128)(2,1)}, bf16[128,2048]{1,0:T(8,128)(2,1)}, u32[]{:S(2)}, u32[]{:S(2)}) collective-permute-start(bf16[128,2048]{1,0:T(8,128)(2,1)} %get-tuple-element.217), channel_id=1, source_target_pairs={{0,1},{1,0},{2,3},{3,2},{4,5},{5,4},{6,7},{7,6},{8,9},{9,8},{10,11... | collective-permute-start | bytes 1572872 | tf_op jit(solution)/shard_map/ppermute | solution.py:45
  603.8 12.9 %collective-permute-start.72 = (bf16[128,2048]{1,0:T(8,128)(2,1)}, bf16[128,2048]{1,0:T(8,128)(2,1)S(1)}, u32[]{:S(2)}, u32[]{:S(2)}) collective-permute-start(bf16[128,2048]{1,0:T(8,128)(2,1)} %get-tuple-element.214), channel_id=1, source_target_pairs={{0,0},{1,2},{2,1},{3,3},{4,4},{5,6},{6,5},{7,7},{8,8},{9,10},{10,9... | collective-permute-start | bytes 1572872 | tf_op jit(solution)/shard_map/ppermute | solution.py:45
  605.7 16.4 %collective-permute-start.71 = (bf16[128,2048]{1,0:T(8,128)(2,1)}, bf16[128,2048]{1,0:T(8,128)(2,1)}, u32[]{:S(2)}, u32[]{:S(2)}) collective-permute-start(bf16[128,2048]{1,0:T(8,128)(2,1)} %get-tuple-element.215), channel_id=1, source_target_pairs={{0,1},{1,0},{2,3},{3,2},{4,5},{5,4},{6,7},{7,6},{8,9},{9,8},{10,11... | collective-permute-start | bytes 1572872 | tf_op jit(solution)/shard_map/ppermute | solution.py:45
  612.7 18.5 %collective-permute-start.78 = (bf16[64,768]{1,0:T(8,128)(2,1)}, bf16[64,768]{1,0:T(8,128)(2,1)S(1)}, u32[]{:S(2)}, u32[]{:S(2)}) collective-permute-start(bf16[64,768]{1,0:T(8,128)(2,1)} %get-tuple-element.274), channel_id=1, source_target_pairs={{0,1},{1,2},{2,3},{3,0},{4,5},{5,6},{6,7},{7,4},{8,9},{9,10},{10,1... | collective-permute-start | bytes 294920 | tf_op jit(solution)/shard_map/ppermute | solution.py:110
  612.7 18.5 %collective-permute-start.77 = (bf16[64,768]{1,0:T(8,128)(2,1)}, bf16[64,768]{1,0:T(8,128)(2,1)S(1)}, u32[]{:S(2)}, u32[]{:S(2)}) collective-permute-start(bf16[64,768]{1,0:T(8,128)(2,1)} %get-tuple-element.275), channel_id=1, source_target_pairs={{0,2},{1,3},{2,0},{3,1},{4,6},{5,7},{6,4},{7,5},{8,10},{9,11},{10,... | collective-permute-start | bytes 294920 | tf_op jit(solution)/shard_map/ppermute | solution.py:110
  614.6 16.6 %collective-permute-start.76 = (bf16[64,768]{1,0:T(8,128)(2,1)S(1)}, bf16[64,768]{1,0:T(8,128)(2,1)S(1)}, u32[]{:S(2)}, u32[]{:S(2)}) collective-permute-start(bf16[64,768]{1,0:T(8,128)(2,1)S(1)} %get-tuple-element.276), channel_id=1, source_target_pairs={{0,3},{1,0},{2,1},{3,2},{4,7},{5,4},{6,5},{7,6},{8,11},{9,8},{10,9... | collective-permute-start | bytes 294920 | tf_op jit(solution)/shard_map/ppermute | solution.py:110
  616.7 22.3 %collective-permute-start.39 = (bf16[128,2048]{1,0:T(8,128)(2,1)}, bf16[128,2048]{1,0:T(8,128)(2,1)}, u32[]{:S(2)}, u32[]{:S(2)}) collective-permute-start(bf16[128,2048]{1,0:T(8,128)(2,1)} %get-tuple-element.230), channel_id=1, source_target_pairs={{0,0},{1,2},{2,1},{3,3},{4,4},{5,6},{6,5},{7,7},{8,8},{9,10},{10,9... | collective-permute-start | bytes 1572872 | tf_op jit(solution)/shard_map/ppermute | solution.py:45
  622.1 17.4 %collective-permute-start.38 = (bf16[128,2048]{1,0:T(8,128)(2,1)}, bf16[128,2048]{1,0:T(8,128)(2,1)}, u32[]{:S(2)}, u32[]{:S(2)}) collective-permute-start(bf16[128,2048]{1,0:T(8,128)(2,1)} %get-tuple-element.231), channel_id=1, source_target_pairs={{0,1},{1,0},{2,3},{3,2},{4,5},{5,4},{6,7},{7,6},{8,9},{9,8},{10,11... | collective-permute-start | bytes 1572872 | tf_op jit(solution)/shard_map/ppermute | solution.py:45
  631.5 13.4 %collective-permute-start.81 = (bf16[64,2560]{1,0:T(8,128)(2,1)S(1)}, bf16[64,2560]{1,0:T(8,128)(2,1)}, u32[]{:S(2)}, u32[]{:S(2)}) collective-permute-start(bf16[64,2560]{1,0:T(8,128)(2,1)S(1)} %constant_dynamic-update-slice_fusion.14), channel_id=1, source_target_pairs={{0,16},{8,24},{16,0},{24,8},{1,17},{9,25},{17,1},{25,9},{2,18},{10... | collective-permute-start | bytes 983048 | tf_op jit(solution)/shard_map/ppermute | solution.py:550
  646.9 33.2 %collective-permute-start.86 = (bf16[128,2560]{1,0:T(8,128)(2,1)}, bf16[128,2560]{1,0:T(8,128)(2,1)}, u32[]{:S(2)}, u32[]{:S(2)}) collective-permute-start(bf16[128,2560]{1,0:T(8,128)(2,1)} %pad_maximum_fusion.9), channel_id=1, source_target_pairs={{0,8},{8,0},{16,24},{24,16},{1,9},{9,1},{17,25},{25,17},{2,10},{10... | collective-permute-start | bytes 1966088 | tf_op jit(solution)/shard_map/ppermute | solution.py:550
  648.4 33.1 %collective-permute-start.85 = (bf16[128,2560]{1,0:T(8,128)(2,1)}, bf16[128,2560]{1,0:T(8,128)(2,1)}, u32[]{:S(2)}, u32[]{:S(2)}) collective-permute-start(bf16[128,2560]{1,0:T(8,128)(2,1)} %pad_maximum_fusion.8), channel_id=1, source_target_pairs={{0,16},{8,24},{16,0},{24,8},{1,17},{9,25},{17,1},{25,9},{2,18},{10... | collective-permute-start | bytes 1966088 | tf_op jit(solution)/shard_map/ppermute | solution.py:550
  653.9 33.7 %collective-permute-start.41 = (bf16[128,2048]{1,0:T(8,128)(2,1)}, bf16[128,2048]{1,0:T(8,128)(2,1)}, u32[]{:S(2)}, u32[]{:S(2)}) collective-permute-start(bf16[128,2048]{1,0:T(8,128)(2,1)} %get-tuple-element.226), channel_id=1, source_target_pairs={{0,1},{1,0},{2,3},{3,2},{4,5},{5,4},{6,7},{7,6},{8,9},{9,8},{10,11... | collective-permute-start | bytes 1572872 | tf_op jit(solution)/shard_map/ppermute | solution.py:45
  653.9 34.7 %collective-permute-start.42 = (bf16[128,2048]{1,0:T(8,128)(2,1)}, bf16[128,2048]{1,0:T(8,128)(2,1)}, u32[]{:S(2)}, u32[]{:S(2)}) collective-permute-start(bf16[128,2048]{1,0:T(8,128)(2,1)} %get-tuple-element.227), channel_id=1, source_target_pairs={{0,0},{1,2},{2,1},{3,3},{4,4},{5,6},{6,5},{7,7},{8,8},{9,10},{10,9... | collective-permute-start | bytes 1572872 | tf_op jit(solution)/shard_map/ppermute | solution.py:45
  681.5 13.3 %collective-permute-start.88 = (bf16[256,2560]{1,0:T(8,128)(2,1)S(1)}, bf16[256,2560]{1,0:T(8,128)(2,1)}, u32[]{:S(2)}, u32[]{:S(2)}) collective-permute-start(bf16[256,2560]{1,0:T(8,128)(2,1)S(1)} %pad_maximum_fusion.7.one), channel_id=1, source_target_pairs={{0,4},{4,0},{1,5},{5,1},{2,6},{6,2},{3,7},{7,3},{8,12},{12,8},{9,1... | collective-permute-start | bytes 3932168 | tf_op jit(solution)/shard_map/ppermute | solution.py:33
  684.4 17.6 %collective-permute-start.87 = (bf16[256,2560]{1,0:T(8,128)(2,1)}, bf16[256,2560]{1,0:T(8,128)(2,1)}, u32[]{:S(2)}, u32[]{:S(2)}) collective-permute-start(bf16[256,2560]{1,0:T(8,128)(2,1)} %pad_maximum_fusion.6.one), channel_id=1, source_target_pairs={{0,4},{4,0},{1,5},{5,1},{2,6},{6,2},{3,7},{7,3},{8,12},{12,8},{9,1... | collective-permute-start | bytes 3932168 | tf_op jit(solution)/shard_map/ppermute | solution.py:33
  (91 other events, 1091.6 us)
Sparse Core Ops, SparseCore 0:
  35.1 32.7 all-gather.9
  130.8 92.0 all-gather.11
  304.6 54.2 reduce-scatter.4
  362.6 86.3 reduce-scatter.2
  451.6 55.7 all-gather.13
  530.7 108.4 all-gather.7

commit v6 on v5

--- a/solution.py
+++ b/solution.py
@@ -509,36 +509,45 @@
     )(own)
 
 
-def cast_columns(_, one, two, *outs):
+def cast_columns(_, *refs):
     half = pl.num_programs(0) // 2
-    for own, mine in ((one, pl.program_id(0) < half), (two, pl.program_id(0) >= half)):
-
-        @pl.when(mine)
-        def _(own=own):
-            at = 0
-            for out in outs:
-                out[...] = own[:, at : at + out.shape[1]].astype(F32)
-                at += out.shape[1]
-
-
-def place_columns(order, one, two, widths):
-    blocks = order.shape[0]
-    rows, cols = one.shape
+    for g in range(2):
+        outs = refs[4 + 2 * g : 6 + 2 * g]
+        for own, mine in (
+            (refs[2 * g], pl.program_id(0) < half),
+            (refs[2 * g + 1], pl.program_id(0) >= half),
+        ):
+
+            @pl.when(mine)
+            def _(own=own, outs=outs):
+                at = 0
+                for out in outs:
+                    out[...] = own[:, at : at + out.shape[1]].astype(F32)
+                    at += out.shape[1]
+
+
+def place_columns(orders, pairs, widths):
+    blocks = orders.shape[1]
     half = blocks // 2
+    rows = pairs[0][0].shape[0]
     step = rows // half
+    in_specs, out_specs, out_shape = [], [], []
+    for g, (one, _) in enumerate(pairs):
+        cols = one.shape[1]
+        in_specs += [
+            pl.BlockSpec((step, cols), lambda r, orders: (jnp.minimum(r, half - 1), 0)),
+            pl.BlockSpec((step, cols), lambda r, orders: (jnp.maximum(r - half, 0), 0)),
+        ]
+        for w in widths[g]:
+            out_specs.append(pl.BlockSpec((step, w), lambda r, orders, g=g: (orders[g, r], 0)))
+            out_shape.append(jax.ShapeDtypeStruct((2 * rows, w), F32))
     return pl.pallas_call(
         cast_columns,
         grid_spec=pltpu.PrefetchScalarGridSpec(
-            num_scalar_prefetch=1,
-            grid=(blocks,),
-            in_specs=[
-                pl.BlockSpec((step, cols), lambda r, order: (jnp.minimum(r, half - 1), 0)),
-                pl.BlockSpec((step, cols), lambda r, order: (jnp.maximum(r - half, 0), 0)),
-            ],
-            out_specs=[pl.BlockSpec((step, w), lambda r, order: (order[r], 0)) for w in widths],
+            num_scalar_prefetch=1, grid=(blocks,), in_specs=in_specs, out_specs=out_specs
         ),
-        out_shape=[jax.ShapeDtypeStruct((2 * rows, w), F32) for w in widths],
-    )(order, one, two)
+        out_shape=out_shape,
+    )(orders, *pairs[0], *pairs[1])
 
 
 def gather_stage(halves, step, pin=()):
@@ -795,11 +804,10 @@
             sums = sums + after(swap_cores(sums), att_all)
     sums = small_chips(sums, att_all)
     others = [swap_cores(a) for a in att_all]
-    query_grad, key_grad = place_columns(
-        gathered_order(0), att_all[0], others[0], (q_cols * count, kv_cols * count)
-    )
-    value_grad, out_grad = place_columns(
-        gathered_order(1), att_all[1], others[1], (kv_cols * count, width)
+    query_grad, key_grad, value_grad, out_grad = place_columns(
+        jnp.stack([gathered_order(0), gathered_order(1)]),
+        list(zip(att_all, others)),
+        ((q_cols * count, kv_cols * count), (kv_cols * count, width)),
     )
     return (
         output,

time: 731 us -> 724 us (level)
    unnamed x134 -> x140, local copies, waits for them, and re-layouts: 17.7 us -> 18.8 us
  transfers between devices with their start and end apart: 95 -> 95, of which waited for: 25 -> 24; matrix products, arithmetic and copies ran while one was open for 23% -> 23% of each run, Pallas kernels for 10% -> 9%
where the time goes in v6:
time: 724 us; the launch traced here: 710 us
  waiting for transfers between devices  207 us (29%)
  starting transfers between devices  202 us (28%)
  matrix products  92.7 us (13%)
  Pallas kernels  72 us (10%)
  other arithmetic  67.5 us (9%)
  local copies, waits for them, and re-layouts  52.7 us (7%)
  between operations  16.2 us (2%)
    ppermute x24, waiting for transfers between devices, line_step(): lax.ppermute(first, 'fsdp', even)  118 us
    ppermute x24, starting transfers between devices, line_step(): lax.ppermute(first, 'fsdp', even)  85.9 us
    ppermute x18, waiting for transfers between devices, exchange_line(): lax.ppermute(piece_for((mine - e) % count), 'fsdp', [(i, (i - e) % count)...  69.9 us
    ppermute x24, starting transfers between devices, line_step(): lax.ppermute(second, 'fsdp', odd)  66.4 us
    dot_general x5, matrix products, mm_last(): lax.dot_general(a, b, (((1,), (1,)), ((), ())), preferred_element_type=F32)  40.2 us
    dot_general x5, matrix products, mm(): return jnp.dot(a, b, preferred_element_type=F32)  28 us
    ppermute x18, starting transfers between devices, exchange_line(): lax.ppermute(piece_for((mine - e) % count), 'fsdp', [(i, (i - e) % count)...  25 us
    dot_general x4, matrix products, mm_first(): lax.dot_general(a, b, (((0,), (0,)), ((), ())), preferred_element_type=F32)  24.5 us
  transfers between devices with their start and end apart: 95, of which 24 were waited for; matrix products, arithmetic and copies ran while one was open for 23% of the time, Pallas kernels for 9%

profile of v6, /device:TPU:0, one launch (start us, length us, event | category | flops | bytes accessed | tf_op | source)
XLA Modules:
  0.0 709.7 jit_solution(15841268215556766777)
XLA Ops:
  7.3 3.1 collective-permute-start.1
  10.4 5.4 collective-permute-start
  21.0 13.1 %collective-permute-done.5 = bf16[64,768]{1,0:T(8,128)(2,1)S(1)} collective-permute-done((bf16[64,768]{1,0:T(8,128)(2,1)S(1)}, bf16[64,768]{1,0:T(8,128)(2,1)S(1)}, u32[]{:S(2)}, u32[]{:S(2)}) %collective-permute-start.5) | collective-permute-done | bytes 98336 | tf_op jit(solution)/shard_map/ppermute | solution.py:110
  35.2 5.4 collective-permute-start.2
  43.1 9.2 %collective-permute-done.3 = bf16[128,2048]{1,0:T(8,128)(2,1)} collective-permute-done((bf16[128,2048]{1,0:T(8,128)(2,1)}, bf16[128,2048]{1,0:T(8,128)(2,1)}, u32[]{:S(2)}, u32[]{:S(2)}) %collective-permute-start.3) | collective-permute-done | bytes 524320 | tf_op jit(solution)/shard_map/ppermute | solution.py:45
  57.2 5.4 collective-permute-start.8
  85.7 6.1 shard_map.237
  96.7 25.9 %collective-permute-done.15 = bf16[128,2048]{1,0:T(8,128)(2,1)} collective-permute-done((bf16[128,2048]{1,0:T(8,128)(2,1)}, bf16[128,2048]{1,0:T(8,128)(2,1)}, u32[]{:S(2)}, u32[]{:S(2)}) %collective-permute-start.15) | collective-permute-done | bytes 524320 | tf_op jit(solution)/shard_map/ppermute | solution.py:110
  133.5 5.4 collective-permute-start.18
  138.9 3.9 collective-permute-start.17
  142.8 12.1 %collective-permute-done.17 = bf16[128,2048]{1,0:T(8,128)(2,1)} collective-permute-done((bf16[128,2048]{1,0:T(8,128)(2,1)}, bf16[128,2048]{1,0:T(8,128)(2,1)}, u32[]{:S(2)}, u32[]{:S(2)}) %collective-permute-start.17) | collective-permute-done | bytes 524320 | tf_op jit(solution)/shard_map/ppermute | solution.py:45
  157.8 3.3 collective-permute-start.19
  161.1 10.9 %collective-permute-done.19.right = bf16[128,2048]{1,0:T(8,128)(2,1)S(1)} collective-permute-done((bf16[128,2048]{1,0:T(8,128)(2,1)S(1)}, bf16[128,2048]{1,0:T(8,128)(2,1)S(1)}, u32[]{:S(2)}, u32[]{:S(2)}) %collective-permute-start.19) | collective-permute-done | bytes 524320 | tf_op jit(solution)/shard_map/ppermute | solution.py:45
  172.0 5.4 collective-permute-start.22
  178.0 3.9 shard_map.238
  181.9 7.8 %collective-permute-done.21 = bf16[128,2048]{1,0:T(8,128)(2,1)} collective-permute-done((bf16[128,2048]{1,0:T(8,128)(2,1)}, bf16[128,2048]{1,0:T(8,128)(2,1)}, u32[]{:S(2)}, u32[]{:S(2)}) %collective-permute-start.21) | collective-permute-done | bytes 524320 | tf_op jit(solution)/shard_map/ppermute | solution.py:45
  191.7 9.3 %collective-permute-done.24 = bf16[128,2048]{1,0:T(8,128)(2,1)S(1)} collective-permute-done((bf16[128,2048]{1,0:T(8,128)(2,1)}, bf16[128,2048]{1,0:T(8,128)(2,1)S(1)}, u32[]{:S(2)}, u32[]{:S(2)}) %collective-permute-start.24) | collective-permute-done | bytes 524320 | tf_op jit(solution)/shard_map/ppermute | solution.py:45
  202.1 4.4 collective-permute-start.27
  206.5 9.4 %collective-permute-start.26 = (bf16[128,2048]{1,0:T(8,128)(2,1)S(1)}, bf16[128,2048]{1,0:T(8,128)(2,1)S(1)}, u32[]{:S(2)}, u32[]{:S(2)}) collective-permute-start(bf16[128,2048]{1,0:T(8,128)(2,1)S(1)} %collective-permute-done.25), channel_id=1, source_target_pairs={{0,1},{1,0},{2,3},{3,2},{4,5},{5,4},{6,7},{7,6},{8,9},{9,8},{10,11... | collective-permute-start | bytes 1572872 | tf_op jit(solution)/shard_map/ppermute | solution.py:45
  218.5 7.3 %collective-permute-done.26 = bf16[128,2048]{1,0:T(8,128)(2,1)S(1)} collective-permute-done((bf16[128,2048]{1,0:T(8,128)(2,1)S(1)}, bf16[128,2048]{1,0:T(8,128)(2,1)S(1)}, u32[]{:S(2)}, u32[]{:S(2)}) %collective-permute-start.26) | collective-permute-done | bytes 524320 | tf_op jit(solution)/shard_map/ppermute | solution.py:45
  229.7 5.4 collective-permute-start.30
  237.9 14.5 %fusion.79 = f32[1024,2048]{1,0:T(8,128)} fusion(bf16[1024,2048]{1,0:T(8,128)(2,1)} %constant_dynamic-update-slice_fusion, bf16[2048,2048]{1,0:T(8,128)(2,1)} %bitcast.299), kind=kOutput, calls=%fused_computation.253 | convolution fusion | flops 8589934592 | bytes 20971520 | tf_op jit(solution)/shard_map/dot_general | solution.py:21
  256.2 10.1 %collective-permute-done.32 = bf16[128,2048]{1,0:T(8,128)(2,1)S(1)} collective-permute-done((bf16[128,2048]{1,0:T(8,128)(2,1)}, bf16[128,2048]{1,0:T(8,128)(2,1)S(1)}, u32[]{:S(2)}, u32[]{:S(2)}) %collective-permute-start.32) | collective-permute-done | bytes 524320 | tf_op jit(solution)/shard_map/ppermute | solution.py:45
  275.2 4.5 collective-permute-done.34
  279.7 3.2 constant_dynamic-update-slice_fusion.5
  282.8 14.1 %multiply_convert_fusion = (bf16[1024,1024]{1,0:T(8,128)(2,1)}, bf16[1024,1024]{1,0:T(8,128)(2,1)}, bf16[1024,1024]{1,0:T(8,128)(2,1)S(1)}) fusion(f32[1024,2048]{1,0:T(8,128)} %fusion.79, bf16[1024,2048]{1,0:T(8,128)(2,1)} %constant_dynamic-update-slice_fusion.5, bf16[2048,2048]{1,0:T(8,128)(2,1)} %param.26, s32[]{:T(128)S(6)} %select_n.652), kind=kOutput, calls=%fused_computation.13 | convolution fusion | flops 4310695936 | bytes 23068676 | tf_op jit(solution)/shard_map/dot_general | solution.py:25
  298.2 6.2 convolution_convert_fusion.1
  306.4 6.0 fusion.13
  314.1 9.7 %convolution_convert_fusion.4 = bf16[512,2048]{1,0:T(8,128)(2,1)} fusion(bf16[512,2048]{1,0:T(8,128)(2,1)S(1)} %get-tuple-element.128, bf16[2048,2048]{1,0:T(8,128)(2,1)} %bitcast.300), kind=kOutput, calls=%fused_computation.30 | convolution fusion | flops 4296015872 | bytes 12582912 | tf_op jit(solution)/shard_map/dot_general | solution.py:25
  324.2 4.4 convert_add_fusion.1
  328.6 13.4 %convolution_convert_fusion = bf16[2048,2048]{1,0:T(8,128)(2,1)} fusion(bf16[1024,2048]{1,0:T(8,128)(2,1)} %constant_dynamic-update-slice_fusion, bf16[1024,2048]{1,0:T(8,128)(2,1)S(1)} %pad_maximum_fusion), kind=kOutput, calls=%fused_computation | convolution fusion | flops 8594128896 | bytes 16777216 | tf_op jit(solution)/shard_map/dot_general | solution.py:29
  342.8 4.0 collective-permute-done.40
  346.8 7.6 %convert_add_fusion = f32[512,2048]{1,0:T(8,128)S(1)} fusion(bf16[512,2048]{1,0:T(8,128)(2,1)S(1)} %collective-permute-done.40, bf16[512,2048]{1,0:T(8,128)(2,1)} %get-tuple-element.133, bf16[2048,2048]{1,0:T(8,128)(2,1)} %bitcast.301), kind=kOutput, calls=%fused_computation.11 | convolution fusion | flops 4297064448 | bytes 16777216 | tf_op jit(solution)/shard_map/dot_general | solution.py:25
  355.3 6.1 collective-permute-start.43
  361.4 12.2 %collective-permute-done.43 = bf16[128,2048]{1,0:T(8,128)(2,1)S(1)} collective-permute-done((bf16[128,2048]{1,0:T(8,128)(2,1)S(1)}, bf16[128,2048]{1,0:T(8,128)(2,1)S(1)}, u32[]{:S(2)}, u32[]{:S(2)}) %collective-permute-start.43) | collective-permute-done | bytes 524320 | tf_op jit(solution)/shard_map/ppermute | solution.py:45
  376.3 11.1 %collective-permute-done.47 = bf16[128,2048]{1,0:T(8,128)(2,1)S(1)} collective-permute-done((bf16[128,2048]{1,0:T(8,128)(2,1)S(1)}, bf16[128,2048]{1,0:T(8,128)(2,1)S(1)}, u32[]{:S(2)}, u32[]{:S(2)}) %collective-permute-start.47) | collective-permute-done | bytes 524320 | tf_op jit(solution)/shard_map/ppermute | solution.py:45
  388.4 6.0 collective-permute-start.45
  394.4 10.3 %collective-permute-done.45.right = bf16[128,2048]{1,0:T(8,128)(2,1)S(1)} collective-permute-done((bf16[128,2048]{1,0:T(8,128)(2,1)S(1)}, bf16[128,2048]{1,0:T(8,128)(2,1)S(1)}, u32[]{:S(2)}, u32[]{:S(2)}) %collective-permute-start.45) | collective-permute-done | bytes 524320 | tf_op jit(solution)/shard_map/ppermute | solution.py:45
  405.5 4.7 shard_map.239
  413.8 8.3 %collective-permute-done.50 = bf16[128,2048]{1,0:T(8,128)(2,1)S(1)} collective-permute-done((bf16[128,2048]{1,0:T(8,128)(2,1)}, bf16[128,2048]{1,0:T(8,128)(2,1)S(1)}, u32[]{:S(2)}, u32[]{:S(2)}) %collective-permute-start.50) | collective-permute-done | bytes 524320 | tf_op jit(solution)/shard_map/ppermute | solution.py:45
  422.8 4.1 collective-permute-start.53
  426.9 10.3 %collective-permute-start.52 = (bf16[128,2048]{1,0:T(8,128)(2,1)S(1)}, bf16[128,2048]{1,0:T(8,128)(2,1)S(1)}, u32[]{:S(2)}, u32[]{:S(2)}) collective-permute-start(bf16[128,2048]{1,0:T(8,128)(2,1)S(1)} %collective-permute-done.51), channel_id=1, source_target_pairs={{0,1},{1,0},{2,3},{3,2},{4,5},{5,4},{6,7},{7,6},{8,9},{9,8},{10,11... | collective-permute-start | bytes 1572872 | tf_op jit(solution)/shard_map/ppermute | solution.py:45
  437.9 8.9 %collective-permute-done.52 = bf16[128,2048]{1,0:T(8,128)(2,1)S(1)} collective-permute-done((bf16[128,2048]{1,0:T(8,128)(2,1)S(1)}, bf16[128,2048]{1,0:T(8,128)(2,1)S(1)}, u32[]{:S(2)}, u32[]{:S(2)}) %collective-permute-start.52) | collective-permute-done | bytes 524320 | tf_op jit(solution)/shard_map/ppermute | solution.py:45
  457.8 12.6 %shard_map.240 = (bf16[512,768]{1,0:T(8,128)(2,1)S(1)}, f32[1,128]{1,0:T(1,128)S(1)}, f32[1,128]{1,0:T(1,128)S(1)}) custom-call(f32[512,768]{1,0:T(8,128)S(1)} %copy-done.2, f32[512,768]{1,0:T(8,128)S(1)} %copy-done.2, f32[512,768]{1,0:T(8,128)S(1)} %copy-done.2, f32[512,512]{1,0:T(8,128)S(1)} %and_select_fusion.bias, f32[512,128]{1,0:T(8,128)S(1)} %copy.64.cosine.cos_own, ...), custom_call_target="tpu_custom_call" | custom-call | tf_op jit(solution)/shard_map/pallas_call | solution.py:378
  476.3 6.7 fusion.80.part
  496.2 3.0 fusion.10
  499.3 13.6 %collective-permute-done.61 = bf16[128,1024]{1,0:T(8,128)(2,1)S(1)} collective-permute-done((bf16[128,1024]{1,0:T(8,128)(2,1)S(1)}, bf16[128,1024]{1,0:T(8,128)(2,1)S(1)}, u32[]{:S(2)}, u32[]{:S(2)}) %collective-permute-start.61) | collective-permute-done | bytes 262176 | tf_op jit(solution)/shard_map/ppermute | solution.py:110
  512.9 15.9 %collective-permute-done.56 = bf16[128,1024]{1,0:T(8,128)(2,1)S(1)} collective-permute-done((bf16[128,1024]{1,0:T(8,128)(2,1)S(1)}, bf16[128,1024]{1,0:T(8,128)(2,1)S(1)}, u32[]{:S(2)}, u32[]{:S(2)}) %collective-permute-start.56) | collective-permute-done | bytes 262176 | tf_op jit(solution)/shard_map/ppermute | solution.py:110
  539.9 5.4 collective-permute-start.64
  545.3 3.0 collective-permute-start.63
  552.1 10.3 %collective-permute-start.36 = (bf16[128,2048]{1,0:T(8,128)(2,1)}, bf16[128,2048]{1,0:T(8,128)(2,1)}, u32[]{:S(2)}, u32[]{:S(2)}) collective-permute-start(bf16[128,2048]{1,0:T(8,128)(2,1)} %get-tuple-element.233), channel_id=1, source_target_pairs={{0,1},{1,0},{2,3},{3,2},{4,5},{5,4},{6,7},{7,6},{8,9},{9,8},{10,11... | collective-permute-start | bytes 1572872 | tf_op jit(solution)/shard_map/ppermute | solution.py:45
  565.6 2.9 fusion.28
  570.2 6.8 collective-permute-start.67
  583.2 5.4 collective-permute-done.70
  590.9 10.3 %shard_map.241 = f32[2048,2048]{1,0:T(8,128)} custom-call(bf16[8,256,2048]{2,1,0:T(8,128)(2,1)} %bitcast.274), custom_call_target="tpu_custom_call" | custom-call | tf_op jit(solution)/shard_map/pallas_call | solution.py:580
  601.2 3.0 fusion.25
  616.9 5.4 collective-permute-start.39
  622.3 4.5 collective-permute-start.38
  626.8 4.5 shard_map.242
  651.1 3.1 fusion.35
  654.2 5.4 collective-permute-start.42
  659.6 10.4 %shard_map.244 = f32[512,8192]{1,0:T(8,128)} custom-call(bf16[4,2,4,128,2048]{4,3,2,1,0:T(8,128)(2,1)} %bitcast.266), custom_call_target="tpu_custom_call" | custom-call | tf_op jit(solution)/shard_map/pallas_call | solution.py:503
  670.0 10.4 %shard_map.243 = f32[512,8192]{1,0:T(8,128)} custom-call(bf16[4,2,4,128,2048]{4,3,2,1,0:T(8,128)(2,1)} %bitcast.267), custom_call_target="tpu_custom_call" | custom-call | tf_op jit(solution)/shard_map/pallas_call | solution.py:503
  693.2 9.1 %shard_map.245 = (f32[512,2048]{1,0:T(8,128)}, f32[512,512]{1,0:T(8,128)}, f32[512,512]{1,0:T(8,128)}, f32[512,2048]{1,0:T(8,128)}) custom-call(s32[2,8]{1,0:T(2,128)} %pad_add_fusion._, bf16[256,2560]{1,0:T(8,128)(2,1)} %copy-done.16, bf16[256,2560]{1,0:T(8,128)(2,1)} %copy-done.43, bf16[256,2560]{1,0:T(8,128)(2,1)} %copy-done.17, ...), custom_call_target="tpu_custom_call" | custom-call | tf_op jit(solution)/shard_map/pallas_call | solution.py:544
  (433 shorter events, 200.1 us)
Async XLA Ops:
  7.2 74.1 %all-gather.10.cloned.1.call-start = ((), (), s32[]{:S(2)}) async-start(), calls=%async_computation.5 | async-start | bytes 3538944 | tf_op jit(solution)/shard_map/all_gather | solution.py:641
  7.3 26.8 %collective-permute-start.1 = (bf16[128,2048]{1,0:T(8,128)(2,1)}, bf16[128,2048]{1,0:T(8,128)(2,1)}, u32[]{:S(2)}, u32[]{:S(2)}) collective-permute-start(bf16[128,2048]{1,0:T(8,128)(2,1)} %wide.1), channel_id=1, source_target_pairs={{0,1},{1,0},{2,3},{3,2},{4,5},{5,4},{6,7},{7,6},{8,9},{9,8},{10,11... | collective-permute-start | bytes 1572872 | tf_op jit(solution)/shard_map/ppermute | solution.py:45
  10.4 23.7 %collective-permute-start = (bf16[128,2048]{1,0:T(8,128)(2,1)}, bf16[128,2048]{1,0:T(8,128)(2,1)}, u32[]{:S(2)}, u32[]{:S(2)}) collective-permute-start(bf16[128,2048]{1,0:T(8,128)(2,1)} %wide.1), channel_id=1, source_target_pairs={{0,0},{1,2},{2,1},{3,3},{4,4},{5,6},{6,5},{7,7},{8,8},{9,10},{10,9... | collective-permute-start | bytes 1572872 | tf_op jit(solution)/shard_map/ppermute | solution.py:45
  17.6 16.5 %collective-permute-start.5 = (bf16[64,768]{1,0:T(8,128)(2,1)S(1)}, bf16[64,768]{1,0:T(8,128)(2,1)S(1)}, u32[]{:S(2)}, u32[]{:S(2)}) collective-permute-start(bf16[64,768]{1,0:T(8,128)(2,1)S(1)} %pad_maximum_fusion.19), channel_id=1, source_target_pairs={{0,2},{1,3},{2,0},{3,1},{4,6},{5,7},{6,4},{7,5},{8,10},{9,11},{10,... | collective-permute-start | bytes 294920 | tf_op jit(solution)/shard_map/ppermute | solution.py:110
  17.7 16.4 %collective-permute-start.4 = (bf16[64,768]{1,0:T(8,128)(2,1)S(1)}, bf16[64,768]{1,0:T(8,128)(2,1)S(1)}, u32[]{:S(2)}, u32[]{:S(2)}) collective-permute-start(bf16[64,768]{1,0:T(8,128)(2,1)S(1)} %pad_maximum_fusion.18), channel_id=1, source_target_pairs={{0,3},{1,0},{2,1},{3,2},{4,7},{5,4},{6,5},{7,6},{8,11},{9,8},{10,9... | collective-permute-start | bytes 294920 | tf_op jit(solution)/shard_map/ppermute | solution.py:110
  20.4 13.7 %collective-permute-start.6 = (bf16[64,768]{1,0:T(8,128)(2,1)S(1)}, bf16[64,768]{1,0:T(8,128)(2,1)S(1)}, u32[]{:S(2)}, u32[]{:S(2)}) collective-permute-start(bf16[64,768]{1,0:T(8,128)(2,1)S(1)} %pad_maximum_fusion.20), channel_id=1, source_target_pairs={{0,1},{1,2},{2,3},{3,0},{4,5},{5,6},{6,7},{7,4},{8,9},{9,10},{10,1... | collective-permute-start | bytes 294920 | tf_op jit(solution)/shard_map/ppermute | solution.py:110
  35.0 202.8 %all-gather.12.cloned.1.call-start = ((), (), s32[]{:S(2)}) async-start(), calls=%async_computation.6 | async-start | bytes 10485760 | tf_op jit(solution)/shard_map/all_gather | solution.py:693
  40.5 11.8 %collective-permute-start.3 = (bf16[128,2048]{1,0:T(8,128)(2,1)}, bf16[128,2048]{1,0:T(8,128)(2,1)}, u32[]{:S(2)}, u32[]{:S(2)}) collective-permute-start(bf16[128,2048]{1,0:T(8,128)(2,1)} %collective-permute-done), channel_id=1, source_target_pairs={{0,1},{1,0},{2,3},{3,2},{4,5},{5,4},{6,7},{7,6},{8,9},{9,8},{10,11... | collective-permute-start | bytes 1572872 | tf_op jit(solution)/shard_map/ppermute | solution.py:45
  52.3 13.1 %collective-permute-start.11 = (bf16[1056]{0:T(1024)(128)(2,1)S(1)}, bf16[1056]{0:T(1024)(128)(2,1)S(1)}, u32[]{:S(2)}, u32[]{:S(2)}) collective-permute-start(bf16[1056]{0:T(1024)(128)(2,1)S(1)} %concatenate.92), channel_id=1, source_target_pairs={{0,1},{1,2},{2,3},{3,0},{4,5},{5,6},{6,7},{7,4},{8,9},{9,10},{10,1... | collective-permute-start | bytes 6344 | tf_op jit(solution)/shard_map/ppermute | solution.py:110
  52.7 12.5 %collective-permute-start.10 = (bf16[1056]{0:T(1024)(128)(2,1)S(1)}, bf16[1056]{0:T(1024)(128)(2,1)S(1)}, u32[]{:S(2)}, u32[]{:S(2)}) collective-permute-start(bf16[1056]{0:T(1024)(128)(2,1)S(1)} %concatenate.92), channel_id=1, source_target_pairs={{0,2},{1,3},{2,0},{3,1},{4,6},{5,7},{6,4},{7,5},{8,10},{9,11},{10,... | collective-permute-start | bytes 6344 | tf_op jit(solution)/shard_map/ppermute | solution.py:110
  71.5 25.2 %collective-permute-start.14 = (bf16[128,2048]{1,0:T(8,128)(2,1)}, bf16[128,2048]{1,0:T(8,128)(2,1)}, u32[]{:S(2)}, u32[]{:S(2)}) collective-permute-start(bf16[128,2048]{1,0:T(8,128)(2,1)} %pad_maximum_fusion.11), channel_id=1, source_target_pairs={{0,3},{1,0},{2,1},{3,2},{4,7},{5,4},{6,5},{7,6},{8,11},{9,8},{10,9... | collective-permute-start | bytes 1572872 | tf_op jit(solution)/shard_map/ppermute | solution.py:110
  74.5 48.2 %collective-permute-start.15 = (bf16[128,2048]{1,0:T(8,128)(2,1)}, bf16[128,2048]{1,0:T(8,128)(2,1)}, u32[]{:S(2)}, u32[]{:S(2)}) collective-permute-start(bf16[128,2048]{1,0:T(8,128)(2,1)} %pad_maximum_fusion.12), channel_id=1, source_target_pairs={{0,2},{1,3},{2,0},{3,1},{4,6},{5,7},{6,4},{7,5},{8,10},{9,11},{10,... | collective-permute-start | bytes 1572872 | tf_op jit(solution)/shard_map/ppermute | solution.py:110
  78.1 44.6 %collective-permute-start.16 = (bf16[128,2048]{1,0:T(8,128)(2,1)}, bf16[128,2048]{1,0:T(8,128)(2,1)}, u32[]{:S(2)}, u32[]{:S(2)}) collective-permute-start(bf16[128,2048]{1,0:T(8,128)(2,1)} %pad_maximum_fusion.13), channel_id=1, source_target_pairs={{0,1},{1,2},{2,3},{3,0},{4,5},{5,6},{6,7},{7,4},{8,9},{9,10},{10,1... | collective-permute-start | bytes 1572872 | tf_op jit(solution)/shard_map/ppermute | solution.py:110
  93.3 29.4 %collective-permute-start.13 = (bf16[128,2048]{1,0:T(8,128)(2,1)S(1)}, bf16[128,2048]{1,0:T(8,128)(2,1)}, u32[]{:S(2)}, u32[]{:S(2)}) collective-permute-start(bf16[128,2048]{1,0:T(8,128)(2,1)S(1)} %get-tuple-element.238), channel_id=1, source_target_pairs={{0,0},{1,2},{2,1},{3,3},{4,4},{5,6},{6,5},{7,7},{8,8},{9,10},{10,9... | collective-permute-start | bytes 1572872 | tf_op jit(solution)/shard_map/ppermute | solution.py:45
  95.3 27.4 %collective-permute-start.12 = (bf16[128,2048]{1,0:T(8,128)(2,1)S(1)}, bf16[128,2048]{1,0:T(8,128)(2,1)}, u32[]{:S(2)}, u32[]{:S(2)}) collective-permute-start(bf16[128,2048]{1,0:T(8,128)(2,1)S(1)} %get-tuple-element.239), channel_id=1, source_target_pairs={{0,1},{1,0},{2,3},{3,2},{4,5},{5,4},{6,7},{7,6},{8,9},{9,8},{10,11... | collective-permute-start | bytes 1572872 | tf_op jit(solution)/shard_map/ppermute | solution.py:45
  130.7 321.1 %reduce-scatter.5.cloned.1.call-start = ((), (), s32[]{:S(2)}) async-start(), calls=%async_computation.3 | async-start | bytes 5242880 | tf_op jit(solution)/shard_map/reduce_scatter | solution.py:716
  138.9 16.0 %collective-permute-start.17 = (bf16[128,2048]{1,0:T(8,128)(2,1)}, bf16[128,2048]{1,0:T(8,128)(2,1)}, u32[]{:S(2)}, u32[]{:S(2)}) collective-permute-start(bf16[128,2048]{1,0:T(8,128)(2,1)} %get-tuple-element.237), channel_id=1, source_target_pairs={{0,1},{1,0},{2,3},{3,2},{4,5},{5,4},{6,7},{7,6},{8,9},{9,8},{10,11... | collective-permute-start | bytes 1572872 | tf_op jit(solution)/shard_map/ppermute | solution.py:45
  157.8 14.2 %collective-permute-start.19 = (bf16[128,2048]{1,0:T(8,128)(2,1)S(1)}, bf16[128,2048]{1,0:T(8,128)(2,1)S(1)}, u32[]{:S(2)}, u32[]{:S(2)}) collective-permute-start(bf16[128,2048]{1,0:T(8,128)(2,1)S(1)} %get-tuple-element.235), channel_id=1, source_target_pairs={{0,1},{1,0},{2,3},{3,2},{4,5},{5,4},{6,7},{7,6},{8,9},{9,8},{10,11... | collective-permute-start | bytes 1572872 | tf_op jit(solution)/shard_map/ppermute | solution.py:45
  177.4 12.3 %collective-permute-start.21 = (bf16[128,2048]{1,0:T(8,128)(2,1)}, bf16[128,2048]{1,0:T(8,128)(2,1)}, u32[]{:S(2)}, u32[]{:S(2)}) collective-permute-start(bf16[128,2048]{1,0:T(8,128)(2,1)} %base.1), channel_id=1, source_target_pairs={{0,1},{1,0},{2,3},{3,2},{4,5},{5,4},{6,7},{7,6},{8,9},{9,8},{10,11... | collective-permute-start | bytes 1572872 | tf_op jit(solution)/shard_map/ppermute | solution.py:45
  190.0 12.1 %collective-permute-start.23 = (bf16[128,2048]{1,0:T(8,128)(2,1)}, bf16[128,2048]{1,0:T(8,128)(2,1)S(1)}, u32[]{:S(2)}, u32[]{:S(2)}) collective-permute-start(bf16[128,2048]{1,0:T(8,128)(2,1)} %get-tuple-element.122), channel_id=1, source_target_pairs={{0,0},{1,2},{2,1},{3,3},{4,4},{5,6},{6,5},{7,7},{8,8},{9,10},{10,9... | collective-permute-start | bytes 1572872 | tf_op jit(solution)/shard_map/ppermute | solution.py:45
  202.1 13.8 %collective-permute-start.27 = (bf16[128,2048]{1,0:T(8,128)(2,1)S(1)}, bf16[128,2048]{1,0:T(8,128)(2,1)S(1)}, u32[]{:S(2)}, u32[]{:S(2)}) collective-permute-start(bf16[128,2048]{1,0:T(8,128)(2,1)S(1)} %collective-permute-done.23), channel_id=1, source_target_pairs={{0,1},{1,0},{2,3},{3,2},{4,5},{5,4},{6,7},{7,6},{8,9},{9,8},{10,11... | collective-permute-start | bytes 1572872 | tf_op jit(solution)/shard_map/ppermute | solution.py:45
  206.5 19.3 %collective-permute-start.26 = (bf16[128,2048]{1,0:T(8,128)(2,1)S(1)}, bf16[128,2048]{1,0:T(8,128)(2,1)S(1)}, u32[]{:S(2)}, u32[]{:S(2)}) collective-permute-start(bf16[128,2048]{1,0:T(8,128)(2,1)S(1)} %collective-permute-done.25), channel_id=1, source_target_pairs={{0,1},{1,0},{2,3},{3,2},{4,5},{5,4},{6,7},{7,6},{8,9},{9,8},{10,11... | collective-permute-start | bytes 1572872 | tf_op jit(solution)/shard_map/ppermute | solution.py:45
  229.7 22.7 %collective-permute-start.30 = (bf16[128,2048]{1,0:T(8,128)(2,1)}, bf16[128,2048]{1,0:T(8,128)(2,1)}, u32[]{:S(2)}, u32[]{:S(2)}) collective-permute-start(bf16[128,2048]{1,0:T(8,128)(2,1)} %collective-permute-done.21), channel_id=1, source_target_pairs={{0,0},{1,2},{2,1},{3,3},{4,4},{5,6},{6,5},{7,7},{8,8},{9,10},{10,9... | collective-permute-start | bytes 1572872 | tf_op jit(solution)/shard_map/ppermute | solution.py:45
  235.0 17.3 %collective-permute-start.31 = (bf16[128,2048]{1,0:T(8,128)(2,1)}, bf16[128,2048]{1,0:T(8,128)(2,1)}, u32[]{:S(2)}, u32[]{:S(2)}) collective-permute-start(bf16[128,2048]{1,0:T(8,128)(2,1)} %collective-permute-done.22), channel_id=1, source_target_pairs={{0,1},{1,0},{2,3},{3,2},{4,5},{5,4},{6,7},{7,6},{8,9},{9,8},{10,11... | collective-permute-start | bytes 1572872 | tf_op jit(solution)/shard_map/ppermute | solution.py:45
  252.3 14.0 %collective-permute-start.32 = (bf16[128,2048]{1,0:T(8,128)(2,1)}, bf16[128,2048]{1,0:T(8,128)(2,1)S(1)}, u32[]{:S(2)}, u32[]{:S(2)}) collective-permute-start(bf16[128,2048]{1,0:T(8,128)(2,1)} %collective-permute-done.30), channel_id=1, source_target_pairs={{0,1},{1,0},{2,3},{3,2},{4,5},{5,4},{6,7},{7,6},{8,9},{9,8},{10,11... | collective-permute-start | bytes 1572872 | tf_op jit(solution)/shard_map/ppermute | solution.py:45
  253.4 12.9 %collective-permute-start.33 = (bf16[128,2048]{1,0:T(8,128)(2,1)}, bf16[128,2048]{1,0:T(8,128)(2,1)S(1)}, u32[]{:S(2)}, u32[]{:S(2)}) collective-permute-start(bf16[128,2048]{1,0:T(8,128)(2,1)} %collective-permute-done.31), channel_id=1, source_target_pairs={{0,0},{1,2},{2,1},{3,3},{4,4},{5,6},{6,5},{7,7},{8,8},{9,10},{10,9... | collective-permute-start | bytes 1572872 | tf_op jit(solution)/shard_map/ppermute | solution.py:45
  304.5 178.5 %reduce-scatter.3.cloned.1.call-start = ((), (), s32[]{:S(2)}) async-start(), calls=%async_computation.2 | async-start | bytes 10485760 | tf_op jit(solution)/shard_map/reduce_scatter | solution.py:722
  312.4 11.8 %collective-permute-start.35 = (bf16[512,2048]{1,0:T(8,128)(2,1)}, bf16[512,2048]{1,0:T(8,128)(2,1)S(1)}, u32[]{:S(2)}, u32[]{:S(2)}) collective-permute-start(bf16[512,2048]{1,0:T(8,128)(2,1)} %fusion.13), channel_id=1, source_target_pairs={{0,4},{4,0},{1,5},{5,1},{2,6},{6,2},{3,7},{7,3},{8,12},{12,8},{9,1... | collective-permute-start | bytes 6291464 | tf_op jit(solution)/shard_map/ppermute | solution.py:33
  342.1 248.8 %all-gather.14.cloned.1.call-start = ((), (), s32[]{:S(2)}) async-start(), calls=%async_computation.7 | async-start | bytes 9437184 | tf_op jit(solution)/shard_map/all_gather | solution.py:739
  355.3 18.2 %collective-permute-start.43 = (bf16[128,2048]{1,0:T(8,128)(2,1)S(1)}, bf16[128,2048]{1,0:T(8,128)(2,1)S(1)}, u32[]{:S(2)}, u32[]{:S(2)}) collective-permute-start(bf16[128,2048]{1,0:T(8,128)(2,1)S(1)} %get-tuple-element.225), channel_id=1, source_target_pairs={{0,1},{1,0},{2,3},{3,2},{4,5},{5,4},{6,7},{7,6},{8,9},{9,8},{10,11... | collective-permute-start | bytes 1572872 | tf_op jit(solution)/shard_map/ppermute | solution.py:45
  373.8 13.6 %collective-permute-start.47 = (bf16[128,2048]{1,0:T(8,128)(2,1)S(1)}, bf16[128,2048]{1,0:T(8,128)(2,1)S(1)}, u32[]{:S(2)}, u32[]{:S(2)}) collective-permute-start(bf16[128,2048]{1,0:T(8,128)(2,1)S(1)} %get-tuple-element.222), channel_id=1, source_target_pairs={{0,1},{1,0},{2,3},{3,2},{4,5},{5,4},{6,7},{7,6},{8,9},{9,8},{10,11... | collective-permute-start | bytes 1572872 | tf_op jit(solution)/shard_map/ppermute | solution.py:45
  388.4 16.3 %collective-permute-start.45 = (bf16[128,2048]{1,0:T(8,128)(2,1)S(1)}, bf16[128,2048]{1,0:T(8,128)(2,1)S(1)}, u32[]{:S(2)}, u32[]{:S(2)}) collective-permute-start(bf16[128,2048]{1,0:T(8,128)(2,1)S(1)} %get-tuple-element.221), channel_id=1, source_target_pairs={{0,1},{1,0},{2,3},{3,2},{4,5},{5,4},{6,7},{7,6},{8,9},{9,8},{10,11... | collective-permute-start | bytes 1572872 | tf_op jit(solution)/shard_map/ppermute | solution.py:45
  410.2 11.9 %collective-permute-start.50 = (bf16[128,2048]{1,0:T(8,128)(2,1)}, bf16[128,2048]{1,0:T(8,128)(2,1)S(1)}, u32[]{:S(2)}, u32[]{:S(2)}) collective-permute-start(bf16[128,2048]{1,0:T(8,128)(2,1)} %get-tuple-element.137), channel_id=1, source_target_pairs={{0,1},{1,0},{2,3},{3,2},{4,5},{5,4},{6,7},{7,6},{8,9},{9,8},{10,11... | collective-permute-start | bytes 1572872 | tf_op jit(solution)/shard_map/ppermute | solution.py:45
  422.8 14.3 %collective-permute-start.53 = (bf16[128,2048]{1,0:T(8,128)(2,1)S(1)}, bf16[128,2048]{1,0:T(8,128)(2,1)S(1)}, u32[]{:S(2)}, u32[]{:S(2)}) collective-permute-start(bf16[128,2048]{1,0:T(8,128)(2,1)S(1)} %collective-permute-done.49), channel_id=1, source_target_pairs={{0,1},{1,0},{2,3},{3,2},{4,5},{5,4},{6,7},{7,6},{8,9},{9,8},{10,11... | collective-permute-start | bytes 1572872 | tf_op jit(solution)/shard_map/ppermute | solution.py:45
  426.9 20.0 %collective-permute-start.52 = (bf16[128,2048]{1,0:T(8,128)(2,1)S(1)}, bf16[128,2048]{1,0:T(8,128)(2,1)S(1)}, u32[]{:S(2)}, u32[]{:S(2)}) collective-permute-start(bf16[128,2048]{1,0:T(8,128)(2,1)S(1)} %collective-permute-done.51), channel_id=1, source_target_pairs={{0,1},{1,0},{2,3},{3,2},{4,5},{5,4},{6,7},{7,6},{8,9},{9,8},{10,11... | collective-permute-start | bytes 1572872 | tf_op jit(solution)/shard_map/ppermute | solution.py:45
  451.8 207.8 %all-gather.8.cloned.1.call-start = ((), (), s32[]{:S(2)}) async-start(), calls=%async_computation.4 | async-start | bytes 18874368 | tf_op jit(solution)/shard_map/all_gather | solution.py:767
  470.5 12.5 %collective-permute-start.59 = (bf16[4,64,2048]{2,1,0:T(8,128)(2,1)S(1)}, bf16[4,64,2048]{2,1,0:T(8,128)(2,1)}, u32[]{:S(2)}, u32[]{:S(2)}) collective-permute-start(bf16[4,64,2048]{2,1,0:T(8,128)(2,1)S(1)} %dynamic-slice_bitcast_fusion.1), channel_id=1, source_target_pairs={{0,4},{4,0},{1,5},{5,1},{2,6},{6,2},{3,7},{7,3},{8,12},{12,8},{9,1... | collective-permute-start | bytes 3145736 | tf_op jit(solution)/shard_map/ppermute | solution.py:126
  475.9 13.0 %collective-permute-start.58 = (bf16[4,4,64,768]{3,2,1,0:T(8,128)(2,1)}, bf16[4,4,64,768]{3,2,1,0:T(8,128)(2,1)}, u32[]{:S(2)}, u32[]{:S(2)}) collective-permute-start(bf16[4,4,64,768]{3,2,1,0:T(8,128)(2,1)} %dynamic-slice_bitcast_fusion), channel_id=1, source_target_pairs={{0,4},{4,0},{1,5},{5,1},{2,6},{6,2},{3,7},{7,3},{8,12},{12,8},{9,1... | collective-permute-start | bytes 4718600 | tf_op jit(solution)/shard_map/ppermute | solution.py:126
  488.9 24.0 %collective-permute-start.57 = (bf16[128,1024]{1,0:T(8,128)(2,1)S(1)}, bf16[128,1024]{1,0:T(8,128)(2,1)S(1)}, u32[]{:S(2)}, u32[]{:S(2)}) collective-permute-start(bf16[128,1024]{1,0:T(8,128)(2,1)S(1)} %get-tuple-element.240), channel_id=1, source_target_pairs={{0,1},{1,2},{2,3},{3,0},{4,5},{5,6},{6,7},{7,4},{8,9},{9,10},{10,1... | collective-permute-start | bytes 786440 | tf_op jit(solution)/shard_map/ppermute | solution.py:110
  490.3 22.7 %collective-permute-start.61 = (bf16[128,1024]{1,0:T(8,128)(2,1)S(1)}, bf16[128,1024]{1,0:T(8,128)(2,1)S(1)}, u32[]{:S(2)}, u32[]{:S(2)}) collective-permute-start(bf16[128,1024]{1,0:T(8,128)(2,1)S(1)} %get-tuple-element.242), channel_id=1, source_target_pairs={{0,2},{1,3},{2,0},{3,1},{4,6},{5,7},{6,4},{7,5},{8,10},{9,11},{10,... | collective-permute-start | bytes 786440 | tf_op jit(solution)/shard_map/ppermute | solution.py:110
  491.3 21.6 %collective-permute-start.60 = (bf16[128,1024]{1,0:T(8,128)(2,1)S(1)}, bf16[128,1024]{1,0:T(8,128)(2,1)S(1)}, u32[]{:S(2)}, u32[]{:S(2)}) collective-permute-start(bf16[128,1024]{1,0:T(8,128)(2,1)S(1)} %get-tuple-element.243), channel_id=1, source_target_pairs={{0,3},{1,0},{2,1},{3,2},{4,7},{5,4},{6,5},{7,6},{8,11},{9,8},{10,9... | collective-permute-start | bytes 786440 | tf_op jit(solution)/shard_map/ppermute | solution.py:110
  492.8 36.1 %collective-permute-start.56 = (bf16[128,1024]{1,0:T(8,128)(2,1)S(1)}, bf16[128,1024]{1,0:T(8,128)(2,1)S(1)}, u32[]{:S(2)}, u32[]{:S(2)}) collective-permute-start(bf16[128,1024]{1,0:T(8,128)(2,1)S(1)} %get-tuple-element.245), channel_id=1, source_target_pairs={{0,2},{1,3},{2,0},{3,1},{4,6},{5,7},{6,4},{7,5},{8,10},{9,11},{10,... | collective-permute-start | bytes 786440 | tf_op jit(solution)/shard_map/ppermute | solution.py:110
  496.1 32.8 %collective-permute-start.55 = (bf16[128,1024]{1,0:T(8,128)(2,1)S(1)}, bf16[128,1024]{1,0:T(8,128)(2,1)S(1)}, u32[]{:S(2)}, u32[]{:S(2)}) collective-permute-start(bf16[128,1024]{1,0:T(8,128)(2,1)S(1)} %get-tuple-element.246), channel_id=1, source_target_pairs={{0,3},{1,0},{2,1},{3,2},{4,7},{5,4},{6,5},{7,6},{8,11},{9,8},{10,9... | collective-permute-start | bytes 786440 | tf_op jit(solution)/shard_map/ppermute | solution.py:110
  533.0 29.5 %collective-permute-start.65 = (bf16[4,2,64,768]{3,2,1,0:T(8,128)(2,1)}, bf16[4,2,64,768]{3,2,1,0:T(8,128)(2,1)}, u32[]{:S(2)}, u32[]{:S(2)}) collective-permute-start(bf16[4,2,64,768]{3,2,1,0:T(8,128)(2,1)} %dynamic-slice_bitcast_fusion.2), channel_id=1, source_target_pairs={{0,8},{8,0},{16,24},{24,16},{1,9},{9,1},{17,25},{25,17},{2,10},{10... | collective-permute-start | bytes 2359304 | tf_op jit(solution)/shard_map/ppermute | solution.py:126
  535.2 17.0 %collective-permute-start.66 = (bf16[2,64,2048]{2,1,0:T(8,128)(2,1)}, bf16[2,64,2048]{2,1,0:T(8,128)(2,1)}, u32[]{:S(2)}, u32[]{:S(2)}) collective-permute-start(bf16[2,64,2048]{2,1,0:T(8,128)(2,1)} %dynamic-slice_bitcast_fusion.3), channel_id=1, source_target_pairs={{0,16},{8,24},{16,0},{24,8},{1,17},{9,25},{17,1},{25,9},{2,18},{10... | collective-permute-start | bytes 1572872 | tf_op jit(solution)/shard_map/ppermute | solution.py:126
  539.9 22.6 %collective-permute-start.64 = (bf16[128,2048]{1,0:T(8,128)(2,1)}, bf16[128,2048]{1,0:T(8,128)(2,1)}, u32[]{:S(2)}, u32[]{:S(2)}) collective-permute-start(bf16[128,2048]{1,0:T(8,128)(2,1)} %get-tuple-element.218), channel_id=1, source_target_pairs={{0,0},{1,2},{2,1},{3,3},{4,4},{5,6},{6,5},{7,7},{8,8},{9,10},{10,9... | collective-permute-start | bytes 1572872 | tf_op jit(solution)/shard_map/ppermute | solution.py:45
  545.3 17.2 %collective-permute-start.63 = (bf16[128,2048]{1,0:T(8,128)(2,1)}, bf16[128,2048]{1,0:T(8,128)(2,1)}, u32[]{:S(2)}, u32[]{:S(2)}) collective-permute-start(bf16[128,2048]{1,0:T(8,128)(2,1)} %get-tuple-element.219), channel_id=1, source_target_pairs={{0,1},{1,0},{2,3},{3,2},{4,5},{5,4},{6,7},{7,6},{8,9},{9,8},{10,11... | collective-permute-start | bytes 1572872 | tf_op jit(solution)/shard_map/ppermute | solution.py:45
  550.7 29.4 %collective-permute-start.37 = (bf16[128,2048]{1,0:T(8,128)(2,1)S(1)}, bf16[128,2048]{1,0:T(8,128)(2,1)}, u32[]{:S(2)}, u32[]{:S(2)}) collective-permute-start(bf16[128,2048]{1,0:T(8,128)(2,1)S(1)} %get-tuple-element.232), channel_id=1, source_target_pairs={{0,0},{1,2},{2,1},{3,3},{4,4},{5,6},{6,5},{7,7},{8,8},{9,10},{10,9... | collective-permute-start | bytes 1572872 | tf_op jit(solution)/shard_map/ppermute | solution.py:45
  552.1 31.0 %collective-permute-start.36 = (bf16[128,2048]{1,0:T(8,128)(2,1)}, bf16[128,2048]{1,0:T(8,128)(2,1)}, u32[]{:S(2)}, u32[]{:S(2)}) collective-permute-start(bf16[128,2048]{1,0:T(8,128)(2,1)} %get-tuple-element.233), channel_id=1, source_target_pairs={{0,1},{1,0},{2,3},{3,2},{4,5},{5,4},{6,7},{7,6},{8,9},{9,8},{10,11... | collective-permute-start | bytes 1572872 | tf_op jit(solution)/shard_map/ppermute | solution.py:45
  568.5 20.1 %collective-permute-start.68 = (bf16[128,2048]{1,0:T(8,128)(2,1)}, bf16[128,2048]{1,0:T(8,128)(2,1)S(1)}, u32[]{:S(2)}, u32[]{:S(2)}) collective-permute-start(bf16[128,2048]{1,0:T(8,128)(2,1)} %get-tuple-element.216), channel_id=1, source_target_pairs={{0,0},{1,2},{2,1},{3,3},{4,4},{5,6},{6,5},{7,7},{8,8},{9,10},{10,9... | collective-permute-start | bytes 1572872 | tf_op jit(solution)/shard_map/ppermute | solution.py:45
  570.2 18.4 %collective-permute-start.67 = (bf16[128,2048]{1,0:T(8,128)(2,1)}, bf16[128,2048]{1,0:T(8,128)(2,1)}, u32[]{:S(2)}, u32[]{:S(2)}) collective-permute-start(bf16[128,2048]{1,0:T(8,128)(2,1)} %get-tuple-element.217), channel_id=1, source_target_pairs={{0,1},{1,0},{2,3},{3,2},{4,5},{5,4},{6,7},{7,6},{8,9},{9,8},{10,11... | collective-permute-start | bytes 1572872 | tf_op jit(solution)/shard_map/ppermute | solution.py:45
  604.2 12.7 %collective-permute-start.72 = (bf16[128,2048]{1,0:T(8,128)(2,1)}, bf16[128,2048]{1,0:T(8,128)(2,1)S(1)}, u32[]{:S(2)}, u32[]{:S(2)}) collective-permute-start(bf16[128,2048]{1,0:T(8,128)(2,1)} %get-tuple-element.214), channel_id=1, source_target_pairs={{0,0},{1,2},{2,1},{3,3},{4,4},{5,6},{6,5},{7,7},{8,8},{9,10},{10,9... | collective-permute-start | bytes 1572872 | tf_op jit(solution)/shard_map/ppermute | solution.py:45
  606.1 16.2 %collective-permute-start.71 = (bf16[128,2048]{1,0:T(8,128)(2,1)}, bf16[128,2048]{1,0:T(8,128)(2,1)}, u32[]{:S(2)}, u32[]{:S(2)}) collective-permute-start(bf16[128,2048]{1,0:T(8,128)(2,1)} %get-tuple-element.215), channel_id=1, source_target_pairs={{0,1},{1,0},{2,3},{3,2},{4,5},{5,4},{6,7},{7,6},{8,9},{9,8},{10,11... | collective-permute-start | bytes 1572872 | tf_op jit(solution)/shard_map/ppermute | solution.py:45
  612.9 18.5 %collective-permute-start.78 = (bf16[64,768]{1,0:T(8,128)(2,1)}, bf16[64,768]{1,0:T(8,128)(2,1)S(1)}, u32[]{:S(2)}, u32[]{:S(2)}) collective-permute-start(bf16[64,768]{1,0:T(8,128)(2,1)} %get-tuple-element.274), channel_id=1, source_target_pairs={{0,1},{1,2},{2,3},{3,0},{4,5},{5,6},{6,7},{7,4},{8,9},{9,10},{10,1... | collective-permute-start | bytes 294920 | tf_op jit(solution)/shard_map/ppermute | solution.py:110
  612.9 18.4 %collective-permute-start.77 = (bf16[64,768]{1,0:T(8,128)(2,1)}, bf16[64,768]{1,0:T(8,128)(2,1)S(1)}, u32[]{:S(2)}, u32[]{:S(2)}) collective-permute-start(bf16[64,768]{1,0:T(8,128)(2,1)} %get-tuple-element.275), channel_id=1, source_target_pairs={{0,2},{1,3},{2,0},{3,1},{4,6},{5,7},{6,4},{7,5},{8,10},{9,11},{10,... | collective-permute-start | bytes 294920 | tf_op jit(solution)/shard_map/ppermute | solution.py:110
  614.9 16.5 %collective-permute-start.76 = (bf16[64,768]{1,0:T(8,128)(2,1)S(1)}, bf16[64,768]{1,0:T(8,128)(2,1)S(1)}, u32[]{:S(2)}, u32[]{:S(2)}) collective-permute-start(bf16[64,768]{1,0:T(8,128)(2,1)S(1)} %get-tuple-element.276), channel_id=1, source_target_pairs={{0,3},{1,0},{2,1},{3,2},{4,7},{5,4},{6,5},{7,6},{8,11},{9,8},{10,9... | collective-permute-start | bytes 294920 | tf_op jit(solution)/shard_map/ppermute | solution.py:110
  616.9 22.4 %collective-permute-start.39 = (bf16[128,2048]{1,0:T(8,128)(2,1)}, bf16[128,2048]{1,0:T(8,128)(2,1)}, u32[]{:S(2)}, u32[]{:S(2)}) collective-permute-start(bf16[128,2048]{1,0:T(8,128)(2,1)} %get-tuple-element.230), channel_id=1, source_target_pairs={{0,0},{1,2},{2,1},{3,3},{4,4},{5,6},{6,5},{7,7},{8,8},{9,10},{10,9... | collective-permute-start | bytes 1572872 | tf_op jit(solution)/shard_map/ppermute | solution.py:45
  622.3 17.4 %collective-permute-start.38 = (bf16[128,2048]{1,0:T(8,128)(2,1)}, bf16[128,2048]{1,0:T(8,128)(2,1)}, u32[]{:S(2)}, u32[]{:S(2)}) collective-permute-start(bf16[128,2048]{1,0:T(8,128)(2,1)} %get-tuple-element.231), channel_id=1, source_target_pairs={{0,1},{1,0},{2,3},{3,2},{4,5},{5,4},{6,7},{7,6},{8,9},{9,8},{10,11... | collective-permute-start | bytes 1572872 | tf_op jit(solution)/shard_map/ppermute | solution.py:45
  631.7 13.5 %collective-permute-start.81 = (bf16[64,2560]{1,0:T(8,128)(2,1)S(1)}, bf16[64,2560]{1,0:T(8,128)(2,1)S(1)}, u32[]{:S(2)}, u32[]{:S(2)}) collective-permute-start(bf16[64,2560]{1,0:T(8,128)(2,1)S(1)} %constant_dynamic-update-slice_fusion.14), channel_id=1, source_target_pairs={{0,16},{8,24},{16,0},{24,8},{1,17},{9,25},{17,1},{25,9},{2,18},{10... | collective-permute-start | bytes 983048 | tf_op jit(solution)/shard_map/ppermute | solution.py:559
  647.2 33.2 %collective-permute-start.85 = (bf16[128,2560]{1,0:T(8,128)(2,1)}, bf16[128,2560]{1,0:T(8,128)(2,1)}, u32[]{:S(2)}, u32[]{:S(2)}) collective-permute-start(bf16[128,2560]{1,0:T(8,128)(2,1)} %pad_maximum_fusion.8), channel_id=1, source_target_pairs={{0,16},{8,24},{16,0},{24,8},{1,17},{9,25},{17,1},{25,9},{2,18},{10... | collective-permute-start | bytes 1966088 | tf_op jit(solution)/shard_map/ppermute | solution.py:559
  648.4 33.5 %collective-permute-start.86 = (bf16[128,2560]{1,0:T(8,128)(2,1)}, bf16[128,2560]{1,0:T(8,128)(2,1)}, u32[]{:S(2)}, u32[]{:S(2)}) collective-permute-start(bf16[128,2560]{1,0:T(8,128)(2,1)} %pad_maximum_fusion.9), channel_id=1, source_target_pairs={{0,8},{8,0},{16,24},{24,16},{1,9},{9,1},{17,25},{25,17},{2,10},{10... | collective-permute-start | bytes 1966088 | tf_op jit(solution)/shard_map/ppermute | solution.py:559
  654.2 31.1 %collective-permute-start.41 = (bf16[128,2048]{1,0:T(8,128)(2,1)}, bf16[128,2048]{1,0:T(8,128)(2,1)}, u32[]{:S(2)}, u32[]{:S(2)}) collective-permute-start(bf16[128,2048]{1,0:T(8,128)(2,1)} %get-tuple-element.226), channel_id=1, source_target_pairs={{0,1},{1,0},{2,3},{3,2},{4,5},{5,4},{6,7},{7,6},{8,9},{9,8},{10,11... | collective-permute-start | bytes 1572872 | tf_op jit(solution)/shard_map/ppermute | solution.py:45
  654.2 32.1 %collective-permute-start.42 = (bf16[128,2048]{1,0:T(8,128)(2,1)}, bf16[128,2048]{1,0:T(8,128)(2,1)}, u32[]{:S(2)}, u32[]{:S(2)}) collective-permute-start(bf16[128,2048]{1,0:T(8,128)(2,1)} %get-tuple-element.227), channel_id=1, source_target_pairs={{0,0},{1,2},{2,1},{3,3},{4,4},{5,6},{6,5},{7,7},{8,8},{9,10},{10,9... | collective-permute-start | bytes 1572872 | tf_op jit(solution)/shard_map/ppermute | solution.py:45
  659.6 25.2 %collective-permute-start.79 = (f32[1056]{0:T(1024)S(1)}, f32[1056]{0:T(1024)S(1)}, u32[]{:S(2)}, u32[]{:S(2)}) collective-permute-start(f32[1056]{0:T(1024)S(1)} %add_add_fusion.1), channel_id=1, source_target_pairs={{0,4},{4,0},{1,5},{5,1},{2,6},{6,2},{3,7},{7,3},{8,12},{12,8},{9,1... | collective-permute-start | bytes 12680 | tf_op jit(solution)/shard_map/ppermute | solution.py:33
  (94 other events, 1112.5 us)
Sparse Core Ops, SparseCore 0:
  35.1 32.7 all-gather.9
  130.8 92.0 all-gather.11
  304.6 54.1 reduce-scatter.4
  362.6 86.4 reduce-scatter.2
  451.9 55.6 all-gather.13
  531.0 108.2 all-gather.7

commit v7 on v6

--- a/solution.py
+++ b/solution.py
@@ -497,7 +497,7 @@
 
 
 def place_pair(own, which, chips, count, part, half):
-    step = min(64, part)
+    step = min(128, part)
     own = own.reshape(chips, 2, count, part, 2 * half)
     cols = count * 2 * half
     return pl.pallas_call(
@@ -506,6 +506,7 @@
         in_specs=[pl.BlockSpec((1, 2, count, step, half), lambda c, r: (c, 0, 0, r, which))],
         out_specs=pl.BlockSpec((step, cols), lambda c, r: (c * (part // step) + r, 0)),
         out_shape=jax.ShapeDtypeStruct((chips * part, cols), F32),
+        compiler_params=pltpu.CompilerParams(vmem_limit_bytes=32 * 2**20),
     )(own)
 
 

time: 724 us -> 721 us (level)
  Pallas kernels: 72 us -> 64.2 us
    pallas_call x2, Pallas kernels: 20.8 us -> 13 us  [place_pair(): pl.pallas_call(cast_pair, grid=(chips, part // step), in_specs=[pl.BlockS...]
    unnamed x140 -> x142, local copies, waits for them, and re-layouts: 18.8 us -> 24.6 us
  transfers between devices with their start and end apart: 95 -> 95, of which waited for: 24 -> 24; matrix products, arithmetic and copies ran while one was open for 23% -> 23% of each run, Pallas kernels for 9% -> 8%
where the time goes in v7:
time: 721 us; the launch traced here: 708 us
  waiting for transfers between devices  206 us (29%)
  starting transfers between devices  202 us (28%)
  matrix products  92.7 us (13%)
  other arithmetic  67.4 us (9%)
  Pallas kernels  64.2 us (9%)
  local copies, waits for them, and re-layouts  58.5 us (8%)
  between operations  16.2 us (2%)
    ppermute x24, waiting for transfers between devices, line_step(): lax.ppermute(first, 'fsdp', even)  118 us
    ppermute x24, starting transfers between devices, line_step(): lax.ppermute(first, 'fsdp', even)  85.6 us
    ppermute x18, waiting for transfers between devices, exchange_line(): lax.ppermute(piece_for((mine - e) % count), 'fsdp', [(i, (i - e) % count)...  69.8 us
    ppermute x24, starting transfers between devices, line_step(): lax.ppermute(second, 'fsdp', odd)  66.3 us
    dot_general x5, matrix products, mm_last(): lax.dot_general(a, b, (((1,), (1,)), ((), ())), preferred_element_type=F32)  40.3 us
    dot_general x5, matrix products, mm(): return jnp.dot(a, b, preferred_element_type=F32)  28 us
    ppermute x18, starting transfers between devices, exchange_line(): lax.ppermute(piece_for((mine - e) % count), 'fsdp', [(i, (i - e) % count)...  25.1 us
    unnamed x142, local copies, waits for them, and re-layouts  24.6 us
  transfers between devices with their start and end apart: 95, of which 24 were waited for; matrix products, arithmetic and copies ran while one was open for 23% of the time, Pallas kernels for 8%

profile of v7, /device:TPU:0, one launch (start us, length us, event | category | flops | bytes accessed | tf_op | source)
XLA Modules:
  0.0 707.5 jit_solution(14573486696704405703)
XLA Ops:
  7.3 3.1 collective-permute-start.1
  10.4 5.4 collective-permute-start
  21.0 13.1 %collective-permute-done.5 = bf16[64,768]{1,0:T(8,128)(2,1)S(1)} collective-permute-done((bf16[64,768]{1,0:T(8,128)(2,1)S(1)}, bf16[64,768]{1,0:T(8,128)(2,1)S(1)}, u32[]{:S(2)}, u32[]{:S(2)}) %collective-permute-start.5) | collective-permute-done | bytes 98336 | tf_op jit(solution)/shard_map/ppermute | solution.py:110
  35.2 5.3 collective-permute-start.2
  43.1 9.2 %collective-permute-done.3 = bf16[128,2048]{1,0:T(8,128)(2,1)} collective-permute-done((bf16[128,2048]{1,0:T(8,128)(2,1)}, bf16[128,2048]{1,0:T(8,128)(2,1)}, u32[]{:S(2)}, u32[]{:S(2)}) %collective-permute-start.3) | collective-permute-done | bytes 524320 | tf_op jit(solution)/shard_map/ppermute | solution.py:45
  57.2 5.4 collective-permute-start.8
  85.7 6.1 shard_map.237
  96.7 26.0 %collective-permute-done.15 = bf16[128,2048]{1,0:T(8,128)(2,1)} collective-permute-done((bf16[128,2048]{1,0:T(8,128)(2,1)}, bf16[128,2048]{1,0:T(8,128)(2,1)}, u32[]{:S(2)}, u32[]{:S(2)}) %collective-permute-start.15) | collective-permute-done | bytes 524320 | tf_op jit(solution)/shard_map/ppermute | solution.py:110
  133.5 5.4 collective-permute-start.18
  138.9 3.9 collective-permute-start.17
  142.8 12.1 %collective-permute-done.17 = bf16[128,2048]{1,0:T(8,128)(2,1)} collective-permute-done((bf16[128,2048]{1,0:T(8,128)(2,1)}, bf16[128,2048]{1,0:T(8,128)(2,1)}, u32[]{:S(2)}, u32[]{:S(2)}) %collective-permute-start.17) | collective-permute-done | bytes 524320 | tf_op jit(solution)/shard_map/ppermute | solution.py:45
  157.7 3.3 collective-permute-start.19
  161.0 10.9 %collective-permute-done.19.right = bf16[128,2048]{1,0:T(8,128)(2,1)S(1)} collective-permute-done((bf16[128,2048]{1,0:T(8,128)(2,1)S(1)}, bf16[128,2048]{1,0:T(8,128)(2,1)S(1)}, u32[]{:S(2)}, u32[]{:S(2)}) %collective-permute-start.19) | collective-permute-done | bytes 524320 | tf_op jit(solution)/shard_map/ppermute | solution.py:45
  171.9 5.4 collective-permute-start.22
  178.0 3.9 shard_map.238
  181.8 7.9 %collective-permute-done.21 = bf16[128,2048]{1,0:T(8,128)(2,1)} collective-permute-done((bf16[128,2048]{1,0:T(8,128)(2,1)}, bf16[128,2048]{1,0:T(8,128)(2,1)}, u32[]{:S(2)}, u32[]{:S(2)}) %collective-permute-start.21) | collective-permute-done | bytes 524320 | tf_op jit(solution)/shard_map/ppermute | solution.py:45
  191.7 9.3 %collective-permute-done.24 = bf16[128,2048]{1,0:T(8,128)(2,1)S(1)} collective-permute-done((bf16[128,2048]{1,0:T(8,128)(2,1)}, bf16[128,2048]{1,0:T(8,128)(2,1)S(1)}, u32[]{:S(2)}, u32[]{:S(2)}) %collective-permute-start.24) | collective-permute-done | bytes 524320 | tf_op jit(solution)/shard_map/ppermute | solution.py:45
  202.1 4.4 collective-permute-start.27
  206.4 9.4 %collective-permute-start.26 = (bf16[128,2048]{1,0:T(8,128)(2,1)S(1)}, bf16[128,2048]{1,0:T(8,128)(2,1)S(1)}, u32[]{:S(2)}, u32[]{:S(2)}) collective-permute-start(bf16[128,2048]{1,0:T(8,128)(2,1)S(1)} %collective-permute-done.25), channel_id=1, source_target_pairs={{0,1},{1,0},{2,3},{3,2},{4,5},{5,4},{6,7},{7,6},{8,9},{9,8},{10,11... | collective-permute-start | bytes 1572872 | tf_op jit(solution)/shard_map/ppermute | solution.py:45
  218.4 7.3 %collective-permute-done.26 = bf16[128,2048]{1,0:T(8,128)(2,1)S(1)} collective-permute-done((bf16[128,2048]{1,0:T(8,128)(2,1)S(1)}, bf16[128,2048]{1,0:T(8,128)(2,1)S(1)}, u32[]{:S(2)}, u32[]{:S(2)}) %collective-permute-start.26) | collective-permute-done | bytes 524320 | tf_op jit(solution)/shard_map/ppermute | solution.py:45
  229.6 5.4 collective-permute-start.30
  237.8 14.5 %fusion.79 = f32[1024,2048]{1,0:T(8,128)} fusion(bf16[1024,2048]{1,0:T(8,128)(2,1)} %constant_dynamic-update-slice_fusion, bf16[2048,2048]{1,0:T(8,128)(2,1)} %bitcast.299), kind=kOutput, calls=%fused_computation.253 | convolution fusion | flops 8589934592 | bytes 20971520 | tf_op jit(solution)/shard_map/dot_general | solution.py:21
  256.2 10.1 %collective-permute-done.32 = bf16[128,2048]{1,0:T(8,128)(2,1)S(1)} collective-permute-done((bf16[128,2048]{1,0:T(8,128)(2,1)}, bf16[128,2048]{1,0:T(8,128)(2,1)S(1)}, u32[]{:S(2)}, u32[]{:S(2)}) %collective-permute-start.32) | collective-permute-done | bytes 524320 | tf_op jit(solution)/shard_map/ppermute | solution.py:45
  275.1 4.5 collective-permute-done.34
  279.6 3.2 constant_dynamic-update-slice_fusion.5
  282.8 14.1 %multiply_convert_fusion = (bf16[1024,1024]{1,0:T(8,128)(2,1)}, bf16[1024,1024]{1,0:T(8,128)(2,1)}, bf16[1024,1024]{1,0:T(8,128)(2,1)S(1)}) fusion(f32[1024,2048]{1,0:T(8,128)} %fusion.79, bf16[1024,2048]{1,0:T(8,128)(2,1)} %constant_dynamic-update-slice_fusion.5, bf16[2048,2048]{1,0:T(8,128)(2,1)} %param.26, s32[]{:T(128)S(6)} %select_n.652), kind=kOutput, calls=%fused_computation.13 | convolution fusion | flops 4310695936 | bytes 23068676 | tf_op jit(solution)/shard_map/dot_general | solution.py:25
  298.2 6.2 convolution_convert_fusion.1
  306.4 6.0 fusion.13
  314.1 9.7 %convolution_convert_fusion.4 = bf16[512,2048]{1,0:T(8,128)(2,1)} fusion(bf16[512,2048]{1,0:T(8,128)(2,1)S(1)} %get-tuple-element.128, bf16[2048,2048]{1,0:T(8,128)(2,1)} %bitcast.300), kind=kOutput, calls=%fused_computation.30 | convolution fusion | flops 4296015872 | bytes 12582912 | tf_op jit(solution)/shard_map/dot_general | solution.py:25
  324.2 4.4 convert_add_fusion.1
  328.6 13.4 %convolution_convert_fusion = bf16[2048,2048]{1,0:T(8,128)(2,1)} fusion(bf16[1024,2048]{1,0:T(8,128)(2,1)} %constant_dynamic-update-slice_fusion, bf16[1024,2048]{1,0:T(8,128)(2,1)S(1)} %pad_maximum_fusion), kind=kOutput, calls=%fused_computation | convolution fusion | flops 8594128896 | bytes 16777216 | tf_op jit(solution)/shard_map/dot_general | solution.py:29
  342.7 4.0 collective-permute-done.40
  346.7 7.6 %convert_add_fusion = f32[512,2048]{1,0:T(8,128)S(1)} fusion(bf16[512,2048]{1,0:T(8,128)(2,1)S(1)} %collective-permute-done.40, bf16[512,2048]{1,0:T(8,128)(2,1)} %get-tuple-element.133, bf16[2048,2048]{1,0:T(8,128)(2,1)} %bitcast.301), kind=kOutput, calls=%fused_computation.11 | convolution fusion | flops 4297064448 | bytes 16777216 | tf_op jit(solution)/shard_map/dot_general | solution.py:25
  355.3 6.1 collective-permute-start.43
  361.3 12.2 %collective-permute-done.43 = bf16[128,2048]{1,0:T(8,128)(2,1)S(1)} collective-permute-done((bf16[128,2048]{1,0:T(8,128)(2,1)S(1)}, bf16[128,2048]{1,0:T(8,128)(2,1)S(1)}, u32[]{:S(2)}, u32[]{:S(2)}) %collective-permute-start.43) | collective-permute-done | bytes 524320 | tf_op jit(solution)/shard_map/ppermute | solution.py:45
  376.3 11.1 %collective-permute-done.47 = bf16[128,2048]{1,0:T(8,128)(2,1)S(1)} collective-permute-done((bf16[128,2048]{1,0:T(8,128)(2,1)S(1)}, bf16[128,2048]{1,0:T(8,128)(2,1)S(1)}, u32[]{:S(2)}, u32[]{:S(2)}) %collective-permute-start.47) | collective-permute-done | bytes 524320 | tf_op jit(solution)/shard_map/ppermute | solution.py:45
  388.3 6.0 collective-permute-start.45
  394.3 10.3 %collective-permute-done.45.right = bf16[128,2048]{1,0:T(8,128)(2,1)S(1)} collective-permute-done((bf16[128,2048]{1,0:T(8,128)(2,1)S(1)}, bf16[128,2048]{1,0:T(8,128)(2,1)S(1)}, u32[]{:S(2)}, u32[]{:S(2)}) %collective-permute-start.45) | collective-permute-done | bytes 524320 | tf_op jit(solution)/shard_map/ppermute | solution.py:45
  405.5 4.7 shard_map.239
  413.8 8.4 %collective-permute-done.50 = bf16[128,2048]{1,0:T(8,128)(2,1)S(1)} collective-permute-done((bf16[128,2048]{1,0:T(8,128)(2,1)}, bf16[128,2048]{1,0:T(8,128)(2,1)S(1)}, u32[]{:S(2)}, u32[]{:S(2)}) %collective-permute-start.50) | collective-permute-done | bytes 524320 | tf_op jit(solution)/shard_map/ppermute | solution.py:45
  422.8 4.0 collective-permute-start.53
  426.8 10.3 %collective-permute-start.52 = (bf16[128,2048]{1,0:T(8,128)(2,1)S(1)}, bf16[128,2048]{1,0:T(8,128)(2,1)S(1)}, u32[]{:S(2)}, u32[]{:S(2)}) collective-permute-start(bf16[128,2048]{1,0:T(8,128)(2,1)S(1)} %collective-permute-done.51), channel_id=1, source_target_pairs={{0,1},{1,0},{2,3},{3,2},{4,5},{5,4},{6,7},{7,6},{8,9},{9,8},{10,11... | collective-permute-start | bytes 1572872 | tf_op jit(solution)/shard_map/ppermute | solution.py:45
  437.9 8.8 %collective-permute-done.52 = bf16[128,2048]{1,0:T(8,128)(2,1)S(1)} collective-permute-done((bf16[128,2048]{1,0:T(8,128)(2,1)S(1)}, bf16[128,2048]{1,0:T(8,128)(2,1)S(1)}, u32[]{:S(2)}, u32[]{:S(2)}) %collective-permute-start.52) | collective-permute-done | bytes 524320 | tf_op jit(solution)/shard_map/ppermute | solution.py:45
  457.7 12.6 %shard_map.240 = (bf16[512,768]{1,0:T(8,128)(2,1)S(1)}, f32[1,128]{1,0:T(1,128)S(1)}, f32[1,128]{1,0:T(1,128)S(1)}) custom-call(f32[512,768]{1,0:T(8,128)S(1)} %copy-done.3, f32[512,768]{1,0:T(8,128)S(1)} %copy-done.3, f32[512,768]{1,0:T(8,128)S(1)} %copy-done.3, f32[512,512]{1,0:T(8,128)S(1)} %and_select_fusion.bias, f32[512,128]{1,0:T(8,128)S(1)} %copy.64.cosine.cos_own, ...), custom_call_target="tpu_custom_call" | custom-call | tf_op jit(solution)/shard_map/pallas_call | solution.py:378
  476.2 6.7 fusion.80.part
  496.2 3.0 fusion.10
  499.2 13.6 %collective-permute-done.61 = bf16[128,1024]{1,0:T(8,128)(2,1)S(1)} collective-permute-done((bf16[128,1024]{1,0:T(8,128)(2,1)S(1)}, bf16[128,1024]{1,0:T(8,128)(2,1)S(1)}, u32[]{:S(2)}, u32[]{:S(2)}) %collective-permute-start.61) | collective-permute-done | bytes 262176 | tf_op jit(solution)/shard_map/ppermute | solution.py:110
  512.9 15.9 %collective-permute-done.56 = bf16[128,1024]{1,0:T(8,128)(2,1)S(1)} collective-permute-done((bf16[128,1024]{1,0:T(8,128)(2,1)S(1)}, bf16[128,1024]{1,0:T(8,128)(2,1)S(1)}, u32[]{:S(2)}, u32[]{:S(2)}) %collective-permute-start.56) | collective-permute-done | bytes 262176 | tf_op jit(solution)/shard_map/ppermute | solution.py:110
  539.8 5.4 collective-permute-start.64
  545.2 3.0 collective-permute-start.63
  552.1 10.4 %collective-permute-start.36 = (bf16[128,2048]{1,0:T(8,128)(2,1)}, bf16[128,2048]{1,0:T(8,128)(2,1)}, u32[]{:S(2)}, u32[]{:S(2)}) collective-permute-start(bf16[128,2048]{1,0:T(8,128)(2,1)} %get-tuple-element.233), channel_id=1, source_target_pairs={{0,1},{1,0},{2,3},{3,2},{4,5},{5,4},{6,7},{7,6},{8,9},{9,8},{10,11... | collective-permute-start | bytes 1572872 | tf_op jit(solution)/shard_map/ppermute | solution.py:45
  570.2 6.6 collective-permute-start.67
  583.1 5.4 collective-permute-done.70
  590.8 10.3 %shard_map.241 = f32[2048,2048]{1,0:T(8,128)} custom-call(bf16[8,256,2048]{2,1,0:T(8,128)(2,1)} %bitcast.274), custom_call_target="tpu_custom_call" | custom-call | tf_op jit(solution)/shard_map/pallas_call | solution.py:581
  601.1 3.0 fusion.25
  616.8 5.4 collective-permute-start.39
  622.2 4.4 collective-permute-start.38
  626.6 4.6 shard_map.242
  651.1 3.1 fusion.35
  654.2 5.3 collective-permute-start.42
  659.5 5.8 copy-done.1
  665.3 6.5 shard_map.244
  671.8 6.5 shard_map.243
  691.0 9.1 %shard_map.245 = (f32[512,2048]{1,0:T(8,128)}, f32[512,512]{1,0:T(8,128)}, f32[512,512]{1,0:T(8,128)}, f32[512,2048]{1,0:T(8,128)}) custom-call(s32[2,8]{1,0:T(2,128)} %pad_add_fusion._, bf16[256,2560]{1,0:T(8,128)(2,1)} %copy-done.17, bf16[256,2560]{1,0:T(8,128)(2,1)} %copy-done.44, bf16[256,2560]{1,0:T(8,128)(2,1)} %copy-done.18, ...), custom_call_target="tpu_custom_call" | custom-call | tf_op jit(solution)/shard_map/pallas_call | solution.py:545
  (435 shorter events, 203.2 us)
Async XLA Ops:
  7.2 74.1 %all-gather.10.cloned.1.call-start = ((), (), s32[]{:S(2)}) async-start(), calls=%async_computation.5 | async-start | bytes 3538944 | tf_op jit(solution)/shard_map/all_gather | solution.py:642
  7.3 26.8 %collective-permute-start.1 = (bf16[128,2048]{1,0:T(8,128)(2,1)}, bf16[128,2048]{1,0:T(8,128)(2,1)}, u32[]{:S(2)}, u32[]{:S(2)}) collective-permute-start(bf16[128,2048]{1,0:T(8,128)(2,1)} %wide.1), channel_id=1, source_target_pairs={{0,1},{1,0},{2,3},{3,2},{4,5},{5,4},{6,7},{7,6},{8,9},{9,8},{10,11... | collective-permute-start | bytes 1572872 | tf_op jit(solution)/shard_map/ppermute | solution.py:45
  10.4 23.7 %collective-permute-start = (bf16[128,2048]{1,0:T(8,128)(2,1)}, bf16[128,2048]{1,0:T(8,128)(2,1)}, u32[]{:S(2)}, u32[]{:S(2)}) collective-permute-start(bf16[128,2048]{1,0:T(8,128)(2,1)} %wide.1), channel_id=1, source_target_pairs={{0,0},{1,2},{2,1},{3,3},{4,4},{5,6},{6,5},{7,7},{8,8},{9,10},{10,9... | collective-permute-start | bytes 1572872 | tf_op jit(solution)/shard_map/ppermute | solution.py:45
  17.6 16.5 %collective-permute-start.5 = (bf16[64,768]{1,0:T(8,128)(2,1)S(1)}, bf16[64,768]{1,0:T(8,128)(2,1)S(1)}, u32[]{:S(2)}, u32[]{:S(2)}) collective-permute-start(bf16[64,768]{1,0:T(8,128)(2,1)S(1)} %pad_maximum_fusion.19), channel_id=1, source_target_pairs={{0,2},{1,3},{2,0},{3,1},{4,6},{5,7},{6,4},{7,5},{8,10},{9,11},{10,... | collective-permute-start | bytes 294920 | tf_op jit(solution)/shard_map/ppermute | solution.py:110
  17.7 16.4 %collective-permute-start.4 = (bf16[64,768]{1,0:T(8,128)(2,1)S(1)}, bf16[64,768]{1,0:T(8,128)(2,1)S(1)}, u32[]{:S(2)}, u32[]{:S(2)}) collective-permute-start(bf16[64,768]{1,0:T(8,128)(2,1)S(1)} %pad_maximum_fusion.18), channel_id=1, source_target_pairs={{0,3},{1,0},{2,1},{3,2},{4,7},{5,4},{6,5},{7,6},{8,11},{9,8},{10,9... | collective-permute-start | bytes 294920 | tf_op jit(solution)/shard_map/ppermute | solution.py:110
  20.4 13.7 %collective-permute-start.6 = (bf16[64,768]{1,0:T(8,128)(2,1)S(1)}, bf16[64,768]{1,0:T(8,128)(2,1)S(1)}, u32[]{:S(2)}, u32[]{:S(2)}) collective-permute-start(bf16[64,768]{1,0:T(8,128)(2,1)S(1)} %pad_maximum_fusion.20), channel_id=1, source_target_pairs={{0,1},{1,2},{2,3},{3,0},{4,5},{5,6},{6,7},{7,4},{8,9},{9,10},{10,1... | collective-permute-start | bytes 294920 | tf_op jit(solution)/shard_map/ppermute | solution.py:110
  35.0 202.8 %all-gather.12.cloned.1.call-start = ((), (), s32[]{:S(2)}) async-start(), calls=%async_computation.6 | async-start | bytes 10485760 | tf_op jit(solution)/shard_map/all_gather | solution.py:694
  40.5 11.8 %collective-permute-start.3 = (bf16[128,2048]{1,0:T(8,128)(2,1)}, bf16[128,2048]{1,0:T(8,128)(2,1)}, u32[]{:S(2)}, u32[]{:S(2)}) collective-permute-start(bf16[128,2048]{1,0:T(8,128)(2,1)} %collective-permute-done), channel_id=1, source_target_pairs={{0,1},{1,0},{2,3},{3,2},{4,5},{5,4},{6,7},{7,6},{8,9},{9,8},{10,11... | collective-permute-start | bytes 1572872 | tf_op jit(solution)/shard_map/ppermute | solution.py:45
  52.3 13.1 %collective-permute-start.11 = (bf16[1056]{0:T(1024)(128)(2,1)S(1)}, bf16[1056]{0:T(1024)(128)(2,1)S(1)}, u32[]{:S(2)}, u32[]{:S(2)}) collective-permute-start(bf16[1056]{0:T(1024)(128)(2,1)S(1)} %concatenate.92), channel_id=1, source_target_pairs={{0,1},{1,2},{2,3},{3,0},{4,5},{5,6},{6,7},{7,4},{8,9},{9,10},{10,1... | collective-permute-start | bytes 6344 | tf_op jit(solution)/shard_map/ppermute | solution.py:110
  52.7 12.5 %collective-permute-start.10 = (bf16[1056]{0:T(1024)(128)(2,1)S(1)}, bf16[1056]{0:T(1024)(128)(2,1)S(1)}, u32[]{:S(2)}, u32[]{:S(2)}) collective-permute-start(bf16[1056]{0:T(1024)(128)(2,1)S(1)} %concatenate.92), channel_id=1, source_target_pairs={{0,2},{1,3},{2,0},{3,1},{4,6},{5,7},{6,4},{7,5},{8,10},{9,11},{10,... | collective-permute-start | bytes 6344 | tf_op jit(solution)/shard_map/ppermute | solution.py:110
  71.4 25.2 %collective-permute-start.14 = (bf16[128,2048]{1,0:T(8,128)(2,1)}, bf16[128,2048]{1,0:T(8,128)(2,1)}, u32[]{:S(2)}, u32[]{:S(2)}) collective-permute-start(bf16[128,2048]{1,0:T(8,128)(2,1)} %pad_maximum_fusion.11), channel_id=1, source_target_pairs={{0,3},{1,0},{2,1},{3,2},{4,7},{5,4},{6,5},{7,6},{8,11},{9,8},{10,9... | collective-permute-start | bytes 1572872 | tf_op jit(solution)/shard_map/ppermute | solution.py:110
  74.5 48.2 %collective-permute-start.15 = (bf16[128,2048]{1,0:T(8,128)(2,1)}, bf16[128,2048]{1,0:T(8,128)(2,1)}, u32[]{:S(2)}, u32[]{:S(2)}) collective-permute-start(bf16[128,2048]{1,0:T(8,128)(2,1)} %pad_maximum_fusion.12), channel_id=1, source_target_pairs={{0,2},{1,3},{2,0},{3,1},{4,6},{5,7},{6,4},{7,5},{8,10},{9,11},{10,... | collective-permute-start | bytes 1572872 | tf_op jit(solution)/shard_map/ppermute | solution.py:110
  78.1 44.6 %collective-permute-start.16 = (bf16[128,2048]{1,0:T(8,128)(2,1)}, bf16[128,2048]{1,0:T(8,128)(2,1)}, u32[]{:S(2)}, u32[]{:S(2)}) collective-permute-start(bf16[128,2048]{1,0:T(8,128)(2,1)} %pad_maximum_fusion.13), channel_id=1, source_target_pairs={{0,1},{1,2},{2,3},{3,0},{4,5},{5,6},{6,7},{7,4},{8,9},{9,10},{10,1... | collective-permute-start | bytes 1572872 | tf_op jit(solution)/shard_map/ppermute | solution.py:110
  93.3 29.4 %collective-permute-start.13 = (bf16[128,2048]{1,0:T(8,128)(2,1)S(1)}, bf16[128,2048]{1,0:T(8,128)(2,1)}, u32[]{:S(2)}, u32[]{:S(2)}) collective-permute-start(bf16[128,2048]{1,0:T(8,128)(2,1)S(1)} %get-tuple-element.238), channel_id=1, source_target_pairs={{0,0},{1,2},{2,1},{3,3},{4,4},{5,6},{6,5},{7,7},{8,8},{9,10},{10,9... | collective-permute-start | bytes 1572872 | tf_op jit(solution)/shard_map/ppermute | solution.py:45
  95.3 27.4 %collective-permute-start.12 = (bf16[128,2048]{1,0:T(8,128)(2,1)S(1)}, bf16[128,2048]{1,0:T(8,128)(2,1)}, u32[]{:S(2)}, u32[]{:S(2)}) collective-permute-start(bf16[128,2048]{1,0:T(8,128)(2,1)S(1)} %get-tuple-element.239), channel_id=1, source_target_pairs={{0,1},{1,0},{2,3},{3,2},{4,5},{5,4},{6,7},{7,6},{8,9},{9,8},{10,11... | collective-permute-start | bytes 1572872 | tf_op jit(solution)/shard_map/ppermute | solution.py:45
  130.7 321.0 %reduce-scatter.5.cloned.1.call-start = ((), (), s32[]{:S(2)}) async-start(), calls=%async_computation.3 | async-start | bytes 5242880 | tf_op jit(solution)/shard_map/reduce_scatter | solution.py:717
  138.9 16.0 %collective-permute-start.17 = (bf16[128,2048]{1,0:T(8,128)(2,1)}, bf16[128,2048]{1,0:T(8,128)(2,1)}, u32[]{:S(2)}, u32[]{:S(2)}) collective-permute-start(bf16[128,2048]{1,0:T(8,128)(2,1)} %get-tuple-element.237), channel_id=1, source_target_pairs={{0,1},{1,0},{2,3},{3,2},{4,5},{5,4},{6,7},{7,6},{8,9},{9,8},{10,11... | collective-permute-start | bytes 1572872 | tf_op jit(solution)/shard_map/ppermute | solution.py:45
  157.7 14.2 %collective-permute-start.19 = (bf16[128,2048]{1,0:T(8,128)(2,1)S(1)}, bf16[128,2048]{1,0:T(8,128)(2,1)S(1)}, u32[]{:S(2)}, u32[]{:S(2)}) collective-permute-start(bf16[128,2048]{1,0:T(8,128)(2,1)S(1)} %get-tuple-element.235), channel_id=1, source_target_pairs={{0,1},{1,0},{2,3},{3,2},{4,5},{5,4},{6,7},{7,6},{8,9},{9,8},{10,11... | collective-permute-start | bytes 1572872 | tf_op jit(solution)/shard_map/ppermute | solution.py:45
  177.3 12.3 %collective-permute-start.21 = (bf16[128,2048]{1,0:T(8,128)(2,1)}, bf16[128,2048]{1,0:T(8,128)(2,1)}, u32[]{:S(2)}, u32[]{:S(2)}) collective-permute-start(bf16[128,2048]{1,0:T(8,128)(2,1)} %base.1), channel_id=1, source_target_pairs={{0,1},{1,0},{2,3},{3,2},{4,5},{5,4},{6,7},{7,6},{8,9},{9,8},{10,11... | collective-permute-start | bytes 1572872 | tf_op jit(solution)/shard_map/ppermute | solution.py:45
  190.0 12.1 %collective-permute-start.23 = (bf16[128,2048]{1,0:T(8,128)(2,1)}, bf16[128,2048]{1,0:T(8,128)(2,1)S(1)}, u32[]{:S(2)}, u32[]{:S(2)}) collective-permute-start(bf16[128,2048]{1,0:T(8,128)(2,1)} %get-tuple-element.122), channel_id=1, source_target_pairs={{0,0},{1,2},{2,1},{3,3},{4,4},{5,6},{6,5},{7,7},{8,8},{9,10},{10,9... | collective-permute-start | bytes 1572872 | tf_op jit(solution)/shard_map/ppermute | solution.py:45
  202.1 13.8 %collective-permute-start.27 = (bf16[128,2048]{1,0:T(8,128)(2,1)S(1)}, bf16[128,2048]{1,0:T(8,128)(2,1)S(1)}, u32[]{:S(2)}, u32[]{:S(2)}) collective-permute-start(bf16[128,2048]{1,0:T(8,128)(2,1)S(1)} %collective-permute-done.23), channel_id=1, source_target_pairs={{0,1},{1,0},{2,3},{3,2},{4,5},{5,4},{6,7},{7,6},{8,9},{9,8},{10,11... | collective-permute-start | bytes 1572872 | tf_op jit(solution)/shard_map/ppermute | solution.py:45
  206.4 19.3 %collective-permute-start.26 = (bf16[128,2048]{1,0:T(8,128)(2,1)S(1)}, bf16[128,2048]{1,0:T(8,128)(2,1)S(1)}, u32[]{:S(2)}, u32[]{:S(2)}) collective-permute-start(bf16[128,2048]{1,0:T(8,128)(2,1)S(1)} %collective-permute-done.25), channel_id=1, source_target_pairs={{0,1},{1,0},{2,3},{3,2},{4,5},{5,4},{6,7},{7,6},{8,9},{9,8},{10,11... | collective-permute-start | bytes 1572872 | tf_op jit(solution)/shard_map/ppermute | solution.py:45
  229.6 22.7 %collective-permute-start.30 = (bf16[128,2048]{1,0:T(8,128)(2,1)}, bf16[128,2048]{1,0:T(8,128)(2,1)}, u32[]{:S(2)}, u32[]{:S(2)}) collective-permute-start(bf16[128,2048]{1,0:T(8,128)(2,1)} %collective-permute-done.21), channel_id=1, source_target_pairs={{0,0},{1,2},{2,1},{3,3},{4,4},{5,6},{6,5},{7,7},{8,8},{9,10},{10,9... | collective-permute-start | bytes 1572872 | tf_op jit(solution)/shard_map/ppermute | solution.py:45
  235.0 17.3 %collective-permute-start.31 = (bf16[128,2048]{1,0:T(8,128)(2,1)}, bf16[128,2048]{1,0:T(8,128)(2,1)}, u32[]{:S(2)}, u32[]{:S(2)}) collective-permute-start(bf16[128,2048]{1,0:T(8,128)(2,1)} %collective-permute-done.22), channel_id=1, source_target_pairs={{0,1},{1,0},{2,3},{3,2},{4,5},{5,4},{6,7},{7,6},{8,9},{9,8},{10,11... | collective-permute-start | bytes 1572872 | tf_op jit(solution)/shard_map/ppermute | solution.py:45
  252.3 14.0 %collective-permute-start.32 = (bf16[128,2048]{1,0:T(8,128)(2,1)}, bf16[128,2048]{1,0:T(8,128)(2,1)S(1)}, u32[]{:S(2)}, u32[]{:S(2)}) collective-permute-start(bf16[128,2048]{1,0:T(8,128)(2,1)} %collective-permute-done.30), channel_id=1, source_target_pairs={{0,1},{1,0},{2,3},{3,2},{4,5},{5,4},{6,7},{7,6},{8,9},{9,8},{10,11... | collective-permute-start | bytes 1572872 | tf_op jit(solution)/shard_map/ppermute | solution.py:45
  253.4 12.9 %collective-permute-start.33 = (bf16[128,2048]{1,0:T(8,128)(2,1)}, bf16[128,2048]{1,0:T(8,128)(2,1)S(1)}, u32[]{:S(2)}, u32[]{:S(2)}) collective-permute-start(bf16[128,2048]{1,0:T(8,128)(2,1)} %collective-permute-done.31), channel_id=1, source_target_pairs={{0,0},{1,2},{2,1},{3,3},{4,4},{5,6},{6,5},{7,7},{8,8},{9,10},{10,9... | collective-permute-start | bytes 1572872 | tf_op jit(solution)/shard_map/ppermute | solution.py:45
  304.4 178.5 %reduce-scatter.3.cloned.1.call-start = ((), (), s32[]{:S(2)}) async-start(), calls=%async_computation.2 | async-start | bytes 10485760 | tf_op jit(solution)/shard_map/reduce_scatter | solution.py:723
  342.0 248.8 %all-gather.14.cloned.1.call-start = ((), (), s32[]{:S(2)}) async-start(), calls=%async_computation.7 | async-start | bytes 9437184 | tf_op jit(solution)/shard_map/all_gather | solution.py:740
  355.3 18.2 %collective-permute-start.43 = (bf16[128,2048]{1,0:T(8,128)(2,1)S(1)}, bf16[128,2048]{1,0:T(8,128)(2,1)S(1)}, u32[]{:S(2)}, u32[]{:S(2)}) collective-permute-start(bf16[128,2048]{1,0:T(8,128)(2,1)S(1)} %get-tuple-element.225), channel_id=1, source_target_pairs={{0,1},{1,0},{2,3},{3,2},{4,5},{5,4},{6,7},{7,6},{8,9},{9,8},{10,11... | collective-permute-start | bytes 1572872 | tf_op jit(solution)/shard_map/ppermute | solution.py:45
  373.8 13.6 %collective-permute-start.47 = (bf16[128,2048]{1,0:T(8,128)(2,1)S(1)}, bf16[128,2048]{1,0:T(8,128)(2,1)S(1)}, u32[]{:S(2)}, u32[]{:S(2)}) collective-permute-start(bf16[128,2048]{1,0:T(8,128)(2,1)S(1)} %get-tuple-element.222), channel_id=1, source_target_pairs={{0,1},{1,0},{2,3},{3,2},{4,5},{5,4},{6,7},{7,6},{8,9},{9,8},{10,11... | collective-permute-start | bytes 1572872 | tf_op jit(solution)/shard_map/ppermute | solution.py:45
  375.6 11.8 %collective-permute-start.44 = (bf16[128,2048]{1,0:T(8,128)(2,1)S(1)}, bf16[128,2048]{1,0:T(8,128)(2,1)S(1)}, u32[]{:S(2)}, u32[]{:S(2)}) collective-permute-start(bf16[128,2048]{1,0:T(8,128)(2,1)S(1)} %get-tuple-element.223), channel_id=1, source_target_pairs={{0,0},{1,2},{2,1},{3,3},{4,4},{5,6},{6,5},{7,7},{8,8},{9,10},{10,9... | collective-permute-start | bytes 1572872 | tf_op jit(solution)/shard_map/ppermute | solution.py:45
  388.3 16.3 %collective-permute-start.45 = (bf16[128,2048]{1,0:T(8,128)(2,1)S(1)}, bf16[128,2048]{1,0:T(8,128)(2,1)S(1)}, u32[]{:S(2)}, u32[]{:S(2)}) collective-permute-start(bf16[128,2048]{1,0:T(8,128)(2,1)S(1)} %get-tuple-element.221), channel_id=1, source_target_pairs={{0,1},{1,0},{2,3},{3,2},{4,5},{5,4},{6,7},{7,6},{8,9},{9,8},{10,11... | collective-permute-start | bytes 1572872 | tf_op jit(solution)/shard_map/ppermute | solution.py:45
  410.2 11.9 %collective-permute-start.50 = (bf16[128,2048]{1,0:T(8,128)(2,1)}, bf16[128,2048]{1,0:T(8,128)(2,1)S(1)}, u32[]{:S(2)}, u32[]{:S(2)}) collective-permute-start(bf16[128,2048]{1,0:T(8,128)(2,1)} %get-tuple-element.137), channel_id=1, source_target_pairs={{0,1},{1,0},{2,3},{3,2},{4,5},{5,4},{6,7},{7,6},{8,9},{9,8},{10,11... | collective-permute-start | bytes 1572872 | tf_op jit(solution)/shard_map/ppermute | solution.py:45
  422.8 14.3 %collective-permute-start.53 = (bf16[128,2048]{1,0:T(8,128)(2,1)S(1)}, bf16[128,2048]{1,0:T(8,128)(2,1)S(1)}, u32[]{:S(2)}, u32[]{:S(2)}) collective-permute-start(bf16[128,2048]{1,0:T(8,128)(2,1)S(1)} %collective-permute-done.49), channel_id=1, source_target_pairs={{0,1},{1,0},{2,3},{3,2},{4,5},{5,4},{6,7},{7,6},{8,9},{9,8},{10,11... | collective-permute-start | bytes 1572872 | tf_op jit(solution)/shard_map/ppermute | solution.py:45
  426.8 19.9 %collective-permute-start.52 = (bf16[128,2048]{1,0:T(8,128)(2,1)S(1)}, bf16[128,2048]{1,0:T(8,128)(2,1)S(1)}, u32[]{:S(2)}, u32[]{:S(2)}) collective-permute-start(bf16[128,2048]{1,0:T(8,128)(2,1)S(1)} %collective-permute-done.51), channel_id=1, source_target_pairs={{0,1},{1,0},{2,3},{3,2},{4,5},{5,4},{6,7},{7,6},{8,9},{9,8},{10,11... | collective-permute-start | bytes 1572872 | tf_op jit(solution)/shard_map/ppermute | solution.py:45
  451.7 207.8 %all-gather.8.cloned.1.call-start = ((), (), s32[]{:S(2)}) async-start(), calls=%async_computation.4 | async-start | bytes 18874368 | tf_op jit(solution)/shard_map/all_gather | solution.py:768
  470.4 12.5 %collective-permute-start.59 = (bf16[4,64,2048]{2,1,0:T(8,128)(2,1)S(1)}, bf16[4,64,2048]{2,1,0:T(8,128)(2,1)}, u32[]{:S(2)}, u32[]{:S(2)}) collective-permute-start(bf16[4,64,2048]{2,1,0:T(8,128)(2,1)S(1)} %dynamic-slice_bitcast_fusion.1), channel_id=1, source_target_pairs={{0,4},{4,0},{1,5},{5,1},{2,6},{6,2},{3,7},{7,3},{8,12},{12,8},{9,1... | collective-permute-start | bytes 3145736 | tf_op jit(solution)/shard_map/ppermute | solution.py:126
  475.8 13.2 %collective-permute-start.58 = (bf16[4,4,64,768]{3,2,1,0:T(8,128)(2,1)}, bf16[4,4,64,768]{3,2,1,0:T(8,128)(2,1)}, u32[]{:S(2)}, u32[]{:S(2)}) collective-permute-start(bf16[4,4,64,768]{3,2,1,0:T(8,128)(2,1)} %dynamic-slice_bitcast_fusion), channel_id=1, source_target_pairs={{0,4},{4,0},{1,5},{5,1},{2,6},{6,2},{3,7},{7,3},{8,12},{12,8},{9,1... | collective-permute-start | bytes 4718600 | tf_op jit(solution)/shard_map/ppermute | solution.py:126
  488.9 23.9 %collective-permute-start.57 = (bf16[128,1024]{1,0:T(8,128)(2,1)S(1)}, bf16[128,1024]{1,0:T(8,128)(2,1)S(1)}, u32[]{:S(2)}, u32[]{:S(2)}) collective-permute-start(bf16[128,1024]{1,0:T(8,128)(2,1)S(1)} %get-tuple-element.240), channel_id=1, source_target_pairs={{0,1},{1,2},{2,3},{3,0},{4,5},{5,6},{6,7},{7,4},{8,9},{9,10},{10,1... | collective-permute-start | bytes 786440 | tf_op jit(solution)/shard_map/ppermute | solution.py:110
  490.2 22.7 %collective-permute-start.61 = (bf16[128,1024]{1,0:T(8,128)(2,1)S(1)}, bf16[128,1024]{1,0:T(8,128)(2,1)S(1)}, u32[]{:S(2)}, u32[]{:S(2)}) collective-permute-start(bf16[128,1024]{1,0:T(8,128)(2,1)S(1)} %get-tuple-element.242), channel_id=1, source_target_pairs={{0,2},{1,3},{2,0},{3,1},{4,6},{5,7},{6,4},{7,5},{8,10},{9,11},{10,... | collective-permute-start | bytes 786440 | tf_op jit(solution)/shard_map/ppermute | solution.py:110
  491.2 21.6 %collective-permute-start.60 = (bf16[128,1024]{1,0:T(8,128)(2,1)S(1)}, bf16[128,1024]{1,0:T(8,128)(2,1)S(1)}, u32[]{:S(2)}, u32[]{:S(2)}) collective-permute-start(bf16[128,1024]{1,0:T(8,128)(2,1)S(1)} %get-tuple-element.243), channel_id=1, source_target_pairs={{0,3},{1,0},{2,1},{3,2},{4,7},{5,4},{6,5},{7,6},{8,11},{9,8},{10,9... | collective-permute-start | bytes 786440 | tf_op jit(solution)/shard_map/ppermute | solution.py:110
  492.8 35.9 %collective-permute-start.56 = (bf16[128,1024]{1,0:T(8,128)(2,1)S(1)}, bf16[128,1024]{1,0:T(8,128)(2,1)S(1)}, u32[]{:S(2)}, u32[]{:S(2)}) collective-permute-start(bf16[128,1024]{1,0:T(8,128)(2,1)S(1)} %get-tuple-element.245), channel_id=1, source_target_pairs={{0,2},{1,3},{2,0},{3,1},{4,6},{5,7},{6,4},{7,5},{8,10},{9,11},{10,... | collective-permute-start | bytes 786440 | tf_op jit(solution)/shard_map/ppermute | solution.py:110
  496.0 32.7 %collective-permute-start.55 = (bf16[128,1024]{1,0:T(8,128)(2,1)S(1)}, bf16[128,1024]{1,0:T(8,128)(2,1)S(1)}, u32[]{:S(2)}, u32[]{:S(2)}) collective-permute-start(bf16[128,1024]{1,0:T(8,128)(2,1)S(1)} %get-tuple-element.246), channel_id=1, source_target_pairs={{0,3},{1,0},{2,1},{3,2},{4,7},{5,4},{6,5},{7,6},{8,11},{9,8},{10,9... | collective-permute-start | bytes 786440 | tf_op jit(solution)/shard_map/ppermute | solution.py:110
  532.8 29.6 %collective-permute-start.65 = (bf16[4,2,64,768]{3,2,1,0:T(8,128)(2,1)}, bf16[4,2,64,768]{3,2,1,0:T(8,128)(2,1)}, u32[]{:S(2)}, u32[]{:S(2)}) collective-permute-start(bf16[4,2,64,768]{3,2,1,0:T(8,128)(2,1)} %dynamic-slice_bitcast_fusion.2), channel_id=1, source_target_pairs={{0,8},{8,0},{16,24},{24,16},{1,9},{9,1},{17,25},{25,17},{2,10},{10... | collective-permute-start | bytes 2359304 | tf_op jit(solution)/shard_map/ppermute | solution.py:126
  535.0 17.0 %collective-permute-start.66 = (bf16[2,64,2048]{2,1,0:T(8,128)(2,1)}, bf16[2,64,2048]{2,1,0:T(8,128)(2,1)}, u32[]{:S(2)}, u32[]{:S(2)}) collective-permute-start(bf16[2,64,2048]{2,1,0:T(8,128)(2,1)} %dynamic-slice_bitcast_fusion.3), channel_id=1, source_target_pairs={{0,16},{8,24},{16,0},{24,8},{1,17},{9,25},{17,1},{25,9},{2,18},{10... | collective-permute-start | bytes 1572872 | tf_op jit(solution)/shard_map/ppermute | solution.py:126
  539.8 22.6 %collective-permute-start.64 = (bf16[128,2048]{1,0:T(8,128)(2,1)}, bf16[128,2048]{1,0:T(8,128)(2,1)}, u32[]{:S(2)}, u32[]{:S(2)}) collective-permute-start(bf16[128,2048]{1,0:T(8,128)(2,1)} %get-tuple-element.218), channel_id=1, source_target_pairs={{0,0},{1,2},{2,1},{3,3},{4,4},{5,6},{6,5},{7,7},{8,8},{9,10},{10,9... | collective-permute-start | bytes 1572872 | tf_op jit(solution)/shard_map/ppermute | solution.py:45
  545.2 17.2 %collective-permute-start.63 = (bf16[128,2048]{1,0:T(8,128)(2,1)}, bf16[128,2048]{1,0:T(8,128)(2,1)}, u32[]{:S(2)}, u32[]{:S(2)}) collective-permute-start(bf16[128,2048]{1,0:T(8,128)(2,1)} %get-tuple-element.219), channel_id=1, source_target_pairs={{0,1},{1,0},{2,3},{3,2},{4,5},{5,4},{6,7},{7,6},{8,9},{9,8},{10,11... | collective-permute-start | bytes 1572872 | tf_op jit(solution)/shard_map/ppermute | solution.py:45
  550.7 29.4 %collective-permute-start.37 = (bf16[128,2048]{1,0:T(8,128)(2,1)S(1)}, bf16[128,2048]{1,0:T(8,128)(2,1)}, u32[]{:S(2)}, u32[]{:S(2)}) collective-permute-start(bf16[128,2048]{1,0:T(8,128)(2,1)S(1)} %get-tuple-element.232), channel_id=1, source_target_pairs={{0,0},{1,2},{2,1},{3,3},{4,4},{5,6},{6,5},{7,7},{8,8},{9,10},{10,9... | collective-permute-start | bytes 1572872 | tf_op jit(solution)/shard_map/ppermute | solution.py:45
  552.1 31.0 %collective-permute-start.36 = (bf16[128,2048]{1,0:T(8,128)(2,1)}, bf16[128,2048]{1,0:T(8,128)(2,1)}, u32[]{:S(2)}, u32[]{:S(2)}) collective-permute-start(bf16[128,2048]{1,0:T(8,128)(2,1)} %get-tuple-element.233), channel_id=1, source_target_pairs={{0,1},{1,0},{2,3},{3,2},{4,5},{5,4},{6,7},{7,6},{8,9},{9,8},{10,11... | collective-permute-start | bytes 1572872 | tf_op jit(solution)/shard_map/ppermute | solution.py:45
  568.5 20.1 %collective-permute-start.68 = (bf16[128,2048]{1,0:T(8,128)(2,1)}, bf16[128,2048]{1,0:T(8,128)(2,1)S(1)}, u32[]{:S(2)}, u32[]{:S(2)}) collective-permute-start(bf16[128,2048]{1,0:T(8,128)(2,1)} %get-tuple-element.216), channel_id=1, source_target_pairs={{0,0},{1,2},{2,1},{3,3},{4,4},{5,6},{6,5},{7,7},{8,8},{9,10},{10,9... | collective-permute-start | bytes 1572872 | tf_op jit(solution)/shard_map/ppermute | solution.py:45
  570.2 18.4 %collective-permute-start.67 = (bf16[128,2048]{1,0:T(8,128)(2,1)}, bf16[128,2048]{1,0:T(8,128)(2,1)}, u32[]{:S(2)}, u32[]{:S(2)}) collective-permute-start(bf16[128,2048]{1,0:T(8,128)(2,1)} %get-tuple-element.217), channel_id=1, source_target_pairs={{0,1},{1,0},{2,3},{3,2},{4,5},{5,4},{6,7},{7,6},{8,9},{9,8},{10,11... | collective-permute-start | bytes 1572872 | tf_op jit(solution)/shard_map/ppermute | solution.py:45
  604.1 12.7 %collective-permute-start.72 = (bf16[128,2048]{1,0:T(8,128)(2,1)}, bf16[128,2048]{1,0:T(8,128)(2,1)S(1)}, u32[]{:S(2)}, u32[]{:S(2)}) collective-permute-start(bf16[128,2048]{1,0:T(8,128)(2,1)} %get-tuple-element.214), channel_id=1, source_target_pairs={{0,0},{1,2},{2,1},{3,3},{4,4},{5,6},{6,5},{7,7},{8,8},{9,10},{10,9... | collective-permute-start | bytes 1572872 | tf_op jit(solution)/shard_map/ppermute | solution.py:45
  606.1 16.1 %collective-permute-start.71 = (bf16[128,2048]{1,0:T(8,128)(2,1)}, bf16[128,2048]{1,0:T(8,128)(2,1)}, u32[]{:S(2)}, u32[]{:S(2)}) collective-permute-start(bf16[128,2048]{1,0:T(8,128)(2,1)} %get-tuple-element.215), channel_id=1, source_target_pairs={{0,1},{1,0},{2,3},{3,2},{4,5},{5,4},{6,7},{7,6},{8,9},{9,8},{10,11... | collective-permute-start | bytes 1572872 | tf_op jit(solution)/shard_map/ppermute | solution.py:45
  612.8 18.4 %collective-permute-start.78 = (bf16[64,768]{1,0:T(8,128)(2,1)}, bf16[64,768]{1,0:T(8,128)(2,1)S(1)}, u32[]{:S(2)}, u32[]{:S(2)}) collective-permute-start(bf16[64,768]{1,0:T(8,128)(2,1)} %get-tuple-element.274), channel_id=1, source_target_pairs={{0,1},{1,2},{2,3},{3,0},{4,5},{5,6},{6,7},{7,4},{8,9},{9,10},{10,1... | collective-permute-start | bytes 294920 | tf_op jit(solution)/shard_map/ppermute | solution.py:110
  612.8 18.3 %collective-permute-start.77 = (bf16[64,768]{1,0:T(8,128)(2,1)}, bf16[64,768]{1,0:T(8,128)(2,1)S(1)}, u32[]{:S(2)}, u32[]{:S(2)}) collective-permute-start(bf16[64,768]{1,0:T(8,128)(2,1)} %get-tuple-element.275), channel_id=1, source_target_pairs={{0,2},{1,3},{2,0},{3,1},{4,6},{5,7},{6,4},{7,5},{8,10},{9,11},{10,... | collective-permute-start | bytes 294920 | tf_op jit(solution)/shard_map/ppermute | solution.py:110
  614.8 16.4 %collective-permute-start.76 = (bf16[64,768]{1,0:T(8,128)(2,1)S(1)}, bf16[64,768]{1,0:T(8,128)(2,1)S(1)}, u32[]{:S(2)}, u32[]{:S(2)}) collective-permute-start(bf16[64,768]{1,0:T(8,128)(2,1)S(1)} %get-tuple-element.276), channel_id=1, source_target_pairs={{0,3},{1,0},{2,1},{3,2},{4,7},{5,4},{6,5},{7,6},{8,11},{9,8},{10,9... | collective-permute-start | bytes 294920 | tf_op jit(solution)/shard_map/ppermute | solution.py:110
  616.8 22.4 %collective-permute-start.39 = (bf16[128,2048]{1,0:T(8,128)(2,1)}, bf16[128,2048]{1,0:T(8,128)(2,1)}, u32[]{:S(2)}, u32[]{:S(2)}) collective-permute-start(bf16[128,2048]{1,0:T(8,128)(2,1)} %get-tuple-element.230), channel_id=1, source_target_pairs={{0,0},{1,2},{2,1},{3,3},{4,4},{5,6},{6,5},{7,7},{8,8},{9,10},{10,9... | collective-permute-start | bytes 1572872 | tf_op jit(solution)/shard_map/ppermute | solution.py:45
  622.2 17.5 %collective-permute-start.38 = (bf16[128,2048]{1,0:T(8,128)(2,1)}, bf16[128,2048]{1,0:T(8,128)(2,1)}, u32[]{:S(2)}, u32[]{:S(2)}) collective-permute-start(bf16[128,2048]{1,0:T(8,128)(2,1)} %get-tuple-element.231), channel_id=1, source_target_pairs={{0,1},{1,0},{2,3},{3,2},{4,5},{5,4},{6,7},{7,6},{8,9},{9,8},{10,11... | collective-permute-start | bytes 1572872 | tf_op jit(solution)/shard_map/ppermute | solution.py:45
  631.5 13.6 %collective-permute-start.81 = (bf16[64,2560]{1,0:T(8,128)(2,1)S(1)}, bf16[64,2560]{1,0:T(8,128)(2,1)S(1)}, u32[]{:S(2)}, u32[]{:S(2)}) collective-permute-start(bf16[64,2560]{1,0:T(8,128)(2,1)S(1)} %constant_dynamic-update-slice_fusion.14), channel_id=1, source_target_pairs={{0,16},{8,24},{16,0},{24,8},{1,17},{9,25},{17,1},{25,9},{2,18},{10... | collective-permute-start | bytes 983048 | tf_op jit(solution)/shard_map/ppermute | solution.py:560
  647.1 31.2 %collective-permute-start.85 = (bf16[128,2560]{1,0:T(8,128)(2,1)}, bf16[128,2560]{1,0:T(8,128)(2,1)}, u32[]{:S(2)}, u32[]{:S(2)}) collective-permute-start(bf16[128,2560]{1,0:T(8,128)(2,1)} %pad_maximum_fusion.8), channel_id=1, source_target_pairs={{0,16},{8,24},{16,0},{24,8},{1,17},{9,25},{17,1},{25,9},{2,18},{10... | collective-permute-start | bytes 1966088 | tf_op jit(solution)/shard_map/ppermute | solution.py:560
  648.4 31.3 %collective-permute-start.86 = (bf16[128,2560]{1,0:T(8,128)(2,1)}, bf16[128,2560]{1,0:T(8,128)(2,1)}, u32[]{:S(2)}, u32[]{:S(2)}) collective-permute-start(bf16[128,2560]{1,0:T(8,128)(2,1)} %pad_maximum_fusion.9), channel_id=1, source_target_pairs={{0,8},{8,0},{16,24},{24,16},{1,9},{9,1},{17,25},{25,17},{2,10},{10... | collective-permute-start | bytes 1966088 | tf_op jit(solution)/shard_map/ppermute | solution.py:560
  654.2 29.0 %collective-permute-start.41 = (bf16[128,2048]{1,0:T(8,128)(2,1)}, bf16[128,2048]{1,0:T(8,128)(2,1)}, u32[]{:S(2)}, u32[]{:S(2)}) collective-permute-start(bf16[128,2048]{1,0:T(8,128)(2,1)} %get-tuple-element.226), channel_id=1, source_target_pairs={{0,1},{1,0},{2,3},{3,2},{4,5},{5,4},{6,7},{7,6},{8,9},{9,8},{10,11... | collective-permute-start | bytes 1572872 | tf_op jit(solution)/shard_map/ppermute | solution.py:45
  654.2 30.0 %collective-permute-start.42 = (bf16[128,2048]{1,0:T(8,128)(2,1)}, bf16[128,2048]{1,0:T(8,128)(2,1)}, u32[]{:S(2)}, u32[]{:S(2)}) collective-permute-start(bf16[128,2048]{1,0:T(8,128)(2,1)} %get-tuple-element.227), channel_id=1, source_target_pairs={{0,0},{1,2},{2,1},{3,3},{4,4},{5,6},{6,5},{7,7},{8,8},{9,10},{10,9... | collective-permute-start | bytes 1572872 | tf_op jit(solution)/shard_map/ppermute | solution.py:45
  659.5 23.2 %collective-permute-start.79 = (f32[1056]{0:T(1024)S(1)}, f32[1056]{0:T(1024)S(1)}, u32[]{:S(2)}, u32[]{:S(2)}) collective-permute-start(f32[1056]{0:T(1024)S(1)} %add_add_fusion.1), channel_id=1, source_target_pairs={{0,4},{4,0},{1,5},{5,1},{2,6},{6,2},{3,7},{7,3},{8,12},{12,8},{9,1... | collective-permute-start | bytes 12680 | tf_op jit(solution)/shard_map/ppermute | solution.py:33
  (95 other events, 1123.0 us)
Sparse Core Ops, SparseCore 0:
  35.1 32.7 all-gather.9
  130.8 92.0 all-gather.11
  304.5 54.1 reduce-scatter.4
  362.5 86.4 reduce-scatter.2
  451.8 55.6 all-gather.13
  530.9 108.3 all-gather.7
